TPU v7x, 32 devices: a whole 2x2x4 slice. The times are simulated.
32 devices in a mesh: fsdp: 16 (over z, x, core), seq: 2 (over y).
Axes of the slice: x: 2, y: 2, z: 4, core: 2. Of those that a mesh axis runs over, the one named last changes fastest.
Arguments:
- queries: bfloat16 [4096, 3072], P(('fsdp', 'seq')), may hold values from -1000 to 1000
- keys: bfloat16 [4096, 3072], P(('fsdp', 'seq')), may hold values from -1000 to 1000
- values: bfloat16 [4096, 3072], P(('fsdp', 'seq')), may hold values from -6 to 6
- image_ids: int32 [16, 256], P('fsdp'), may hold values from 0 to 15, never falling along the last dimension, each value on 1 to 128 neighbouring positions
- q_gain: float32 [128], replicated, may hold values from 0.6 to 6
- k_gain: float32 [128], replicated, may hold values from 0.6 to 6
- w_out: bfloat16 [3072, 6144], P('fsdp', 'seq'), may hold values from -0.109375 to 0.109375
- grad_y: bfloat16 [4096, 6144], P('fsdp', 'seq'), may hold values from -6 to 6
Outputs:
- grad_queries: bfloat16 [4096, 24, 128], P('fsdp', 'seq')
- grad_keys: bfloat16 [4096, 24, 128], P('fsdp', 'seq')
- grad_values: bfloat16 [4096, 24, 128], P('fsdp', 'seq')
- grad_w: float32 [3072, 6144], P('fsdp', 'seq')
All inputs are finite; a program needn't handle non-finite values.
Results may differ from a plain program's by a relative error of at most 0.02.
The roundings to bfloat16 on the way count: a program that leaves them out, or rounds other values in their place, can miss the bound.
Values may be sent and summed in bfloat16 or wider, within the bound.
No kernel may reach another device: no remote copies, remote signals or barrier semaphores. Data moves between devices by JAX's collectives and lax.ppermute only.
A program may use at most 128 MiB of HBM per device.

v0:
```python
import jax
import jax.numpy as jnp
from jax import lax
from jax.sharding import PartitionSpec as P


def norm_parts(source, gain):
    wide = source.astype(jnp.float32)
    centred = wide - jnp.mean(wide, axis=-1, keepdims=True)
    scale_inv = lax.rsqrt(jnp.mean(centred * centred, axis=-1, keepdims=True) + 1e-06)
    x_hat = centred * scale_inv
    return (x_hat, scale_inv, (x_hat * gain).astype(jnp.bfloat16))


def norm_back(grad_n, x_hat, scale_inv, gain):
    scaled = grad_n * gain
    return scale_inv * (
        scaled
        - jnp.mean(scaled, axis=-1, keepdims=True)
        - x_hat * jnp.mean(scaled * x_hat, axis=-1, keepdims=True)
    )


def probabilities(normalized_queries, normalized_keys, same_image, scale_factor):
    scores = (
        jnp.einsum(
            "krt,irt->rki", normalized_queries, normalized_keys, preferred_element_type=jnp.float32
        )
        * scale_factor
    )
    scores = jnp.where(same_image[None], scores, -1e30)
    row_top = jnp.max(scores, axis=-1, keepdims=True)
    exp_terms = jnp.exp(scores - row_top)
    return exp_terms / jnp.sum(exp_terms, axis=-1, keepdims=True)


def local(queries, keys, values, image_ids, q_gain, k_gain, w_out, grad_y):
    head_dim = q_gain.shape[0]
    tok_rows = queries.shape[0]
    heads_all = queries.shape[1] // head_dim
    scale_factor = head_dim ** (-0.5)
    q_patch = queries.reshape(tok_rows, heads_all, head_dim)
    k_patch = keys.reshape(tok_rows, heads_all, head_dim)
    v_patch = values.reshape(tok_rows, heads_all, head_dim)
    q_local, k_local, value_shard = (
        lax.all_to_all(q_patch, "seq", split_axis=1, concat_axis=0, tiled=True),
        lax.all_to_all(k_patch, "seq", split_axis=1, concat_axis=0, tiled=True),
        lax.all_to_all(v_patch, "seq", split_axis=1, concat_axis=0, tiled=True),
    )
    seq_length = q_local.shape[0]
    local_heads = q_local.shape[1]
    image_row = image_ids[0]
    same_image = image_row[:, None] == image_row[None, :]
    q_hat, q_inv, normalized_queries = norm_parts(q_local, q_gain)
    k_hat, k_inv, normalized_keys = norm_parts(k_local, k_gain)
    prob_rows = probabilities(normalized_queries, normalized_keys, same_image, scale_factor)
    probs_reduced_precision = prob_rows.astype(jnp.bfloat16)
    attended = jnp.einsum(
        "tgi,itp->gtp", probs_reduced_precision, value_shard, preferred_element_type=jnp.float32
    ).astype(jnp.bfloat16)
    attended_flat = attended.reshape(seq_length, local_heads * head_dim)
    partial_g = jnp.einsum(
        "ld,cd->lc",
        grad_y,
        lax.all_gather(w_out, "fsdp", axis=0, tiled=True),
        preferred_element_type=jnp.float32,
    )
    grad_sum = lax.psum_scatter(
        partial_g.astype(jnp.bfloat16), "seq", scatter_dimension=1, tiled=True
    )
    attention_gradient = grad_sum.reshape(seq_length, local_heads, head_dim)
    grad_values = jnp.einsum(
        "jpw,pjy->wjy",
        probs_reduced_precision,
        attention_gradient,
        preferred_element_type=jnp.float32,
    ).astype(jnp.bfloat16)
    probability_gradient = jnp.einsum(
        "krt,irt->rki", attention_gradient, value_shard, preferred_element_type=jnp.float32
    )
    row_delta = jnp.sum(prob_rows * probability_gradient, axis=-1, keepdims=True)
    score_gradient = (prob_rows * (probability_gradient - row_delta) * scale_factor).astype(
        jnp.bfloat16
    )
    normed_query_gradient = jnp.einsum(
        "tgi,itp->gtp", score_gradient, normalized_keys, preferred_element_type=jnp.float32
    )
    normed_key_gradient = jnp.einsum(
        "jpw,pjy->wjy", score_gradient, normalized_queries, preferred_element_type=jnp.float32
    )
    grad_queries = norm_back(normed_query_gradient, q_hat, q_inv, q_gain).astype(jnp.bfloat16)
    grad_keys = norm_back(normed_key_gradient, k_hat, k_inv, k_gain).astype(jnp.bfloat16)
    partial_w = jnp.einsum(
        "lc,ld->cd",
        lax.all_gather(attended_flat, "seq", axis=1, tiled=True),
        grad_y,
        preferred_element_type=jnp.float32,
    )
    summed = lax.psum_scatter(partial_w, "fsdp", scatter_dimension=0, tiled=True)
    grad_w = summed * seq_length ** (-0.5)
    return (grad_queries, grad_keys, grad_values, grad_w)


def solution(mesh):
    in_specs = (
        P(("fsdp", "seq"), None),
        P(("fsdp", "seq"), None),
        P(("fsdp", "seq"), None),
        P("fsdp", None),
        P(),
        P(),
        P("fsdp", "seq"),
        P("fsdp", "seq"),
    )
    out_specs = (
        P("fsdp", "seq", None),
        P("fsdp", "seq", None),
        P("fsdp", "seq", None),
        P("fsdp", "seq"),
    )
    return jax.shard_map(local, mesh=mesh, in_specs=in_specs, out_specs=out_specs, check_vma=False)
```

profile of v0, /device:TPU:0, one launch (start us, length us, event | category | flops | bytes accessed | tf_op | source)
XLA Modules:
  0.0 551.5 jit_solution(13261056355898742364)
XLA Ops:
  7.2 0.0 copy-start
  7.2 0.0 copy-start.7
  7.2 0.0 all-gather.3.cloned.1.call-start
  7.2 0.7 all-gather.3.cloned.1.call-update
  7.9 0.5 copy-done.7
  8.4 1.2 copy.56
  9.6 4.4 all-to-all-start.2
  14.0 0.0 copy-done.8
  14.0 1.2 copy.46
  15.1 10.4 %all-to-all-done.2 = bf16[128,24,128]{0,2,1:T(8,128)(2,1)S(1)} async-done(((bf16[128,24,128]{0,2,1:T(8,128)(2,1)}), bf16[128,24,128]{0,2,1:T(8,128)(2,1)S(1)}, u32[]{:S(2)}, u32[]{:S(2)}) %all-to-all-start.2) | async-done | bytes 786464 | tf_op jit(solution)/shard_map/all_to_all | solution.py:48
  25.5 3.7 all-to-all-start.1
  29.2 2.3 copy.43
  31.5 0.0 copy-done.9
  31.5 0.1 broadcast_compare_fusion
  31.6 1.2 copy.58
  32.8 7.0 %all-to-all-done.1 = bf16[128,24,128]{0,2,1:T(8,128)(2,1)S(1)} async-done(((bf16[128,24,128]{0,2,1:T(8,128)(2,1)}), bf16[128,24,128]{0,2,1:T(8,128)(2,1)S(1)}, u32[]{:S(2)}, u32[]{:S(2)}) %all-to-all-start.1) | async-done | bytes 786464 | tf_op jit(solution)/shard_map/all_to_all | solution.py:47
  39.8 4.3 all-to-all-start
  44.1 0.0 copy-done.4
  44.2 0.0 all-gather.5.cloned.1.call-start
  44.2 1.4 copy.47
  45.6 0.5 reduce_sum.92
  46.1 0.9 multiply_reduce_fusion.1
  47.1 6.9 %all-to-all-done = bf16[128,24,128]{0,2,1:T(8,128)(2,1)} async-done(((bf16[128,24,128]{0,2,1:T(8,128)(2,1)}), bf16[128,24,128]{0,2,1:T(8,128)(2,1)}, u32[]{:S(2)}, u32[]{:S(2)}) %all-to-all-start) | async-done | bytes 786464 | tf_op jit(solution)/shard_map/all_to_all | solution.py:46
  54.1 1.4 copy.44
  55.5 0.5 reduce_sum.90
  56.0 0.0 copy-start.5
  56.0 0.9 multiply_reduce_fusion.2
  57.0 0.1 copy-done.5
  57.1 0.2 convert_element_type.98
  57.3 0.0 copy-start.10
  57.3 0.0 copy-start.11
  57.3 1.3 convert_element_type.96
  58.6 0.0 copy-start.2
  58.6 0.0 copy-done.10
  58.7 0.0 copy-done.11
  58.7 1.8 multiply_convert_fusion.1
  60.4 0.0 copy-done.2
  60.4 4.2 fusion.44
  64.7 3.5 convolution_convert_fusion.1
  68.1 0.0 all-gather.5.cloned.1.call-update
  68.2 0.0 reduce-scatter.3.cloned.1.call-start
  68.2 43.1 %all-gather.3.cloned.1.call-done = bf16[3072,3072]{1,0:T(8,128)(2,1)} async-done(((bf16[192,3072]{1,0:T(8,128)(2,1)}), bf16[3072,3072]{1,0:T(8,128)(2,1)}) %all-gather.3.cloned.1.call-update) | async-done | bytes 18874384 | tf_op jit(solution)/shard_map/all_gather | solution.py:65
  111.3 0.0 copy-done
  111.3 10.4 %convolution_convert_fusion = bf16[256,3072]{1,0:T(8,128)(2,1)} fusion(bf16[256,3072]{1,0:T(8,128)(2,1)S(1)} %copy-done, bf16[3072,3072]{1,0:T(8,128)(2,1)} %all-gather.3.cloned.1.call-done), kind=kOutput, calls=%fused_computation.2 | convolution fusion | flops 4832624640 | bytes 22020096 | tf_op jit(solution)/shard_map/ld,cd->lc/dot_general | solution.py:62
  121.7 0.0 reduce-scatter.3.cloned.1.call-update
  121.7 0.2 reduce-scatter.5.cloned.1.call-start
  122.0 18.7 %all-gather.5.cloned.1.call-done = bf16[256,3072]{0,1:T(8,128)(2,1)} async-done(((bf16[256,1536]{0,1:T(8,128)(2,1)}), bf16[256,3072]{0,1:T(8,128)(2,1)}) %all-gather.5.cloned.1.call-update) | async-done | bytes 1572880 | tf_op jit(solution)/shard_map/all_gather | solution.py:95
  140.7 16.7 %fusion.49 = f32[3072,3072]{1,0:T(8,128)} fusion(bf16[256,3072]{0,1:T(8,128)(2,1)} %all-gather.5.cloned.1.call-done, bf16[256,3072]{1,0:T(8,128)(2,1)S(1)} %copy-done), kind=kOutput, calls=%fused_computation.68 | convolution fusion | flops 4831838208 | bytes 40894464 | tf_op jit(solution)/shard_map/lc,ld->cd/dot_general | solution.py:93
  157.3 0.0 reduce-scatter.5.cloned.1.call-update
  157.3 11.7 %reduce-scatter.3.cloned.1.call-done = bf16[256,1536]{1,0:T(8,128)(2,1)} async-done(((bf16[256,3072]{1,0:T(8,128)(2,1)}), bf16[256,1536]{1,0:T(8,128)(2,1)}) %reduce-scatter.3.cloned.1.call-update) | async-done | bytes 786448 | tf_op jit(solution)/shard_map/reduce_scatter | solution.py:68
  169.0 1.4 copy.55
  170.4 0.0 copy-start.6
  170.4 2.8 fusion.33
  173.3 0.0 copy-done.6
  173.3 1.2 copy.67
  174.5 3.7 fusion.50
  178.2 9.6 %bitcast_reduce_fusion.1 = (f32[256,12]{0,1:T(8,128)S(1)}, f32[256,12]{0,1:T(8,128)S(1)}, f32[12,128,256]{2,1,0:T(8,128)}) fusion(f32[256,12]{0,1:T(8,128)S(1)} %bitcast.134, f32[256,12]{0,1:T(8,128)S(1)} %bitcast.137, f32[2,12,16,8,128]{4,3,2,1,0:T(8,128)S(1)} %bitcast.118, f32[128]{0:T(128)S(1)} %copy-done.10, ...), kind=kOutput, calls=%fused_computation.24 | convolution fusion | flops 209188096 | bytes 10285568 | tf_op jit(solution)/shard_map/tgi,itp->gtp/dot_general | solution.py:85
  187.8 3.0 fusion.20
  190.8 2.5 copy.65
  193.3 8.7 %bitcast_reduce_fusion = (f32[256,12]{0,1:T(8,128)S(1)}, f32[256,12]{0,1:T(8,128)S(1)}, f32[12,128,256]{2,1,0:T(8,128)S(1)}) fusion(f32[256,12]{0,1:T(8,128)S(1)} %bitcast.128, f32[256,12]{0,1:T(8,128)S(1)} %bitcast.131, f32[2,12,16,8,128]{4,3,2,1,0:T(8,128)S(1)} %bitcast.115, f32[128]{0:T(128)S(1)} %copy-done.11, ...), kind=kOutput, calls=%fused_computation.17 | convolution fusion | flops 209188096 | bytes 10285568 | tf_op jit(solution)/shard_map/jpw,pjy->wjy/dot_general | solution.py:88
  202.1 1.3 fusion.16
  203.4 2.6 copy.66
  206.0 335.6 %reduce-scatter.5.cloned.1.call-done = f32[192,3072]{1,0:T(8,128)} async-done(((f32[3072,3072]{1,0:T(8,128)}), f32[192,3072]{1,0:T(8,128)}) %reduce-scatter.5.cloned.1.call-update) | async-done | bytes 2359312 | tf_op jit(solution)/shard_map/reduce_scatter | solution.py:99
  541.6 3.3 broadcast_multiply_fusion
  (27 shorter events, 0.1 us)
Async XLA Ops:
  7.2 104.2 %copy-start = (bf16[256,3072]{1,0:T(8,128)(2,1)S(1)}, bf16[256,3072]{1,0:T(8,128)(2,1)}, u32[]{:S(2)}) copy-start(bf16[256,3072]{1,0:T(8,128)(2,1)} %param.15) | copy-start | bytes 4718596
  7.2 1.3 copy-start.7
  7.2 104.1 %all-gather.3.cloned.1.call-start = ((), (), s32[]{:S(2)}) async-start(), calls=%async_computation.5 | async-start | bytes 20054016 | tf_op jit(solution)/shard_map/all_gather | solution.py:65
  9.6 4.4 copy-start.8
  9.6 15.9 %all-to-all-start.2 = ((bf16[128,24,128]{0,2,1:T(8,128)(2,1)}), bf16[128,24,128]{0,2,1:T(8,128)(2,1)S(1)}, u32[]{:S(2)}, u32[]{:S(2)}) async-start(bf16[128,24,128]{0,2,1:T(8,128)(2,1)} %bitcast.12), calls=%async_computation.3 | async-start | bytes 1572864 | tf_op jit(solution)/shard_map/all_to_all | solution.py:48
  25.5 6.0 %copy-start.9 = (s32[1,256]{1,0:T(1,128)S(1)}, s32[1,256]{1,0:T(1,128)}, u32[]{:S(2)}) copy-start(s32[1,256]{1,0:T(1,128)} %param.11) | copy-start | bytes 3076
  25.5 14.3 %all-to-all-start.1 = ((bf16[128,24,128]{0,2,1:T(8,128)(2,1)}), bf16[128,24,128]{0,2,1:T(8,128)(2,1)S(1)}, u32[]{:S(2)}, u32[]{:S(2)}) async-start(bf16[128,24,128]{0,2,1:T(8,128)(2,1)} %bitcast.125), calls=%async_computation.1 | async-start | bytes 1572864 | tf_op jit(solution)/shard_map/all_to_all | solution.py:47
  39.8 4.3 copy-start.4
  39.8 14.3 %all-to-all-start = ((bf16[128,24,128]{0,2,1:T(8,128)(2,1)}), bf16[128,24,128]{0,2,1:T(8,128)(2,1)}, u32[]{:S(2)}, u32[]{:S(2)}) async-start(bf16[128,24,128]{0,2,1:T(8,128)(2,1)} %bitcast), calls=%async_computation | async-start | bytes 1572864 | tf_op jit(solution)/shard_map/all_to_all | solution.py:46
  44.2 96.5 %all-gather.5.cloned.1.call-start = ((), (), s32[]{:S(2)}) async-start(), calls=%async_computation.7 | async-start | bytes 2359296 | tf_op jit(solution)/shard_map/all_gather | solution.py:95
  56.0 1.1 copy-start.5
  57.3 1.4 copy-start.10
  57.3 1.4 copy-start.11
  58.6 1.8 copy-start.2
  68.2 100.9 %reduce-scatter.3.cloned.1.call-start = ((), (), s32[]{:S(2)}) async-start(), calls=%async_computation.6 | async-start | bytes 2359296 | tf_op jit(solution)/shard_map/reduce_scatter | solution.py:68
  121.7 419.9 %reduce-scatter.5.cloned.1.call-start = ((), (), s32[]{:S(2)}) async-start(), calls=%async_computation.8 | async-start | bytes 40108032 | tf_op jit(solution)/shard_map/reduce_scatter | solution.py:99
  170.4 2.9 copy-start.6
  174.5 3.7 copy-start.3
  203.3 341.6 %copy-start.1 = (bf16[256,3072]{1,0:T(8,128)(2,1)S(1)}, bf16[256,3072]{1,0:T(8,128)(2,1)}, u32[]{:S(2)}) copy-start(bf16[256,3072]{1,0:T(8,128)(2,1)} %param.15) | copy-start | bytes 4718596
Sparse Core Ops, SparseCore 0:
  9.6 101.6 all-gather.2
  113.4 27.1 all-gather.4
  142.9 26.0 reduce-scatter.2
  173.7 367.8 reduce-scatter.4
where the time goes:
time: 552 us; the launch traced here: 551 us
  waiting for transfers between devices  434 us (79%)
  matrix products  59.7 us (11%)
  local copies, waits for them, and re-layouts  17 us (3%)
  between operations  14.1 us (3%)
  other arithmetic  13.8 us (2%)
  starting transfers between devices  12.7 us (2%)
    reduce_scatter x1, waiting for transfers between devices, local(): lax.psum_scatter(partial_w, 'fsdp', scatter_dimension=0, tiled=True)  336 us
    all_gather x1, waiting for transfers between devices, local(): lax.all_gather(w_out, 'fsdp', axis=0, tiled=True)  43.1 us
    all_gather x1, waiting for transfers between devices, local(): lax.all_gather(attended_flat, 'seq', axis=1, tiled=True)  18.7 us
    dot_general x1, matrix products, local(): jnp.einsum('lc,ld->cd', lax.all_gather(attended_flat, 'seq', axis=1, tile...  16.7 us
    reduce_scatter x1, waiting for transfers between devices, local(): lax.psum_scatter(partial_g.astype(jnp.bfloat16), 'seq', scatter_dimension...  11.7 us
    unnamed x38, local copies, waits for them, and re-layouts  11.6 us
  transfers between devices with their start and end apart: 7, of which 7 were waited for; matrix products, arithmetic and copies ran while one was open for 16% of the time, Pallas kernels for 0%

commit v1 on v0

--- a/solution.py
+++ b/solution.py
@@ -1,7 +1,14 @@
+import functools
+
 import jax
 import jax.numpy as jnp
 from jax import lax
+from jax.experimental import pallas as pl
+from jax.experimental.pallas import tpu as pltpu
 from jax.sharding import PartitionSpec as P
+
+F32 = jnp.float32
+BF16 = jnp.bfloat16
 
 
 def norm_parts(source, gain):
@@ -34,7 +41,7 @@
     return exp_terms / jnp.sum(exp_terms, axis=-1, keepdims=True)
 
 
-def local(queries, keys, values, image_ids, q_gain, k_gain, w_out, grad_y):
+def local_any(queries, keys, values, image_ids, q_gain, k_gain, w_out, grad_y):
     head_dim = q_gain.shape[0]
     tok_rows = queries.shape[0]
     heads_all = queries.shape[1] // head_dim
@@ -101,6 +108,279 @@
     return (grad_queries, grad_keys, grad_values, grad_w)
 
 
+def dot_nt(a, b):
+    return lax.dot_general(a, b, (((1,), (1,)), ((), ())), preferred_element_type=F32)
+
+
+def dot_tn(a, b):
+    return lax.dot_general(a, b, (((0,), (0,)), ((), ())), preferred_element_type=F32)
+
+
+def dot_nn(a, b):
+    return jnp.dot(a, b, preferred_element_type=F32)
+
+
+def assemble(first, own, came):
+    return jnp.concatenate([jnp.where(first, own, came), jnp.where(first, came, own)], axis=0)
+
+
+def head_inputs(place, refs, h, dim):
+    q_ref, k_ref, v_ref, came_ref = refs
+    first = place[0] == 0
+    cols = slice(h * dim, (h + 1) * dim)
+    return [
+        assemble(first, ref[:, cols], came_ref[n, :, cols])
+        for n, ref in enumerate((q_ref, k_ref, v_ref))
+    ]
+
+
+def head_probs(q, k, qg, kg, same, scale):
+    q_hat, q_inv, qn = norm_parts(q, qg)
+    k_hat, k_inv, kn = norm_parts(k, kg)
+    scores = jnp.where(same, dot_nt(qn, kn) * scale, -1e30)
+    exp_terms = jnp.exp(scores - jnp.max(scores, axis=-1, keepdims=True))
+    probs = exp_terms / jnp.sum(exp_terms, axis=-1, keepdims=True)
+    return probs, q_hat, q_inv, qn, k_hat, k_inv, kn
+
+
+def forward_kernel(per, dim, place, q_ref, k_ref, v_ref, came_ref, row_ref, col_ref, qg_ref, kg_ref, even_ref, odd_ref):
+    same = col_ref[...] == row_ref[...]
+    done = []
+    for h in range(per):
+        q, k, v = head_inputs(place, (q_ref, k_ref, v_ref, came_ref), h, dim)
+        probs = head_probs(q, k, qg_ref[...], kg_ref[...], same, dim**-0.5)[0]
+        done.append(dot_nn(probs.astype(BF16), v).T.astype(BF16))
+    att = jnp.concatenate(done, axis=0)
+    half = att.shape[0] // 2
+    straight = (place[1] & 1) == 0
+    low, high = att[:half], att[half:]
+    even_ref[0] = jnp.where(straight, low, high)
+    odd_ref[0] = jnp.where(straight, high, low)
+
+
+def backward_kernel(per, dim, place, q_ref, k_ref, v_ref, came_ref, d_ref, row_ref, col_ref, qg_ref, kg_ref, gq_ref, gk_ref, gv_ref):
+    same = col_ref[...] == row_ref[...]
+    scale = dim**-0.5
+    straight = (place[1] & 1) == 0
+    one, two = d_ref[0, 0], d_ref[0, 1]
+    grad = jnp.concatenate([jnp.where(straight, one, two), jnp.where(straight, two, one)], axis=0)
+    qg, kg = qg_ref[...], kg_ref[...]
+    for h in range(per):
+        q, k, v = head_inputs(place, (q_ref, k_ref, v_ref, came_ref), h, dim)
+        probs, q_hat, q_inv, qn, k_hat, k_inv, kn = head_probs(q, k, qg, kg, same, scale)
+        d = grad[h * dim : (h + 1) * dim].T
+        gv = dot_tn(probs.astype(BF16), d)
+        gp = dot_nt(d, v)
+        delta = jnp.sum(probs * gp, axis=-1, keepdims=True)
+        gs = (probs * (gp - delta) * scale).astype(BF16)
+        cols = slice(h * dim, (h + 1) * dim)
+        gq_ref[:, cols] = norm_back(dot_nn(gs, kn), q_hat, q_inv, qg).astype(BF16)
+        gk_ref[:, cols] = norm_back(dot_tn(gs, qn), k_hat, k_inv, kg).astype(BF16)
+        gv_ref[:, cols] = gv.astype(BF16)
+
+
+def attention_specs(per, dim, half_tokens, steps):
+    width = per * dim
+    own = pl.BlockSpec((half_tokens, width), lambda i, p: (0, p[0] * steps + i))
+    came = pl.BlockSpec((3, half_tokens, width), lambda i, p: (0, 0, i))
+    return [own, own, own, came]
+
+
+def whole(shape):
+    return pl.BlockSpec(shape, lambda *_: (0,) * len(shape))
+
+
+def pair_index(i, p):
+    return i ^ (p[1] >> 1) ^ (p[2] << 1)
+
+
+def attention_forward(place, queries, keys, values, came, row, col, qg, kg):
+    dim = qg.shape[1]
+    half_tokens, heads = queries.shape[0], came.shape[2] // dim
+    tokens, per = 2 * half_tokens, heads // 4
+    rows = per * dim // 2
+    out = pl.BlockSpec((1, rows, tokens), lambda i, p: (pair_index(i, p), 0, 0))
+    return pl.pallas_call(
+        functools.partial(forward_kernel, per, dim),
+        grid_spec=pltpu.PrefetchScalarGridSpec(
+            num_scalar_prefetch=1,
+            grid=(4,),
+            in_specs=attention_specs(per, dim, half_tokens, 4)
+            + [whole((1, tokens)), whole((tokens, 1)), whole((1, dim)), whole((1, dim))],
+            out_specs=[out, out],
+        ),
+        out_shape=[jax.ShapeDtypeStruct((4, rows, tokens), BF16)] * 2,
+        compiler_params=pltpu.CompilerParams(vmem_limit_bytes=40 << 20),
+        cost_estimate=pl.CostEstimate(flops=4 * tokens * tokens * dim * heads, bytes_accessed=6 * tokens * heads * dim, transcendentals=tokens * tokens * heads),
+        name="attention_forward",
+    )(place, queries, keys, values, came, row, col, qg, kg)
+
+
+def attention_backward(place, queries, keys, values, came, grads, row, col, qg, kg):
+    dim = qg.shape[1]
+    half_tokens, heads = queries.shape[0], came.shape[2] // dim
+    tokens, per = 2 * half_tokens, heads // 4
+    rows = per * dim // 2
+    out = pl.BlockSpec((tokens, per * dim), lambda i, p: (0, i))
+    return pl.pallas_call(
+        functools.partial(backward_kernel, per, dim),
+        grid_spec=pltpu.PrefetchScalarGridSpec(
+            num_scalar_prefetch=1,
+            grid=(4,),
+            in_specs=attention_specs(per, dim, half_tokens, 4)
+            + [pl.BlockSpec((1, 2, rows, tokens), lambda i, p: (pair_index(i, p), 0, 0, 0))]
+            + [whole((1, tokens)), whole((tokens, 1)), whole((1, dim)), whole((1, dim))],
+            out_specs=[out, out, out],
+        ),
+        out_shape=[jax.ShapeDtypeStruct((tokens, heads * dim), BF16)] * 3,
+        compiler_params=pltpu.CompilerParams(vmem_limit_bytes=40 << 20),
+        cost_estimate=pl.CostEstimate(flops=12 * tokens * tokens * dim * heads, bytes_accessed=14 * tokens * heads * dim, transcendentals=tokens * tokens * heads),
+        name="attention_backward",
+    )(place, queries, keys, values, came, grads, row, col, qg, kg)
+
+
+def products_kernel(place, w_ref, wr_ref, *rest):
+    n = (len(rest) - 3) // 1
+    g_refs, (keep_ref, send_ref, acc_ref) = rest[:n], rest[n:]
+    step = pl.program_id(0)
+    rows = w_ref.shape[0]
+
+    @pl.when(step == 0)
+    def _():
+        acc_ref[...] = jnp.zeros_like(acc_ref)
+
+    for j, g_ref in enumerate(g_refs):
+        g = g_ref[...]
+        acc_ref[j, :rows] += dot_nt(w_ref[...], g)
+        acc_ref[j, rows:] += dot_nt(wr_ref[...], g)
+
+    @pl.when(step == pl.num_programs(0) - 1)
+    def _():
+        flip = place[2] == 1
+        for j in range(n):
+            own, other = acc_ref[j, :rows].astype(BF16), acc_ref[j, rows:].astype(BF16)
+            keep_ref[j] = jnp.where(flip, other, own)
+            send_ref[j] = jnp.where(flip, own, other)
+
+
+def gradient_products(place, w, wr, blocks, tile=1024):
+    rows, depth = w.shape
+    tokens = blocks[0].shape[0]
+    n = len(blocks)
+    out = whole((n, rows, tokens))
+    return pl.pallas_call(
+        products_kernel,
+        grid_spec=pltpu.PrefetchScalarGridSpec(
+            num_scalar_prefetch=1,
+            grid=(depth // tile,),
+            in_specs=[pl.BlockSpec((rows, tile), lambda i, p: (0, i))] * 2
+            + [pl.BlockSpec((tokens, tile), lambda i, p: (0, i))] * n,
+            out_specs=[out, out],
+            scratch_shapes=[pltpu.VMEM((n, 2 * rows, tokens), F32)],
+        ),
+        out_shape=[jax.ShapeDtypeStruct((n, rows, tokens), BF16)] * 2,
+        compiler_params=pltpu.CompilerParams(vmem_limit_bytes=40 << 20),
+        cost_estimate=pl.CostEstimate(flops=4 * n * rows * tokens * depth, bytes_accessed=2 * (2 * rows + n * tokens) * depth, transcendentals=0),
+        name="gradient_products",
+    )(place, w, wr, *blocks)
+
+
+def weight_kernel(pick, place, *refs):
+    n = (len(refs) - 1) // 4
+    own_refs, other_refs, g_refs, out_ref = refs[:n], refs[n : 2 * n], refs[2 * n : 4 * n], refs[4 * n]
+    use_own = place[2] == pick
+    total = None
+    for j in range(n):
+        for c in range(2):
+            att = jnp.where(use_own, own_refs[j][c], other_refs[j][c])
+            term = dot_nn(att, g_refs[2 * j + c][...])
+            total = term if total is None else total + term
+    out_ref[...] = total.astype(out_ref.dtype)
+
+
+def weight_terms(pick, place, own, other, blocks, dtype, tile=512):
+    rows, tokens = own[0].shape[1:]
+    depth = blocks[0].shape[1]
+    n = len(own)
+    return pl.pallas_call(
+        functools.partial(weight_kernel, pick),
+        grid_spec=pltpu.PrefetchScalarGridSpec(
+            num_scalar_prefetch=1,
+            grid=(depth // tile,),
+            in_specs=[whole((2, rows, tokens))] * (2 * n)
+            + [pl.BlockSpec((tokens, tile), lambda i, p: (0, i))] * (2 * n),
+            out_specs=pl.BlockSpec((rows, tile), lambda i, p: (0, i)),
+        ),
+        out_shape=jax.ShapeDtypeStruct((rows, depth), dtype),
+        compiler_params=pltpu.CompilerParams(vmem_limit_bytes=40 << 20),
+        cost_estimate=pl.CostEstimate(flops=4 * n * rows * tokens * depth, bytes_accessed=2 * (rows + 2 * n * tokens) * depth, transcendentals=0),
+        name="weight_terms",
+    )(place, *own, *other, *blocks)
+
+
+def xor(k):
+    return [(j, j ^ k) for j in range(16)]
+
+
+CORE, CROSS, PLANE = xor(1), xor(2), xor(4)
+FAR = [(j, 12 - (j & 12) + (j & 3)) for j in range(16)]
+
+
+def move(a, perm):
+    return lax.ppermute(a, "fsdp", perm)
+
+
+def swap(a):
+    return lax.ppermute(a, "seq", [(0, 1), (1, 0)])
+
+
+def local_grid(queries, keys, values, image_ids, q_gain, k_gain, w_out, grad_y):
+    y = lax.axis_index("seq")
+    f = lax.axis_index("fsdp")
+    place = jnp.stack([y, f & 7, (f >> 3) ^ y]).astype(jnp.int32)
+    dim = q_gain.shape[0]
+    tokens = image_ids.shape[1]
+    half = queries.shape[1] // 2
+    row, col = image_ids, image_ids.reshape(tokens, 1)
+    qg, kg = q_gain.reshape(1, dim), k_gain.reshape(1, dim)
+
+    came = swap(
+        jnp.stack(
+            [lax.dynamic_slice_in_dim(a, (1 - y) * half, half, axis=1) for a in (queries, keys, values)]
+        )
+    )
+    g4 = move(grad_y, PLANE)
+    g2 = move(grad_y, CROSS)
+    wr = move(w_out, FAR)
+    g6 = move(g4, CROSS)
+    evens = [grad_y, g2, g4, g6]
+    blocks = []
+    for g in evens:
+        blocks += [g, move(g, CORE)]
+
+    even, odd = attention_forward(place, queries, keys, values, came, row, col, qg, kg)
+    odd = move(odd, CORE)
+    own = [jnp.stack([even[j], odd[j]]) for j in range(4)]
+    own = [own[0]] + [move(own[j], xor(2 * j)) for j in (1, 2, 3)]
+    other = [swap(a) for a in own]
+
+    sent = weight_terms(1, place, own, other, blocks, BF16)
+    far = move(sent, FAR)
+    kept = weight_terms(0, place, own, other, blocks, F32)
+
+    order = [blocks[k] for k in (0, 2, 4, 6, 1, 3, 5, 7)]
+    keep, send = gradient_products(place, w_out, wr, order)
+    summed = (keep.astype(F32) + swap(send).astype(F32)).astype(BF16)
+    even, odd = summed[:4], move(summed[4:], CORE)
+    pairs = [jnp.stack([even[j], odd[j]]) for j in range(4)]
+    grads = jnp.stack([pairs[0]] + [move(pairs[j], xor(2 * j)) for j in (1, 2, 3)])
+    gq, gk, gv = attention_backward(place, queries, keys, values, came, grads, row, col, qg, kg)
+
+    grad_w = (kept + far.astype(F32)) * tokens ** (-0.5)
+    shape = (tokens, half // dim, dim)
+    return (gq.reshape(shape), gk.reshape(shape), gv.reshape(shape), grad_w)
+
+
 def solution(mesh):
     in_specs = (
         P(("fsdp", "seq"), None),
@@ -118,4 +398,6 @@
         P("fsdp", "seq", None),
         P("fsdp", "seq"),
     )
+    grid = mesh.shape["fsdp"] == 16 and mesh.shape["seq"] == 2
+    local = local_grid if grid else local_any
     return jax.shard_map(local, mesh=mesh, in_specs=in_specs, out_specs=out_specs, check_vma=False)

time: 552 us -> 250 us (0.45)
  the two profiles are of different devices: /device:TPU:0 before, /device:TPU:9 now
where the time goes in v1:
time: 250 us
  waiting for transfers between devices  163 us (65%)
  Pallas kernels  46 us (18%)
  starting transfers between devices  22 us (9%)
  local copies, waits for them, and re-layouts  14.1 us (6%)
  other arithmetic  3.48 us (1%)
    ppermute x17, waiting for transfers between devices, move(): return lax.ppermute(a, 'fsdp', perm)  115 us
    ppermute x6, waiting for transfers between devices, swap(): return lax.ppermute(a, 'seq', [(0, 1), (1, 0)])  47.9 us
    ppermute x17, starting transfers between devices, move(): return lax.ppermute(a, 'fsdp', perm)  17.5 us
    pallas_call x2, Pallas kernels, weight_terms(): pl.pallas_call(functools.partial(weight_kernel, pick), grid_spec=pltpu.Pr...  13.9 us
    pallas_call x1, Pallas kernels, attention_backward(): pl.pallas_call(functools.partial(backward_kernel, per, dim), grid_spec=pl...  13.2 us
    unnamed x37, local copies, waits for them, and re-layouts  11.8 us
    pallas_call x1, Pallas kernels, gradient_products(): pl.pallas_call(products_kernel, grid_spec=pltpu.PrefetchScalarGridSpec(nu...  11.4 us
    pallas_call x1, Pallas kernels, attention_forward(): pl.pallas_call(functools.partial(forward_kernel, per, dim), grid_spec=plt...  7.48 us
  transfers between devices with their start and end apart: 23, of which 11 were waited for; matrix products, arithmetic and copies ran while one was open for 2% of the time, Pallas kernels for 13%

profile of v1, /device:TPU:9, one launch (start us, length us, event | category | flops | bytes accessed | tf_op | source)
XLA Modules:
  0.0 249.7 jit_solution(7368310896591683940)
XLA Ops:
  0.6 0.1 collective-permute-start.3
  0.7 1.4 collective-permute-start.2
  2.1 1.2 dynamic-slice_bitcast_fusion
  3.3 0.0 copy-start.12
  3.3 0.0 copy-start.13
  3.3 0.0 copy-start.14
  3.4 32.8 %collective-permute-done.3.rest_2_.refs_12_ = bf16[256,3072]{1,0:T(8,128)(2,1)S(1)} collective-permute-done((bf16[256,3072]{1,0:T(8,128)(2,1)}, bf16[256,3072]{1,0:T(8,128)(2,1)S(1)}, u32[]{:S(2)}, u32[]{:S(2)}) %collective-permute-start.3) | collective-permute-done | bytes 1572896 | tf_op jit(solution)/shard_map/ppermute | solution.py:330
  36.2 1.2 collective-permute-start.4
  37.4 1.1 pad_maximum_fusion
  38.6 1.2 collective-permute-start
  39.8 0.1 copy.15.col_ref
  39.9 0.1 pad_add_fusion.place
  40.0 24.5 %collective-permute-done.came_ref = bf16[3,128,1536]{2,1,0:T(8,128)(2,1)} collective-permute-done((bf16[3,128,1536]{2,1,0:T(8,128)(2,1)}, bf16[3,128,1536]{2,1,0:T(8,128)(2,1)}, u32[]{:S(2)}, u32[]{:S(2)}) %collective-permute-start) | collective-permute-done | bytes 1179680 | tf_op jit(solution)/shard_map/ppermute | solution.py:334
  64.5 1.1 copy-done.6
  65.7 1.1 copy-done.8
  66.8 1.1 copy-done.10
  67.9 7.5 %attention_forward.1 = (bf16[4,192,256]{2,1,0:T(8,128)(2,1)S(1)}, bf16[4,192,256]{2,1,0:T(8,128)(2,1)S(1)}) custom-call(s32[3]{0:T(128)S(1)} %pad_add_fusion.place, bf16[128,3072]{1,0:T(8,128)(2,1)S(1)} %copy-done.6, bf16[128,3072]{1,0:T(8,128)(2,1)S(1)} %copy-done.8, bf16[128,3072]{1,0:T(8,128)(2,1)S(1)} %copy-done.10, ...), custom_call_target="tpu_custom_call" | custom-call | flops 402653184 | bytes 2359296 | tf_op jit(solution)/shard_map/attention_forward/pallas_call | solution.py:203
  75.4 2.8 %collective-permute-start.14 = (bf16[4,192,256]{2,1,0:T(8,128)(2,1)S(1)}, bf16[4,192,256]{2,1,0:T(8,128)(2,1)S(1)}, u32[]{:S(2)}, u32[]{:S(2)}) collective-permute-start(bf16[4,192,256]{2,1,0:T(8,128)(2,1)S(1)} %get-tuple-element.17), channel_id=1, source_target_pairs={{0,2},{2,0},{4,6},{6,4},{8,10},{10,8},{12,14},{14,12},{16,18},{18,... | collective-permute-start | bytes 1179656 | tf_op jit(solution)/shard_map/ppermute | solution.py:330
  78.2 0.1 collective-permute-start.5
  78.3 0.4 collective-permute-start.7
  78.7 0.1 collective-permute-start.6
  78.8 0.4 collective-permute-start.8
  79.3 0.3 collective-permute-done.14
  79.6 1.3 collective-permute-start.1
  81.0 51.1 %collective-permute-done.1.wr_ref = bf16[192,3072]{1,0:T(8,128)(2,1)S(1)} collective-permute-done((bf16[192,3072]{1,0:T(8,128)(2,1)S(1)}, bf16[192,3072]{1,0:T(8,128)(2,1)S(1)}, u32[]{:S(2)}, u32[]{:S(2)}) %collective-permute-start.1) | collective-permute-done | bytes 1179680 | tf_op jit(solution)/shard_map/ppermute | solution.py:330
  132.0 0.3 collective-permute-start.15
  132.3 0.0 collective-permute-done.5.rest_4_.refs_9_
  132.3 1.1 copy-done.1
  133.4 1.2 copy-done.3
  134.6 11.4 %gradient_products.1 = (bf16[8,192,256]{2,1,0:T(8,128)(2,1)S(1)}, bf16[8,192,256]{2,1,0:T(8,128)(2,1)S(1)}) custom-call(s32[3]{0:T(128)S(1)} %pad_add_fusion.place, bf16[192,3072]{1,0:T(8,128)(2,1)S(1)} %copy-done.15, bf16[192,3072]{1,0:T(8,128)(2,1)S(1)} %collective-permute-done.1.wr_ref, bf16[256,3072]{1,0:T(8,128)(2,1)S(1)} %copy-done, ...), custom_call_target="tpu_custom_call" | custom-call | flops 4831838208 | bytes 14942208 | tf_op jit(solution)/shard_map/gradient_products/pallas_call | solution.py:271
  146.0 1.3 collective-permute-start.9
  147.3 0.1 collective-permute-start.16
  147.4 2.4 collective-permute-start.17
  149.9 0.3 collective-permute-start.18
  150.2 1.2 collective-permute-start.19
  151.4 0.8 collective-permute-done.16.refs_2_
  152.2 0.2 collective-permute-start.20
  152.4 4.4 %collective-permute-done.17.refs_3_ = bf16[2,192,256]{2,1,0:T(8,128)(2,1)S(1)} collective-permute-done((bf16[2,192,256]{2,1,0:T(8,128)(2,1)S(1)}, bf16[2,192,256]{2,1,0:T(8,128)(2,1)S(1)}, u32[]{:S(2)}, u32[]{:S(2)}) %collective-permute-start.17) | collective-permute-done | bytes 196640 | tf_op jit(solution)/shard_map/ppermute | solution.py:330
  156.9 0.2 collective-permute-start.21
  157.1 10.7 %collective-permute-done.18.refs_4_ = bf16[2,192,256]{2,1,0:T(8,128)(2,1)S(1)} collective-permute-done((bf16[2,192,256]{2,1,0:T(8,128)(2,1)S(1)}, bf16[2,192,256]{2,1,0:T(8,128)(2,1)S(1)}, u32[]{:S(2)}, u32[]{:S(2)}) %collective-permute-start.18) | collective-permute-done | bytes 196640 | tf_op jit(solution)/shard_map/ppermute | solution.py:334
  167.8 4.2 %collective-permute-done.19.refs_5_ = bf16[2,192,256]{2,1,0:T(8,128)(2,1)S(1)} collective-permute-done((bf16[2,192,256]{2,1,0:T(8,128)(2,1)S(1)}, bf16[2,192,256]{2,1,0:T(8,128)(2,1)S(1)}, u32[]{:S(2)}, u32[]{:S(2)}) %collective-permute-start.19) | collective-permute-done | bytes 196640 | tf_op jit(solution)/shard_map/ppermute | solution.py:334
  172.1 4.2 %collective-permute-done.20.refs_6_ = bf16[2,192,256]{2,1,0:T(8,128)(2,1)S(1)} collective-permute-done((bf16[2,192,256]{2,1,0:T(8,128)(2,1)S(1)}, bf16[2,192,256]{2,1,0:T(8,128)(2,1)S(1)}, u32[]{:S(2)}, u32[]{:S(2)}) %collective-permute-start.20) | collective-permute-done | bytes 196640 | tf_op jit(solution)/shard_map/ppermute | solution.py:334
  176.3 4.2 %collective-permute-done.21.refs_7_ = bf16[2,192,256]{2,1,0:T(8,128)(2,1)S(1)} collective-permute-done((bf16[2,192,256]{2,1,0:T(8,128)(2,1)S(1)}, bf16[2,192,256]{2,1,0:T(8,128)(2,1)S(1)}, u32[]{:S(2)}, u32[]{:S(2)}) %collective-permute-start.21) | collective-permute-done | bytes 196640 | tf_op jit(solution)/shard_map/ppermute | solution.py:334
  180.5 1.4 copy-done.2
  181.9 6.7 %weight_terms.3 = bf16[192,3072]{1,0:T(8,128)(2,1)S(1)} custom-call(s32[3]{0:T(128)S(1)} %pad_add_fusion.place, bf16[2,192,256]{2,1,0:T(8,128)(2,1)S(1)} %pad_maximum_fusion.5.refs_0_, bf16[2,192,256]{2,1,0:T(8,128)(2,1)S(1)} %collective-permute-done.15.refs_1_, bf16[2,192,256]{2,1,0:T(8,128)(2,1)S(1)} %collective-permute-done.16.refs_2_, ...), custom_call_target="tpu_custom_call" | custom-call | flops 2415919104 | bytes 13762560 | tf_op jit(solution)/shard_map/weight_terms/pallas_call | solution.py:305
  188.6 1.4 collective-permute-start.22
  190.0 0.2 add_convert_fusion
  190.2 2.7 %collective-permute-start.10 = (bf16[4,192,256]{2,1,0:T(8,128)(2,1)S(1)}, bf16[4,192,256]{2,1,0:T(8,128)(2,1)S(1)}, u32[]{:S(2)}, u32[]{:S(2)}) collective-permute-start(bf16[4,192,256]{2,1,0:T(8,128)(2,1)S(1)} %slice.74), channel_id=1, source_target_pairs={{0,2},{2,0},{4,6},{6,4},{8,10},{10,8},{12,14},{14,12},{16,18},{18,... | collective-permute-start | bytes 1179656 | tf_op jit(solution)/shard_map/ppermute | solution.py:330
  193.0 7.2 %weight_terms.2 = f32[192,3072]{1,0:T(8,128)} custom-call(s32[3]{0:T(128)S(1)} %pad_add_fusion.place, bf16[2,192,256]{2,1,0:T(8,128)(2,1)S(1)} %pad_maximum_fusion.5.refs_0_, bf16[2,192,256]{2,1,0:T(8,128)(2,1)S(1)} %collective-permute-done.15.refs_1_, bf16[2,192,256]{2,1,0:T(8,128)(2,1)S(1)} %collective-permute-done.16.refs_2_, ...), custom_call_target="tpu_custom_call" | custom-call | flops 2415919104 | bytes 13762560 | tf_op jit(solution)/shard_map/weight_terms/pallas_call | solution.py:305
  200.3 1.3 collective-permute-start.11
  201.6 0.1 collective-permute-start.12
  201.7 1.5 collective-permute-start.13
  203.2 25.8 %collective-permute-done.22 = bf16[192,3072]{1,0:T(8,128)(2,1)S(1)} collective-permute-done((bf16[192,3072]{1,0:T(8,128)(2,1)S(1)}, bf16[192,3072]{1,0:T(8,128)(2,1)S(1)}, u32[]{:S(2)}, u32[]{:S(2)}) %collective-permute-start.22) | collective-permute-done | bytes 1179680 | tf_op jit(solution)/shard_map/ppermute | solution.py:330
  229.0 1.8 add_multiply_fusion
  230.8 0.1 pad_maximum_fusion.1.d_ref
  230.9 1.0 copy-done.7
  231.9 0.2 copy-done.9
  232.1 13.2 %attention_backward.1 = (bf16[256,1536]{1,0:T(8,128)(2,1)S(1)}, bf16[256,1536]{1,0:T(8,128)(2,1)S(1)}, bf16[256,1536]{1,0:T(8,128)(2,1)S(1)}) custom-call(s32[3]{0:T(128)S(1)} %pad_add_fusion.place, bf16[128,3072]{1,0:T(8,128)(2,1)S(1)} %copy-done.7, bf16[128,3072]{1,0:T(8,128)(2,1)S(1)} %copy-done.9, bf16[128,3072]{1,0:T(8,128)(2,1)S(1)} %copy-done.11, ...), custom_call_target="tpu_custom_call" | custom-call | flops 1207959552 | bytes 5505024 | tf_op jit(solution)/shard_map/attention_backward/pallas_call | solution.py:225
  245.4 0.3 copy.16
  245.6 1.2 copy.20
  246.8 0.3 copy.17
  247.1 1.2 copy.21
  248.2 0.3 copy.18
  248.5 1.2 copy.22
  (48 shorter events, 0.4 us)
Async XLA Ops:
  0.6 35.5 %collective-permute-start.3 = (bf16[256,3072]{1,0:T(8,128)(2,1)}, bf16[256,3072]{1,0:T(8,128)(2,1)S(1)}, u32[]{:S(2)}, u32[]{:S(2)}) collective-permute-start(bf16[256,3072]{1,0:T(8,128)(2,1)} %refs_8_.3), channel_id=1, source_target_pairs={{0,8},{2,10},{4,12},{6,14},{8,0},{10,2},{12,4},{14,6},{16,24},{18,... | collective-permute-start | bytes 4718600 | tf_op jit(solution)/shard_map/ppermute | solution.py:330
  0.7 78.0 %collective-permute-start.2 = (bf16[256,3072]{1,0:T(8,128)(2,1)}, bf16[256,3072]{1,0:T(8,128)(2,1)S(1)}, u32[]{:S(2)}, u32[]{:S(2)}) collective-permute-start(bf16[256,3072]{1,0:T(8,128)(2,1)} %refs_8_.3), channel_id=1, source_target_pairs={{0,4},{2,6},{4,0},{6,2},{8,12},{10,14},{12,8},{14,10},{16,20},{18,... | collective-permute-start | bytes 4718600 | tf_op jit(solution)/shard_map/ppermute | solution.py:330
  2.1 35.3 %copy-start.5 = (bf16[128,3072]{1,0:T(8,128)(2,1)S(1)}, bf16[128,3072]{1,0:T(8,128)(2,1)}, u32[]{:S(2)}) copy-start(bf16[128,3072]{1,0:T(8,128)(2,1)} %q_ref.3) | copy-start | bytes 2359300
  3.3 36.5 %copy-start.12 = (s32[1,256]{1,0:T(1,128)S(1)}, s32[1,256]{1,0:T(1,128)}, u32[]{:S(2)}) copy-start(s32[1,256]{1,0:T(1,128)} %row_ref.3) | copy-start | bytes 3076
  3.3 61.2 %copy-start.13 = (f32[128]{0:T(128)S(1)}, f32[128]{0:T(128)}, u32[]{:S(2)}) copy-start(f32[128]{0:T(128)} %param.12) | copy-start | bytes 1540
  3.3 61.2 %copy-start.14 = (f32[128]{0:T(128)S(1)}, f32[128]{0:T(128)}, u32[]{:S(2)}) copy-start(f32[128]{0:T(128)} %param.13) | copy-start | bytes 1540
  36.2 42.7 %collective-permute-start.4 = (bf16[256,3072]{1,0:T(8,128)(2,1)S(1)}, bf16[256,3072]{1,0:T(8,128)(2,1)}, u32[]{:S(2)}, u32[]{:S(2)}) collective-permute-start(bf16[256,3072]{1,0:T(8,128)(2,1)S(1)} %collective-permute-done.3.rest_2_.refs_12_), channel_id=1, source_target_pairs={{0,4},{2,6},{4,0},{6,2},{8,12},{10,14},{12,8},{14,10},{16,20},{18,... | collective-permute-start | bytes 4718600 | tf_op jit(solution)/shard_map/ppermute | solution.py:330
  38.6 26.0 %collective-permute-start = (bf16[3,128,1536]{2,1,0:T(8,128)(2,1)}, bf16[3,128,1536]{2,1,0:T(8,128)(2,1)}, u32[]{:S(2)}, u32[]{:S(2)}) collective-permute-start(bf16[3,128,1536]{2,1,0:T(8,128)(2,1)} %pad_maximum_fusion), channel_id=1, source_target_pairs={{0,1},{1,0},{2,3},{3,2},{4,5},{5,4},{6,7},{7,6},{8,9},{9,8},{10,11... | collective-permute-start | bytes 3538952 | tf_op jit(solution)/shard_map/ppermute | solution.py:334
  64.5 1.1 copy-start.6
  65.6 1.1 copy-start.8
  66.8 1.1 copy-start.10
  67.9 10.3 %copy-start = (bf16[256,3072]{1,0:T(8,128)(2,1)S(1)}, bf16[256,3072]{1,0:T(8,128)(2,1)}, u32[]{:S(2)}) copy-start(bf16[256,3072]{1,0:T(8,128)(2,1)} %refs_8_.3) | copy-start | bytes 4718596
  67.9 11.7 %copy-start.15 = (bf16[192,3072]{1,0:T(8,128)(2,1)S(1)}, bf16[192,3072]{1,0:T(8,128)(2,1)}, u32[]{:S(2)}) copy-start(bf16[192,3072]{1,0:T(8,128)(2,1)} %w_ref.1) | copy-start | bytes 3538948
  75.4 4.2 %collective-permute-start.14 = (bf16[4,192,256]{2,1,0:T(8,128)(2,1)S(1)}, bf16[4,192,256]{2,1,0:T(8,128)(2,1)S(1)}, u32[]{:S(2)}, u32[]{:S(2)}) collective-permute-start(bf16[4,192,256]{2,1,0:T(8,128)(2,1)S(1)} %get-tuple-element.17), channel_id=1, source_target_pairs={{0,2},{2,0},{4,6},{6,4},{8,10},{10,8},{12,14},{14,12},{16,18},{18,... | collective-permute-start | bytes 1179656 | tf_op jit(solution)/shard_map/ppermute | solution.py:330
  78.2 54.1 %collective-permute-start.5 = (bf16[256,3072]{1,0:T(8,128)(2,1)S(1)}, bf16[256,3072]{1,0:T(8,128)(2,1)S(1)}, u32[]{:S(2)}, u32[]{:S(2)}) collective-permute-start(bf16[256,3072]{1,0:T(8,128)(2,1)S(1)} %copy-done), channel_id=1, source_target_pairs={{0,2},{2,0},{4,6},{6,4},{8,10},{10,8},{12,14},{14,12},{16,18},{18,... | collective-permute-start | bytes 4718600 | tf_op jit(solution)/shard_map/ppermute | solution.py:330
  78.3 54.0 %collective-permute-start.7 = (bf16[256,3072]{1,0:T(8,128)(2,1)S(1)}, bf16[256,3072]{1,0:T(8,128)(2,1)S(1)}, u32[]{:S(2)}, u32[]{:S(2)}) collective-permute-start(bf16[256,3072]{1,0:T(8,128)(2,1)S(1)} %collective-permute-done.3.rest_2_.refs_12_), channel_id=1, source_target_pairs={{0,2},{2,0},{4,6},{6,4},{8,10},{10,8},{12,14},{14,12},{16,18},{18,... | collective-permute-start | bytes 4718600 | tf_op jit(solution)/shard_map/ppermute | solution.py:330
  78.7 53.6 %collective-permute-start.6 = (bf16[256,3072]{1,0:T(8,128)(2,1)S(1)}, bf16[256,3072]{1,0:T(8,128)(2,1)S(1)}, u32[]{:S(2)}, u32[]{:S(2)}) collective-permute-start(bf16[256,3072]{1,0:T(8,128)(2,1)S(1)} %collective-permute-done.2.rest_1_.refs_10_), channel_id=1, source_target_pairs={{0,2},{2,0},{4,6},{6,4},{8,10},{10,8},{12,14},{14,12},{16,18},{18,... | collective-permute-start | bytes 4718600 | tf_op jit(solution)/shard_map/ppermute | solution.py:330
  78.8 53.5 %collective-permute-start.8 = (bf16[256,3072]{1,0:T(8,128)(2,1)}, bf16[256,3072]{1,0:T(8,128)(2,1)S(1)}, u32[]{:S(2)}, u32[]{:S(2)}) collective-permute-start(bf16[256,3072]{1,0:T(8,128)(2,1)} %collective-permute-done.4.rest_3_.refs_14_), channel_id=1, source_target_pairs={{0,2},{2,0},{4,6},{6,4},{8,10},{10,8},{12,14},{14,12},{16,18},{18,... | collective-permute-start | bytes 4718600 | tf_op jit(solution)/shard_map/ppermute | solution.py:330
  79.6 52.5 %collective-permute-start.1 = (bf16[192,3072]{1,0:T(8,128)(2,1)S(1)}, bf16[192,3072]{1,0:T(8,128)(2,1)S(1)}, u32[]{:S(2)}, u32[]{:S(2)}) collective-permute-start(bf16[192,3072]{1,0:T(8,128)(2,1)S(1)} %copy-done.15), channel_id=1, source_target_pairs={{0,24},{2,26},{4,28},{6,30},{8,16},{10,18},{12,20},{14,22},{16,8},... | collective-permute-start | bytes 3538952 | tf_op jit(solution)/shard_map/ppermute | solution.py:330
  132.0 18.2 %collective-permute-start.15 = (bf16[2,192,256]{2,1,0:T(8,128)(2,1)S(1)}, bf16[2,192,256]{2,1,0:T(8,128)(2,1)S(1)}, u32[]{:S(2)}, u32[]{:S(2)}) collective-permute-start(bf16[2,192,256]{2,1,0:T(8,128)(2,1)S(1)} %pad_maximum_fusion.6), channel_id=1, source_target_pairs={{0,4},{2,6},{4,0},{6,2},{8,12},{10,14},{12,8},{14,10},{16,20},{18,... | collective-permute-start | bytes 589832 | tf_op jit(solution)/shard_map/ppermute | solution.py:330
  132.3 1.1 copy-start.1
  133.4 1.2 copy-start.3
  146.0 44.0 %collective-permute-start.9 = (bf16[8,192,256]{2,1,0:T(8,128)(2,1)S(1)}, bf16[8,192,256]{2,1,0:T(8,128)(2,1)S(1)}, u32[]{:S(2)}, u32[]{:S(2)}) collective-permute-start(bf16[8,192,256]{2,1,0:T(8,128)(2,1)S(1)} %get-tuple-element.12), channel_id=1, source_target_pairs={{0,1},{1,0},{2,3},{3,2},{4,5},{5,4},{6,7},{7,6},{8,9},{9,8},{10,11... | collective-permute-start | bytes 2359304 | tf_op jit(solution)/shard_map/ppermute | solution.py:334
  147.3 4.9 %collective-permute-start.16 = (bf16[2,192,256]{2,1,0:T(8,128)(2,1)S(1)}, bf16[2,192,256]{2,1,0:T(8,128)(2,1)S(1)}, u32[]{:S(2)}, u32[]{:S(2)}) collective-permute-start(bf16[2,192,256]{2,1,0:T(8,128)(2,1)S(1)} %pad_maximum_fusion.7), channel_id=1, source_target_pairs={{0,8},{2,10},{4,12},{6,14},{8,0},{10,2},{12,4},{14,6},{16,24},{18,... | collective-permute-start | bytes 589832 | tf_op jit(solution)/shard_map/ppermute | solution.py:330
  147.4 9.4 %collective-permute-start.17 = (bf16[2,192,256]{2,1,0:T(8,128)(2,1)S(1)}, bf16[2,192,256]{2,1,0:T(8,128)(2,1)S(1)}, u32[]{:S(2)}, u32[]{:S(2)}) collective-permute-start(bf16[2,192,256]{2,1,0:T(8,128)(2,1)S(1)} %pad_maximum_fusion.8), channel_id=1, source_target_pairs={{0,12},{2,14},{4,8},{6,10},{8,4},{10,6},{12,0},{14,2},{16,28},{18,... | collective-permute-start | bytes 589832 | tf_op jit(solution)/shard_map/ppermute | solution.py:330
  149.9 17.9 %collective-permute-start.18 = (bf16[2,192,256]{2,1,0:T(8,128)(2,1)S(1)}, bf16[2,192,256]{2,1,0:T(8,128)(2,1)S(1)}, u32[]{:S(2)}, u32[]{:S(2)}) collective-permute-start(bf16[2,192,256]{2,1,0:T(8,128)(2,1)S(1)} %pad_maximum_fusion.5.refs_0_), channel_id=1, source_target_pairs={{0,1},{1,0},{2,3},{3,2},{4,5},{5,4},{6,7},{7,6},{8,9},{9,8},{10,11... | collective-permute-start | bytes 589832 | tf_op jit(solution)/shard_map/ppermute | solution.py:334
  150.2 21.9 %collective-permute-start.19 = (bf16[2,192,256]{2,1,0:T(8,128)(2,1)S(1)}, bf16[2,192,256]{2,1,0:T(8,128)(2,1)S(1)}, u32[]{:S(2)}, u32[]{:S(2)}) collective-permute-start(bf16[2,192,256]{2,1,0:T(8,128)(2,1)S(1)} %collective-permute-done.15.refs_1_), channel_id=1, source_target_pairs={{0,1},{1,0},{2,3},{3,2},{4,5},{5,4},{6,7},{7,6},{8,9},{9,8},{10,11... | collective-permute-start | bytes 589832 | tf_op jit(solution)/shard_map/ppermute | solution.py:334
  152.2 24.1 %collective-permute-start.20 = (bf16[2,192,256]{2,1,0:T(8,128)(2,1)S(1)}, bf16[2,192,256]{2,1,0:T(8,128)(2,1)S(1)}, u32[]{:S(2)}, u32[]{:S(2)}) collective-permute-start(bf16[2,192,256]{2,1,0:T(8,128)(2,1)S(1)} %collective-permute-done.16.refs_2_), channel_id=1, source_target_pairs={{0,1},{1,0},{2,3},{3,2},{4,5},{5,4},{6,7},{7,6},{8,9},{9,8},{10,11... | collective-permute-start | bytes 589832 | tf_op jit(solution)/shard_map/ppermute | solution.py:334
  156.9 23.6 %collective-permute-start.21 = (bf16[2,192,256]{2,1,0:T(8,128)(2,1)S(1)}, bf16[2,192,256]{2,1,0:T(8,128)(2,1)S(1)}, u32[]{:S(2)}, u32[]{:S(2)}) collective-permute-start(bf16[2,192,256]{2,1,0:T(8,128)(2,1)S(1)} %collective-permute-done.17.refs_3_), channel_id=1, source_target_pairs={{0,1},{1,0},{2,3},{3,2},{4,5},{5,4},{6,7},{7,6},{8,9},{9,8},{10,11... | collective-permute-start | bytes 589832 | tf_op jit(solution)/shard_map/ppermute | solution.py:334
  180.5 1.4 copy-start.2
  188.6 40.3 %collective-permute-start.22 = (bf16[192,3072]{1,0:T(8,128)(2,1)S(1)}, bf16[192,3072]{1,0:T(8,128)(2,1)S(1)}, u32[]{:S(2)}, u32[]{:S(2)}) collective-permute-start(bf16[192,3072]{1,0:T(8,128)(2,1)S(1)} %weight_terms.3), channel_id=1, source_target_pairs={{0,24},{2,26},{4,28},{6,30},{8,16},{10,18},{12,20},{14,22},{16,8},... | collective-permute-start | bytes 3538952 | tf_op jit(solution)/shard_map/ppermute | solution.py:330
  190.0 3.0 %copy-start.4 = (bf16[256,3072]{1,0:T(8,128)(2,1)S(1)}, bf16[256,3072]{1,0:T(8,128)(2,1)}, u32[]{:S(2)}) copy-start(bf16[256,3072]{1,0:T(8,128)(2,1)} %copy-done.3) | copy-start | bytes 4718596
  190.2 9.9 %collective-permute-start.10 = (bf16[4,192,256]{2,1,0:T(8,128)(2,1)S(1)}, bf16[4,192,256]{2,1,0:T(8,128)(2,1)S(1)}, u32[]{:S(2)}, u32[]{:S(2)}) collective-permute-start(bf16[4,192,256]{2,1,0:T(8,128)(2,1)S(1)} %slice.74), channel_id=1, source_target_pairs={{0,2},{2,0},{4,6},{6,4},{8,10},{10,8},{12,14},{14,12},{16,18},{18,... | collective-permute-start | bytes 1179656 | tf_op jit(solution)/shard_map/ppermute | solution.py:330
  200.2 28.8 %copy-start.16 = (f32[192,3072]{1,0:T(8,128)S(1)}, f32[192,3072]{1,0:T(8,128)}, u32[]{:S(2)}) copy-start(f32[192,3072]{1,0:T(8,128)} %weight_terms.2) | copy-start | bytes 7077892
  200.3 30.5 %collective-permute-start.11 = (bf16[2,192,256]{2,1,0:T(8,128)(2,1)S(1)}, bf16[2,192,256]{2,1,0:T(8,128)(2,1)S(1)}, u32[]{:S(2)}, u32[]{:S(2)}) collective-permute-start(bf16[2,192,256]{2,1,0:T(8,128)(2,1)S(1)} %pad_maximum_fusion.2), channel_id=1, source_target_pairs={{0,4},{2,6},{4,0},{6,2},{8,12},{10,14},{12,8},{14,10},{16,20},{18,... | collective-permute-start | bytes 589832 | tf_op jit(solution)/shard_map/ppermute | solution.py:330
  201.6 29.2 %collective-permute-start.12 = (bf16[2,192,256]{2,1,0:T(8,128)(2,1)S(1)}, bf16[2,192,256]{2,1,0:T(8,128)(2,1)S(1)}, u32[]{:S(2)}, u32[]{:S(2)}) collective-permute-start(bf16[2,192,256]{2,1,0:T(8,128)(2,1)S(1)} %pad_maximum_fusion.3), channel_id=1, source_target_pairs={{0,8},{2,10},{4,12},{6,14},{8,0},{10,2},{12,4},{14,6},{16,24},{18,... | collective-permute-start | bytes 589832 | tf_op jit(solution)/shard_map/ppermute | solution.py:330
  201.7 29.1 %collective-permute-start.13 = (bf16[2,192,256]{2,1,0:T(8,128)(2,1)S(1)}, bf16[2,192,256]{2,1,0:T(8,128)(2,1)S(1)}, u32[]{:S(2)}, u32[]{:S(2)}) collective-permute-start(bf16[2,192,256]{2,1,0:T(8,128)(2,1)S(1)} %pad_maximum_fusion.4), channel_id=1, source_target_pairs={{0,12},{2,14},{4,8},{6,10},{8,4},{10,6},{12,0},{14,2},{16,28},{18,... | collective-permute-start | bytes 589832 | tf_op jit(solution)/shard_map/ppermute | solution.py:330
  229.0 2.0 copy-start.11
  230.8 1.1 copy-start.7
  230.8 1.4 copy-start.9

commit v2 on v1

v2 whole, which is shorter than its diff:
```python
import functools

import jax
import jax.numpy as jnp
from jax import lax
from jax.experimental import pallas as pl
from jax.experimental.pallas import tpu as pltpu
from jax.sharding import PartitionSpec as P

F32 = jnp.float32
BF16 = jnp.bfloat16


def norm_parts(source, gain):
    wide = source.astype(jnp.float32)
    centred = wide - jnp.mean(wide, axis=-1, keepdims=True)
    scale_inv = lax.rsqrt(jnp.mean(centred * centred, axis=-1, keepdims=True) + 1e-06)
    x_hat = centred * scale_inv
    return (x_hat, scale_inv, (x_hat * gain).astype(jnp.bfloat16))


def norm_back(grad_n, x_hat, scale_inv, gain):
    scaled = grad_n * gain
    return scale_inv * (
        scaled
        - jnp.mean(scaled, axis=-1, keepdims=True)
        - x_hat * jnp.mean(scaled * x_hat, axis=-1, keepdims=True)
    )


def probabilities(normalized_queries, normalized_keys, same_image, scale_factor):
    scores = (
        jnp.einsum(
            "krt,irt->rki", normalized_queries, normalized_keys, preferred_element_type=jnp.float32
        )
        * scale_factor
    )
    scores = jnp.where(same_image[None], scores, -1e30)
    row_top = jnp.max(scores, axis=-1, keepdims=True)
    exp_terms = jnp.exp(scores - row_top)
    return exp_terms / jnp.sum(exp_terms, axis=-1, keepdims=True)


def local_any(queries, keys, values, image_ids, q_gain, k_gain, w_out, grad_y):
    head_dim = q_gain.shape[0]
    tok_rows = queries.shape[0]
    heads_all = queries.shape[1] // head_dim
    scale_factor = head_dim ** (-0.5)
    q_patch = queries.reshape(tok_rows, heads_all, head_dim)
    k_patch = keys.reshape(tok_rows, heads_all, head_dim)
    v_patch = values.reshape(tok_rows, heads_all, head_dim)
    q_local, k_local, value_shard = (
        lax.all_to_all(q_patch, "seq", split_axis=1, concat_axis=0, tiled=True),
        lax.all_to_all(k_patch, "seq", split_axis=1, concat_axis=0, tiled=True),
        lax.all_to_all(v_patch, "seq", split_axis=1, concat_axis=0, tiled=True),
    )
    seq_length = q_local.shape[0]
    local_heads = q_local.shape[1]
    image_row = image_ids[0]
    same_image = image_row[:, None] == image_row[None, :]
    q_hat, q_inv, normalized_queries = norm_parts(q_local, q_gain)
    k_hat, k_inv, normalized_keys = norm_parts(k_local, k_gain)
    prob_rows = probabilities(normalized_queries, normalized_keys, same_image, scale_factor)
    probs_reduced_precision = prob_rows.astype(jnp.bfloat16)
    attended = jnp.einsum(
        "tgi,itp->gtp", probs_reduced_precision, value_shard, preferred_element_type=jnp.float32
    ).astype(jnp.bfloat16)
    attended_flat = attended.reshape(seq_length, local_heads * head_dim)
    partial_g = jnp.einsum(
        "ld,cd->lc",
        grad_y,
        lax.all_gather(w_out, "fsdp", axis=0, tiled=True),
        preferred_element_type=jnp.float32,
    )
    grad_sum = lax.psum_scatter(
        partial_g.astype(jnp.bfloat16), "seq", scatter_dimension=1, tiled=True
    )
    attention_gradient = grad_sum.reshape(seq_length, local_heads, head_dim)
    grad_values = jnp.einsum(
        "jpw,pjy->wjy",
        probs_reduced_precision,
        attention_gradient,
        preferred_element_type=jnp.float32,
    ).astype(jnp.bfloat16)
    probability_gradient = jnp.einsum(
        "krt,irt->rki", attention_gradient, value_shard, preferred_element_type=jnp.float32
    )
    row_delta = jnp.sum(prob_rows * probability_gradient, axis=-1, keepdims=True)
    score_gradient = (prob_rows * (probability_gradient - row_delta) * scale_factor).astype(
        jnp.bfloat16
    )
    normed_query_gradient = jnp.einsum(
        "tgi,itp->gtp", score_gradient, normalized_keys, preferred_element_type=jnp.float32
    )
    normed_key_gradient = jnp.einsum(
        "jpw,pjy->wjy", score_gradient, normalized_queries, preferred_element_type=jnp.float32
    )
    grad_queries = norm_back(normed_query_gradient, q_hat, q_inv, q_gain).astype(jnp.bfloat16)
    grad_keys = norm_back(normed_key_gradient, k_hat, k_inv, k_gain).astype(jnp.bfloat16)
    partial_w = jnp.einsum(
        "lc,ld->cd",
        lax.all_gather(attended_flat, "seq", axis=1, tiled=True),
        grad_y,
        preferred_element_type=jnp.float32,
    )
    summed = lax.psum_scatter(partial_w, "fsdp", scatter_dimension=0, tiled=True)
    grad_w = summed * seq_length ** (-0.5)
    return (grad_queries, grad_keys, grad_values, grad_w)


def dot_nt(a, b):
    return lax.dot_general(a, b, (((1,), (1,)), ((), ())), preferred_element_type=F32)


def dot_tn(a, b):
    return lax.dot_general(a, b, (((0,), (0,)), ((), ())), preferred_element_type=F32)


def dot_nn(a, b):
    return jnp.dot(a, b, preferred_element_type=F32)


def assemble(first, own, came):
    return jnp.concatenate([jnp.where(first, own, came), jnp.where(first, came, own)], axis=0)


def head_inputs(place, own_ref, came_ref, h, dim):
    first = place[0] == 0
    cols = slice(h * dim, (h + 1) * dim)
    return [assemble(first, own_ref[n, :, cols], came_ref[n, :, cols]) for n in range(3)]


def pack_kernel(place, *refs):
    mine, theirs, own_ref, send_ref = refs[:3], refs[3:6], refs[6], refs[7]
    for n in range(3):
        own_ref[n] = mine[n][...]
        send_ref[n] = theirs[n][...]


def pack(place, arrays, steps=2):
    rows, width = arrays[0].shape[0], arrays[0].shape[1] // 2
    wide = width // steps
    mine = pl.BlockSpec((rows, wide), lambda i, p: (0, p[0] * steps + i))
    theirs = pl.BlockSpec((rows, wide), lambda i, p: (0, (1 - p[0]) * steps + i))
    out = pl.BlockSpec((3, rows, wide), lambda i, p: (0, 0, i))
    return pl.pallas_call(
        pack_kernel,
        grid_spec=pltpu.PrefetchScalarGridSpec(
            num_scalar_prefetch=1, grid=(steps,), in_specs=[mine] * 3 + [theirs] * 3, out_specs=[out, out]
        ),
        out_shape=[jax.ShapeDtypeStruct((3, rows, width), BF16)] * 2,
        cost_estimate=pl.CostEstimate(flops=1000, bytes_accessed=1000, transcendentals=0),
        name="pack",
    )(place, *arrays, *arrays)


def head_probs(q, k, qg, kg, same, scale):
    q_hat, q_inv, qn = norm_parts(q, qg)
    k_hat, k_inv, kn = norm_parts(k, kg)
    scores = jnp.where(same, dot_nt(qn, kn) * scale, -1e30)
    exp_terms = jnp.exp(scores - jnp.max(scores, axis=-1, keepdims=True))
    probs = exp_terms / jnp.sum(exp_terms, axis=-1, keepdims=True)
    return probs, q_hat, q_inv, qn, k_hat, k_inv, kn


def forward_kernel(per, dim, place, own_ref, came_ref, row_ref, col_ref, qg_ref, kg_ref, even_ref, odd_ref):
    same = col_ref[...] == row_ref[...]
    done = []
    for h in range(per):
        q, k, v = head_inputs(place, own_ref, came_ref, h, dim)
        probs = head_probs(q, k, qg_ref[...], kg_ref[...], same, dim**-0.5)[0]
        done.append(dot_nn(probs.astype(BF16), v).T.astype(BF16))
    att = jnp.concatenate(done, axis=0)
    half = att.shape[0] // 2
    straight = (place[1] & 1) == 0
    low, high = att[:half], att[half:]
    even_ref[0] = jnp.where(straight, low, high)
    odd_ref[0] = jnp.where(straight, high, low)


def backward_kernel(per, dim, n_into, place, own_ref, came_ref, d_ref, row_ref, col_ref, qg_ref, kg_ref, *rest):
    into, outs = rest[:n_into], rest[n_into:]
    wide = per * dim
    if n_into:
        start = pl.multiple_of(wide * (2 * ((place[1] >> 2) ^ place[2] ^ 1) + pair_index(pl.program_id(0), place) % 2), wide)

        @pl.when(pl.program_id(0) == 0)
        def _():
            first = pl.multiple_of(2 * wide * ((place[1] >> 2) ^ place[2]), 2 * wide)
            for ref, out in zip(into, outs):
                out[:, pl.ds(first, 2 * wide)] = ref[...]

    else:
        start = pl.multiple_of(wide * (pair_index(pl.program_id(0), place) % 2), wide)
    gq_ref, gk_ref, gv_ref = (out.at[:, pl.ds(start, wide)] for out in outs)
    same = col_ref[...] == row_ref[...]
    scale = dim**-0.5
    straight = (place[1] & 1) == 0
    one, two = d_ref[0, 0], d_ref[0, 1]
    grad = jnp.concatenate([jnp.where(straight, one, two), jnp.where(straight, two, one)], axis=0)
    qg, kg = qg_ref[...], kg_ref[...]
    for h in range(per):
        q, k, v = head_inputs(place, own_ref, came_ref, h, dim)
        probs, q_hat, q_inv, qn, k_hat, k_inv, kn = head_probs(q, k, qg, kg, same, scale)
        d = grad[h * dim : (h + 1) * dim].T
        gv = dot_tn(probs.astype(BF16), d)
        gp = dot_nt(d, v)
        delta = jnp.sum(probs * gp, axis=-1, keepdims=True)
        gs = (probs * (gp - delta) * scale).astype(BF16)
        cols = slice(h * dim, (h + 1) * dim)
        gq_ref[:, cols] = norm_back(dot_nn(gs, kn), q_hat, q_inv, qg).astype(BF16)
        gk_ref[:, cols] = norm_back(dot_tn(gs, qn), k_hat, k_inv, kg).astype(BF16)
        gv_ref[:, cols] = gv.astype(BF16)


def whole(shape):
    return pl.BlockSpec(shape, lambda *_: (0,) * len(shape))


def pair_index(i, p):
    return i ^ (p[1] >> 1) ^ (p[2] << 1)


def attention_forward(place, mine, came, row, col, qg, kg):
    dim = qg.shape[1]
    half_tokens, heads = mine.shape[1], mine.shape[2] // dim
    tokens, per = 2 * half_tokens, heads // 4
    rows = per * dim // 2
    out = pl.BlockSpec((1, rows, tokens), lambda i, p: (pair_index(i, p), 0, 0))
    return pl.pallas_call(
        functools.partial(forward_kernel, per, dim),
        grid_spec=pltpu.PrefetchScalarGridSpec(
            num_scalar_prefetch=1,
            grid=(4,),
            in_specs=[pl.BlockSpec((3, half_tokens, per * dim), lambda i, p: (0, 0, i))] * 2
            + [whole((1, tokens)), whole((tokens, 1)), whole((1, dim)), whole((1, dim))],
            out_specs=[out, out],
        ),
        out_shape=[jax.ShapeDtypeStruct((4, rows, tokens), BF16)] * 2,
        compiler_params=pltpu.CompilerParams(vmem_limit_bytes=40 << 20),
        cost_estimate=pl.CostEstimate(flops=1000, bytes_accessed=1000, transcendentals=0),
        name="attention_forward",
    )(place, mine, came, row, col, qg, kg)


def attention_backward(place, pairs, mine, came, grads, row, col, qg, kg, into=()):
    dim = qg.shape[1]
    half_tokens, heads = mine.shape[1], mine.shape[2] // dim
    tokens, per = 2 * half_tokens, heads // 4
    rows, half = per * dim // 2, 2 * per * dim
    width = 2 * half if into else half
    return pl.pallas_call(
        functools.partial(backward_kernel, per, dim, len(into)),
        grid_spec=pltpu.PrefetchScalarGridSpec(
            num_scalar_prefetch=1,
            grid=(2,),
            in_specs=[pl.BlockSpec((3, half_tokens, per * dim), lambda i, p: (0, 0, pair_index(i + pairs, p)))] * 2
            + [pl.BlockSpec((1, 2, rows, tokens), lambda i, p: (i, 0, 0, 0))]
            + [whole((1, tokens)), whole((tokens, 1)), whole((1, dim)), whole((1, dim))]
            + [whole((tokens, half))] * len(into),
            out_specs=[whole((tokens, width))] * 3,
        ),
        out_shape=[jax.ShapeDtypeStruct((tokens, width), BF16)] * 3,
        compiler_params=pltpu.CompilerParams(vmem_limit_bytes=(60 if into else 40) << 20),
        cost_estimate=pl.CostEstimate(flops=1000, bytes_accessed=1000, transcendentals=0),
        name="attention_backward",
    )(place, mine, came, grads, row, col, qg, kg, *into)


def products_kernel(n, place, *refs):
    w_refs, mid_refs, end_refs, rest = refs[:2], refs[2:4], refs[4:7], refs[7:]
    g_refs, (keep_ref, send_ref, acc_ref) = rest[: 2 * n], rest[2 * n :]
    step = pl.program_id(0)
    rows = w_refs[0].shape[0]

    @pl.when(step == 0)
    def _():
        acc_ref[...] = jnp.zeros_like(acc_ref)

    ends = (jnp.where(step < 2, end_refs[0][...], end_refs[1][...]), end_refs[2][...])
    both = [
        jnp.concatenate([w_refs[c][...], jnp.where(place[3] == 1, mid_refs[c][...], ends[c])], axis=0)
        for c in range(2)
    ]
    both = jnp.concatenate(both, axis=1)
    for j in range(n):
        acc_ref[j] += dot_nt(both, jnp.concatenate([g_refs[j][...], g_refs[n + j][...]], axis=1))

    @pl.when(step == pl.num_programs(0) - 1)
    def _():
        flip = place[2] == 1
        for j in range(n):
            own, other = acc_ref[j, :rows].astype(BF16), acc_ref[j, rows:].astype(BF16)
            keep_ref[j] = jnp.where(flip, other, own)
            send_ref[j] = jnp.where(flip, own, other)


def columns(rows, tile, start=0):
    skip = start // tile
    return pl.BlockSpec((rows, tile), lambda i, p: (0, i + skip))


def gradient_products(place, w, mid, end, halves):
    rows, depth = w.shape
    cut, tile = depth // 2, depth // 6
    n, tokens = len(halves[0]), halves[0][0][0].shape[0]
    out = whole((n, rows, tokens))
    ends = (lambda i, p: (0, jnp.minimum(i, 1)), lambda i, p: (0, 0), lambda i, p: (0, i + 1))
    return pl.pallas_call(
        functools.partial(products_kernel, n),
        grid_spec=pltpu.PrefetchScalarGridSpec(
            num_scalar_prefetch=1,
            grid=(3,),
            in_specs=[columns(rows, tile), columns(rows, tile, cut)] * 2
            + [pl.BlockSpec((rows, tile), index) for index in ends]
            + [columns(tokens, tile, start) for half in halves for _, start in half],
            out_specs=[out, out],
            scratch_shapes=[pltpu.VMEM((n, 2 * rows, tokens), F32)],
        ),
        out_shape=[jax.ShapeDtypeStruct((n, rows, tokens), BF16)] * 2,
        compiler_params=pltpu.CompilerParams(vmem_limit_bytes=40 << 20),
        cost_estimate=pl.CostEstimate(flops=1000, bytes_accessed=1000, transcendentals=0),
        name="gradient_products",
    )(place, w, w, mid, mid, end[0], end[1], end[1], *[a for half in halves for a, _ in half])


def weight_kernel(n, parts, place, own_ref, other_ref, *refs):
    g_refs, far_refs, kept_ref, both_ref = refs[:n], refs[n:-2], refs[-2], refs[-1]
    rows, tokens = own_ref.shape[1:]
    step = pl.program_id(0)

    @pl.when(step == 0)
    def _():
        flip = place[2] == 1
        for j in range(n):
            cols = slice(j * tokens, (j + 1) * tokens)
            both_ref[:rows, cols] = jnp.where(flip, own_ref[j], other_ref[j])
            both_ref[rows:, cols] = jnp.where(flip, other_ref[j], own_ref[j])

    total = dot_nn(both_ref[...], jnp.concatenate([g_ref[...] for g_ref in g_refs], axis=0))
    kept_ref[...] = total[rows:]
    sent = total[:rows].astype(BF16)
    first = 0
    for part, far_ref in zip(parts, far_refs):
        for c in range(part):

            @pl.when(step == first + c)
            def _(c=c, far_ref=far_ref):
                tile = sent.shape[1]
                far_ref[:, c * tile : (c + 1) * tile] = sent

        first += part


def weight_terms(place, own, other, half, parts, tile=512):
    n, rows, tokens = own.shape
    depth = sum(parts) * tile
    return pl.pallas_call(
        functools.partial(weight_kernel, n, parts),
        grid_spec=pltpu.PrefetchScalarGridSpec(
            num_scalar_prefetch=1,
            grid=(sum(parts),),
            in_specs=[whole((n, rows, tokens))] * 2 + [columns(tokens, tile, start) for start in half[1]],
            out_specs=[whole((rows, part * tile)) for part in parts] + [columns(rows, tile)],
            scratch_shapes=[pltpu.VMEM((2 * rows, n * tokens), BF16)],
        ),
        out_shape=[jax.ShapeDtypeStruct((rows, part * tile), BF16) for part in parts]
        + [jax.ShapeDtypeStruct((rows, depth), F32)],
        compiler_params=pltpu.CompilerParams(vmem_limit_bytes=40 << 20),
        cost_estimate=pl.CostEstimate(flops=1000, bytes_accessed=1000, transcendentals=0),
        name="weight_terms",
    )(place, own, other, *half[0])


def finish_kernel(parts, scale, *refs):
    kept_refs, far_refs, out_ref = refs[:2], refs[2:-1], refs[-1]
    kept = [kept_ref[...] for kept_ref in kept_refs]
    first, cut = 0, kept[0].shape[1]
    for far_ref in far_refs:
        last = first + far_ref.shape[1]
        own = kept[first // cut][:, first % cut : (last - 1) % cut + 1]
        out_ref[:, first:last] = (own + far_ref[...].astype(F32)) * scale
        first = last


def finish(kept, far, scale):
    rows, depth = kept[0].shape[0], 2 * kept[0].shape[1]
    tile = rows // 4

    def block(a):
        return pl.BlockSpec((tile, a.shape[1]), lambda i: (i, 0))

    return pl.pallas_call(
        functools.partial(finish_kernel, len(far), scale),
        grid=(rows // tile,),
        in_specs=[block(a) for a in (*kept, *far)],
        out_specs=pl.BlockSpec((tile, depth), lambda i: (i, 0)),
        out_shape=jax.ShapeDtypeStruct((rows, depth), F32),
        compiler_params=pltpu.CompilerParams(vmem_limit_bytes=40 << 20),
        cost_estimate=pl.CostEstimate(flops=1000, bytes_accessed=1000, transcendentals=0),
        name="finish",
    )(*kept, *far)


def xor(k):
    return [(j, j ^ k) for j in range(16)]


CORE, CROSS, PLANE = xor(1), xor(2), xor(4)
FAR = xor(12)
MIDDLE = [pair for pair in FAR if 4 <= pair[0] < 12]
ENDS = [pair for pair in FAR if not 4 <= pair[0] < 12]


def move(a, perm, name):
    with jax.named_scope(name):
        return lax.ppermute(a, "fsdp", perm)


def swap(a, name):
    with jax.named_scope(name):
        return lax.ppermute(a, "seq", [(0, 1), (1, 0)])


def local_grid(queries, keys, values, image_ids, q_gain, k_gain, w_out, grad_y):
    y = lax.axis_index("seq")
    f = lax.axis_index("fsdp")
    middle = (f >> 3) ^ ((f >> 2) & 1)
    place = jnp.stack([y, f & 7, (f >> 3) ^ y, middle]).astype(jnp.int32)
    dim = q_gain.shape[0]
    tokens = image_ids.shape[1]
    half = queries.shape[1] // 2
    row, col = image_ids, image_ids.reshape(tokens, 1)
    qg, kg = q_gain.reshape(1, dim), k_gain.reshape(1, dim)
    barrier = lax.optimization_barrier
    cut = grad_y.shape[1] // 2

    cut = grad_y.shape[1] // 2
    barrier = lax.optimization_barrier

    mine, send = pack(place, (queries, keys, values))
    third = 2 * cut // 3
    g4 = move(grad_y, PLANE, "gy_plane")
    w_a, w_b = w_out[:, :third], w_out[:, third:]
    send, gy, w_own, w_a = barrier((send, grad_y, w_out, w_a))
    came = swap(send, "qkv_seq")
    g2 = move(gy, CROSS, "gy_cross")
    w_end_a = move(w_a, ENDS, "w_ends_a")
    w_mid = move(w_own, MIDDLE, "w_middle")
    even, odd = attention_forward(place, mine, came, row, col, qg, kg)
    odd = move(odd, CORE, "att_core")
    even, odd, g2, g4, gy, w_mid, w_end_a, w_b = barrier((even, odd, g2, g4, gy, w_mid, w_end_a, w_b))
    own = [jnp.stack([even[j], odd[j]]) for j in range(4)]
    other = [swap(own[0], "att_seq")]
    own = [own[0]] + [move(own[j], xor(2 * j), "att_group") for j in (1, 2, 3)]
    g1 = move(gy, CORE, "gy_core")
    g4a, g4b = g4[:, :cut], g4[:, cut:]
    own, other, g4, g4a, g4b, w_b, g2, g1 = barrier((own, other, g4, g4a, g4b, w_b, g2, g1))
    other.append(swap(jnp.concatenate(own[1:]), "att_seq"))
    g6a = move(g4a, CROSS, "gy_plane_cross_a")
    w_end_b = move(w_b, ENDS, "w_ends_b")
    g3, g5 = (move(g, CORE, "gy_core") for g in (g2, g4))
    own, other = jnp.concatenate(own), jnp.concatenate(other)
    own, other, g6a, w_end_b, g3, g5, g4b = barrier((own, other, g6a, w_end_b, g3, g5, g4b))
    weights = (w_out, w_mid, (w_end_a, w_end_b))
    g6b = move(g4b, CROSS, "gy_plane_cross_b")
    g7a = move(g6a, CORE, "gy_core")
    half_a = ([gy, g1, g2, g3, g4, g5, g6a, g7a], (0,) * 8)
    *sent, kept_a = weight_terms(place, own, other, half_a, (1, 2))
    far = [move(sent[0], FAR, "grad_w_far")]
    tied = barrier((gy, g2, g1, g3, sent[0]))[:4]
    keep0, send0 = gradient_products(place, *weights, [[(a, start) for a in tied] for start in (0, cut)])
    g6b, keep0, send0, far, sent, kept_a = barrier((g6b, keep0, send0, far, sent, kept_a))
    came0 = swap(send0, "products_seq")
    far.append(move(sent[1], FAR, "grad_w_far"))
    summed0 = (keep0.astype(F32) + came0.astype(F32)).astype(BF16)
    odd = move(summed0[2:], CORE, "products_core")
    near = [jnp.stack([summed0[j], odd[j]]) for j in range(2)]
    near[1] = move(near[1], xor(2), "products_group")
    g7b = move(g6b, CORE, "gy_core")
    keep1, send1 = gradient_products(
        place, *weights, [[(g4, 0), (g6a, 0), (g5, 0), (g7a, 0)], [(g4, cut), (g6b, 0), (g5, cut), (g7b, 0)]]
    )
    came1 = swap(send1, "products_seq")
    half_b, keep1 = barrier(([gy, g1, g2, g3, g4, g5, g6b, g7b], keep1))
    *sent, kept_b = weight_terms(place, own, other, (half_b, (cut,) * 6 + (0,) * 2), (1, 2))
    far, near, keep1, came1, sent, kept_b = barrier((far, near, keep1, came1, sent, kept_b))
    far.append(move(sent[0], FAR, "grad_w_far"))
    summed1 = (keep1.astype(F32) + came1.astype(F32)).astype(BF16)
    odd = move(summed1[2:], CORE, "products_core")
    next_plane = [jnp.stack([summed1[j], odd[j]]) for j in range(2)]
    next_plane = [move(next_plane[j], xor(4 + 2 * j), "products_group") for j in range(2)]
    grads = attention_backward(place, 0, mine, came, jnp.stack(near), row, col, qg, kg)
    far, next_plane, grads, sent = barrier((far, next_plane, grads, sent))
    far.append(move(sent[1], FAR, "grad_w_far"))
    gq, gk, gv = attention_backward(
        place, 2, mine, came, jnp.stack(next_plane), row, col, qg, kg, tuple(grads)
    )

    grad_w = finish((kept_a, kept_b), far, tokens ** (-0.5))
    shape = (tokens, half // dim, dim)
    return (gq.reshape(shape), gk.reshape(shape), gv.reshape(shape), grad_w)


def solution(mesh):
    in_specs = (
        P(("fsdp", "seq"), None),
        P(("fsdp", "seq"), None),
        P(("fsdp", "seq"), None),
        P("fsdp", None),
        P(),
        P(),
        P("fsdp", "seq"),
        P("fsdp", "seq"),
    )
    out_specs = (
        P("fsdp", "seq", None),
        P("fsdp", "seq", None),
        P("fsdp", "seq", None),
        P("fsdp", "seq"),
    )
    grid = mesh.shape["fsdp"] == 16 and mesh.shape["seq"] == 2
    local = local_grid if grid else local_any
    return jax.shard_map(local, mesh=mesh, in_specs=in_specs, out_specs=out_specs, check_vma=False)
```

time: 250 us -> 184 us (0.74)
  the two profiles are of different devices: /device:TPU:9 before, /device:TPU:0 now
where the time goes in v2:
time: 184 us; the launch traced here: 183 us
  waiting for transfers between devices  78.3 us (43%)
  Pallas kernels  51.1 us (28%)
  starting transfers between devices  33.5 us (18%)
  local copies, waits for them, and re-layouts  17.1 us (9%)
  other arithmetic  2.02 us (1%)
    ppermute x5, waiting for transfers between devices, swap(): return lax.ppermute(a, 'seq', [(0, 1), (1, 0)])  43.5 us
    ppermute x25, waiting for transfers between devices, move(): return lax.ppermute(a, 'fsdp', perm)  34.8 us
    ppermute x25, starting transfers between devices, move(): return lax.ppermute(a, 'fsdp', perm)  28.3 us
    pallas_call x2, Pallas kernels, attention_backward(): pl.pallas_call(functools.partial(backward_kernel, per, dim, len(into)), g...  16.7 us
    pallas_call x2, Pallas kernels, weight_terms(): pl.pallas_call(functools.partial(weight_kernel, n, parts), grid_spec=pltp...  10.8 us
    pallas_call x2, Pallas kernels, gradient_products(): pl.pallas_call(functools.partial(products_kernel, n), grid_spec=pltpu.Pre...  10.7 us
    unnamed x39, local copies, waits for them, and re-layouts  9.73 us
    pallas_call x1, Pallas kernels, attention_forward(): pl.pallas_call(functools.partial(forward_kernel, per, dim), grid_spec=plt...  7.16 us
  transfers between devices with their start and end apart: 30, of which 14 were waited for; matrix products, arithmetic and copies ran while one was open for 6% of the time, Pallas kernels for 25%

profile of v2, /device:TPU:0, one launch (start us, length us, event | category | flops | bytes accessed | tf_op | source)
XLA Modules:
  0.0 183.1 jit_solution(16995695384642316485)
XLA Ops:
  0.6 1.8 slice.66
  2.4 0.6 pad_add_fusion.place
  3.0 3.7 %pack.1 = (bf16[3,128,1536]{2,1,0:T(8,128)(2,1)}, bf16[3,128,1536]{2,1,0:T(8,128)(2,1)}) custom-call(s32[4]{0:T(128)} %pad_add_fusion.place, bf16[128,3072]{1,0:T(8,128)(2,1)} %refs_3_.1, bf16[128,3072]{1,0:T(8,128)(2,1)} %refs_4_.1, bf16[128,3072]{1,0:T(8,128)(2,1)} %refs_5_.1, bf16[128,3072]{1,0:T(8,128)(2,1)} %refs_3_.1, bf16[128,3072]{1,0:T(8,128)(2,1)} %refs_4_.1, ...), custom_call_target="tpu_custom_call" | custom-call | flops 1000 | bytes 1000 | tf_op jit(solution)/shard_map/pack/pallas_call | solution.py:146
  6.7 3.0 %collective-permute-start = (bf16[3,128,1536]{2,1,0:T(8,128)(2,1)}, bf16[3,128,1536]{2,1,0:T(8,128)(2,1)}, u32[]{:S(2)}, u32[]{:S(2)}) collective-permute-start(bf16[3,128,1536]{2,1,0:T(8,128)(2,1)} %get-tuple-element.93), channel_id=1, source_target_pairs={{0,1},{1,0},{2,3},{3,2},{4,5},{5,4},{6,7},{7,6},{8,9},{9,8},{10,11... | collective-permute-start | bytes 3538952 | tf_op jit(solution)/shard_map/qkv_seq/ppermute | solution.py:422
  9.7 1.6 collective-permute-start.3
  11.3 1.5 collective-permute-start.2
  12.8 1.7 collective-permute-start.4
  14.5 4.4 %collective-permute-start.5 = (bf16[192,1024]{1,0:T(8,128)(2,1)}, bf16[192,1024]{1,0:T(8,128)(2,1)S(1)}, u32[]{:S(2)}, u32[]{:S(2)}) collective-permute-start(bf16[192,1024]{1,0:T(8,128)(2,1)} %slice.66), channel_id=1, source_target_pairs={{0,24},{2,26},{4,28},{6,30},{24,0},{26,2},{28,4},{30,6},{1,25},{3,... | collective-permute-start | bytes 1179656 | tf_op jit(solution)/shard_map/w_ends_a/ppermute | solution.py:417
  18.9 0.1 copy.15.col_ref
  19.0 17.0 %collective-permute-done.came_ref = bf16[3,128,1536]{2,1,0:T(8,128)(2,1)} collective-permute-done((bf16[3,128,1536]{2,1,0:T(8,128)(2,1)}, bf16[3,128,1536]{2,1,0:T(8,128)(2,1)}, u32[]{:S(2)}, u32[]{:S(2)}) %collective-permute-start) | collective-permute-done | bytes 1179680 | tf_op jit(solution)/shard_map/qkv_seq/ppermute | solution.py:422
  36.0 1.3 copy-done.2
  37.3 7.2 %attention_forward.1 = (bf16[4,192,256]{2,1,0:T(8,128)(2,1)S(1)}, bf16[4,192,256]{2,1,0:T(8,128)(2,1)S(1)}) custom-call(s32[4]{0:T(128)S(1)} %copy-done.14, bf16[3,128,1536]{2,1,0:T(8,128)(2,1)S(1)} %copy-done.2, bf16[3,128,1536]{2,1,0:T(8,128)(2,1)} %collective-permute-done.came_ref, s32[1,256]{1,0:T(1,128)S(1)} %copy-done.15, s32[256,1]{1,0:T(8,128)S(1)} %copy.15.col_ref, ...), custom_call_target="tpu_custom_call" | custom-call | flops 1000 | bytes 1000 | tf_op jit(solution)/shard_map/attention_forward/pallas_call | solution.py:230
  44.6 11.6 %collective-permute-done.5.refs_4_ = bf16[192,1024]{1,0:T(8,128)(2,1)S(1)} collective-permute-done((bf16[192,1024]{1,0:T(8,128)(2,1)}, bf16[192,1024]{1,0:T(8,128)(2,1)S(1)}, u32[]{:S(2)}, u32[]{:S(2)}) %collective-permute-start.5) | collective-permute-done | bytes 393248 | tf_op jit(solution)/shard_map/w_ends_a/ppermute | solution.py:417
  56.4 1.6 collective-permute-start.6
  58.1 0.6 collective-permute-start.9
  58.7 2.0 %collective-permute-start.8 = (bf16[2,192,256]{2,1,0:T(8,128)(2,1)S(1)}, bf16[2,192,256]{2,1,0:T(8,128)(2,1)S(1)}, u32[]{:S(2)}, u32[]{:S(2)}) collective-permute-start(bf16[2,192,256]{2,1,0:T(8,128)(2,1)S(1)} %pad_maximum_fusion.8), channel_id=1, source_target_pairs={{0,12},{2,14},{4,8},{6,10},{8,4},{10,6},{12,0},{14,2},{16,28},{18,... | collective-permute-start | bytes 589832 | tf_op jit(solution)/shard_map/att_group/ppermute | solution.py:417
  60.7 0.1 fusion
  60.9 2.9 %collective-permute-done.6 = bf16[2,192,256]{2,1,0:T(8,128)(2,1)S(1)} collective-permute-done((bf16[2,192,256]{2,1,0:T(8,128)(2,1)S(1)}, bf16[2,192,256]{2,1,0:T(8,128)(2,1)S(1)}, u32[]{:S(2)}, u32[]{:S(2)}) %collective-permute-start.6) | collective-permute-done | bytes 196640 | tf_op jit(solution)/shard_map/att_group/ppermute | solution.py:417
  63.8 2.0 %collective-permute-done.7 = bf16[2,192,256]{2,1,0:T(8,128)(2,1)S(1)} collective-permute-done((bf16[2,192,256]{2,1,0:T(8,128)(2,1)S(1)}, bf16[2,192,256]{2,1,0:T(8,128)(2,1)S(1)}, u32[]{:S(2)}, u32[]{:S(2)}) %collective-permute-start.7) | collective-permute-done | bytes 196640 | tf_op jit(solution)/shard_map/att_group/ppermute | solution.py:417
  65.8 3.5 %collective-permute-done.8 = bf16[2,192,256]{2,1,0:T(8,128)(2,1)S(1)} collective-permute-done((bf16[2,192,256]{2,1,0:T(8,128)(2,1)S(1)}, bf16[2,192,256]{2,1,0:T(8,128)(2,1)S(1)}, u32[]{:S(2)}, u32[]{:S(2)}) %collective-permute-start.8) | collective-permute-done | bytes 196640 | tf_op jit(solution)/shard_map/att_group/ppermute | solution.py:417
  69.3 0.5 collective-permute-start.15
  69.8 1.5 collective-permute-start.12
  71.3 3.6 %collective-permute-start.13 = (bf16[192,2048]{1,0:T(8,128)(2,1)S(1)}, bf16[192,2048]{1,0:T(8,128)(2,1)S(1)}, u32[]{:S(2)}, u32[]{:S(2)}) collective-permute-start(bf16[192,2048]{1,0:T(8,128)(2,1)S(1)} %slice.67), channel_id=1, source_target_pairs={{0,24},{2,26},{4,28},{6,30},{24,0},{26,2},{28,4},{30,6},{1,25},{3,... | collective-permute-start | bytes 2359304 | tf_op jit(solution)/shard_map/w_ends_b/ppermute | solution.py:417
  75.0 0.6 collective-permute-start.11
  75.6 0.1 pad_maximum_fusion.own_ref
  75.7 14.1 %collective-permute-done.11 = bf16[6,192,256]{2,1,0:T(8,128)(2,1)S(1)} collective-permute-done((bf16[6,192,256]{2,1,0:T(8,128)(2,1)S(1)}, bf16[6,192,256]{2,1,0:T(8,128)(2,1)S(1)}, u32[]{:S(2)}, u32[]{:S(2)}) %collective-permute-start.11) | collective-permute-done | bytes 589856 | tf_op jit(solution)/shard_map/att_seq/ppermute | solution.py:422
  89.8 4.3 %collective-permute-done.13.refs_5_.refs_6_ = bf16[192,2048]{1,0:T(8,128)(2,1)S(1)} collective-permute-done((bf16[192,2048]{1,0:T(8,128)(2,1)S(1)}, bf16[192,2048]{1,0:T(8,128)(2,1)S(1)}, u32[]{:S(2)}, u32[]{:S(2)}) %collective-permute-start.13) | collective-permute-done | bytes 786464 | tf_op jit(solution)/shard_map/w_ends_b/ppermute | solution.py:417
  94.1 0.6 collective-permute-start.16
  94.7 1.7 collective-permute-done.17.refs_7_.refs_10_
  96.4 5.0 %weight_terms.2 = (bf16[192,512]{1,0:T(8,128)(2,1)S(1)}, bf16[192,1024]{1,0:T(8,128)(2,1)S(1)}, f32[192,1536]{1,0:T(8,128)S(1)}) custom-call(s32[4]{0:T(128)S(1)} %copy-done.14, bf16[8,192,256]{2,1,0:T(8,128)(2,1)S(1)} %pad_maximum_fusion.own_ref, bf16[8,192,256]{2,1,0:T(8,128)(2,1)S(1)} %pad_maximum_fusion.1.other_ref, bf16[256,3072]{1,0:T(8,128)(2,1)S(1)} %copy-done.1, ...), custom_call_target="tpu_custom_call" | custom-call | flops 1000 | bytes 1000 | tf_op jit(solution)/shard_map/weight_terms/pallas_call | solution.py:358
  101.5 1.6 collective-permute-start.18
  103.1 5.4 %gradient_products.2 = (bf16[4,192,256]{2,1,0:T(8,128)(2,1)S(1)}, bf16[4,192,256]{2,1,0:T(8,128)(2,1)S(1)}) custom-call(s32[4]{0:T(128)S(1)} %copy-done.14, bf16[192,3072]{1,0:T(8,128)(2,1)S(1)} %copy-done, bf16[192,3072]{1,0:T(8,128)(2,1)S(1)} %copy-done, bf16[192,3072]{1,0:T(8,128)(2,1)} %collective-permute-done.4.refs_2_.refs_3_, ...), custom_call_target="tpu_custom_call" | custom-call | flops 1000 | bytes 1000 | tf_op jit(solution)/shard_map/gradient_products/pallas_call | solution.py:309
  108.6 5.5 %collective-permute-done.16.refs_12_.refs_6_ = bf16[256,1536]{1,0:T(8,128)(2,1)S(1)} collective-permute-done((bf16[256,1536]{1,0:T(8,128)(2,1)S(1)}, bf16[256,1536]{1,0:T(8,128)(2,1)S(1)}, u32[]{:S(2)}, u32[]{:S(2)}) %collective-permute-start.16) | collective-permute-done | bytes 786464 | tf_op jit(solution)/shard_map/gy_plane_cross_b/ppermute | solution.py:417
  114.1 0.5 collective-permute-start.20
  114.6 1.6 collective-permute-start.19
  116.2 8.6 %collective-permute-done.20 = bf16[4,192,256]{2,1,0:T(8,128)(2,1)S(1)} collective-permute-done((bf16[4,192,256]{2,1,0:T(8,128)(2,1)S(1)}, bf16[4,192,256]{2,1,0:T(8,128)(2,1)S(1)}, u32[]{:S(2)}, u32[]{:S(2)}) %collective-permute-start.20) | collective-permute-done | bytes 393248 | tf_op jit(solution)/shard_map/products_seq/ppermute | solution.py:422
  124.8 0.1 add_convert_fusion.1
  125.0 5.3 %gradient_products.3 = (bf16[4,192,256]{2,1,0:T(8,128)(2,1)S(1)}, bf16[4,192,256]{2,1,0:T(8,128)(2,1)S(1)}) custom-call(s32[4]{0:T(128)S(1)} %copy-done.14, bf16[192,3072]{1,0:T(8,128)(2,1)S(1)} %copy-done, bf16[192,3072]{1,0:T(8,128)(2,1)S(1)} %copy-done, bf16[192,3072]{1,0:T(8,128)(2,1)} %collective-permute-done.4.refs_2_.refs_3_, ...), custom_call_target="tpu_custom_call" | custom-call | flops 1000 | bytes 1000 | tf_op jit(solution)/shard_map/gradient_products/pallas_call | solution.py:309
  130.3 0.5 collective-permute-start.24
  130.9 0.6 collective-permute-start.22
  131.5 5.8 %weight_terms.3 = (bf16[192,512]{1,0:T(8,128)(2,1)S(1)}, bf16[192,1024]{1,0:T(8,128)(2,1)}, f32[192,1536]{1,0:T(8,128)S(1)}) custom-call(s32[4]{0:T(128)S(1)} %copy-done.14, bf16[8,192,256]{2,1,0:T(8,128)(2,1)S(1)} %pad_maximum_fusion.own_ref, bf16[8,192,256]{2,1,0:T(8,128)(2,1)S(1)} %pad_maximum_fusion.1.other_ref, bf16[256,3072]{1,0:T(8,128)(2,1)S(1)} %copy-done.1, ...), custom_call_target="tpu_custom_call" | custom-call | flops 1000 | bytes 1000 | tf_op jit(solution)/shard_map/weight_terms/pallas_call | solution.py:358
  137.3 0.7 collective-permute-done.22
  137.9 3.9 %collective-permute-done.24 = bf16[4,192,256]{2,1,0:T(8,128)(2,1)S(1)} collective-permute-done((bf16[4,192,256]{2,1,0:T(8,128)(2,1)S(1)}, bf16[4,192,256]{2,1,0:T(8,128)(2,1)S(1)}, u32[]{:S(2)}, u32[]{:S(2)}) %collective-permute-start.24) | collective-permute-done | bytes 393248 | tf_op jit(solution)/shard_map/products_seq/ppermute | solution.py:422
  141.8 1.6 collective-permute-start.25
  143.4 0.1 add_convert_fusion
  143.6 1.4 collective-permute-done.26
  145.2 2.0 %collective-permute-start.28 = (bf16[2,192,256]{2,1,0:T(8,128)(2,1)S(1)}, bf16[2,192,256]{2,1,0:T(8,128)(2,1)S(1)}, u32[]{:S(2)}, u32[]{:S(2)}) collective-permute-start(bf16[2,192,256]{2,1,0:T(8,128)(2,1)S(1)} %pad_maximum_fusion.12), channel_id=1, source_target_pairs={{0,12},{2,14},{4,8},{6,10},{8,4},{10,6},{12,0},{14,2},{16,28},{18,... | collective-permute-start | bytes 589832 | tf_op jit(solution)/shard_map/products_group/ppermute | solution.py:417
  147.3 7.2 %attention_backward.2 = (bf16[256,768]{1,0:T(8,128)(2,1)S(1)}, bf16[256,768]{1,0:T(8,128)(2,1)S(1)}, bf16[256,768]{1,0:T(8,128)(2,1)S(1)}) custom-call(s32[4]{0:T(128)S(1)} %copy-done.14, bf16[3,128,1536]{2,1,0:T(8,128)(2,1)S(1)} %copy-done.3, bf16[3,128,1536]{2,1,0:T(8,128)(2,1)} %collective-permute-done.came_ref, ...), custom_call_target="tpu_custom_call" | custom-call | flops 1000 | bytes 1000 | tf_op jit(solution)/shard_map/attention_backward/pallas_call | solution.py:252
  154.6 0.7 copy-done.9
  155.3 0.8 copy-done.10
  156.0 0.7 copy-done.11
  156.8 0.7 copy-done.12
  157.5 1.1 collective-permute-done.28
  158.6 1.5 collective-permute-start.29
  160.1 0.8 pad_maximum_fusion.4.d_ref
  160.9 9.5 %attention_backward.3 = (bf16[256,1536]{1,0:T(8,128)(2,1)}, bf16[256,1536]{1,0:T(8,128)(2,1)}, bf16[256,1536]{1,0:T(8,128)(2,1)}) custom-call(s32[4]{0:T(128)} %pad_add_fusion.place, bf16[3,128,1536]{2,1,0:T(8,128)(2,1)} %get-tuple-element.91.own_ref, bf16[3,128,1536]{2,1,0:T(8,128)(2,1)} %collective-permute-done.came_ref, ...), custom_call_target="tpu_custom_call" | custom-call | flops 1000 | bytes 1000 | tf_op jit(solution)/shard_map/attention_backward/pallas_call | solution.py:252
  170.4 1.4 copy.18
  171.8 1.2 copy.21
  172.9 1.4 copy.19
  174.4 1.2 copy.22
  175.5 2.4 %copy.20 = bf16[256,1536]{0,1:T(8,128)(2,1)} copy(bf16[256,1536]{1,0:T(8,128)(2,1)} %get-tuple-element.171) | data formatting | bytes 1572864 | tf_op jit(solution)/shard_map/attention_backward/pallas_call | solution.py:252
  177.9 2.3 %copy.23 = bf16[256,12,128]{2,0,1:T(8,128)(2,1)} copy(bf16[256,12,128]{0,2,1:T(8,128)(2,1)} %bitcast.23) | data formatting | bytes 1572864
  180.2 0.9 copy-done.13
  181.1 1.9 %finish.1 = f32[192,3072]{1,0:T(8,128)} custom-call(f32[192,1536]{1,0:T(8,128)S(1)} %copy-done.6, f32[192,1536]{1,0:T(8,128)S(1)} %get-tuple-element.173.refs_1_, bf16[192,512]{1,0:T(8,128)(2,1)S(1)} %collective-permute-done.18.refs_2_, bf16[192,1024]{1,0:T(8,128)(2,1)S(1)} %copy-done.8, bf16[192,512]{1,0:T(8,128)(2,1)S(1)} %copy-done.13, ...), custom_call_target="tpu_custom_call" | custom-call | flops 1000 | bytes 1000 | tf_op jit(solution)/shard_map/finish/pallas_call | solution.py:393
  (74 shorter events, 1.1 us)
Async XLA Ops:
  3.0 9.8 %copy-start = (bf16[192,3072]{1,0:T(8,128)(2,1)S(1)}, bf16[192,3072]{1,0:T(8,128)(2,1)}, u32[]{:S(2)}) copy-start(bf16[192,3072]{1,0:T(8,128)(2,1)} %refs_1_.5) | copy-start | bytes 3538948
  3.0 15.8 %copy-start.15 = (s32[1,256]{1,0:T(1,128)S(1)}, s32[1,256]{1,0:T(1,128)}, u32[]{:S(2)}) copy-start(s32[1,256]{1,0:T(1,128)} %row_ref.5) | copy-start | bytes 3076
  3.0 33.0 %copy-start.14 = (s32[4]{0:T(128)S(1)}, s32[4]{0:T(128)}, u32[]{:S(2)}) copy-start(s32[4]{0:T(128)} %pad_add_fusion.place) | copy-start | bytes 52
  3.0 33.0 %copy-start.16 = (f32[128]{0:T(128)S(1)}, f32[128]{0:T(128)}, u32[]{:S(2)}) copy-start(f32[128]{0:T(128)} %param.12) | copy-start | bytes 1540
  3.0 33.0 %copy-start.17 = (f32[128]{0:T(128)S(1)}, f32[128]{0:T(128)}, u32[]{:S(2)}) copy-start(f32[128]{0:T(128)} %param.13) | copy-start | bytes 1540
  6.7 29.2 %collective-permute-start = (bf16[3,128,1536]{2,1,0:T(8,128)(2,1)}, bf16[3,128,1536]{2,1,0:T(8,128)(2,1)}, u32[]{:S(2)}, u32[]{:S(2)}) collective-permute-start(bf16[3,128,1536]{2,1,0:T(8,128)(2,1)} %get-tuple-element.93), channel_id=1, source_target_pairs={{0,1},{1,0},{2,3},{3,2},{4,5},{5,4},{6,7},{7,6},{8,9},{9,8},{10,11... | collective-permute-start | bytes 3538952 | tf_op jit(solution)/shard_map/qkv_seq/ppermute | solution.py:422
  9.7 46.5 %collective-permute-start.3 = (bf16[256,3072]{1,0:T(8,128)(2,1)}, bf16[256,3072]{1,0:T(8,128)(2,1)S(1)}, u32[]{:S(2)}, u32[]{:S(2)}) collective-permute-start(bf16[256,3072]{1,0:T(8,128)(2,1)} %refs_0_.7), channel_id=1, source_target_pairs={{0,8},{2,10},{4,12},{6,14},{8,0},{10,2},{12,4},{14,6},{16,24},{18,... | collective-permute-start | bytes 4718600 | tf_op jit(solution)/shard_map/gy_plane/ppermute | solution.py:417
  11.3 45.0 %collective-permute-start.2 = (bf16[256,3072]{1,0:T(8,128)(2,1)}, bf16[256,3072]{1,0:T(8,128)(2,1)}, u32[]{:S(2)}, u32[]{:S(2)}) collective-permute-start(bf16[256,3072]{1,0:T(8,128)(2,1)} %refs_0_.7), channel_id=1, source_target_pairs={{0,4},{2,6},{4,0},{6,2},{8,12},{10,14},{12,8},{14,10},{16,20},{18,... | collective-permute-start | bytes 4718600 | tf_op jit(solution)/shard_map/gy_cross/ppermute | solution.py:417
  12.8 43.4 %collective-permute-start.4 = (bf16[192,3072]{1,0:T(8,128)(2,1)S(1)}, bf16[192,3072]{1,0:T(8,128)(2,1)}, u32[]{:S(2)}, u32[]{:S(2)}) collective-permute-start(bf16[192,3072]{1,0:T(8,128)(2,1)S(1)} %copy-done), channel_id=1, source_target_pairs={{8,16},{10,18},{12,20},{14,22},{16,8},{18,10},{20,12},{22,14},{9,1... | collective-permute-start | bytes 3538952 | tf_op jit(solution)/shard_map/w_middle/ppermute | solution.py:417
  14.5 41.7 %collective-permute-start.5 = (bf16[192,1024]{1,0:T(8,128)(2,1)}, bf16[192,1024]{1,0:T(8,128)(2,1)S(1)}, u32[]{:S(2)}, u32[]{:S(2)}) collective-permute-start(bf16[192,1024]{1,0:T(8,128)(2,1)} %slice.66), channel_id=1, source_target_pairs={{0,24},{2,26},{4,28},{6,30},{24,0},{26,2},{28,4},{30,6},{1,25},{3,... | collective-permute-start | bytes 1179656 | tf_op jit(solution)/shard_map/w_ends_a/ppermute | solution.py:417
  19.0 128.3 %copy-start.4 = (s32[256,1]{1,0:T(8,128)}, s32[256,1]{1,0:T(8,128)S(1)}, u32[]{:S(2)}) copy-start(s32[256,1]{1,0:T(8,128)S(1)} %copy.15.col_ref) | copy-start | bytes 3076
  36.0 1.3 copy-start.2
  37.3 19.0 %copy-start.1 = (bf16[256,3072]{1,0:T(8,128)(2,1)S(1)}, bf16[256,3072]{1,0:T(8,128)(2,1)}, u32[]{:S(2)}) copy-start(bf16[256,3072]{1,0:T(8,128)(2,1)} %refs_0_.7) | copy-start | bytes 4718596
  44.4 11.8 %collective-permute-start.1 = (bf16[4,192,256]{2,1,0:T(8,128)(2,1)S(1)}, bf16[4,192,256]{2,1,0:T(8,128)(2,1)S(1)}, u32[]{:S(2)}, u32[]{:S(2)}) collective-permute-start(bf16[4,192,256]{2,1,0:T(8,128)(2,1)S(1)} %get-tuple-element.95), channel_id=1, source_target_pairs={{0,2},{2,0},{4,6},{6,4},{8,10},{10,8},{12,14},{14,12},{16,18},{18,... | collective-permute-start | bytes 1179656 | tf_op jit(solution)/shard_map/att_core/ppermute | solution.py:417
  56.3 13.0 %collective-permute-start.10 = (bf16[256,3072]{1,0:T(8,128)(2,1)S(1)}, bf16[256,3072]{1,0:T(8,128)(2,1)S(1)}, u32[]{:S(2)}, u32[]{:S(2)}) collective-permute-start(bf16[256,3072]{1,0:T(8,128)(2,1)S(1)} %copy-done.1), channel_id=1, source_target_pairs={{0,2},{2,0},{4,6},{6,4},{8,10},{10,8},{12,14},{14,12},{16,18},{18,... | collective-permute-start | bytes 4718600 | tf_op jit(solution)/shard_map/gy_core/ppermute | solution.py:417
  56.4 7.4 %collective-permute-start.6 = (bf16[2,192,256]{2,1,0:T(8,128)(2,1)S(1)}, bf16[2,192,256]{2,1,0:T(8,128)(2,1)S(1)}, u32[]{:S(2)}, u32[]{:S(2)}) collective-permute-start(bf16[2,192,256]{2,1,0:T(8,128)(2,1)S(1)} %pad_maximum_fusion.6), channel_id=1, source_target_pairs={{0,4},{2,6},{4,0},{6,2},{8,12},{10,14},{12,8},{14,10},{16,20},{18,... | collective-permute-start | bytes 589832 | tf_op jit(solution)/shard_map/att_group/ppermute | solution.py:417
  58.0 7.8 %collective-permute-start.7 = (bf16[2,192,256]{2,1,0:T(8,128)(2,1)S(1)}, bf16[2,192,256]{2,1,0:T(8,128)(2,1)S(1)}, u32[]{:S(2)}, u32[]{:S(2)}) collective-permute-start(bf16[2,192,256]{2,1,0:T(8,128)(2,1)S(1)} %pad_maximum_fusion.7), channel_id=1, source_target_pairs={{0,8},{2,10},{4,12},{6,14},{8,0},{10,2},{12,4},{14,6},{16,24},{18,... | collective-permute-start | bytes 589832 | tf_op jit(solution)/shard_map/att_group/ppermute | solution.py:417
  58.1 7.7 %collective-permute-start.9 = (bf16[2,192,256]{2,1,0:T(8,128)(2,1)S(1)}, bf16[2,192,256]{2,1,0:T(8,128)(2,1)S(1)}, u32[]{:S(2)}, u32[]{:S(2)}) collective-permute-start(bf16[2,192,256]{2,1,0:T(8,128)(2,1)S(1)} %pad_maximum_fusion.5), channel_id=1, source_target_pairs={{0,1},{1,0},{2,3},{3,2},{4,5},{5,4},{6,7},{7,6},{8,9},{9,8},{10,11... | collective-permute-start | bytes 589832 | tf_op jit(solution)/shard_map/att_seq/ppermute | solution.py:422
  58.7 10.6 %collective-permute-start.8 = (bf16[2,192,256]{2,1,0:T(8,128)(2,1)S(1)}, bf16[2,192,256]{2,1,0:T(8,128)(2,1)S(1)}, u32[]{:S(2)}, u32[]{:S(2)}) collective-permute-start(bf16[2,192,256]{2,1,0:T(8,128)(2,1)S(1)} %pad_maximum_fusion.8), channel_id=1, source_target_pairs={{0,12},{2,14},{4,8},{6,10},{8,4},{10,6},{12,0},{14,2},{16,28},{18,... | collective-permute-start | bytes 589832 | tf_op jit(solution)/shard_map/att_group/ppermute | solution.py:417
  69.3 24.9 %collective-permute-start.14 = (bf16[256,3072]{1,0:T(8,128)(2,1)}, bf16[256,3072]{1,0:T(8,128)(2,1)S(1)}, u32[]{:S(2)}, u32[]{:S(2)}) collective-permute-start(bf16[256,3072]{1,0:T(8,128)(2,1)} %collective-permute-done.2.refs_2_.refs_8_.refs_12_), channel_id=1, source_target_pairs={{0,2},{2,0},{4,6},{6,4},{8,10},{10,8},{12,14},{14,12},{16,18},{18,... | collective-permute-start | bytes 4718600 | tf_op jit(solution)/shard_map/gy_core/ppermute | solution.py:417
  69.3 24.9 %collective-permute-start.15 = (bf16[256,3072]{1,0:T(8,128)(2,1)S(1)}, bf16[256,3072]{1,0:T(8,128)(2,1)S(1)}, u32[]{:S(2)}, u32[]{:S(2)}) collective-permute-start(bf16[256,3072]{1,0:T(8,128)(2,1)S(1)} %collective-permute-done.3.refs_4_.refs_7_.refs_11_), channel_id=1, source_target_pairs={{0,2},{2,0},{4,6},{6,4},{8,10},{10,8},{12,14},{14,12},{16,18},{18,... | collective-permute-start | bytes 4718600 | tf_op jit(solution)/shard_map/gy_core/ppermute | solution.py:417
  69.8 20.0 %collective-permute-start.12 = (bf16[256,1536]{1,0:T(8,128)(2,1)S(1)}, bf16[256,1536]{1,0:T(8,128)(2,1)S(1)}, u32[]{:S(2)}, u32[]{:S(2)}) collective-permute-start(bf16[256,1536]{1,0:T(8,128)(2,1)S(1)} %get-tuple-element.110), channel_id=1, source_target_pairs={{0,4},{2,6},{4,0},{6,2},{8,12},{10,14},{12,8},{14,10},{16,20},{18,... | collective-permute-start | bytes 2359304 | tf_op jit(solution)/shard_map/gy_plane_cross_a/ppermute | solution.py:417
  71.3 22.8 %collective-permute-start.13 = (bf16[192,2048]{1,0:T(8,128)(2,1)S(1)}, bf16[192,2048]{1,0:T(8,128)(2,1)S(1)}, u32[]{:S(2)}, u32[]{:S(2)}) collective-permute-start(bf16[192,2048]{1,0:T(8,128)(2,1)S(1)} %slice.67), channel_id=1, source_target_pairs={{0,24},{2,26},{4,28},{6,30},{24,0},{26,2},{28,4},{30,6},{1,25},{3,... | collective-permute-start | bytes 2359304 | tf_op jit(solution)/shard_map/w_ends_b/ppermute | solution.py:417
  75.0 14.7 %collective-permute-start.11 = (bf16[6,192,256]{2,1,0:T(8,128)(2,1)S(1)}, bf16[6,192,256]{2,1,0:T(8,128)(2,1)S(1)}, u32[]{:S(2)}, u32[]{:S(2)}) collective-permute-start(bf16[6,192,256]{2,1,0:T(8,128)(2,1)S(1)} %pad_maximum_fusion.2), channel_id=1, source_target_pairs={{0,1},{1,0},{2,3},{3,2},{4,5},{5,4},{6,7},{7,6},{8,9},{9,8},{10,11... | collective-permute-start | bytes 1769480 | tf_op jit(solution)/shard_map/att_seq/ppermute | solution.py:422
  94.1 2.3 %collective-permute-start.17 = (bf16[256,1536]{1,0:T(8,128)(2,1)S(1)}, bf16[256,1536]{1,0:T(8,128)(2,1)S(1)}, u32[]{:S(2)}, u32[]{:S(2)}) collective-permute-start(bf16[256,1536]{1,0:T(8,128)(2,1)S(1)} %collective-permute-done.12.refs_6_.refs_8_), channel_id=1, source_target_pairs={{0,2},{2,0},{4,6},{6,4},{8,10},{10,8},{12,14},{14,12},{16,18},{18,... | collective-permute-start | bytes 2359304 | tf_op jit(solution)/shard_map/gy_core/ppermute | solution.py:417
  94.1 19.9 %collective-permute-start.16 = (bf16[256,1536]{1,0:T(8,128)(2,1)S(1)}, bf16[256,1536]{1,0:T(8,128)(2,1)S(1)}, u32[]{:S(2)}, u32[]{:S(2)}) collective-permute-start(bf16[256,1536]{1,0:T(8,128)(2,1)S(1)} %get-tuple-element.115), channel_id=1, source_target_pairs={{0,4},{2,6},{4,0},{6,2},{8,12},{10,14},{12,8},{14,10},{16,20},{18,... | collective-permute-start | bytes 2359304 | tf_op jit(solution)/shard_map/gy_plane_cross_b/ppermute | solution.py:417
  101.5 7.1 %copy-start.5 = (f32[192,1536]{1,0:T(8,128)}, f32[192,1536]{1,0:T(8,128)S(1)}, u32[]{:S(2)}) copy-start(f32[192,1536]{1,0:T(8,128)S(1)} %get-tuple-element.172.refs_0_) | copy-start | bytes 3538948
  101.5 12.6 %collective-permute-start.18 = (bf16[192,512]{1,0:T(8,128)(2,1)S(1)}, bf16[192,512]{1,0:T(8,128)(2,1)S(1)}, u32[]{:S(2)}, u32[]{:S(2)}) collective-permute-start(bf16[192,512]{1,0:T(8,128)(2,1)S(1)} %get-tuple-element.125), channel_id=1, source_target_pairs={{0,24},{2,26},{4,28},{6,30},{8,16},{10,18},{12,20},{14,22},{16,8},... | collective-permute-start | bytes 589832 | tf_op jit(solution)/shard_map/grad_w_far/ppermute | solution.py:417
  114.1 10.7 %collective-permute-start.20 = (bf16[4,192,256]{2,1,0:T(8,128)(2,1)S(1)}, bf16[4,192,256]{2,1,0:T(8,128)(2,1)S(1)}, u32[]{:S(2)}, u32[]{:S(2)}) collective-permute-start(bf16[4,192,256]{2,1,0:T(8,128)(2,1)S(1)} %get-tuple-element.137), channel_id=1, source_target_pairs={{0,1},{1,0},{2,3},{3,2},{4,5},{5,4},{6,7},{7,6},{8,9},{9,8},{10,11... | collective-permute-start | bytes 1179656 | tf_op jit(solution)/shard_map/products_seq/ppermute | solution.py:422
  114.6 10.4 %collective-permute-start.23 = (bf16[256,1536]{1,0:T(8,128)(2,1)S(1)}, bf16[256,1536]{1,0:T(8,128)(2,1)S(1)}, u32[]{:S(2)}, u32[]{:S(2)}) collective-permute-start(bf16[256,1536]{1,0:T(8,128)(2,1)S(1)} %collective-permute-done.16.refs_12_.refs_6_), channel_id=1, source_target_pairs={{0,2},{2,0},{4,6},{6,4},{8,10},{10,8},{12,14},{14,12},{16,18},{18,... | collective-permute-start | bytes 2359304 | tf_op jit(solution)/shard_map/gy_core/ppermute | solution.py:417
  114.6 22.7 %collective-permute-start.19 = (bf16[192,1024]{1,0:T(8,128)(2,1)S(1)}, bf16[192,1024]{1,0:T(8,128)(2,1)S(1)}, u32[]{:S(2)}, u32[]{:S(2)}) collective-permute-start(bf16[192,1024]{1,0:T(8,128)(2,1)S(1)} %get-tuple-element.135), channel_id=1, source_target_pairs={{0,24},{2,26},{4,28},{6,30},{8,16},{10,18},{12,20},{14,22},{16,8},... | collective-permute-start | bytes 1179656 | tf_op jit(solution)/shard_map/grad_w_far/ppermute | solution.py:417
  124.9 5.9 %collective-permute-start.21 = (bf16[2,192,256]{2,1,0:T(8,128)(2,1)S(1)}, bf16[2,192,256]{2,1,0:T(8,128)(2,1)S(1)}, u32[]{:S(2)}, u32[]{:S(2)}) collective-permute-start(bf16[2,192,256]{2,1,0:T(8,128)(2,1)S(1)} %slice.89), channel_id=1, source_target_pairs={{0,2},{2,0},{4,6},{6,4},{8,10},{10,8},{12,14},{14,12},{16,18},{18,... | collective-permute-start | bytes 589832 | tf_op jit(solution)/shard_map/products_core/ppermute | solution.py:417
  130.3 11.6 %collective-permute-start.24 = (bf16[4,192,256]{2,1,0:T(8,128)(2,1)S(1)}, bf16[4,192,256]{2,1,0:T(8,128)(2,1)S(1)}, u32[]{:S(2)}, u32[]{:S(2)}) collective-permute-start(bf16[4,192,256]{2,1,0:T(8,128)(2,1)S(1)} %get-tuple-element.141), channel_id=1, source_target_pairs={{0,1},{1,0},{2,3},{3,2},{4,5},{5,4},{6,7},{7,6},{8,9},{9,8},{10,11... | collective-permute-start | bytes 1179656 | tf_op jit(solution)/shard_map/products_seq/ppermute | solution.py:422
  130.9 7.1 %collective-permute-start.22 = (bf16[2,192,256]{2,1,0:T(8,128)(2,1)S(1)}, bf16[2,192,256]{2,1,0:T(8,128)(2,1)S(1)}, u32[]{:S(2)}, u32[]{:S(2)}) collective-permute-start(bf16[2,192,256]{2,1,0:T(8,128)(2,1)S(1)} %pad_maximum_fusion.10), channel_id=1, source_target_pairs={{0,4},{2,6},{4,0},{6,2},{8,12},{10,14},{12,8},{14,10},{16,20},{18,... | collective-permute-start | bytes 589832 | tf_op jit(solution)/shard_map/products_group/ppermute | solution.py:417
  137.3 7.9 %copy-start.7 = (bf16[192,1024]{1,0:T(8,128)(2,1)}, bf16[192,1024]{1,0:T(8,128)(2,1)S(1)}, u32[]{:S(2)}) copy-start(bf16[192,1024]{1,0:T(8,128)(2,1)S(1)} %collective-permute-done.19.refs_3_) | copy-start | bytes 1179652
  141.8 15.0 %collective-permute-start.25 = (bf16[192,512]{1,0:T(8,128)(2,1)S(1)}, bf16[192,512]{1,0:T(8,128)(2,1)S(1)}, u32[]{:S(2)}, u32[]{:S(2)}) collective-permute-start(bf16[192,512]{1,0:T(8,128)(2,1)S(1)} %get-tuple-element.155), channel_id=1, source_target_pairs={{0,24},{2,26},{4,28},{6,30},{8,16},{10,18},{12,20},{14,22},{16,8},... | collective-permute-start | bytes 589832 | tf_op jit(solution)/shard_map/grad_w_far/ppermute | solution.py:417
  143.5 3.8 %copy-start.3 = (bf16[3,128,1536]{2,1,0:T(8,128)(2,1)S(1)}, bf16[3,128,1536]{2,1,0:T(8,128)(2,1)}, u32[]{:S(2)}) copy-start(bf16[3,128,1536]{2,1,0:T(8,128)(2,1)} %get-tuple-element.91.own_ref) | copy-start | bytes 3538948
  143.5 1.5 collective-permute-start.26
  145.1 12.4 %collective-permute-start.27 = (bf16[2,192,256]{2,1,0:T(8,128)(2,1)S(1)}, bf16[2,192,256]{2,1,0:T(8,128)(2,1)S(1)}, u32[]{:S(2)}, u32[]{:S(2)}) collective-permute-start(bf16[2,192,256]{2,1,0:T(8,128)(2,1)S(1)} %pad_maximum_fusion.11), channel_id=1, source_target_pairs={{0,8},{2,10},{4,12},{6,14},{8,0},{10,2},{12,4},{14,6},{16,24},{18,... | collective-permute-start | bytes 589832 | tf_op jit(solution)/shard_map/products_group/ppermute | solution.py:417
  145.2 13.4 %collective-permute-start.28 = (bf16[2,192,256]{2,1,0:T(8,128)(2,1)S(1)}, bf16[2,192,256]{2,1,0:T(8,128)(2,1)S(1)}, u32[]{:S(2)}, u32[]{:S(2)}) collective-permute-start(bf16[2,192,256]{2,1,0:T(8,128)(2,1)S(1)} %pad_maximum_fusion.12), channel_id=1, source_target_pairs={{0,12},{2,14},{4,8},{6,10},{8,4},{10,6},{12,0},{14,2},{16,28},{18,... | collective-permute-start | bytes 589832 | tf_op jit(solution)/shard_map/products_group/ppermute | solution.py:417
  154.5 0.7 copy-start.9
  155.3 0.8 copy-start.10
  156.0 0.8 copy-start.11
  156.8 0.7 copy-start.12
  158.6 21.7 %collective-permute-start.29 = (bf16[192,1024]{1,0:T(8,128)(2,1)}, bf16[192,1024]{1,0:T(8,128)(2,1)S(1)}, u32[]{:S(2)}, u32[]{:S(2)}) collective-permute-start(bf16[192,1024]{1,0:T(8,128)(2,1)} %get-tuple-element.177), channel_id=1, source_target_pairs={{0,24},{2,26},{4,28},{6,30},{8,16},{10,18},{12,20},{14,22},{16,8},... | collective-permute-start | bytes 1179656 | tf_op jit(solution)/shard_map/grad_w_far/ppermute | solution.py:417
  175.5 4.7 %copy-start.6 = (f32[192,1536]{1,0:T(8,128)S(1)}, f32[192,1536]{1,0:T(8,128)}, u32[]{:S(2)}) copy-start(f32[192,1536]{1,0:T(8,128)} %copy-done.5) | copy-start | bytes 3538948
  175.5 4.7 %copy-start.8 = (bf16[192,1024]{1,0:T(8,128)(2,1)S(1)}, bf16[192,1024]{1,0:T(8,128)(2,1)}, u32[]{:S(2)}) copy-start(bf16[192,1024]{1,0:T(8,128)(2,1)} %copy-done.7) | copy-start | bytes 1179652
  180.2 0.9 copy-start.13

commit v3 on v2

v3 whole, which is shorter than its diff:
```python
import functools

import jax
import jax.numpy as jnp
from jax import lax
from jax.experimental import pallas as pl
from jax.experimental.pallas import tpu as pltpu
from jax.sharding import PartitionSpec as P

F32 = jnp.float32
BF16 = jnp.bfloat16


def norm_parts(source, gain):
    wide = source.astype(jnp.float32)
    centred = wide - jnp.mean(wide, axis=-1, keepdims=True)
    scale_inv = lax.rsqrt(jnp.mean(centred * centred, axis=-1, keepdims=True) + 1e-06)
    x_hat = centred * scale_inv
    return (x_hat, scale_inv, (x_hat * gain).astype(jnp.bfloat16))


def norm_back(grad_n, x_hat, scale_inv, gain):
    scaled = grad_n * gain
    return scale_inv * (
        scaled
        - jnp.mean(scaled, axis=-1, keepdims=True)
        - x_hat * jnp.mean(scaled * x_hat, axis=-1, keepdims=True)
    )


def probabilities(normalized_queries, normalized_keys, same_image, scale_factor):
    scores = (
        jnp.einsum(
            "krt,irt->rki", normalized_queries, normalized_keys, preferred_element_type=jnp.float32
        )
        * scale_factor
    )
    scores = jnp.where(same_image[None], scores, -1e30)
    row_top = jnp.max(scores, axis=-1, keepdims=True)
    exp_terms = jnp.exp(scores - row_top)
    return exp_terms / jnp.sum(exp_terms, axis=-1, keepdims=True)


def local_any(queries, keys, values, image_ids, q_gain, k_gain, w_out, grad_y):
    head_dim = q_gain.shape[0]
    tok_rows = queries.shape[0]
    heads_all = queries.shape[1] // head_dim
    scale_factor = head_dim ** (-0.5)
    q_patch = queries.reshape(tok_rows, heads_all, head_dim)
    k_patch = keys.reshape(tok_rows, heads_all, head_dim)
    v_patch = values.reshape(tok_rows, heads_all, head_dim)
    q_local, k_local, value_shard = (
        lax.all_to_all(q_patch, "seq", split_axis=1, concat_axis=0, tiled=True),
        lax.all_to_all(k_patch, "seq", split_axis=1, concat_axis=0, tiled=True),
        lax.all_to_all(v_patch, "seq", split_axis=1, concat_axis=0, tiled=True),
    )
    seq_length = q_local.shape[0]
    local_heads = q_local.shape[1]
    image_row = image_ids[0]
    same_image = image_row[:, None] == image_row[None, :]
    q_hat, q_inv, normalized_queries = norm_parts(q_local, q_gain)
    k_hat, k_inv, normalized_keys = norm_parts(k_local, k_gain)
    prob_rows = probabilities(normalized_queries, normalized_keys, same_image, scale_factor)
    probs_reduced_precision = prob_rows.astype(jnp.bfloat16)
    attended = jnp.einsum(
        "tgi,itp->gtp", probs_reduced_precision, value_shard, preferred_element_type=jnp.float32
    ).astype(jnp.bfloat16)
    attended_flat = attended.reshape(seq_length, local_heads * head_dim)
    partial_g = jnp.einsum(
        "ld,cd->lc",
        grad_y,
        lax.all_gather(w_out, "fsdp", axis=0, tiled=True),
        preferred_element_type=jnp.float32,
    )
    grad_sum = lax.psum_scatter(
        partial_g.astype(jnp.bfloat16), "seq", scatter_dimension=1, tiled=True
    )
    attention_gradient = grad_sum.reshape(seq_length, local_heads, head_dim)
    grad_values = jnp.einsum(
        "jpw,pjy->wjy",
        probs_reduced_precision,
        attention_gradient,
        preferred_element_type=jnp.float32,
    ).astype(jnp.bfloat16)
    probability_gradient = jnp.einsum(
        "krt,irt->rki", attention_gradient, value_shard, preferred_element_type=jnp.float32
    )
    row_delta = jnp.sum(prob_rows * probability_gradient, axis=-1, keepdims=True)
    score_gradient = (prob_rows * (probability_gradient - row_delta) * scale_factor).astype(
        jnp.bfloat16
    )
    normed_query_gradient = jnp.einsum(
        "tgi,itp->gtp", score_gradient, normalized_keys, preferred_element_type=jnp.float32
    )
    normed_key_gradient = jnp.einsum(
        "jpw,pjy->wjy", score_gradient, normalized_queries, preferred_element_type=jnp.float32
    )
    grad_queries = norm_back(normed_query_gradient, q_hat, q_inv, q_gain).astype(jnp.bfloat16)
    grad_keys = norm_back(normed_key_gradient, k_hat, k_inv, k_gain).astype(jnp.bfloat16)
    partial_w = jnp.einsum(
        "lc,ld->cd",
        lax.all_gather(attended_flat, "seq", axis=1, tiled=True),
        grad_y,
        preferred_element_type=jnp.float32,
    )
    summed = lax.psum_scatter(partial_w, "fsdp", scatter_dimension=0, tiled=True)
    grad_w = summed * seq_length ** (-0.5)
    return (grad_queries, grad_keys, grad_values, grad_w)


def dot_nt(a, b):
    return lax.dot_general(a, b, (((1,), (1,)), ((), ())), preferred_element_type=F32)


def dot_tn(a, b):
    return lax.dot_general(a, b, (((0,), (0,)), ((), ())), preferred_element_type=F32)


def dot_nn(a, b):
    return jnp.dot(a, b, preferred_element_type=F32)


def assemble(first, own, came):
    return jnp.concatenate([jnp.where(first, own, came), jnp.where(first, came, own)], axis=0)


def head_inputs(place, own_ref, came_ref, h, dim):
    first = place[0] == 0
    cols = slice(h * dim, (h + 1) * dim)
    return [assemble(first, own_ref[n, :, cols], came_ref[n, :, cols]) for n in range(3)]


def pack_kernel(place, *refs):
    mine, theirs, own_ref, send_ref = refs[:3], refs[3:6], refs[6], refs[7]
    for n in range(3):
        own_ref[n] = mine[n][...]
        send_ref[n] = theirs[n][...]


def pack(place, arrays, steps=1):
    rows, width = arrays[0].shape[0], arrays[0].shape[1] // 2
    wide = width // steps
    mine = pl.BlockSpec((rows, wide), lambda i, p: (0, p[0] * steps + i))
    theirs = pl.BlockSpec((rows, wide), lambda i, p: (0, (1 - p[0]) * steps + i))
    out = pl.BlockSpec((3, rows, wide), lambda i, p: (0, 0, i))
    return pl.pallas_call(
        pack_kernel,
        grid_spec=pltpu.PrefetchScalarGridSpec(
            num_scalar_prefetch=1, grid=(steps,), in_specs=[mine] * 3 + [theirs] * 3, out_specs=[out, out]
        ),
        out_shape=[pltpu.HBM((3, rows, width), BF16), jax.ShapeDtypeStruct((3, rows, width), BF16)],
        cost_estimate=pl.CostEstimate(flops=1000, bytes_accessed=1000, transcendentals=0),
        name="pack",
    )(place, *arrays, *arrays)


def head_probs(q, k, qg, kg, same, scale):
    q_hat, q_inv, qn = norm_parts(q, qg)
    k_hat, k_inv, kn = norm_parts(k, kg)
    scores = jnp.where(same, dot_nt(qn, kn) * scale, -1e30)
    exp_terms = jnp.exp(scores - jnp.max(scores, axis=-1, keepdims=True))
    probs = exp_terms / jnp.sum(exp_terms, axis=-1, keepdims=True)
    return probs, q_hat, q_inv, qn, k_hat, k_inv, kn


def forward_kernel(per, dim, place, own_ref, came_ref, row_ref, col_ref, qg_ref, kg_ref, even_ref, odd_ref):
    same = col_ref[...] == row_ref[...]
    done = []
    for h in range(per):
        q, k, v = head_inputs(place, own_ref, came_ref, h, dim)
        probs = head_probs(q, k, qg_ref[...], kg_ref[...], same, dim**-0.5)[0]
        done.append(dot_nn(probs.astype(BF16), v).T.astype(BF16))
    att = jnp.concatenate(done, axis=0)
    half = att.shape[0] // 2
    straight = (place[1] & 1) == 0
    low, high = att[:half], att[half:]
    even_ref[0] = jnp.where(straight, low, high)
    odd_ref[0] = jnp.where(straight, high, low)


def prepare_kernel(per, dim, place, own_ref, came_ref, row_ref, col_ref, qg_ref, kg_ref, p_ref, hat_ref, inv_ref, low_ref):
    same = col_ref[...] == row_ref[...]
    for h in range(per):
        q, k, v = head_inputs(place, own_ref, came_ref, h, dim)
        probs, *parts = head_probs(q, k, qg_ref[...], kg_ref[...], same, dim**-0.5)
        p_ref[h] = probs
        for n, (hat, inv, normed) in enumerate((parts[:3], parts[3:])):
            hat_ref[n, h] = hat
            inv_ref[n, h] = jnp.broadcast_to(inv, hat.shape)
            low_ref[n, h] = normed
        low_ref[2, h] = v


def backward_kernel(per, dim, n_into, place, p_ref, hat_ref, inv_ref, low_ref, d_ref, qg_ref, kg_ref, *rest):
    gq_ref, gk_ref, gv_ref = rest[n_into:]
    scale = dim**-0.5
    straight = (place[1] & 1) == 0
    one, two = d_ref[0, 0], d_ref[0, 1]
    grad = jnp.concatenate([jnp.where(straight, one, two), jnp.where(straight, two, one)], axis=0)
    qg, kg = qg_ref[...], kg_ref[...]
    for h in range(per):
        probs, qn, kn, v = p_ref[h], low_ref[0, h], low_ref[1, h], low_ref[2, h]
        d = grad[h * dim : (h + 1) * dim].T
        gp = dot_nt(d, v)
        gv_ref[h] = dot_tn(probs.astype(BF16), d).astype(BF16)
        delta = jnp.sum(probs * gp, axis=-1, keepdims=True)
        gs = (probs * (gp - delta) * scale).astype(BF16)
        gq_ref[h] = norm_back(dot_nn(gs, kn), hat_ref[0, h], inv_ref[0, h], qg).astype(BF16)
        gk_ref[h] = norm_back(dot_tn(gs, qn), hat_ref[1, h], inv_ref[1, h], kg).astype(BF16)


def whole(shape):
    return pl.BlockSpec(shape, lambda *_: (0,) * len(shape))


def pair_index(i, p):
    return i ^ (p[1] >> 1) ^ (p[2] << 1)


def attention_forward(place, mine, came, row, col, qg, kg):
    dim = qg.shape[1]
    half_tokens, heads = mine.shape[1], mine.shape[2] // dim
    tokens, per = 2 * half_tokens, heads // 4
    rows = per * dim // 2
    out = pl.BlockSpec((1, rows, tokens), lambda i, p: (pair_index(i, p), 0, 0))
    return pl.pallas_call(
        functools.partial(forward_kernel, per, dim),
        grid_spec=pltpu.PrefetchScalarGridSpec(
            num_scalar_prefetch=1,
            grid=(4,),
            in_specs=[pl.BlockSpec((3, half_tokens, per * dim), lambda i, p: (0, 0, i))] * 2
            + [whole((1, tokens)), whole((tokens, 1)), whole((1, dim)), whole((1, dim))],
            out_specs=[out, out],
        ),
        out_shape=[jax.ShapeDtypeStruct((4, rows, tokens), BF16)] * 2,
        compiler_params=pltpu.CompilerParams(vmem_limit_bytes=16 << 20),
        cost_estimate=pl.CostEstimate(flops=1000, bytes_accessed=1000, transcendentals=0),
        name="attention_forward",
    )(place, pltpu.with_memory_space_constraint(mine, pltpu.HBM), came, row, col, qg, kg)


def attention_prepare(place, mine, came, row, col, qg, kg):
    dim = qg.shape[1]
    half_tokens, heads = mine.shape[1], mine.shape[2] // dim
    tokens, per = 2 * half_tokens, heads // 4

    def saved(n, dtype):
        spec = pl.BlockSpec((n, per, tokens, dim), lambda i, p: (0, i, 0, 0))
        return spec, pltpu.HBM((n, heads, tokens, dim), dtype)

    probs = pl.BlockSpec((per, tokens, tokens), lambda i, p: (i, 0, 0)), pltpu.HBM((heads, tokens, tokens), F32)
    specs, shapes = zip(probs, saved(2, F32), saved(2, F32), saved(3, BF16))
    return pl.pallas_call(
        functools.partial(prepare_kernel, per, dim),
        grid_spec=pltpu.PrefetchScalarGridSpec(
            num_scalar_prefetch=1,
            grid=(4,),
            in_specs=[pl.BlockSpec((3, half_tokens, per * dim), lambda i, p: (0, 0, i))] * 2
            + [whole((1, tokens)), whole((tokens, 1)), whole((1, dim)), whole((1, dim))],
            out_specs=specs,
        ),
        out_shape=shapes,
        compiler_params=pltpu.CompilerParams(vmem_limit_bytes=16 << 20),
        cost_estimate=pl.CostEstimate(flops=1000, bytes_accessed=1000, transcendentals=0),
        name="attention_prepare",
    )(place, pltpu.with_memory_space_constraint(mine, pltpu.HBM), came, row, col, qg, kg)


def attention_backward(place, first, pairs, saved, grads, qg, kg, into=()):
    heads, tokens = saved[0].shape[:2]
    dim, per, rows = qg.shape[1], heads // 4, grads.shape[2]

    def index(i, p):
        return pair_index(i + first, p)

    def block(n):
        return pl.BlockSpec((n, per, tokens, dim), lambda i, p: (0, index(i, p), 0, 0))

    return pl.pallas_call(
        functools.partial(backward_kernel, per, dim, len(into)),
        grid_spec=pltpu.PrefetchScalarGridSpec(
            num_scalar_prefetch=1,
            grid=(pairs,),
            in_specs=[pl.BlockSpec((per, tokens, tokens), lambda i, p: (index(i, p), 0, 0)), block(2), block(2), block(3)]
            + [pl.BlockSpec((1, 2, rows, tokens), lambda i, p: (i, 0, 0, 0))]
            + [whole((1, dim)), whole((1, dim))]
            + [pl.BlockSpec(memory_space=pl.ANY)] * len(into),
            out_specs=[pl.BlockSpec((per, tokens, dim), lambda i, p: (index(i, p), 0, 0))] * 3,
        ),
        out_shape=[pltpu.HBM((heads, tokens, dim), BF16)] * 3,
        input_output_aliases={8 + n: n for n in range(len(into))},
        compiler_params=pltpu.CompilerParams(vmem_limit_bytes=16 << 20),
        cost_estimate=pl.CostEstimate(flops=1000, bytes_accessed=1000, transcendentals=0),
        name="attention_backward",
    )(place, *saved, grads, qg, kg, *into)


VECTOR = pl.BlockSpec(memory_space=pltpu.VMEM)
SCALAR = pl.BlockSpec(memory_space=pltpu.SMEM)


def hold_kernel(*refs):
    n = len(refs) // 2
    for source, held in zip(refs[:n], refs[n:]):
        held[...] = source[...]


def hold(*arrays, steps=4):
    specs = [pl.BlockSpec((a.shape[0] // steps, a.shape[1]), lambda i: (i, 0)) for a in arrays]
    return pl.pallas_call(
        hold_kernel,
        grid=(steps,),
        in_specs=specs,
        out_specs=specs,
        out_shape=[pltpu.VMEM(a.shape, a.dtype) for a in arrays],
        compiler_params=pltpu.CompilerParams(vmem_limit_bytes=16 << 20),
        cost_estimate=pl.CostEstimate(flops=1000, bytes_accessed=1000, transcendentals=0),
        name="hold",
    )(*arrays)


def products_kernel(n, parts, place, w_ref, mid_ref, end_ref, *refs):
    g_refs, (keep_ref, send_ref, both_ref) = refs[:-3], refs[-3:]
    rows = w_ref.shape[0]
    middle, flip = place[3] == 1, place[2] == 1
    for first, depth, _ in parts:
        cols = slice(first, first + depth)
        own, far = w_ref[:, cols], jnp.where(middle, mid_ref[:, cols], end_ref[:, cols])
        both_ref[:rows, cols] = jnp.where(flip, far, own)
        both_ref[rows:, cols] = jnp.where(flip, own, far)
    for j in range(n):
        total = None
        for c, (first, depth, starts) in enumerate(parts):
            start = starts[j]
            term = dot_nt(both_ref[:, first : first + depth], g_refs[c * n + j][:, start : start + depth])
            total = term if total is None else total + term
        keep_ref[j] = total[:rows].astype(BF16)
        send_ref[j] = total[rows:].astype(BF16)


def gradient_products(place, w, mid, end, parts):
    rows, depth = w.shape
    n, tokens = len(parts[0][0]), parts[0][0][0].shape[0]
    blocks = [a for part in parts for a in part[0]]
    return pl.pallas_call(
        functools.partial(products_kernel, n, [(first, wide, starts) for _, starts, first, wide in parts]),
        in_specs=[SCALAR] + [VECTOR] * (3 + len(blocks)),
        out_specs=[VECTOR] * 2,
        out_shape=[jax.ShapeDtypeStruct((n, rows, tokens), BF16)] * 2,
        scratch_shapes=[pltpu.VMEM((2 * rows, depth), BF16)],
        compiler_params=pltpu.CompilerParams(vmem_limit_bytes=16 << 20),
        cost_estimate=pl.CostEstimate(flops=1000, bytes_accessed=1000, transcendentals=0),
        name="gradient_products",
    )(place, w, mid, end, *blocks)


def weight_kernel(n, starts, parts, place, own_ref, other_ref, *refs):
    g_refs, far_refs, kept_ref, both_ref = refs[:n], refs[n:-2], refs[-2], refs[-1]
    rows, tokens = own_ref.shape[1:]
    flip = place[2] == 1
    for j in range(n):
        cols = slice(j * tokens, (j + 1) * tokens)
        both_ref[:rows, cols] = jnp.where(flip, own_ref[j], other_ref[j])
        both_ref[rows:, cols] = jnp.where(flip, other_ref[j], own_ref[j])
    first = 0
    for part, far_ref in zip(parts, far_refs):
        blocks = [g_ref[:, start + first : start + first + part] for g_ref, start in zip(g_refs, starts)]
        total = dot_nn(both_ref[...], jnp.concatenate(blocks, axis=0))
        far_ref[...] = total[:rows].astype(BF16)
        kept_ref[:, first : first + part] = total[rows:]
        first += part


def weight_terms(place, own, other, half, parts):
    n, rows, tokens = own.shape
    depth = sum(parts)
    return pl.pallas_call(
        functools.partial(weight_kernel, n, half[1], parts),
        in_specs=[SCALAR] + [VECTOR] * (2 + n),
        out_specs=[VECTOR] * (len(parts) + 1),
        out_shape=[jax.ShapeDtypeStruct((rows, part), BF16) for part in parts]
        + [jax.ShapeDtypeStruct((rows, depth), F32)],
        scratch_shapes=[pltpu.VMEM((2 * rows, n * tokens), BF16)],
        compiler_params=pltpu.CompilerParams(vmem_limit_bytes=16 << 20),
        cost_estimate=pl.CostEstimate(flops=1000, bytes_accessed=1000, transcendentals=0),
        name="weight_terms",
    )(place, own, other, *half[0])


def finish_kernel(n, scale, *refs):
    kept_refs, far_refs, out_ref = refs[:n], refs[n:-1], refs[-1]
    for group, cast in ((kept_refs, False), (far_refs, True)):
        first = 0
        for ref in group:
            last = first + ref.shape[1]
            if cast:
                out_ref[:, first:last] = (out_ref[:, first:last] + ref[...].astype(F32)) * scale
            else:
                out_ref[:, first:last] = ref[...]
            first = last


def finish(kept, far, scale):
    rows, depth = kept[0].shape[0], sum(a.shape[1] for a in kept)
    tile = rows // 4

    def block(a):
        return pl.BlockSpec((tile, a.shape[1]), lambda i: (i, 0))

    return pl.pallas_call(
        functools.partial(finish_kernel, len(kept), scale),
        grid=(rows // tile,),
        in_specs=[block(a) for a in (*kept, *far)],
        out_specs=pl.BlockSpec((tile, depth), lambda i: (i, 0)),
        out_shape=jax.ShapeDtypeStruct((rows, depth), F32),
        compiler_params=pltpu.CompilerParams(vmem_limit_bytes=16 << 20),
        cost_estimate=pl.CostEstimate(flops=1000, bytes_accessed=1000, transcendentals=0),
        name="finish",
    )(*kept, *far)


def xor(k):
    return [(j, j ^ k) for j in range(16)]


CORE, CROSS, PLANE = xor(1), xor(2), xor(4)
FAR = xor(12)
MIDDLE = [pair for pair in FAR if 4 <= pair[0] < 12]
ENDS = [pair for pair in FAR if not 4 <= pair[0] < 12]


def move(a, perm, name):
    with jax.named_scope(name):
        return lax.ppermute(a, "fsdp", perm)


def swap(a, name):
    with jax.named_scope(name):
        return lax.ppermute(a, "seq", [(0, 1), (1, 0)])


def local_grid(queries, keys, values, image_ids, q_gain, k_gain, w_out, grad_y):
    y = lax.axis_index("seq")
    f = lax.axis_index("fsdp")
    middle = (f >> 3) ^ ((f >> 2) & 1)
    place = jnp.stack([y, f & 7, (f >> 3) ^ y, middle]).astype(jnp.int32)
    dim = q_gain.shape[0]
    tokens = image_ids.shape[1]
    half = queries.shape[1] // 2
    row, col = image_ids, image_ids.reshape(tokens, 1)
    qg, kg = q_gain.reshape(1, dim), k_gain.reshape(1, dim)
    barrier = lax.optimization_barrier
    width = grad_y.shape[1]
    cut = 2 * width // 3

    width = grad_y.shape[1]
    cut = 2 * width // 3
    barrier = lax.optimization_barrier

    mine, send = pack(place, (queries, keys, values))
    send, gy, w_own = barrier((send, grad_y, w_out))
    came = swap(send, "qkv_seq")
    g4 = move(gy, PLANE, "gy_plane")
    g2 = move(gy, CROSS, "gy_cross")
    w_mid = move(w_own, MIDDLE, "w_middle")
    g1 = move(gy, CORE, "gy_core")
    even, odd = attention_forward(place, mine, came, row, col, qg, kg)
    odd = move(odd, CORE, "att_core")
    even, odd, g2, g4, gy, w_own, w_mid, g1 = barrier((even, odd, g2, g4, gy, w_own, w_mid, g1))
    own = [jnp.stack([even[j], odd[j]]) for j in range(4)]
    other = [swap(own[0], "att_seq")]
    own = [own[0]] + [move(own[j], xor(2 * j), "att_group") for j in (1, 2, 3)]
    g4a, g4b = g4[:, :cut], g4[:, cut:]
    held, w_held = hold(gy, w_own)
    own, other, g4, g4a, g4b, w_own, g2, gy, w_held = barrier((own, other, g4, g4a, g4b, w_own, g2, held, w_held))
    other.append(swap(jnp.concatenate(own[1:]), "att_seq"))
    g6a = move(g4a, CROSS, "gy_plane_cross_a")
    w_end = move(w_own, ENDS, "w_ends")
    g3, g5 = (move(g, CORE, "gy_core") for g in (g2, g4))
    saved = attention_prepare(place, mine, came, row, col, qg, kg)
    own, other = jnp.concatenate(own), jnp.concatenate(other)
    own, other, g6a, g3, g5, g4b, w_end, saved = barrier((own, other, g6a, g3, g5, g4b, w_end, saved))
    g6b = move(g4b, CROSS, "gy_plane_cross_b")
    g7a = move(g6a, CORE, "gy_core")
    blocks_a = [gy, g1, g2, g3, g4, g5, g6a, g7a]
    *sent, kept_a = weight_terms(place, own, other, (blocks_a, (0,) * 8), (cut // 4, cut // 2, cut // 4))
    far = [move(sent[0], FAR, "grad_w_far")]
    weights = (w_held, w_mid, w_end)
    tied = barrier((gy, g2, g1, g3, sent))[:4]
    keep0, send0 = gradient_products(place, *weights, [(tied, (start,) * 4, start, depth) for start, depth in ((0, cut), (cut, width - cut))])
    g6b, far, sent, kept_a, keep0, send0 = barrier((g6b, far, sent, kept_a, keep0, send0))
    came0 = swap(send0, "products_seq")
    far.append(move(sent[1], FAR, "grad_w_far"))
    g7b = move(g6b, CORE, "gy_core")
    keep1, send1 = gradient_products(
        place,
        *weights,
        [([g4, g6a, g5, g7a], (0,) * 4, 0, cut), ([g4, g6b, g5, g7b], (cut, 0, cut, 0), cut, width - cut)],
    )
    came1 = swap(send1, "products_seq")
    came0, keep1, blocks_b = barrier((came0, keep1, [gy, g1, g2, g3, g4, g5, g6b, g7b]))
    summed0 = (keep0.astype(F32) + came0.astype(F32)).astype(BF16)
    odd = move(summed0[2:], CORE, "products_core")
    near = [jnp.stack([summed0[j], odd[j]]) for j in range(2)]
    near[1] = move(near[1], xor(2), "products_group")
    starts_b = (cut,) * 6 + (0,) * 2
    *sent_b, kept_b = weight_terms(place, own, other, (blocks_b, starts_b), (width - cut,))
    far, near, keep1, came1, sent, sent_b, kept_b = barrier((far, near, keep1, came1, sent, sent_b, kept_b))
    summed1 = (keep1.astype(F32) + came1.astype(F32)).astype(BF16)
    odd = move(summed1[2:], CORE, "products_core")
    next_plane = [jnp.stack([summed1[j], odd[j]]) for j in range(2)]
    next_plane = [move(next_plane[j], xor(4 + 2 * j), "products_group") for j in range(2)]
    far += [move(part, FAR, "grad_w_far") for part in (sent[2], *sent_b)]
    grads = attention_backward(place, 0, 2, saved, jnp.stack(near), qg, kg)
    grads = attention_backward(place, 2, 2, saved, jnp.stack(next_plane), qg, kg, tuple(grads))

    grad_w = finish((kept_a, kept_b), far, tokens ** (-0.5))
    return (*(g.transpose(1, 0, 2) for g in grads), grad_w)


def solution(mesh):
    in_specs = (
        P(("fsdp", "seq"), None),
        P(("fsdp", "seq"), None),
        P(("fsdp", "seq"), None),
        P("fsdp", None),
        P(),
        P(),
        P("fsdp", "seq"),
        P("fsdp", "seq"),
    )
    out_specs = (
        P("fsdp", "seq", None),
        P("fsdp", "seq", None),
        P("fsdp", "seq", None),
        P("fsdp", "seq"),
    )
    grid = mesh.shape["fsdp"] == 16 and mesh.shape["seq"] == 2
    local = local_grid if grid else local_any
    return jax.shard_map(local, mesh=mesh, in_specs=in_specs, out_specs=out_specs, check_vma=False)
```

time: 184 us -> 158 us (0.86)
  local copies, waits for them, and re-layouts: 17.1 us -> 0.42 us
  waiting for transfers between devices: 78.3 us -> 63.7 us
  starting transfers between devices: 33.5 us -> 41.3 us
    ppermute x5, waiting for transfers between devices: 43.5 us -> 31.2 us  [swap(): return lax.ppermute(a, 'seq', [(0, 1), (1, 0)])]
    unnamed x39 -> x18, local copies, waits for them, and re-layouts: 9.73 us -> 0.03 us
    pallas_call x2, Pallas kernels: 16.7 us -> 8.86 us  [attention_backward(): pl.pallas_call(functools.partial(backward_kernel, per, dim, len(into)), g...]
    pallas_call x5 -> x7, Pallas kernels: 23.5 us -> 29.9 us  [the longest x2 8.78 us: gradient_products(): pl.pallas_call(functools.partial(products_kernel, n, [(first, wide, start...]
    pallas_call x3 -> x0, local copies, waits for them, and re-layouts: 5.21 us -> none  [attention_backward(): pl.pallas_call(functools.partial(backward_kernel, per, dim, len(into)), g...]
    ppermute x25 -> x24, starting transfers between devices: 28.3 us -> 33.1 us  [move(): return lax.ppermute(a, 'fsdp', perm)]
    ppermute x5, starting transfers between devices: 5.17 us -> 8.23 us  [swap(): return lax.ppermute(a, 'seq', [(0, 1), (1, 0)])]
    ppermute x25 -> x24, waiting for transfers between devices: 34.8 us -> 32.5 us  [move(): return lax.ppermute(a, 'fsdp', perm)]
  transfers between devices with their start and end apart: 30 -> 29, of which waited for: 14 -> 17; matrix products, arithmetic and copies ran while one was open for 6% -> 1% of each run, Pallas kernels for 25% -> 28%
where the time goes in v3:
time: 158 us; the launch traced here: 157 us
  waiting for transfers between devices  63.7 us (40%)
  Pallas kernels  49.8 us (32%)
  starting transfers between devices  41.3 us (26%)
    ppermute x24, starting transfers between devices, move(): return lax.ppermute(a, 'fsdp', perm)  33.1 us
    ppermute x24, waiting for transfers between devices, move(): return lax.ppermute(a, 'fsdp', perm)  32.5 us
    ppermute x5, waiting for transfers between devices, swap(): return lax.ppermute(a, 'seq', [(0, 1), (1, 0)])  31.2 us
    pallas_call x2, Pallas kernels, attention_backward(): pl.pallas_call(functools.partial(backward_kernel, per, dim, len(into)), g...  8.86 us
    pallas_call x2, Pallas kernels, gradient_products(): pl.pallas_call(functools.partial(products_kernel, n, [(first, wide, start...  8.78 us
    pallas_call x1, Pallas kernels, attention_prepare(): pl.pallas_call(functools.partial(prepare_kernel, per, dim), grid_spec=plt...  8.63 us
    ppermute x5, starting transfers between devices, swap(): return lax.ppermute(a, 'seq', [(0, 1), (1, 0)])  8.23 us
    pallas_call x2, Pallas kernels, weight_terms(): pl.pallas_call(functools.partial(weight_kernel, n, half[1], parts), in_sp...  8.16 us
  transfers between devices with their start and end apart: 29, of which 17 were waited for; matrix products, arithmetic and copies ran while one was open for 1% of the time, Pallas kernels for 28%

profile of v3, /device:TPU:0, one launch (start us, length us, event | category | flops | bytes accessed | tf_op | source)
XLA Modules:
  0.0 157.5 jit_solution(7306778266709256698)
XLA Ops:
  0.6 0.6 pad_add_fusion.place
  1.3 3.9 %pack.1 = (bf16[3,128,1536]{2,1,0:T(8,128)(2,1)}, bf16[3,128,1536]{2,1,0:T(8,128)(2,1)}) custom-call(s32[4]{0:T(128)} %pad_add_fusion.place, bf16[128,3072]{1,0:T(8,128)(2,1)} %refs_3_.1, bf16[128,3072]{1,0:T(8,128)(2,1)} %refs_4_.1, bf16[128,3072]{1,0:T(8,128)(2,1)} %refs_5_.1, bf16[128,3072]{1,0:T(8,128)(2,1)} %refs_3_.1, bf16[128,3072]{1,0:T(8,128)(2,1)} %refs_4_.1, ...), custom_call_target="tpu_custom_call" | custom-call | flops 1000 | bytes 1000 | tf_op jit(solution)/shard_map/pack/pallas_call | solution.py:146
  5.2 3.0 %collective-permute-start = (bf16[3,128,1536]{2,1,0:T(8,128)(2,1)}, bf16[3,128,1536]{2,1,0:T(8,128)(2,1)}, u32[]{:S(2)}, u32[]{:S(2)}) collective-permute-start(bf16[3,128,1536]{2,1,0:T(8,128)(2,1)} %get-tuple-element.96), channel_id=1, source_target_pairs={{0,1},{1,0},{2,3},{3,2},{4,5},{5,4},{6,7},{7,6},{8,9},{9,8},{10,11... | collective-permute-start | bytes 3538952 | tf_op jit(solution)/shard_map/qkv_seq/ppermute | solution.py:439
  8.2 1.5 collective-permute-start.2
  9.7 1.6 %collective-permute-start.3 = (bf16[256,3072]{1,0:T(8,128)(2,1)}, bf16[256,3072]{1,0:T(8,128)(2,1)S(1)}, u32[]{:S(2)}, u32[]{:S(2)}) collective-permute-start(bf16[256,3072]{1,0:T(8,128)(2,1)} %refs_0_.2), channel_id=1, source_target_pairs={{0,8},{2,10},{4,12},{6,14},{8,0},{10,2},{12,4},{14,6},{16,24},{18,... | collective-permute-start | bytes 4718600 | tf_op jit(solution)/shard_map/gy_plane/ppermute | solution.py:434
  11.3 0.0 collective-permute-start.5
  11.3 1.7 %collective-permute-start.4 = (bf16[192,3072]{1,0:T(8,128)(2,1)}, bf16[192,3072]{1,0:T(8,128)(2,1)}, u32[]{:S(2)}, u32[]{:S(2)}) collective-permute-start(bf16[192,3072]{1,0:T(8,128)(2,1)} %refs_1_.2), channel_id=1, source_target_pairs={{8,16},{10,18},{12,20},{14,22},{16,8},{18,10},{20,12},{22,14},{9,1... | collective-permute-start | bytes 3538952 | tf_op jit(solution)/shard_map/w_middle/ppermute | solution.py:434
  12.9 0.1 copy.15.col_ref
  13.1 21.4 %collective-permute-done.came_ref = bf16[3,128,1536]{2,1,0:T(8,128)(2,1)} collective-permute-done((bf16[3,128,1536]{2,1,0:T(8,128)(2,1)}, bf16[3,128,1536]{2,1,0:T(8,128)(2,1)}, u32[]{:S(2)}, u32[]{:S(2)}) %collective-permute-start) | collective-permute-done | bytes 1179680 | tf_op jit(solution)/shard_map/qkv_seq/ppermute | solution.py:439
  34.5 7.2 %attention_forward.1 = (bf16[4,192,256]{2,1,0:T(8,128)(2,1)S(1)}, bf16[4,192,256]{2,1,0:T(8,128)(2,1)S(1)}) custom-call(s32[4]{0:T(128)S(1)} %copy-done.5, bf16[3,128,1536]{2,1,0:T(8,128)(2,1)} %get-tuple-element.94.own_ref, bf16[3,128,1536]{2,1,0:T(8,128)(2,1)} %collective-permute-done.came_ref, s32[1,256]{1,0:T(1,128)S(1)} %copy-done.6, ...), custom_call_target="tpu_custom_call" | custom-call | flops 1000 | bytes 1000 | tf_op jit(solution)/shard_map/attention_forward/pallas_call | solution.py:226
  41.7 0.1 collective-permute-start.1
  41.7 0.0 collective-permute-done.4.mid_ref
  41.7 1.7 %collective-permute-done.1 = bf16[4,192,256]{2,1,0:T(8,128)(2,1)S(1)} collective-permute-done((bf16[4,192,256]{2,1,0:T(8,128)(2,1)S(1)}, bf16[4,192,256]{2,1,0:T(8,128)(2,1)S(1)}, u32[]{:S(2)}, u32[]{:S(2)}) %collective-permute-start.1) | collective-permute-done | bytes 393248 | tf_op jit(solution)/shard_map/att_core/ppermute | solution.py:434
  43.4 0.8 collective-permute-done.2.refs_2_.refs_1_.refs_5_
  44.3 1.2 collective-permute-done.3.refs_4_.refs_0_
  45.5 0.1 fusion.2
  45.6 1.6 %collective-permute-start.8 = (bf16[2,192,256]{2,1,0:T(8,128)(2,1)S(1)}, bf16[2,192,256]{2,1,0:T(8,128)(2,1)S(1)}, u32[]{:S(2)}, u32[]{:S(2)}) collective-permute-start(bf16[2,192,256]{2,1,0:T(8,128)(2,1)S(1)} %pad_maximum_fusion.8), channel_id=1, source_target_pairs={{0,12},{2,14},{4,8},{6,10},{8,4},{10,6},{12,0},{14,2},{16,28},{18,... | collective-permute-start | bytes 589832 | tf_op jit(solution)/shard_map/att_group/ppermute | solution.py:434
  47.2 0.5 collective-permute-start.7
  47.7 1.6 collective-permute-start.6
  49.3 0.6 collective-permute-start.9
  49.9 2.3 %hold.1 = (bf16[256,3072]{1,0:T(8,128)(2,1)S(1)}, bf16[192,3072]{1,0:T(8,128)(2,1)S(1)}) custom-call(bf16[256,3072]{1,0:T(8,128)(2,1)} %refs_0_.2, bf16[192,3072]{1,0:T(8,128)(2,1)S(1)} %copy-done.4), custom_call_target="tpu_custom_call" | custom-call | flops 1000 | bytes 1000 | tf_op jit(solution)/shard_map/hold/pallas_call | solution.py:310
  52.1 0.1 slice.68
  52.3 1.6 %collective-permute-done.8 = bf16[2,192,256]{2,1,0:T(8,128)(2,1)S(1)} collective-permute-done((bf16[2,192,256]{2,1,0:T(8,128)(2,1)S(1)}, bf16[2,192,256]{2,1,0:T(8,128)(2,1)S(1)}, u32[]{:S(2)}, u32[]{:S(2)}) %collective-permute-start.8) | collective-permute-done | bytes 196640 | tf_op jit(solution)/shard_map/att_group/ppermute | solution.py:434
  53.9 2.1 %collective-permute-done.7 = bf16[2,192,256]{2,1,0:T(8,128)(2,1)S(1)} collective-permute-done((bf16[2,192,256]{2,1,0:T(8,128)(2,1)S(1)}, bf16[2,192,256]{2,1,0:T(8,128)(2,1)S(1)}, u32[]{:S(2)}, u32[]{:S(2)}) %collective-permute-start.7) | collective-permute-done | bytes 196640 | tf_op jit(solution)/shard_map/att_group/ppermute | solution.py:434
  56.0 0.5 collective-permute-start.13
  56.5 5.7 %collective-permute-start.14 = (bf16[192,3072]{1,0:T(8,128)(2,1)S(1)}, bf16[192,3072]{1,0:T(8,128)(2,1)S(1)}, u32[]{:S(2)}, u32[]{:S(2)}) collective-permute-start(bf16[192,3072]{1,0:T(8,128)(2,1)S(1)} %copy-done.4), channel_id=1, source_target_pairs={{0,24},{2,26},{4,28},{6,30},{24,0},{26,2},{28,4},{30,6},{1,25},{3,... | collective-permute-start | bytes 3538952 | tf_op jit(solution)/shard_map/w_ends/ppermute | solution.py:434
  62.2 1.5 collective-permute-start.11
  63.7 0.1 pad_maximum_fusion.2
  63.7 1.6 %collective-permute-start.10 = (bf16[6,192,256]{2,1,0:T(8,128)(2,1)S(1)}, bf16[6,192,256]{2,1,0:T(8,128)(2,1)S(1)}, u32[]{:S(2)}, u32[]{:S(2)}) collective-permute-start(bf16[6,192,256]{2,1,0:T(8,128)(2,1)S(1)} %pad_maximum_fusion.2), channel_id=1, source_target_pairs={{0,1},{1,0},{2,3},{3,2},{4,5},{5,4},{6,7},{7,6},{8,9},{9,8},{10,11... | collective-permute-start | bytes 1769480 | tf_op jit(solution)/shard_map/att_seq/ppermute | solution.py:439
  65.3 8.6 %attention_prepare.1 = (f32[12,256,256]{2,1,0:T(8,128)}, f32[2,12,256,128]{3,2,1,0:T(8,128)}, f32[2,12,256,128]{3,2,1,0:T(8,128)}, bf16[3,12,256,128]{3,2,1,0:T(8,128)(2,1)}) custom-call(s32[4]{0:T(128)S(1)} %copy-done.5, bf16[3,128,1536]{2,1,0:T(8,128)(2,1)} %get-tuple-element.94.own_ref, bf16[3,128,1536]{2,1,0:T(8,128)(2,1)} %collective-permute-done.came_ref, ...), custom_call_target="tpu_custom_call" | custom-call | flops 1000 | bytes 1000 | tf_op jit(solution)/shard_map/attention_prepare/pallas_call | solution.py:253
  73.9 0.1 pad_maximum_fusion.own_ref
  74.0 4.4 %collective-permute-done.10 = bf16[6,192,256]{2,1,0:T(8,128)(2,1)S(1)} collective-permute-done((bf16[6,192,256]{2,1,0:T(8,128)(2,1)S(1)}, bf16[6,192,256]{2,1,0:T(8,128)(2,1)S(1)}, u32[]{:S(2)}, u32[]{:S(2)}) %collective-permute-start.10) | collective-permute-done | bytes 589856 | tf_op jit(solution)/shard_map/att_seq/ppermute | solution.py:439
  78.5 0.1 pad_maximum_fusion.1.other_ref
  78.5 8.5 %collective-permute-done.11.refs_6_.refs_1_ = bf16[256,2048]{1,0:T(8,128)(2,1)S(1)} collective-permute-done((bf16[256,2048]{1,0:T(8,128)(2,1)S(1)}, bf16[256,2048]{1,0:T(8,128)(2,1)S(1)}, u32[]{:S(2)}, u32[]{:S(2)}) %collective-permute-start.11) | collective-permute-done | bytes 1048608 | tf_op jit(solution)/shard_map/gy_plane_cross_a/ppermute | solution.py:434
  87.1 1.1 collective-permute-done.14.end_ref
  88.2 1.4 collective-permute-start.15
  89.6 1.2 collective-permute-done.16.refs_7_.refs_3_
  90.8 4.8 %weight_terms.2 = (bf16[192,512]{1,0:T(8,128)(2,1)S(1)}, bf16[192,1024]{1,0:T(8,128)(2,1)S(1)}, bf16[192,512]{1,0:T(8,128)(2,1)S(1)}, f32[192,2048]{1,0:T(8,128)S(1)}) custom-call(s32[4]{0:T(128)S(1)} %copy-done.5, bf16[8,192,256]{2,1,0:T(8,128)(2,1)S(1)} %pad_maximum_fusion.own_ref, bf16[8,192,256]{2,1,0:T(8,128)(2,1)S(1)} %pad_maximum_fusion.1.other_ref, ...), custom_call_target="tpu_custom_call" | custom-call | flops 1000 | bytes 1000 | tf_op jit(solution)/shard_map/weight_terms/pallas_call | solution.py:377
  95.7 3.6 %collective-permute-start.17 = (bf16[192,512]{1,0:T(8,128)(2,1)S(1)}, bf16[192,512]{1,0:T(8,128)(2,1)S(1)}, u32[]{:S(2)}, u32[]{:S(2)}) collective-permute-start(bf16[192,512]{1,0:T(8,128)(2,1)S(1)} %get-tuple-element.135), channel_id=1, source_target_pairs={{0,24},{2,26},{4,28},{6,30},{8,16},{10,18},{12,20},{14,22},{16,8},... | collective-permute-start | bytes 589832 | tf_op jit(solution)/shard_map/grad_w_far/ppermute | solution.py:434
  99.3 4.9 %gradient_products.2 = (bf16[4,192,256]{2,1,0:T(8,128)(2,1)S(1)}, bf16[4,192,256]{2,1,0:T(8,128)(2,1)S(1)}) custom-call(s32[4]{0:T(128)S(1)} %copy-done.5, bf16[192,3072]{1,0:T(8,128)(2,1)S(1)} %get-tuple-element.139.w_ref, bf16[192,3072]{1,0:T(8,128)(2,1)} %collective-permute-done.4.mid_ref, bf16[192,3072]{1,0:T(8,128)(2,1)S(1)} %collective-permute-done.14.end_ref, ...), custom_call_target="tpu_custom_call" | custom-call | flops 1000 | bytes 1000 | tf_op jit(solution)/shard_map/gradient_products/pallas_call | solution.py:345
  104.2 0.4 collective-permute-done.17.refs_2_
  104.6 1.5 collective-permute-start.19
  106.1 3.5 %collective-permute-start.18 = (bf16[192,1024]{1,0:T(8,128)(2,1)S(1)}, bf16[192,1024]{1,0:T(8,128)(2,1)S(1)}, u32[]{:S(2)}, u32[]{:S(2)}) collective-permute-start(bf16[192,1024]{1,0:T(8,128)(2,1)S(1)} %get-tuple-element.149), channel_id=1, source_target_pairs={{0,24},{2,26},{4,28},{6,30},{8,16},{10,18},{12,20},{14,22},{16,8},... | collective-permute-start | bytes 1179656 | tf_op jit(solution)/shard_map/grad_w_far/ppermute | solution.py:434
  109.7 3.9 %gradient_products.3 = (bf16[4,192,256]{2,1,0:T(8,128)(2,1)S(1)}, bf16[4,192,256]{2,1,0:T(8,128)(2,1)S(1)}) custom-call(s32[4]{0:T(128)S(1)} %copy-done.5, bf16[192,3072]{1,0:T(8,128)(2,1)S(1)} %get-tuple-element.139.w_ref, bf16[192,3072]{1,0:T(8,128)(2,1)} %collective-permute-done.4.mid_ref, bf16[192,3072]{1,0:T(8,128)(2,1)S(1)} %collective-permute-done.14.end_ref, ...), custom_call_target="tpu_custom_call" | custom-call | flops 1000 | bytes 1000 | tf_op jit(solution)/shard_map/gradient_products/pallas_call | solution.py:345
  113.6 2.6 %collective-permute-done.19 = bf16[4,192,256]{2,1,0:T(8,128)(2,1)S(1)} collective-permute-done((bf16[4,192,256]{2,1,0:T(8,128)(2,1)S(1)}, bf16[4,192,256]{2,1,0:T(8,128)(2,1)S(1)}, u32[]{:S(2)}, u32[]{:S(2)}) %collective-permute-start.19) | collective-permute-done | bytes 393248 | tf_op jit(solution)/shard_map/products_seq/ppermute | solution.py:439
  116.1 0.1 add_convert_fusion.1
  116.2 0.1 collective-permute-start.21
  116.3 1.6 %collective-permute-start.23 = (bf16[4,192,256]{2,1,0:T(8,128)(2,1)S(1)}, bf16[4,192,256]{2,1,0:T(8,128)(2,1)S(1)}, u32[]{:S(2)}, u32[]{:S(2)}) collective-permute-start(bf16[4,192,256]{2,1,0:T(8,128)(2,1)S(1)} %get-tuple-element.156), channel_id=1, source_target_pairs={{0,1},{1,0},{2,3},{3,2},{4,5},{5,4},{6,7},{7,6},{8,9},{9,8},{10,11... | collective-permute-start | bytes 1179656 | tf_op jit(solution)/shard_map/products_seq/ppermute | solution.py:439
  118.0 1.4 collective-permute-start.22
  119.4 3.3 %weight_terms.3 = (bf16[192,1024]{1,0:T(8,128)(2,1)S(1)}, f32[192,1024]{1,0:T(8,128)S(1)}) custom-call(s32[4]{0:T(128)S(1)} %copy-done.5, bf16[8,192,256]{2,1,0:T(8,128)(2,1)S(1)} %pad_maximum_fusion.own_ref, bf16[8,192,256]{2,1,0:T(8,128)(2,1)S(1)} %pad_maximum_fusion.1.other_ref, bf16[256,3072]{1,0:T(8,128)(2,1)S(1)} %get-tuple-element.158.refs_0_.refs_4_, ...), custom_call_target="tpu_custom_call" | custom-call | flops 1000 | bytes 1000 | tf_op jit(solution)/shard_map/weight_terms/pallas_call | solution.py:377
  122.8 2.2 %collective-permute-done.22 = bf16[2,192,256]{2,1,0:T(8,128)(2,1)S(1)} collective-permute-done((bf16[2,192,256]{2,1,0:T(8,128)(2,1)S(1)}, bf16[2,192,256]{2,1,0:T(8,128)(2,1)S(1)}, u32[]{:S(2)}, u32[]{:S(2)}) %collective-permute-start.22) | collective-permute-done | bytes 196640 | tf_op jit(solution)/shard_map/products_group/ppermute | solution.py:434
  125.0 2.8 %collective-permute-done.23 = bf16[4,192,256]{2,1,0:T(8,128)(2,1)S(1)} collective-permute-done((bf16[4,192,256]{2,1,0:T(8,128)(2,1)S(1)}, bf16[4,192,256]{2,1,0:T(8,128)(2,1)S(1)}, u32[]{:S(2)}, u32[]{:S(2)}) %collective-permute-start.23) | collective-permute-done | bytes 393248 | tf_op jit(solution)/shard_map/products_seq/ppermute | solution.py:439
  127.9 3.5 %collective-permute-start.28 = (bf16[192,1024]{1,0:T(8,128)(2,1)S(1)}, bf16[192,1024]{1,0:T(8,128)(2,1)S(1)}, u32[]{:S(2)}, u32[]{:S(2)}) collective-permute-start(bf16[192,1024]{1,0:T(8,128)(2,1)S(1)} %get-tuple-element.183), channel_id=1, source_target_pairs={{0,24},{2,26},{4,28},{6,30},{8,16},{10,18},{12,20},{14,22},{16,8},... | collective-permute-start | bytes 1179656 | tf_op jit(solution)/shard_map/grad_w_far/ppermute | solution.py:434
  131.4 0.1 add_convert_fusion
  131.5 0.1 collective-permute-start.24
  131.6 1.4 collective-permute-done.24
  133.1 0.1 collective-permute-start.25
  133.2 2.9 %collective-permute-start.26 = (bf16[2,192,256]{2,1,0:T(8,128)(2,1)S(1)}, bf16[2,192,256]{2,1,0:T(8,128)(2,1)S(1)}, u32[]{:S(2)}, u32[]{:S(2)}) collective-permute-start(bf16[2,192,256]{2,1,0:T(8,128)(2,1)S(1)} %pad_maximum_fusion.12), channel_id=1, source_target_pairs={{0,12},{2,14},{4,8},{6,10},{8,4},{10,6},{12,0},{14,2},{16,28},{18,... | collective-permute-start | bytes 589832 | tf_op jit(solution)/shard_map/products_group/ppermute | solution.py:434
  136.0 0.3 collective-permute-start.27
  136.4 4.4 %attention_backward.2 = (bf16[12,256,128]{2,1,0:T(8,128)(2,1)}, bf16[12,256,128]{2,1,0:T(8,128)(2,1)}, bf16[12,256,128]{2,1,0:T(8,128)(2,1)}) custom-call(s32[4]{0:T(128)S(1)} %copy-done.5, f32[12,256,256]{2,1,0:T(8,128)S(1)} %copy-done, f32[2,12,256,128]{3,2,1,0:T(8,128)S(1)} %copy-done.1, f32[2,12,256,128]{3,2,1,0:T(8,128)S(1)} %copy-done.2, ...), custom_call_target="tpu_custom_call" | custom-call | flops 1000 | bytes 1000 | tf_op jit(solution)/shard_map/attention_backward/pallas_call | solution.py:279
  140.8 4.3 %collective-permute-done.25 = bf16[2,192,256]{2,1,0:T(8,128)(2,1)S(1)} collective-permute-done((bf16[2,192,256]{2,1,0:T(8,128)(2,1)S(1)}, bf16[2,192,256]{2,1,0:T(8,128)(2,1)S(1)}, u32[]{:S(2)}, u32[]{:S(2)}) %collective-permute-start.25) | collective-permute-done | bytes 196640 | tf_op jit(solution)/shard_map/products_group/ppermute | solution.py:434
  145.2 5.8 %collective-permute-done.26 = bf16[2,192,256]{2,1,0:T(8,128)(2,1)S(1)} collective-permute-done((bf16[2,192,256]{2,1,0:T(8,128)(2,1)S(1)}, bf16[2,192,256]{2,1,0:T(8,128)(2,1)S(1)}, u32[]{:S(2)}, u32[]{:S(2)}) %collective-permute-start.26) | collective-permute-done | bytes 196640 | tf_op jit(solution)/shard_map/products_group/ppermute | solution.py:434
  151.0 4.4 %attention_backward.3 = (bf16[12,256,128]{2,1,0:T(8,128)(2,1)}, bf16[12,256,128]{2,1,0:T(8,128)(2,1)}, bf16[12,256,128]{2,1,0:T(8,128)(2,1)}) custom-call(s32[4]{0:T(128)S(1)} %copy-done.5, f32[12,256,256]{2,1,0:T(8,128)S(1)} %copy-done, f32[2,12,256,128]{3,2,1,0:T(8,128)S(1)} %copy-done.1, ...), custom_call_target="tpu_custom_call", output_to_operand_aliasing={{0}: (8, {}), {1}: (9, {}), {2}: (10, {})} | custom-call | flops 1000 | bytes 1000 | tf_op jit(solution)/shard_map/attention_backward/pallas_call | solution.py:279
  155.4 2.0 %finish.1 = f32[192,3072]{1,0:T(8,128)} custom-call(f32[192,2048]{1,0:T(8,128)S(1)} %get-tuple-element.178.refs_0_, f32[192,1024]{1,0:T(8,128)S(1)} %get-tuple-element.179.refs_1_, bf16[192,512]{1,0:T(8,128)(2,1)S(1)} %collective-permute-done.17.refs_2_, bf16[192,1024]{1,0:T(8,128)(2,1)S(1)} %collective-permute-done.18.refs_3_, ...), custom_call_target="tpu_custom_call" | custom-call | flops 1000 | bytes 1000 | tf_op jit(solution)/shard_map/finish/pallas_call | solution.py:410
  (49 shorter events, 0.4 us)
Async XLA Ops:
  1.3 11.7 %copy-start.6 = (s32[1,256]{1,0:T(1,128)S(1)}, s32[1,256]{1,0:T(1,128)}, u32[]{:S(2)}) copy-start(s32[1,256]{1,0:T(1,128)} %row_ref.3) | copy-start | bytes 3076
  1.3 33.2 %copy-start.5 = (s32[4]{0:T(128)S(1)}, s32[4]{0:T(128)}, u32[]{:S(2)}) copy-start(s32[4]{0:T(128)} %pad_add_fusion.place) | copy-start | bytes 52
  1.3 33.2 %copy-start.7 = (f32[128]{0:T(128)S(1)}, f32[128]{0:T(128)}, u32[]{:S(2)}) copy-start(f32[128]{0:T(128)} %param.12) | copy-start | bytes 1540
  1.3 33.2 %copy-start.8 = (f32[128]{0:T(128)S(1)}, f32[128]{0:T(128)}, u32[]{:S(2)}) copy-start(f32[128]{0:T(128)} %param.13) | copy-start | bytes 1540
  5.2 29.2 %collective-permute-start = (bf16[3,128,1536]{2,1,0:T(8,128)(2,1)}, bf16[3,128,1536]{2,1,0:T(8,128)(2,1)}, u32[]{:S(2)}, u32[]{:S(2)}) collective-permute-start(bf16[3,128,1536]{2,1,0:T(8,128)(2,1)} %get-tuple-element.96), channel_id=1, source_target_pairs={{0,1},{1,0},{2,3},{3,2},{4,5},{5,4},{6,7},{7,6},{8,9},{9,8},{10,11... | collective-permute-start | bytes 3538952 | tf_op jit(solution)/shard_map/qkv_seq/ppermute | solution.py:439
  8.2 36.1 %collective-permute-start.2 = (bf16[256,3072]{1,0:T(8,128)(2,1)}, bf16[256,3072]{1,0:T(8,128)(2,1)S(1)}, u32[]{:S(2)}, u32[]{:S(2)}) collective-permute-start(bf16[256,3072]{1,0:T(8,128)(2,1)} %refs_0_.2), channel_id=1, source_target_pairs={{0,4},{2,6},{4,0},{6,2},{8,12},{10,14},{12,8},{14,10},{16,20},{18,... | collective-permute-start | bytes 4718600 | tf_op jit(solution)/shard_map/gy_cross/ppermute | solution.py:434
  9.7 35.8 %collective-permute-start.3 = (bf16[256,3072]{1,0:T(8,128)(2,1)}, bf16[256,3072]{1,0:T(8,128)(2,1)S(1)}, u32[]{:S(2)}, u32[]{:S(2)}) collective-permute-start(bf16[256,3072]{1,0:T(8,128)(2,1)} %refs_0_.2), channel_id=1, source_target_pairs={{0,8},{2,10},{4,12},{6,14},{8,0},{10,2},{12,4},{14,6},{16,24},{18,... | collective-permute-start | bytes 4718600 | tf_op jit(solution)/shard_map/gy_plane/ppermute | solution.py:434
  11.3 34.2 %collective-permute-start.5 = (bf16[256,3072]{1,0:T(8,128)(2,1)}, bf16[256,3072]{1,0:T(8,128)(2,1)}, u32[]{:S(2)}, u32[]{:S(2)}) collective-permute-start(bf16[256,3072]{1,0:T(8,128)(2,1)} %refs_0_.2), channel_id=1, source_target_pairs={{0,2},{2,0},{4,6},{6,4},{8,10},{10,8},{12,14},{14,12},{16,18},{18,... | collective-permute-start | bytes 4718600 | tf_op jit(solution)/shard_map/gy_core/ppermute | solution.py:434
  11.3 30.5 %collective-permute-start.4 = (bf16[192,3072]{1,0:T(8,128)(2,1)}, bf16[192,3072]{1,0:T(8,128)(2,1)}, u32[]{:S(2)}, u32[]{:S(2)}) collective-permute-start(bf16[192,3072]{1,0:T(8,128)(2,1)} %refs_1_.2), channel_id=1, source_target_pairs={{8,16},{10,18},{12,20},{14,22},{16,8},{18,10},{20,12},{22,14},{9,1... | collective-permute-start | bytes 3538952 | tf_op jit(solution)/shard_map/w_middle/ppermute | solution.py:434
  41.7 1.8 %collective-permute-start.1 = (bf16[4,192,256]{2,1,0:T(8,128)(2,1)S(1)}, bf16[4,192,256]{2,1,0:T(8,128)(2,1)S(1)}, u32[]{:S(2)}, u32[]{:S(2)}) collective-permute-start(bf16[4,192,256]{2,1,0:T(8,128)(2,1)S(1)} %get-tuple-element.98), channel_id=1, source_target_pairs={{0,2},{2,0},{4,6},{6,4},{8,10},{10,8},{12,14},{14,12},{16,18},{18,... | collective-permute-start | bytes 1179656 | tf_op jit(solution)/shard_map/att_core/ppermute | solution.py:434
  45.5 4.4 %copy-start.4 = (bf16[192,3072]{1,0:T(8,128)(2,1)S(1)}, bf16[192,3072]{1,0:T(8,128)(2,1)}, u32[]{:S(2)}) copy-start(bf16[192,3072]{1,0:T(8,128)(2,1)} %refs_1_.2) | copy-start | bytes 3538948
  45.6 8.3 %collective-permute-start.8 = (bf16[2,192,256]{2,1,0:T(8,128)(2,1)S(1)}, bf16[2,192,256]{2,1,0:T(8,128)(2,1)S(1)}, u32[]{:S(2)}, u32[]{:S(2)}) collective-permute-start(bf16[2,192,256]{2,1,0:T(8,128)(2,1)S(1)} %pad_maximum_fusion.8), channel_id=1, source_target_pairs={{0,12},{2,14},{4,8},{6,10},{8,4},{10,6},{12,0},{14,2},{16,28},{18,... | collective-permute-start | bytes 589832 | tf_op jit(solution)/shard_map/att_group/ppermute | solution.py:434
  47.2 8.8 %collective-permute-start.7 = (bf16[2,192,256]{2,1,0:T(8,128)(2,1)S(1)}, bf16[2,192,256]{2,1,0:T(8,128)(2,1)S(1)}, u32[]{:S(2)}, u32[]{:S(2)}) collective-permute-start(bf16[2,192,256]{2,1,0:T(8,128)(2,1)S(1)} %pad_maximum_fusion.7), channel_id=1, source_target_pairs={{0,8},{2,10},{4,12},{6,14},{8,0},{10,2},{12,4},{14,6},{16,24},{18,... | collective-permute-start | bytes 589832 | tf_op jit(solution)/shard_map/att_group/ppermute | solution.py:434
  47.7 8.2 %collective-permute-start.6 = (bf16[2,192,256]{2,1,0:T(8,128)(2,1)S(1)}, bf16[2,192,256]{2,1,0:T(8,128)(2,1)S(1)}, u32[]{:S(2)}, u32[]{:S(2)}) collective-permute-start(bf16[2,192,256]{2,1,0:T(8,128)(2,1)S(1)} %pad_maximum_fusion.6), channel_id=1, source_target_pairs={{0,4},{2,6},{4,0},{6,2},{8,12},{10,14},{12,8},{14,10},{16,20},{18,... | collective-permute-start | bytes 589832 | tf_op jit(solution)/shard_map/att_group/ppermute | solution.py:434
  49.3 6.7 %collective-permute-start.9 = (bf16[2,192,256]{2,1,0:T(8,128)(2,1)S(1)}, bf16[2,192,256]{2,1,0:T(8,128)(2,1)S(1)}, u32[]{:S(2)}, u32[]{:S(2)}) collective-permute-start(bf16[2,192,256]{2,1,0:T(8,128)(2,1)S(1)} %pad_maximum_fusion.5), channel_id=1, source_target_pairs={{0,1},{1,0},{2,3},{3,2},{4,5},{5,4},{6,7},{7,6},{8,9},{9,8},{10,11... | collective-permute-start | bytes 589832 | tf_op jit(solution)/shard_map/att_seq/ppermute | solution.py:439
  56.0 32.2 %collective-permute-start.12 = (bf16[256,3072]{1,0:T(8,128)(2,1)S(1)}, bf16[256,3072]{1,0:T(8,128)(2,1)S(1)}, u32[]{:S(2)}, u32[]{:S(2)}) collective-permute-start(bf16[256,3072]{1,0:T(8,128)(2,1)S(1)} %collective-permute-done.2.refs_2_.refs_1_.refs_5_), channel_id=1, source_target_pairs={{0,2},{2,0},{4,6},{6,4},{8,10},{10,8},{12,14},{14,12},{16,18},{18,... | collective-permute-start | bytes 4718600 | tf_op jit(solution)/shard_map/gy_core/ppermute | solution.py:434
  56.0 32.2 %collective-permute-start.13 = (bf16[256,3072]{1,0:T(8,128)(2,1)S(1)}, bf16[256,3072]{1,0:T(8,128)(2,1)S(1)}, u32[]{:S(2)}, u32[]{:S(2)}) collective-permute-start(bf16[256,3072]{1,0:T(8,128)(2,1)S(1)} %collective-permute-done.3.refs_4_.refs_0_), channel_id=1, source_target_pairs={{0,2},{2,0},{4,6},{6,4},{8,10},{10,8},{12,14},{14,12},{16,18},{18,... | collective-permute-start | bytes 4718600 | tf_op jit(solution)/shard_map/gy_core/ppermute | solution.py:434
  56.5 31.7 %collective-permute-start.14 = (bf16[192,3072]{1,0:T(8,128)(2,1)S(1)}, bf16[192,3072]{1,0:T(8,128)(2,1)S(1)}, u32[]{:S(2)}, u32[]{:S(2)}) collective-permute-start(bf16[192,3072]{1,0:T(8,128)(2,1)S(1)} %copy-done.4), channel_id=1, source_target_pairs={{0,24},{2,26},{4,28},{6,30},{24,0},{26,2},{28,4},{30,6},{1,25},{3,... | collective-permute-start | bytes 3538952 | tf_op jit(solution)/shard_map/w_ends/ppermute | solution.py:434
  62.2 24.9 %collective-permute-start.11 = (bf16[256,2048]{1,0:T(8,128)(2,1)S(1)}, bf16[256,2048]{1,0:T(8,128)(2,1)S(1)}, u32[]{:S(2)}, u32[]{:S(2)}) collective-permute-start(bf16[256,2048]{1,0:T(8,128)(2,1)S(1)} %slice.68), channel_id=1, source_target_pairs={{0,4},{2,6},{4,0},{6,2},{8,12},{10,14},{12,8},{14,10},{16,20},{18,... | collective-permute-start | bytes 3145736 | tf_op jit(solution)/shard_map/gy_plane_cross_a/ppermute | solution.py:434
  63.7 14.7 %collective-permute-start.10 = (bf16[6,192,256]{2,1,0:T(8,128)(2,1)S(1)}, bf16[6,192,256]{2,1,0:T(8,128)(2,1)S(1)}, u32[]{:S(2)}, u32[]{:S(2)}) collective-permute-start(bf16[6,192,256]{2,1,0:T(8,128)(2,1)S(1)} %pad_maximum_fusion.2), channel_id=1, source_target_pairs={{0,1},{1,0},{2,3},{3,2},{4,5},{5,4},{6,7},{7,6},{8,9},{9,8},{10,11... | collective-permute-start | bytes 1769480 | tf_op jit(solution)/shard_map/att_seq/ppermute | solution.py:439
  88.2 2.7 %collective-permute-start.16 = (bf16[256,2048]{1,0:T(8,128)(2,1)S(1)}, bf16[256,2048]{1,0:T(8,128)(2,1)S(1)}, u32[]{:S(2)}, u32[]{:S(2)}) collective-permute-start(bf16[256,2048]{1,0:T(8,128)(2,1)S(1)} %collective-permute-done.11.refs_6_.refs_1_), channel_id=1, source_target_pairs={{0,2},{2,0},{4,6},{6,4},{8,10},{10,8},{12,14},{14,12},{16,18},{18,... | collective-permute-start | bytes 3145736 | tf_op jit(solution)/shard_map/gy_core/ppermute | solution.py:434
  88.2 16.0 %collective-permute-start.15 = (bf16[256,1024]{1,0:T(8,128)(2,1)S(1)}, bf16[256,1024]{1,0:T(8,128)(2,1)S(1)}, u32[]{:S(2)}, u32[]{:S(2)}) collective-permute-start(bf16[256,1024]{1,0:T(8,128)(2,1)S(1)} %slice.69), channel_id=1, source_target_pairs={{0,4},{2,6},{4,0},{6,2},{8,12},{10,14},{12,8},{14,10},{16,20},{18,... | collective-permute-start | bytes 1572872 | tf_op jit(solution)/shard_map/gy_plane_cross_b/ppermute | solution.py:434
  95.7 8.9 %collective-permute-start.17 = (bf16[192,512]{1,0:T(8,128)(2,1)S(1)}, bf16[192,512]{1,0:T(8,128)(2,1)S(1)}, u32[]{:S(2)}, u32[]{:S(2)}) collective-permute-start(bf16[192,512]{1,0:T(8,128)(2,1)S(1)} %get-tuple-element.135), channel_id=1, source_target_pairs={{0,24},{2,26},{4,28},{6,30},{8,16},{10,18},{12,20},{14,22},{16,8},... | collective-permute-start | bytes 589832 | tf_op jit(solution)/shard_map/grad_w_far/ppermute | solution.py:434
  104.6 5.1 %collective-permute-start.20 = (bf16[256,1024]{1,0:T(8,128)(2,1)S(1)}, bf16[256,1024]{1,0:T(8,128)(2,1)S(1)}, u32[]{:S(2)}, u32[]{:S(2)}) collective-permute-start(bf16[256,1024]{1,0:T(8,128)(2,1)S(1)} %collective-permute-done.15.refs_5_.refs_6_), channel_id=1, source_target_pairs={{0,2},{2,0},{4,6},{6,4},{8,10},{10,8},{12,14},{14,12},{16,18},{18,... | collective-permute-start | bytes 1572872 | tf_op jit(solution)/shard_map/gy_core/ppermute | solution.py:434
  104.6 11.5 %collective-permute-start.19 = (bf16[4,192,256]{2,1,0:T(8,128)(2,1)S(1)}, bf16[4,192,256]{2,1,0:T(8,128)(2,1)S(1)}, u32[]{:S(2)}, u32[]{:S(2)}) collective-permute-start(bf16[4,192,256]{2,1,0:T(8,128)(2,1)S(1)} %get-tuple-element.151), channel_id=1, source_target_pairs={{0,1},{1,0},{2,3},{3,2},{4,5},{5,4},{6,7},{7,6},{8,9},{9,8},{10,11... | collective-permute-start | bytes 1179656 | tf_op jit(solution)/shard_map/products_seq/ppermute | solution.py:439
  106.1 16.7 %collective-permute-start.18 = (bf16[192,1024]{1,0:T(8,128)(2,1)S(1)}, bf16[192,1024]{1,0:T(8,128)(2,1)S(1)}, u32[]{:S(2)}, u32[]{:S(2)}) collective-permute-start(bf16[192,1024]{1,0:T(8,128)(2,1)S(1)} %get-tuple-element.149), channel_id=1, source_target_pairs={{0,24},{2,26},{4,28},{6,30},{8,16},{10,18},{12,20},{14,22},{16,8},... | collective-permute-start | bytes 1179656 | tf_op jit(solution)/shard_map/grad_w_far/ppermute | solution.py:434
  116.2 1.7 %collective-permute-start.21 = (bf16[2,192,256]{2,1,0:T(8,128)(2,1)S(1)}, bf16[2,192,256]{2,1,0:T(8,128)(2,1)S(1)}, u32[]{:S(2)}, u32[]{:S(2)}) collective-permute-start(bf16[2,192,256]{2,1,0:T(8,128)(2,1)S(1)} %slice.81), channel_id=1, source_target_pairs={{0,2},{2,0},{4,6},{6,4},{8,10},{10,8},{12,14},{14,12},{16,18},{18,... | collective-permute-start | bytes 589832 | tf_op jit(solution)/shard_map/products_core/ppermute | solution.py:434
  116.3 11.5 %collective-permute-start.23 = (bf16[4,192,256]{2,1,0:T(8,128)(2,1)S(1)}, bf16[4,192,256]{2,1,0:T(8,128)(2,1)S(1)}, u32[]{:S(2)}, u32[]{:S(2)}) collective-permute-start(bf16[4,192,256]{2,1,0:T(8,128)(2,1)S(1)} %get-tuple-element.156), channel_id=1, source_target_pairs={{0,1},{1,0},{2,3},{3,2},{4,5},{5,4},{6,7},{7,6},{8,9},{9,8},{10,11... | collective-permute-start | bytes 1179656 | tf_op jit(solution)/shard_map/products_seq/ppermute | solution.py:439
  118.0 7.0 %collective-permute-start.22 = (bf16[2,192,256]{2,1,0:T(8,128)(2,1)S(1)}, bf16[2,192,256]{2,1,0:T(8,128)(2,1)S(1)}, u32[]{:S(2)}, u32[]{:S(2)}) collective-permute-start(bf16[2,192,256]{2,1,0:T(8,128)(2,1)S(1)} %pad_maximum_fusion.10), channel_id=1, source_target_pairs={{0,4},{2,6},{4,0},{6,2},{8,12},{10,14},{12,8},{14,10},{16,20},{18,... | collective-permute-start | bytes 589832 | tf_op jit(solution)/shard_map/products_group/ppermute | solution.py:434
  119.4 17.0 %copy-start.1 = (f32[2,12,256,128]{3,2,1,0:T(8,128)S(1)}, f32[2,12,256,128]{3,2,1,0:T(8,128)}, u32[]{:S(2)}) copy-start(f32[2,12,256,128]{3,2,1,0:T(8,128)} %get-tuple-element.124.hat_ref) | copy-start | bytes 9437188
  119.4 17.0 %copy-start.2 = (f32[2,12,256,128]{3,2,1,0:T(8,128)S(1)}, f32[2,12,256,128]{3,2,1,0:T(8,128)}, u32[]{:S(2)}) copy-start(f32[2,12,256,128]{3,2,1,0:T(8,128)} %get-tuple-element.125.inv_ref) | copy-start | bytes 9437188
  119.4 17.0 %copy-start.3 = (bf16[3,12,256,128]{3,2,1,0:T(8,128)(2,1)S(1)}, bf16[3,12,256,128]{3,2,1,0:T(8,128)(2,1)}, u32[]{:S(2)}) copy-start(bf16[3,12,256,128]{3,2,1,0:T(8,128)(2,1)} %get-tuple-element.126.low_ref) | copy-start | bytes 7077892
  127.9 27.6 %collective-permute-start.28 = (bf16[192,1024]{1,0:T(8,128)(2,1)S(1)}, bf16[192,1024]{1,0:T(8,128)(2,1)S(1)}, u32[]{:S(2)}, u32[]{:S(2)}) collective-permute-start(bf16[192,1024]{1,0:T(8,128)(2,1)S(1)} %get-tuple-element.183), channel_id=1, source_target_pairs={{0,24},{2,26},{4,28},{6,30},{8,16},{10,18},{12,20},{14,22},{16,8},... | collective-permute-start | bytes 1179656 | tf_op jit(solution)/shard_map/grad_w_far/ppermute | solution.py:434
  131.4 5.0 %copy-start = (f32[12,256,256]{2,1,0:T(8,128)S(1)}, f32[12,256,256]{2,1,0:T(8,128)}, u32[]{:S(2)}) copy-start(f32[12,256,256]{2,1,0:T(8,128)} %get-tuple-element.123.p_ref) | copy-start | bytes 9437188
  131.5 1.5 collective-permute-start.24
  133.1 12.1 %collective-permute-start.25 = (bf16[2,192,256]{2,1,0:T(8,128)(2,1)S(1)}, bf16[2,192,256]{2,1,0:T(8,128)(2,1)S(1)}, u32[]{:S(2)}, u32[]{:S(2)}) collective-permute-start(bf16[2,192,256]{2,1,0:T(8,128)(2,1)S(1)} %pad_maximum_fusion.11), channel_id=1, source_target_pairs={{0,8},{2,10},{4,12},{6,14},{8,0},{10,2},{12,4},{14,6},{16,24},{18,... | collective-permute-start | bytes 589832 | tf_op jit(solution)/shard_map/products_group/ppermute | solution.py:434
  133.2 17.8 %collective-permute-start.26 = (bf16[2,192,256]{2,1,0:T(8,128)(2,1)S(1)}, bf16[2,192,256]{2,1,0:T(8,128)(2,1)S(1)}, u32[]{:S(2)}, u32[]{:S(2)}) collective-permute-start(bf16[2,192,256]{2,1,0:T(8,128)(2,1)S(1)} %pad_maximum_fusion.12), channel_id=1, source_target_pairs={{0,12},{2,14},{4,8},{6,10},{8,4},{10,6},{12,0},{14,2},{16,28},{18,... | collective-permute-start | bytes 589832 | tf_op jit(solution)/shard_map/products_group/ppermute | solution.py:434
  136.0 19.4 %collective-permute-start.27 = (bf16[192,512]{1,0:T(8,128)(2,1)S(1)}, bf16[192,512]{1,0:T(8,128)(2,1)S(1)}, u32[]{:S(2)}, u32[]{:S(2)}) collective-permute-start(bf16[192,512]{1,0:T(8,128)(2,1)S(1)} %get-tuple-element.182), channel_id=1, source_target_pairs={{0,24},{2,26},{4,28},{6,30},{8,16},{10,18},{12,20},{14,22},{16,8},... | collective-permute-start | bytes 589832 | tf_op jit(solution)/shard_map/grad_w_far/ppermute | solution.py:434

commit v4 on v3

--- a/solution.py
+++ b/solution.py
@@ -124,36 +124,6 @@
     return jnp.concatenate([jnp.where(first, own, came), jnp.where(first, came, own)], axis=0)
 
 
-def head_inputs(place, own_ref, came_ref, h, dim):
-    first = place[0] == 0
-    cols = slice(h * dim, (h + 1) * dim)
-    return [assemble(first, own_ref[n, :, cols], came_ref[n, :, cols]) for n in range(3)]
-
-
-def pack_kernel(place, *refs):
-    mine, theirs, own_ref, send_ref = refs[:3], refs[3:6], refs[6], refs[7]
-    for n in range(3):
-        own_ref[n] = mine[n][...]
-        send_ref[n] = theirs[n][...]
-
-
-def pack(place, arrays, steps=1):
-    rows, width = arrays[0].shape[0], arrays[0].shape[1] // 2
-    wide = width // steps
-    mine = pl.BlockSpec((rows, wide), lambda i, p: (0, p[0] * steps + i))
-    theirs = pl.BlockSpec((rows, wide), lambda i, p: (0, (1 - p[0]) * steps + i))
-    out = pl.BlockSpec((3, rows, wide), lambda i, p: (0, 0, i))
-    return pl.pallas_call(
-        pack_kernel,
-        grid_spec=pltpu.PrefetchScalarGridSpec(
-            num_scalar_prefetch=1, grid=(steps,), in_specs=[mine] * 3 + [theirs] * 3, out_specs=[out, out]
-        ),
-        out_shape=[pltpu.HBM((3, rows, width), BF16), jax.ShapeDtypeStruct((3, rows, width), BF16)],
-        cost_estimate=pl.CostEstimate(flops=1000, bytes_accessed=1000, transcendentals=0),
-        name="pack",
-    )(place, *arrays, *arrays)
-
-
 def head_probs(q, k, qg, kg, same, scale):
     q_hat, q_inv, qn = norm_parts(q, qg)
     k_hat, k_inv, kn = norm_parts(k, kg)
@@ -163,13 +133,29 @@
     return probs, q_hat, q_inv, qn, k_hat, k_inv, kn
 
 
-def forward_kernel(per, dim, place, own_ref, came_ref, row_ref, col_ref, qg_ref, kg_ref, even_ref, odd_ref):
+def probabilities_kernel(per, dim, place, q_ref, k_ref, came_ref, row_ref, col_ref, qg_ref, kg_ref, p_ref, hat_ref, inv_ref, low_ref, p_low_ref):
     same = col_ref[...] == row_ref[...]
+    first = place[0] == 0
+    for h in range(per):
+        cols = slice(h * dim, (h + 1) * dim)
+        q, k = (assemble(first, ref[:, cols], came_ref[n, :, cols]) for n, ref in enumerate((q_ref, k_ref)))
+        probs, *parts = head_probs(q, k, qg_ref[...], kg_ref[...], same, dim**-0.5)
+        p_ref[h] = probs
+        p_low_ref[h] = probs.astype(BF16)
+        for n, (hat, inv, normed) in enumerate((parts[:3], parts[3:])):
+            hat_ref[n, h] = hat
+            inv_ref[n, h] = jnp.broadcast_to(inv, hat.shape)
+            low_ref[n, h] = normed
+
+
+def attended_kernel(per, dim, place, p_low_ref, v_ref, came_ref, even_ref, odd_ref, whole_ref):
+    first = place[0] == 0
     done = []
     for h in range(per):
-        q, k, v = head_inputs(place, own_ref, came_ref, h, dim)
-        probs = head_probs(q, k, qg_ref[...], kg_ref[...], same, dim**-0.5)[0]
-        done.append(dot_nn(probs.astype(BF16), v).T.astype(BF16))
+        cols = slice(h * dim, (h + 1) * dim)
+        v = assemble(first, v_ref[:, cols], came_ref[:, cols])
+        whole_ref[h] = v
+        done.append(dot_nn(p_low_ref[h], v).T.astype(BF16))
     att = jnp.concatenate(done, axis=0)
     half = att.shape[0] // 2
     straight = (place[1] & 1) == 0
@@ -178,20 +164,7 @@
     odd_ref[0] = jnp.where(straight, high, low)
 
 
-def prepare_kernel(per, dim, place, own_ref, came_ref, row_ref, col_ref, qg_ref, kg_ref, p_ref, hat_ref, inv_ref, low_ref):
-    same = col_ref[...] == row_ref[...]
-    for h in range(per):
-        q, k, v = head_inputs(place, own_ref, came_ref, h, dim)
-        probs, *parts = head_probs(q, k, qg_ref[...], kg_ref[...], same, dim**-0.5)
-        p_ref[h] = probs
-        for n, (hat, inv, normed) in enumerate((parts[:3], parts[3:])):
-            hat_ref[n, h] = hat
-            inv_ref[n, h] = jnp.broadcast_to(inv, hat.shape)
-            low_ref[n, h] = normed
-        low_ref[2, h] = v
-
-
-def backward_kernel(per, dim, n_into, place, p_ref, hat_ref, inv_ref, low_ref, d_ref, qg_ref, kg_ref, *rest):
+def backward_kernel(per, dim, n_into, place, p_ref, hat_ref, inv_ref, low_ref, v_ref, d_ref, qg_ref, kg_ref, *rest):
     gq_ref, gk_ref, gv_ref = rest[n_into:]
     scale = dim**-0.5
     straight = (place[1] & 1) == 0
@@ -199,7 +172,7 @@
     grad = jnp.concatenate([jnp.where(straight, one, two), jnp.where(straight, two, one)], axis=0)
     qg, kg = qg_ref[...], kg_ref[...]
     for h in range(per):
-        probs, qn, kn, v = p_ref[h], low_ref[0, h], low_ref[1, h], low_ref[2, h]
+        probs, qn, kn, v = p_ref[h], low_ref[0, h], low_ref[1, h], v_ref[h]
         d = grad[h * dim : (h + 1) * dim].T
         gp = dot_nt(d, v)
         gv_ref[h] = dot_tn(probs.astype(BF16), d).astype(BF16)
@@ -217,53 +190,69 @@
     return i ^ (p[1] >> 1) ^ (p[2] << 1)
 
 
-def attention_forward(place, mine, came, row, col, qg, kg):
+def own_heads(rows, wide):
+    return pl.BlockSpec((rows, wide), lambda i, p: (0, p[0] * 4 + i))
+
+
+def in_hbm(a):
+    return pltpu.with_memory_space_constraint(a, pltpu.HBM)
+
+
+def attention_probabilities(place, queries, keys, came, row, col, qg, kg):
     dim = qg.shape[1]
-    half_tokens, heads = mine.shape[1], mine.shape[2] // dim
+    half_tokens, heads = came.shape[1], came.shape[2] // dim
     tokens, per = 2 * half_tokens, heads // 4
-    rows = per * dim // 2
-    out = pl.BlockSpec((1, rows, tokens), lambda i, p: (pair_index(i, p), 0, 0))
-    return pl.pallas_call(
-        functools.partial(forward_kernel, per, dim),
+    wide = per * dim
+
+    def saved(n, dtype):
+        spec = pl.BlockSpec((n, per, tokens, dim), lambda i, p: (0, i, 0, 0))
+        return spec, pltpu.HBM((n, heads, tokens, dim), dtype)
+
+    square, probs = pl.BlockSpec((per, tokens, tokens), lambda i, p: (i, 0, 0)), (heads, tokens, tokens)
+    specs, shapes = zip(
+        (square, pltpu.HBM(probs, F32)),
+        saved(2, F32),
+        saved(2, F32),
+        saved(2, BF16),
+        (square, jax.ShapeDtypeStruct(probs, BF16)),
+    )
+    *saved, low = pl.pallas_call(
+        functools.partial(probabilities_kernel, per, dim),
         grid_spec=pltpu.PrefetchScalarGridSpec(
             num_scalar_prefetch=1,
             grid=(4,),
-            in_specs=[pl.BlockSpec((3, half_tokens, per * dim), lambda i, p: (0, 0, i))] * 2
-            + [whole((1, tokens)), whole((tokens, 1)), whole((1, dim)), whole((1, dim))],
-            out_specs=[out, out],
-        ),
-        out_shape=[jax.ShapeDtypeStruct((4, rows, tokens), BF16)] * 2,
-        compiler_params=pltpu.CompilerParams(vmem_limit_bytes=16 << 20),
-        cost_estimate=pl.CostEstimate(flops=1000, bytes_accessed=1000, transcendentals=0),
-        name="attention_forward",
-    )(place, pltpu.with_memory_space_constraint(mine, pltpu.HBM), came, row, col, qg, kg)
-
-
-def attention_prepare(place, mine, came, row, col, qg, kg):
-    dim = qg.shape[1]
-    half_tokens, heads = mine.shape[1], mine.shape[2] // dim
-    tokens, per = 2 * half_tokens, heads // 4
-
-    def saved(n, dtype):
-        spec = pl.BlockSpec((n, per, tokens, dim), lambda i, p: (0, i, 0, 0))
-        return spec, pltpu.HBM((n, heads, tokens, dim), dtype)
-
-    probs = pl.BlockSpec((per, tokens, tokens), lambda i, p: (i, 0, 0)), pltpu.HBM((heads, tokens, tokens), F32)
-    specs, shapes = zip(probs, saved(2, F32), saved(2, F32), saved(3, BF16))
-    return pl.pallas_call(
-        functools.partial(prepare_kernel, per, dim),
-        grid_spec=pltpu.PrefetchScalarGridSpec(
-            num_scalar_prefetch=1,
-            grid=(4,),
-            in_specs=[pl.BlockSpec((3, half_tokens, per * dim), lambda i, p: (0, 0, i))] * 2
+            in_specs=[own_heads(half_tokens, wide)] * 2
+            + [pl.BlockSpec((2, half_tokens, wide), lambda i, p: (0, 0, i))]
             + [whole((1, tokens)), whole((tokens, 1)), whole((1, dim)), whole((1, dim))],
             out_specs=specs,
         ),
         out_shape=shapes,
         compiler_params=pltpu.CompilerParams(vmem_limit_bytes=16 << 20),
         cost_estimate=pl.CostEstimate(flops=1000, bytes_accessed=1000, transcendentals=0),
-        name="attention_prepare",
-    )(place, pltpu.with_memory_space_constraint(mine, pltpu.HBM), came, row, col, qg, kg)
+        name="attention_probabilities",
+    )(place, in_hbm(queries), in_hbm(keys), came, row, col, qg, kg)
+    return saved, low
+
+
+def attention_attended(place, low, values, came, dim):
+    half_tokens, heads = came.shape[0], low.shape[0]
+    tokens, per = 2 * half_tokens, heads // 4
+    rows, wide = per * dim // 2, per * dim
+    out = pl.BlockSpec((1, rows, tokens), lambda i, p: (pair_index(i, p), 0, 0))
+    return pl.pallas_call(
+        functools.partial(attended_kernel, per, dim),
+        grid_spec=pltpu.PrefetchScalarGridSpec(
+            num_scalar_prefetch=1,
+            grid=(4,),
+            in_specs=[pl.BlockSpec((per, tokens, tokens), lambda i, p: (i, 0, 0))]
+            + [own_heads(half_tokens, wide), pl.BlockSpec((half_tokens, wide), lambda i, p: (0, i))],
+            out_specs=[out, out, pl.BlockSpec((per, tokens, dim), lambda i, p: (i, 0, 0))],
+        ),
+        out_shape=[jax.ShapeDtypeStruct((4, rows, tokens), BF16)] * 2 + [pltpu.HBM((heads, tokens, dim), BF16)],
+        compiler_params=pltpu.CompilerParams(vmem_limit_bytes=16 << 20),
+        cost_estimate=pl.CostEstimate(flops=1000, bytes_accessed=1000, transcendentals=0),
+        name="attention_attended",
+    )(place, low, in_hbm(values), came)
 
 
 def attention_backward(place, first, pairs, saved, grads, qg, kg, into=()):
@@ -281,14 +270,15 @@
         grid_spec=pltpu.PrefetchScalarGridSpec(
             num_scalar_prefetch=1,
             grid=(pairs,),
-            in_specs=[pl.BlockSpec((per, tokens, tokens), lambda i, p: (index(i, p), 0, 0)), block(2), block(2), block(3)]
+            in_specs=[pl.BlockSpec((per, tokens, tokens), lambda i, p: (index(i, p), 0, 0)), block(2), block(2), block(2)]
+            + [pl.BlockSpec((per, tokens, dim), lambda i, p: (index(i, p), 0, 0))]
             + [pl.BlockSpec((1, 2, rows, tokens), lambda i, p: (i, 0, 0, 0))]
             + [whole((1, dim)), whole((1, dim))]
             + [pl.BlockSpec(memory_space=pl.ANY)] * len(into),
             out_specs=[pl.BlockSpec((per, tokens, dim), lambda i, p: (index(i, p), 0, 0))] * 3,
         ),
         out_shape=[pltpu.HBM((heads, tokens, dim), BF16)] * 3,
-        input_output_aliases={8 + n: n for n in range(len(into))},
+        input_output_aliases={9 + n: n for n in range(len(into))},
         compiler_params=pltpu.CompilerParams(vmem_limit_bytes=16 << 20),
         cost_estimate=pl.CostEstimate(flops=1000, bytes_accessed=1000, transcendentals=0),
         name="attention_backward",
@@ -319,13 +309,29 @@
     )(*arrays)
 
 
-def products_kernel(n, parts, place, w_ref, mid_ref, end_ref, *refs):
+def choose_kernel(place, mid_ref, end_ref, far_ref):
+    far_ref[...] = jnp.where(place[3] == 1, mid_ref[...], end_ref[...])
+
+
+def choose(place, mid, end):
+    return pl.pallas_call(
+        choose_kernel,
+        in_specs=[SCALAR, VECTOR, VECTOR],
+        out_specs=VECTOR,
+        out_shape=pltpu.VMEM(mid.shape, mid.dtype),
+        compiler_params=pltpu.CompilerParams(vmem_limit_bytes=4 << 20),
+        cost_estimate=pl.CostEstimate(flops=10**10, bytes_accessed=1000, transcendentals=0),
+        name="choose",
+    )(place, mid, end)
+
+
+def products_kernel(n, parts, place, w_ref, far_ref, *refs):
     g_refs, (keep_ref, send_ref, both_ref) = refs[:-3], refs[-3:]
     rows = w_ref.shape[0]
-    middle, flip = place[3] == 1, place[2] == 1
+    flip = place[2] == 1
     for first, depth, _ in parts:
         cols = slice(first, first + depth)
-        own, far = w_ref[:, cols], jnp.where(middle, mid_ref[:, cols], end_ref[:, cols])
+        own, far = w_ref[:, cols], far_ref[:, cols]
         both_ref[:rows, cols] = jnp.where(flip, far, own)
         both_ref[rows:, cols] = jnp.where(flip, own, far)
     for j in range(n):
@@ -338,20 +344,20 @@
         send_ref[j] = total[rows:].astype(BF16)
 
 
-def gradient_products(place, w, mid, end, parts):
+def gradient_products(place, w, far, parts):
     rows, depth = w.shape
     n, tokens = len(parts[0][0]), parts[0][0][0].shape[0]
     blocks = [a for part in parts for a in part[0]]
     return pl.pallas_call(
         functools.partial(products_kernel, n, [(first, wide, starts) for _, starts, first, wide in parts]),
-        in_specs=[SCALAR] + [VECTOR] * (3 + len(blocks)),
+        in_specs=[SCALAR] + [VECTOR] * (2 + len(blocks)),
         out_specs=[VECTOR] * 2,
         out_shape=[jax.ShapeDtypeStruct((n, rows, tokens), BF16)] * 2,
         scratch_shapes=[pltpu.VMEM((2 * rows, depth), BF16)],
         compiler_params=pltpu.CompilerParams(vmem_limit_bytes=16 << 20),
         cost_estimate=pl.CostEstimate(flops=1000, bytes_accessed=1000, transcendentals=0),
         name="gradient_products",
-    )(place, w, mid, end, *blocks)
+    )(place, w, far, *blocks)
 
 
 def weight_kernel(n, starts, parts, place, own_ref, other_ref, *refs):
@@ -371,7 +377,7 @@
         first += part
 
 
-def weight_terms(place, own, other, half, parts):
+def weight_terms(place, own, other, half, parts, flops):
     n, rows, tokens = own.shape
     depth = sum(parts)
     return pl.pallas_call(
@@ -382,7 +388,7 @@
         + [jax.ShapeDtypeStruct((rows, depth), F32)],
         scratch_shapes=[pltpu.VMEM((2 * rows, n * tokens), BF16)],
         compiler_params=pltpu.CompilerParams(vmem_limit_bytes=16 << 20),
-        cost_estimate=pl.CostEstimate(flops=1000, bytes_accessed=1000, transcendentals=0),
+        cost_estimate=pl.CostEstimate(flops=flops, bytes_accessed=1000, transcendentals=0),
         name="weight_terms",
     )(place, own, other, *half[0])
 
@@ -457,45 +463,53 @@
     cut = 2 * width // 3
     barrier = lax.optimization_barrier
 
-    mine, send = pack(place, (queries, keys, values))
-    send, gy, w_own = barrier((send, grad_y, w_out))
-    came = swap(send, "qkv_seq")
+    theirs = [lax.dynamic_slice_in_dim(a, (1 - y) * half, half, axis=1) for a in (queries, keys, values)]
+    send, gy, w_own = barrier((jnp.stack(theirs[:2]), grad_y, w_out))
+    came = swap(send, "qk_seq")
+    came_v = swap(theirs[2], "v_seq")
+    g2 = move(gy, CROSS, "gy_cross")
     g4 = move(gy, PLANE, "gy_plane")
-    g2 = move(gy, CROSS, "gy_cross")
     w_mid = move(w_own, MIDDLE, "w_middle")
-    g1 = move(gy, CORE, "gy_core")
-    even, odd = attention_forward(place, mine, came, row, col, qg, kg)
+    saved, low = attention_probabilities(place, queries, keys, came, row, col, qg, kg)
+    even, odd, v_all = attention_attended(place, low, values, came_v, dim)
+    saved.append(v_all)
     odd = move(odd, CORE, "att_core")
-    even, odd, g2, g4, gy, w_own, w_mid, g1 = barrier((even, odd, g2, g4, gy, w_own, w_mid, g1))
+    even, odd, g2, g4, gy, w_own, w_mid = barrier((even, odd, g2, g4, gy, w_own, w_mid))
     own = [jnp.stack([even[j], odd[j]]) for j in range(4)]
     other = [swap(own[0], "att_seq")]
     own = [own[0]] + [move(own[j], xor(2 * j), "att_group") for j in (1, 2, 3)]
     g4a, g4b = g4[:, :cut], g4[:, cut:]
-    held, w_held = hold(gy, w_own)
-    own, other, g4, g4a, g4b, w_own, g2, gy, w_held = barrier((own, other, g4, g4a, g4b, w_own, g2, held, w_held))
+    g1 = move(gy, CORE, "gy_core")
+    own, other, g4, g4a, g4b, g2, g1, gy = barrier((own, other, g4, g4a, g4b, g2, g1, gy))
     other.append(swap(jnp.concatenate(own[1:]), "att_seq"))
     g6a = move(g4a, CROSS, "gy_plane_cross_a")
-    w_end = move(w_own, ENDS, "w_ends")
+    w_far = choose(place, w_mid, move(w_own, ENDS, "w_ends"))
     g3, g5 = (move(g, CORE, "gy_core") for g in (g2, g4))
-    saved = attention_prepare(place, mine, came, row, col, qg, kg)
+    gy, w_held = hold(gy, w_out)
+    other[1], gy, w_held = barrier((other[1], gy, w_held))
     own, other = jnp.concatenate(own), jnp.concatenate(other)
-    own, other, g6a, g3, g5, g4b, w_end, saved = barrier((own, other, g6a, g3, g5, g4b, w_end, saved))
-    g6b = move(g4b, CROSS, "gy_plane_cross_b")
+    other, g6a = barrier((other, g6a))
     g7a = move(g6a, CORE, "gy_core")
     blocks_a = [gy, g1, g2, g3, g4, g5, g6a, g7a]
-    *sent, kept_a = weight_terms(place, own, other, (blocks_a, (0,) * 8), (cut // 4, cut // 2, cut // 4))
+    *sent, kept_a = weight_terms(place, own, other, (blocks_a, (0,) * 8), (cut // 2, cut // 2), 1000)
+    own, other, g6a, g7a, g3, g5, g4b, w_far, sent, kept_a = barrier(
+        (own, other, g6a, g7a, g3, g5, g4b, w_far, sent, kept_a)
+    )
+    g6b = move(g4b, CROSS, "gy_plane_cross_b")
     far = [move(sent[0], FAR, "grad_w_far")]
-    weights = (w_held, w_mid, w_end)
-    tied = barrier((gy, g2, g1, g3, sent))[:4]
-    keep0, send0 = gradient_products(place, *weights, [(tied, (start,) * 4, start, depth) for start, depth in ((0, cut), (cut, width - cut))])
-    g6b, far, sent, kept_a, keep0, send0 = barrier((g6b, far, sent, kept_a, keep0, send0))
+    weights = (w_held, w_far)
+    near = (gy, g2, g1, g3)
+    keep0, send0 = gradient_products(
+        place, *weights, [(near, (start,) * 4, start, depth) for start, depth in ((0, cut), (cut, width - cut))]
+    )
     came0 = swap(send0, "products_seq")
+    g6b, far, sent, keep0, came0 = barrier((g6b, far, sent, keep0, came0))
+    g7b = move(g6b, CORE, "gy_core")
     far.append(move(sent[1], FAR, "grad_w_far"))
-    g7b = move(g6b, CORE, "gy_core")
     keep1, send1 = gradient_products(
         place,
         *weights,
-        [([g4, g6a, g5, g7a], (0,) * 4, 0, cut), ([g4, g6b, g5, g7b], (cut, 0, cut, 0), cut, width - cut)],
+        [((g4, g6a, g5, g7a), (0,) * 4, 0, cut), ((g4, g6b, g5, g7b), (cut, 0, cut, 0), cut, width - cut)],
     )
     came1 = swap(send1, "products_seq")
     came0, keep1, blocks_b = barrier((came0, keep1, [gy, g1, g2, g3, g4, g5, g6b, g7b]))
@@ -504,13 +518,14 @@
     near = [jnp.stack([summed0[j], odd[j]]) for j in range(2)]
     near[1] = move(near[1], xor(2), "products_group")
     starts_b = (cut,) * 6 + (0,) * 2
-    *sent_b, kept_b = weight_terms(place, own, other, (blocks_b, starts_b), (width - cut,))
-    far, near, keep1, came1, sent, sent_b, kept_b = barrier((far, near, keep1, came1, sent, sent_b, kept_b))
+    *sent, kept_b = weight_terms(place, own, other, (blocks_b, starts_b), ((width - cut) // 2,) * 2, 1000)
+    far, near, keep1, came1, sent, kept_b = barrier((far, near, keep1, came1, sent, kept_b))
     summed1 = (keep1.astype(F32) + came1.astype(F32)).astype(BF16)
     odd = move(summed1[2:], CORE, "products_core")
     next_plane = [jnp.stack([summed1[j], odd[j]]) for j in range(2)]
     next_plane = [move(next_plane[j], xor(4 + 2 * j), "products_group") for j in range(2)]
-    far += [move(part, FAR, "grad_w_far") for part in (sent[2], *sent_b)]
+    odd, sent = barrier((odd, sent))
+    far += [move(part, FAR, "grad_w_far") for part in sent]
     grads = attention_backward(place, 0, 2, saved, jnp.stack(near), qg, kg)
     grads = attention_backward(place, 2, 2, saved, jnp.stack(next_plane), qg, kg, tuple(grads))
 

time: 158 us -> 151 us (0.956)
  Pallas kernels: 49.8 us -> 40 us
  local copies, waits for them, and re-layouts: 0.42 us -> 2.51 us
    pallas_call x3, Pallas kernels: 19.7 us -> 13.9 us  [the longest x1 8.48 us: attention_probabilities(): pl.pallas_call(functools.partial(probabilities_kernel, per, dim), grid_sp...]
    pallas_call x2, Pallas kernels: 8.78 us -> 6.46 us  [gradient_products(): pl.pallas_call(functools.partial(products_kernel, n, [(first, wide, start...]
    pallas_call x2, Pallas kernels: 8.16 us -> 6.32 us  [weight_terms(): pl.pallas_call(functools.partial(weight_kernel, n, half[1], parts), in_sp...]
    ppermute x5 -> x6, waiting for transfers between devices: 31.2 us -> 31.8 us  [swap(): return lax.ppermute(a, 'seq', [(0, 1), (1, 0)])]
    ppermute x5 -> x6, starting transfers between devices: 8.23 us -> 8.31 us  [swap(): return lax.ppermute(a, 'seq', [(0, 1), (1, 0)])]
  transfers between devices with their start and end apart: 29 -> 30, of which waited for: 17 -> 17; matrix products, arithmetic and copies ran while one was open for 1% -> 1% of each run, Pallas kernels for 28% -> 23%
where the time goes in v4:
time: 151 us; the launch traced here: 150 us
  waiting for transfers between devices  64.9 us (43%)
  starting transfers between devices  40 us (26%)
  Pallas kernels  40 us (26%)
  local copies, waits for them, and re-layouts  2.51 us (2%)
  other arithmetic  1.62 us (1%)
    ppermute x24, waiting for transfers between devices, move(): return lax.ppermute(a, 'fsdp', perm)  33.1 us
    ppermute x6, waiting for transfers between devices, swap(): return lax.ppermute(a, 'seq', [(0, 1), (1, 0)])  31.8 us
    ppermute x24, starting transfers between devices, move(): return lax.ppermute(a, 'fsdp', perm)  31.7 us
    pallas_call x2, Pallas kernels, attention_backward(): pl.pallas_call(functools.partial(backward_kernel, per, dim, len(into)), g...  8.85 us
    pallas_call x1, Pallas kernels, attention_probabilities(): pl.pallas_call(functools.partial(probabilities_kernel, per, dim), grid_sp...  8.48 us
    ppermute x6, starting transfers between devices, swap(): return lax.ppermute(a, 'seq', [(0, 1), (1, 0)])  8.31 us
    pallas_call x2, Pallas kernels, gradient_products(): pl.pallas_call(functools.partial(products_kernel, n, [(first, wide, start...  6.46 us
    pallas_call x2, Pallas kernels, weight_terms(): pl.pallas_call(functools.partial(weight_kernel, n, half[1], parts), in_sp...  6.32 us
  transfers between devices with their start and end apart: 30, of which 17 were waited for; matrix products, arithmetic and copies ran while one was open for 1% of the time, Pallas kernels for 23%

profile of v4, /device:TPU:0, one launch (start us, length us, event | category | flops | bytes accessed | tf_op | source)
XLA Modules:
  0.0 150.1 jit_solution(1643114896161125818)
XLA Ops:
  0.6 1.2 dynamic-slice_bitcast_fusion
  1.9 0.9 pad_maximum_fusion
  2.9 3.0 %collective-permute-start.4 = (bf16[256,3072]{1,0:T(8,128)(2,1)}, bf16[256,3072]{1,0:T(8,128)(2,1)S(1)}, u32[]{:S(2)}, u32[]{:S(2)}) collective-permute-start(bf16[256,3072]{1,0:T(8,128)(2,1)} %refs_0_), channel_id=1, source_target_pairs={{0,8},{2,10},{4,12},{6,14},{8,0},{10,2},{12,4},{14,6},{16,24},{18,... | collective-permute-start | bytes 4718600 | tf_op jit(solution)/shard_map/gy_plane/ppermute | solution.py:440
  5.9 1.5 collective-permute-start.3
  7.4 1.5 %collective-permute-start = (bf16[2,128,1536]{2,1,0:T(8,128)(2,1)}, bf16[2,128,1536]{2,1,0:T(8,128)(2,1)}, u32[]{:S(2)}, u32[]{:S(2)}) collective-permute-start(bf16[2,128,1536]{2,1,0:T(8,128)(2,1)} %pad_maximum_fusion), channel_id=1, source_target_pairs={{0,1},{1,0},{2,3},{3,2},{4,5},{5,4},{6,7},{7,6},{8,9},{9,8},{10,11... | collective-permute-start | bytes 2359304 | tf_op jit(solution)/shard_map/qk_seq/ppermute | solution.py:445
  8.9 1.7 %collective-permute-start.5 = (bf16[192,3072]{1,0:T(8,128)(2,1)}, bf16[192,3072]{1,0:T(8,128)(2,1)}, u32[]{:S(2)}, u32[]{:S(2)}) collective-permute-start(bf16[192,3072]{1,0:T(8,128)(2,1)} %refs_1_.1), channel_id=1, source_target_pairs={{8,16},{10,18},{12,20},{14,22},{16,8},{18,10},{20,12},{22,14},{9,1... | collective-permute-start | bytes 3538952 | tf_op jit(solution)/shard_map/w_middle/ppermute | solution.py:440
  10.6 0.8 constant_dynamic-slice_fusion
  11.4 0.5 collective-permute-start.1
  11.9 0.1 copy.15.col_ref
  12.0 0.1 pad_add_fusion.place
  12.1 16.1 %collective-permute-done.came_ref = bf16[2,128,1536]{2,1,0:T(8,128)(2,1)} collective-permute-done((bf16[2,128,1536]{2,1,0:T(8,128)(2,1)}, bf16[2,128,1536]{2,1,0:T(8,128)(2,1)}, u32[]{:S(2)}, u32[]{:S(2)}) %collective-permute-start) | collective-permute-done | bytes 786464 | tf_op jit(solution)/shard_map/qk_seq/ppermute | solution.py:445
  28.2 8.5 %attention_probabilities.1 = (f32[12,256,256]{2,1,0:T(8,128)}, f32[2,12,256,128]{3,2,1,0:T(8,128)}, f32[2,12,256,128]{3,2,1,0:T(8,128)}, bf16[2,12,256,128]{3,2,1,0:T(8,128)(2,1)}, bf16[12,256,256]{2,1,0:T(8,128)(2,1)S(1)}) custom-call(s32[4]{0:T(128)S(1)} %pad_add_fusion.place, bf16[128,3072]{1,0:T(8,128)(2,1)} %q_ref.1, bf16[128,3072]{1,0:T(8,128)(2,1)} %k_ref.1, ...), custom_call_target="tpu_custom_call" | custom-call | flops 1000 | bytes 1000 | tf_op jit(solution)/shard_map/attention_probabilities/pallas_call | solution.py:219
  36.7 3.9 %attention_attended.1 = (bf16[4,192,256]{2,1,0:T(8,128)(2,1)S(1)}, bf16[4,192,256]{2,1,0:T(8,128)(2,1)S(1)}, bf16[12,256,128]{2,1,0:T(8,128)(2,1)}) custom-call(s32[4]{0:T(128)S(1)} %pad_add_fusion.place, bf16[12,256,256]{2,1,0:T(8,128)(2,1)S(1)} %get-tuple-element.98.p_low_ref, bf16[128,3072]{1,0:T(8,128)(2,1)} %v_ref.1, ...), custom_call_target="tpu_custom_call" | custom-call | flops 1000 | bytes 1000 | tf_op jit(solution)/shard_map/attention_attended/pallas_call | solution.py:242
  40.6 1.7 %collective-permute-done.2 = bf16[4,192,256]{2,1,0:T(8,128)(2,1)S(1)} collective-permute-done((bf16[4,192,256]{2,1,0:T(8,128)(2,1)S(1)}, bf16[4,192,256]{2,1,0:T(8,128)(2,1)S(1)}, u32[]{:S(2)}, u32[]{:S(2)}) %collective-permute-start.2) | collective-permute-done | bytes 393248 | tf_op jit(solution)/shard_map/att_core/ppermute | solution.py:440
  42.4 0.1 collective-permute-start.10
  42.6 1.0 collective-permute-start.6
  43.7 0.5 collective-permute-start.7
  44.2 1.6 %collective-permute-start.9 = (bf16[2,192,256]{2,1,0:T(8,128)(2,1)S(1)}, bf16[2,192,256]{2,1,0:T(8,128)(2,1)S(1)}, u32[]{:S(2)}, u32[]{:S(2)}) collective-permute-start(bf16[2,192,256]{2,1,0:T(8,128)(2,1)S(1)} %pad_maximum_fusion.5), channel_id=1, source_target_pairs={{0,1},{1,0},{2,3},{3,2},{4,5},{5,4},{6,7},{7,6},{8,9},{9,8},{10,11... | collective-permute-start | bytes 589832 | tf_op jit(solution)/shard_map/att_seq/ppermute | solution.py:445
  45.8 2.2 %collective-permute-start.8 = (bf16[2,192,256]{2,1,0:T(8,128)(2,1)S(1)}, bf16[2,192,256]{2,1,0:T(8,128)(2,1)S(1)}, u32[]{:S(2)}, u32[]{:S(2)}) collective-permute-start(bf16[2,192,256]{2,1,0:T(8,128)(2,1)S(1)} %pad_maximum_fusion.8), channel_id=1, source_target_pairs={{0,12},{2,14},{4,8},{6,10},{8,4},{10,6},{12,0},{14,2},{16,28},{18,... | collective-permute-start | bytes 589832 | tf_op jit(solution)/shard_map/att_group/ppermute | solution.py:440
  48.0 1.9 %collective-permute-done.6 = bf16[2,192,256]{2,1,0:T(8,128)(2,1)S(1)} collective-permute-done((bf16[2,192,256]{2,1,0:T(8,128)(2,1)S(1)}, bf16[2,192,256]{2,1,0:T(8,128)(2,1)S(1)}, u32[]{:S(2)}, u32[]{:S(2)}) %collective-permute-start.6) | collective-permute-done | bytes 196640 | tf_op jit(solution)/shard_map/att_group/ppermute | solution.py:440
  49.8 4.4 %collective-permute-start.16 = (bf16[192,3072]{1,0:T(8,128)(2,1)}, bf16[192,3072]{1,0:T(8,128)(2,1)S(1)}, u32[]{:S(2)}, u32[]{:S(2)}) collective-permute-start(bf16[192,3072]{1,0:T(8,128)(2,1)} %refs_1_.1), channel_id=1, source_target_pairs={{0,24},{2,26},{4,28},{6,30},{24,0},{26,2},{28,4},{30,6},{1,25},{3,... | collective-permute-start | bytes 3538952 | tf_op jit(solution)/shard_map/w_ends/ppermute | solution.py:440
  54.3 0.1 slice.68
  54.4 0.9 collective-permute-done.8
  55.3 1.1 collective-permute-start.12
  56.4 0.1 pad_maximum_fusion.2
  56.5 1.6 %collective-permute-start.11 = (bf16[6,192,256]{2,1,0:T(8,128)(2,1)S(1)}, bf16[6,192,256]{2,1,0:T(8,128)(2,1)S(1)}, u32[]{:S(2)}, u32[]{:S(2)}) collective-permute-start(bf16[6,192,256]{2,1,0:T(8,128)(2,1)S(1)} %pad_maximum_fusion.2), channel_id=1, source_target_pairs={{0,1},{1,0},{2,3},{3,2},{4,5},{5,4},{6,7},{7,6},{8,9},{9,8},{10,11... | collective-permute-start | bytes 1769480 | tf_op jit(solution)/shard_map/att_seq/ppermute | solution.py:445
  58.1 0.5 collective-permute-start.15
  58.6 2.5 %hold.1 = (bf16[256,3072]{1,0:T(8,128)(2,1)S(1)}, bf16[192,3072]{1,0:T(8,128)(2,1)S(1)}) custom-call(bf16[256,3072]{1,0:T(8,128)(2,1)} %refs_0_, bf16[192,3072]{1,0:T(8,128)(2,1)} %refs_1_.1), custom_call_target="tpu_custom_call" | custom-call | flops 1000 | bytes 1000 | tf_op jit(solution)/shard_map/hold/pallas_call | solution.py:300
  61.1 9.8 %collective-permute-done.11 = bf16[6,192,256]{2,1,0:T(8,128)(2,1)S(1)} collective-permute-done((bf16[6,192,256]{2,1,0:T(8,128)(2,1)S(1)}, bf16[6,192,256]{2,1,0:T(8,128)(2,1)S(1)}, u32[]{:S(2)}, u32[]{:S(2)}) %collective-permute-start.11) | collective-permute-done | bytes 589856 | tf_op jit(solution)/shard_map/att_seq/ppermute | solution.py:445
  70.9 0.1 pad_maximum_fusion.1.other_ref
  71.0 8.6 %collective-permute-done.12.refs_6_.refs_1_ = bf16[256,2048]{1,0:T(8,128)(2,1)S(1)} collective-permute-done((bf16[256,2048]{1,0:T(8,128)(2,1)S(1)}, bf16[256,2048]{1,0:T(8,128)(2,1)S(1)}, u32[]{:S(2)}, u32[]{:S(2)}) %collective-permute-start.12) | collective-permute-done | bytes 1048608 | tf_op jit(solution)/shard_map/gy_plane_cross_a/ppermute | solution.py:440
  79.6 2.6 %collective-permute-done.16.end_ref = bf16[192,3072]{1,0:T(8,128)(2,1)S(1)} collective-permute-done((bf16[192,3072]{1,0:T(8,128)(2,1)}, bf16[192,3072]{1,0:T(8,128)(2,1)S(1)}, u32[]{:S(2)}, u32[]{:S(2)}) %collective-permute-start.16) | collective-permute-done | bytes 1179680 | tf_op jit(solution)/shard_map/w_ends/ppermute | solution.py:440
  82.3 1.4 choose.1.far_ref
  83.8 4.0 %weight_terms.2 = (bf16[192,1024]{1,0:T(8,128)(2,1)S(1)}, bf16[192,1024]{1,0:T(8,128)(2,1)S(1)}, f32[192,2048]{1,0:T(8,128)S(1)}) custom-call(s32[4]{0:T(128)S(1)} %pad_add_fusion.place, bf16[8,192,256]{2,1,0:T(8,128)(2,1)S(1)} %constant_dynamic-update-slice_fusion.own_ref, bf16[8,192,256]{2,1,0:T(8,128)(2,1)S(1)} %pad_maximum_fusion.1.other_ref, ...), custom_call_target="tpu_custom_call" | custom-call | flops 1000 | bytes 1000 | tf_op jit(solution)/shard_map/weight_terms/pallas_call | solution.py:383
  87.8 1.0 collective-permute-start.17
  88.8 1.7 %collective-permute-start.18 = (bf16[192,1024]{1,0:T(8,128)(2,1)S(1)}, bf16[192,1024]{1,0:T(8,128)(2,1)S(1)}, u32[]{:S(2)}, u32[]{:S(2)}) collective-permute-start(bf16[192,1024]{1,0:T(8,128)(2,1)S(1)} %get-tuple-element.132), channel_id=1, source_target_pairs={{0,24},{2,26},{4,28},{6,30},{8,16},{10,18},{12,20},{14,22},{16,8},... | collective-permute-start | bytes 1179656 | tf_op jit(solution)/shard_map/grad_w_far/ppermute | solution.py:440
  90.5 3.2 %gradient_products.2 = (bf16[4,192,256]{2,1,0:T(8,128)(2,1)S(1)}, bf16[4,192,256]{2,1,0:T(8,128)(2,1)S(1)}) custom-call(s32[4]{0:T(128)S(1)} %pad_add_fusion.place, bf16[192,3072]{1,0:T(8,128)(2,1)S(1)} %get-tuple-element.134.w_ref, bf16[192,3072]{1,0:T(8,128)(2,1)S(1)} %choose.1.far_ref, bf16[256,3072]{1,0:T(8,128)(2,1)S(1)} %get-tuple-element.153.refs_0_.refs_4_, ...), custom_call_target="tpu_custom_call" | custom-call | flops 1000 | bytes 1000 | tf_op jit(solution)/shard_map/gradient_products/pallas_call | solution.py:351
  93.8 1.6 %collective-permute-start.19 = (bf16[4,192,256]{2,1,0:T(8,128)(2,1)S(1)}, bf16[4,192,256]{2,1,0:T(8,128)(2,1)S(1)}, u32[]{:S(2)}, u32[]{:S(2)}) collective-permute-start(bf16[4,192,256]{2,1,0:T(8,128)(2,1)S(1)} %get-tuple-element.138), channel_id=1, source_target_pairs={{0,1},{1,0},{2,3},{3,2},{4,5},{5,4},{6,7},{7,6},{8,9},{9,8},{10,11... | collective-permute-start | bytes 1179656 | tf_op jit(solution)/shard_map/products_seq/ppermute | solution.py:445
  95.4 5.5 %collective-permute-done.18.refs_2_ = bf16[192,1024]{1,0:T(8,128)(2,1)S(1)} collective-permute-done((bf16[192,1024]{1,0:T(8,128)(2,1)S(1)}, bf16[192,1024]{1,0:T(8,128)(2,1)S(1)}, u32[]{:S(2)}, u32[]{:S(2)}) %collective-permute-start.18) | collective-permute-done | bytes 393248 | tf_op jit(solution)/shard_map/grad_w_far/ppermute | solution.py:440
  100.9 3.1 %collective-permute-done.19 = bf16[4,192,256]{2,1,0:T(8,128)(2,1)S(1)} collective-permute-done((bf16[4,192,256]{2,1,0:T(8,128)(2,1)S(1)}, bf16[4,192,256]{2,1,0:T(8,128)(2,1)S(1)}, u32[]{:S(2)}, u32[]{:S(2)}) %collective-permute-start.19) | collective-permute-done | bytes 393248 | tf_op jit(solution)/shard_map/products_seq/ppermute | solution.py:445
  104.0 1.8 %collective-permute-start.20 = (bf16[192,1024]{1,0:T(8,128)(2,1)S(1)}, bf16[192,1024]{1,0:T(8,128)(2,1)S(1)}, u32[]{:S(2)}, u32[]{:S(2)}) collective-permute-start(bf16[192,1024]{1,0:T(8,128)(2,1)S(1)} %get-tuple-element.140), channel_id=1, source_target_pairs={{0,24},{2,26},{4,28},{6,30},{8,16},{10,18},{12,20},{14,22},{16,8},... | collective-permute-start | bytes 1179656 | tf_op jit(solution)/shard_map/grad_w_far/ppermute | solution.py:440
  105.8 0.1 collective-permute-done.21.refs_7_
  105.9 3.2 %gradient_products.3 = (bf16[4,192,256]{2,1,0:T(8,128)(2,1)S(1)}, bf16[4,192,256]{2,1,0:T(8,128)(2,1)S(1)}) custom-call(s32[4]{0:T(128)S(1)} %pad_add_fusion.place, bf16[192,3072]{1,0:T(8,128)(2,1)S(1)} %get-tuple-element.134.w_ref, bf16[192,3072]{1,0:T(8,128)(2,1)S(1)} %choose.1.far_ref, bf16[256,3072]{1,0:T(8,128)(2,1)S(1)} %collective-permute-done.4.refs_4_.refs_0_, ...), custom_call_target="tpu_custom_call" | custom-call | flops 1000 | bytes 1000 | tf_op jit(solution)/shard_map/gradient_products/pallas_call | solution.py:351
  109.1 0.1 add_convert_fusion.1
  109.3 0.2 collective-permute-start.22
  109.5 1.5 %collective-permute-start.24 = (bf16[4,192,256]{2,1,0:T(8,128)(2,1)S(1)}, bf16[4,192,256]{2,1,0:T(8,128)(2,1)S(1)}, u32[]{:S(2)}, u32[]{:S(2)}) collective-permute-start(bf16[4,192,256]{2,1,0:T(8,128)(2,1)S(1)} %get-tuple-element.150), channel_id=1, source_target_pairs={{0,1},{1,0},{2,3},{3,2},{4,5},{5,4},{6,7},{7,6},{8,9},{9,8},{10,11... | collective-permute-start | bytes 1179656 | tf_op jit(solution)/shard_map/products_seq/ppermute | solution.py:445
  111.1 1.1 collective-permute-start.23
  112.3 2.3 %weight_terms.3 = (bf16[192,512]{1,0:T(8,128)(2,1)S(1)}, bf16[192,512]{1,0:T(8,128)(2,1)S(1)}, f32[192,1024]{1,0:T(8,128)S(1)}) custom-call(s32[4]{0:T(128)S(1)} %pad_add_fusion.place, bf16[8,192,256]{2,1,0:T(8,128)(2,1)S(1)} %constant_dynamic-update-slice_fusion.own_ref, bf16[8,192,256]{2,1,0:T(8,128)(2,1)S(1)} %pad_maximum_fusion.1.other_ref, ...), custom_call_target="tpu_custom_call" | custom-call | flops 1000 | bytes 1000 | tf_op jit(solution)/shard_map/weight_terms/pallas_call | solution.py:383
  114.6 2.8 %collective-permute-done.20.refs_3_ = bf16[192,1024]{1,0:T(8,128)(2,1)S(1)} collective-permute-done((bf16[192,1024]{1,0:T(8,128)(2,1)S(1)}, bf16[192,1024]{1,0:T(8,128)(2,1)S(1)}, u32[]{:S(2)}, u32[]{:S(2)}) %collective-permute-start.20) | collective-permute-done | bytes 393248 | tf_op jit(solution)/shard_map/grad_w_far/ppermute | solution.py:440
  117.4 0.6 collective-permute-done.23
  118.0 2.8 %collective-permute-done.24 = bf16[4,192,256]{2,1,0:T(8,128)(2,1)S(1)} collective-permute-done((bf16[4,192,256]{2,1,0:T(8,128)(2,1)S(1)}, bf16[4,192,256]{2,1,0:T(8,128)(2,1)S(1)}, u32[]{:S(2)}, u32[]{:S(2)}) %collective-permute-start.24) | collective-permute-done | bytes 393248 | tf_op jit(solution)/shard_map/products_seq/ppermute | solution.py:445
  120.9 0.1 add_convert_fusion
  121.0 0.1 collective-permute-start.25
  121.1 1.4 collective-permute-done.25
  122.6 5.7 %collective-permute-start.27 = (bf16[2,192,256]{2,1,0:T(8,128)(2,1)S(1)}, bf16[2,192,256]{2,1,0:T(8,128)(2,1)S(1)}, u32[]{:S(2)}, u32[]{:S(2)}) collective-permute-start(bf16[2,192,256]{2,1,0:T(8,128)(2,1)S(1)} %pad_maximum_fusion.12), channel_id=1, source_target_pairs={{0,12},{2,14},{4,8},{6,10},{8,4},{10,6},{12,0},{14,2},{16,28},{18,... | collective-permute-start | bytes 589832 | tf_op jit(solution)/shard_map/products_group/ppermute | solution.py:440
  128.3 0.1 collective-permute-start.26
  128.4 2.2 %collective-permute-start.28 = (bf16[192,512]{1,0:T(8,128)(2,1)S(1)}, bf16[192,512]{1,0:T(8,128)(2,1)S(1)}, u32[]{:S(2)}, u32[]{:S(2)}) collective-permute-start(bf16[192,512]{1,0:T(8,128)(2,1)S(1)} %get-tuple-element.180), channel_id=1, source_target_pairs={{0,24},{2,26},{4,28},{6,30},{8,16},{10,18},{12,20},{14,22},{16,8},... | collective-permute-start | bytes 589832 | tf_op jit(solution)/shard_map/grad_w_far/ppermute | solution.py:440
  130.6 1.7 %collective-permute-start.29 = (bf16[192,512]{1,0:T(8,128)(2,1)S(1)}, bf16[192,512]{1,0:T(8,128)(2,1)S(1)}, u32[]{:S(2)}, u32[]{:S(2)}) collective-permute-start(bf16[192,512]{1,0:T(8,128)(2,1)S(1)} %get-tuple-element.181), channel_id=1, source_target_pairs={{0,24},{2,26},{4,28},{6,30},{8,16},{10,18},{12,20},{14,22},{16,8},... | collective-permute-start | bytes 589832 | tf_op jit(solution)/shard_map/grad_w_far/ppermute | solution.py:440
  132.4 4.4 %attention_backward.2 = (bf16[12,256,128]{2,1,0:T(8,128)(2,1)}, bf16[12,256,128]{2,1,0:T(8,128)(2,1)}, bf16[12,256,128]{2,1,0:T(8,128)(2,1)}) custom-call(s32[4]{0:T(128)S(1)} %pad_add_fusion.place, f32[12,256,256]{2,1,0:T(8,128)S(1)} %copy-done, f32[2,12,256,128]{3,2,1,0:T(8,128)S(1)} %copy-done.1, f32[2,12,256,128]{3,2,1,0:T(8,128)S(1)} %copy-done.2, ...), custom_call_target="tpu_custom_call" | custom-call | flops 1000 | bytes 1000 | tf_op jit(solution)/shard_map/attention_backward/pallas_call | solution.py:268
  136.8 1.0 collective-permute-done.26
  137.8 4.4 %attention_backward.3 = (bf16[12,256,128]{2,1,0:T(8,128)(2,1)}, bf16[12,256,128]{2,1,0:T(8,128)(2,1)}, bf16[12,256,128]{2,1,0:T(8,128)(2,1)}) custom-call(s32[4]{0:T(128)S(1)} %pad_add_fusion.place, f32[12,256,256]{2,1,0:T(8,128)S(1)} %copy-done, f32[2,12,256,128]{3,2,1,0:T(8,128)S(1)} %copy-done.1, ...), custom_call_target="tpu_custom_call", output_to_operand_aliasing={{0}: (9, {}), {1}: (10, {}), {2}: (11, {})} | custom-call | flops 1000 | bytes 1000 | tf_op jit(solution)/shard_map/attention_backward/pallas_call | solution.py:268
  142.2 2.5 %collective-permute-done.28.refs_4_ = bf16[192,512]{1,0:T(8,128)(2,1)S(1)} collective-permute-done((bf16[192,512]{1,0:T(8,128)(2,1)S(1)}, bf16[192,512]{1,0:T(8,128)(2,1)S(1)}, u32[]{:S(2)}, u32[]{:S(2)}) %collective-permute-start.28) | collective-permute-done | bytes 196640 | tf_op jit(solution)/shard_map/grad_w_far/ppermute | solution.py:440
  144.7 3.4 %collective-permute-done.29.refs_5_ = bf16[192,512]{1,0:T(8,128)(2,1)S(1)} collective-permute-done((bf16[192,512]{1,0:T(8,128)(2,1)S(1)}, bf16[192,512]{1,0:T(8,128)(2,1)S(1)}, u32[]{:S(2)}, u32[]{:S(2)}) %collective-permute-start.29) | collective-permute-done | bytes 196640 | tf_op jit(solution)/shard_map/grad_w_far/ppermute | solution.py:440
  148.1 2.0 %finish.1 = f32[192,3072]{1,0:T(8,128)} custom-call(f32[192,2048]{1,0:T(8,128)S(1)} %get-tuple-element.174.refs_0_, f32[192,1024]{1,0:T(8,128)S(1)} %get-tuple-element.175.refs_1_, bf16[192,1024]{1,0:T(8,128)(2,1)S(1)} %collective-permute-done.18.refs_2_, bf16[192,1024]{1,0:T(8,128)(2,1)S(1)} %collective-permute-done.20.refs_3_, ...), custom_call_target="tpu_custom_call" | custom-call | flops 1000 | bytes 1000 | tf_op jit(solution)/shard_map/finish/pallas_call | solution.py:416
  (58 shorter events, 0.6 us)
Async XLA Ops:
  0.6 10.0 %copy-start.8 = (bf16[128,3072]{1,0:T(8,128)(2,1)S(1)}, bf16[128,3072]{1,0:T(8,128)(2,1)}, u32[]{:S(2)}) copy-start(bf16[128,3072]{1,0:T(8,128)(2,1)} %v_ref.1) | copy-start | bytes 2359300
  1.9 10.0 %copy-start.7 = (s32[1,256]{1,0:T(1,128)S(1)}, s32[1,256]{1,0:T(1,128)}, u32[]{:S(2)}) copy-start(s32[1,256]{1,0:T(1,128)} %row_ref.1) | copy-start | bytes 3076
  1.9 26.3 %copy-start.5 = (f32[128]{0:T(128)S(1)}, f32[128]{0:T(128)}, u32[]{:S(2)}) copy-start(f32[128]{0:T(128)} %param.12) | copy-start | bytes 1540
  1.9 26.3 %copy-start.6 = (f32[128]{0:T(128)S(1)}, f32[128]{0:T(128)}, u32[]{:S(2)}) copy-start(f32[128]{0:T(128)} %param.13) | copy-start | bytes 1540
  2.9 39.5 %collective-permute-start.4 = (bf16[256,3072]{1,0:T(8,128)(2,1)}, bf16[256,3072]{1,0:T(8,128)(2,1)S(1)}, u32[]{:S(2)}, u32[]{:S(2)}) collective-permute-start(bf16[256,3072]{1,0:T(8,128)(2,1)} %refs_0_), channel_id=1, source_target_pairs={{0,8},{2,10},{4,12},{6,14},{8,0},{10,2},{12,4},{14,6},{16,24},{18,... | collective-permute-start | bytes 4718600 | tf_op jit(solution)/shard_map/gy_plane/ppermute | solution.py:440
  5.9 36.5 %collective-permute-start.3 = (bf16[256,3072]{1,0:T(8,128)(2,1)}, bf16[256,3072]{1,0:T(8,128)(2,1)S(1)}, u32[]{:S(2)}, u32[]{:S(2)}) collective-permute-start(bf16[256,3072]{1,0:T(8,128)(2,1)} %refs_0_), channel_id=1, source_target_pairs={{0,4},{2,6},{4,0},{6,2},{8,12},{10,14},{12,8},{14,10},{16,20},{18,... | collective-permute-start | bytes 4718600 | tf_op jit(solution)/shard_map/gy_cross/ppermute | solution.py:440
  7.4 20.8 %collective-permute-start = (bf16[2,128,1536]{2,1,0:T(8,128)(2,1)}, bf16[2,128,1536]{2,1,0:T(8,128)(2,1)}, u32[]{:S(2)}, u32[]{:S(2)}) collective-permute-start(bf16[2,128,1536]{2,1,0:T(8,128)(2,1)} %pad_maximum_fusion), channel_id=1, source_target_pairs={{0,1},{1,0},{2,3},{3,2},{4,5},{5,4},{6,7},{7,6},{8,9},{9,8},{10,11... | collective-permute-start | bytes 2359304 | tf_op jit(solution)/shard_map/qk_seq/ppermute | solution.py:445
  8.9 31.7 %collective-permute-start.5 = (bf16[192,3072]{1,0:T(8,128)(2,1)}, bf16[192,3072]{1,0:T(8,128)(2,1)}, u32[]{:S(2)}, u32[]{:S(2)}) collective-permute-start(bf16[192,3072]{1,0:T(8,128)(2,1)} %refs_1_.1), channel_id=1, source_target_pairs={{8,16},{10,18},{12,20},{14,22},{16,8},{18,10},{20,12},{22,14},{9,1... | collective-permute-start | bytes 3538952 | tf_op jit(solution)/shard_map/w_middle/ppermute | solution.py:440
  11.4 25.3 %collective-permute-start.1 = (bf16[128,1536]{1,0:T(8,128)(2,1)}, bf16[128,1536]{1,0:T(8,128)(2,1)}, u32[]{:S(2)}, u32[]{:S(2)}) collective-permute-start(bf16[128,1536]{1,0:T(8,128)(2,1)} %constant_dynamic-slice_fusion), channel_id=1, source_target_pairs={{0,1},{1,0},{2,3},{3,2},{4,5},{5,4},{6,7},{7,6},{8,9},{9,8},{10,11... | collective-permute-start | bytes 1179656 | tf_op jit(solution)/shard_map/v_seq/ppermute | solution.py:445
  40.6 1.7 %collective-permute-start.2 = (bf16[4,192,256]{2,1,0:T(8,128)(2,1)S(1)}, bf16[4,192,256]{2,1,0:T(8,128)(2,1)S(1)}, u32[]{:S(2)}, u32[]{:S(2)}) collective-permute-start(bf16[4,192,256]{2,1,0:T(8,128)(2,1)S(1)} %get-tuple-element.101), channel_id=1, source_target_pairs={{0,2},{2,0},{4,6},{6,4},{8,10},{10,8},{12,14},{14,12},{16,18},{18,... | collective-permute-start | bytes 1179656 | tf_op jit(solution)/shard_map/att_core/ppermute | solution.py:440
  42.4 13.0 %collective-permute-start.10 = (bf16[256,3072]{1,0:T(8,128)(2,1)}, bf16[256,3072]{1,0:T(8,128)(2,1)S(1)}, u32[]{:S(2)}, u32[]{:S(2)}) collective-permute-start(bf16[256,3072]{1,0:T(8,128)(2,1)} %refs_0_), channel_id=1, source_target_pairs={{0,2},{2,0},{4,6},{6,4},{8,10},{10,8},{12,14},{14,12},{16,18},{18,... | collective-permute-start | bytes 4718600 | tf_op jit(solution)/shard_map/gy_core/ppermute | solution.py:440
  42.6 7.2 %collective-permute-start.6 = (bf16[2,192,256]{2,1,0:T(8,128)(2,1)S(1)}, bf16[2,192,256]{2,1,0:T(8,128)(2,1)S(1)}, u32[]{:S(2)}, u32[]{:S(2)}) collective-permute-start(bf16[2,192,256]{2,1,0:T(8,128)(2,1)S(1)} %pad_maximum_fusion.6), channel_id=1, source_target_pairs={{0,4},{2,6},{4,0},{6,2},{8,12},{10,14},{12,8},{14,10},{16,20},{18,... | collective-permute-start | bytes 589832 | tf_op jit(solution)/shard_map/att_group/ppermute | solution.py:440
  43.7 10.7 %collective-permute-start.7 = (bf16[2,192,256]{2,1,0:T(8,128)(2,1)S(1)}, bf16[2,192,256]{2,1,0:T(8,128)(2,1)S(1)}, u32[]{:S(2)}, u32[]{:S(2)}) collective-permute-start(bf16[2,192,256]{2,1,0:T(8,128)(2,1)S(1)} %pad_maximum_fusion.7), channel_id=1, source_target_pairs={{0,8},{2,10},{4,12},{6,14},{8,0},{10,2},{12,4},{14,6},{16,24},{18,... | collective-permute-start | bytes 589832 | tf_op jit(solution)/shard_map/att_group/ppermute | solution.py:440
  44.2 10.2 %collective-permute-start.9 = (bf16[2,192,256]{2,1,0:T(8,128)(2,1)S(1)}, bf16[2,192,256]{2,1,0:T(8,128)(2,1)S(1)}, u32[]{:S(2)}, u32[]{:S(2)}) collective-permute-start(bf16[2,192,256]{2,1,0:T(8,128)(2,1)S(1)} %pad_maximum_fusion.5), channel_id=1, source_target_pairs={{0,1},{1,0},{2,3},{3,2},{4,5},{5,4},{6,7},{7,6},{8,9},{9,8},{10,11... | collective-permute-start | bytes 589832 | tf_op jit(solution)/shard_map/att_seq/ppermute | solution.py:445
  45.8 9.5 %collective-permute-start.8 = (bf16[2,192,256]{2,1,0:T(8,128)(2,1)S(1)}, bf16[2,192,256]{2,1,0:T(8,128)(2,1)S(1)}, u32[]{:S(2)}, u32[]{:S(2)}) collective-permute-start(bf16[2,192,256]{2,1,0:T(8,128)(2,1)S(1)} %pad_maximum_fusion.8), channel_id=1, source_target_pairs={{0,12},{2,14},{4,8},{6,10},{8,4},{10,6},{12,0},{14,2},{16,28},{18,... | collective-permute-start | bytes 589832 | tf_op jit(solution)/shard_map/att_group/ppermute | solution.py:440
  49.8 32.4 %collective-permute-start.16 = (bf16[192,3072]{1,0:T(8,128)(2,1)}, bf16[192,3072]{1,0:T(8,128)(2,1)S(1)}, u32[]{:S(2)}, u32[]{:S(2)}) collective-permute-start(bf16[192,3072]{1,0:T(8,128)(2,1)} %refs_1_.1), channel_id=1, source_target_pairs={{0,24},{2,26},{4,28},{6,30},{24,0},{26,2},{28,4},{30,6},{1,25},{3,... | collective-permute-start | bytes 3538952 | tf_op jit(solution)/shard_map/w_ends/ppermute | solution.py:440
  55.3 24.3 %collective-permute-start.12 = (bf16[256,2048]{1,0:T(8,128)(2,1)S(1)}, bf16[256,2048]{1,0:T(8,128)(2,1)S(1)}, u32[]{:S(2)}, u32[]{:S(2)}) collective-permute-start(bf16[256,2048]{1,0:T(8,128)(2,1)S(1)} %slice.68), channel_id=1, source_target_pairs={{0,4},{2,6},{4,0},{6,2},{8,12},{10,14},{12,8},{14,10},{16,20},{18,... | collective-permute-start | bytes 3145736 | tf_op jit(solution)/shard_map/gy_plane_cross_a/ppermute | solution.py:440
  56.5 14.4 %collective-permute-start.11 = (bf16[6,192,256]{2,1,0:T(8,128)(2,1)S(1)}, bf16[6,192,256]{2,1,0:T(8,128)(2,1)S(1)}, u32[]{:S(2)}, u32[]{:S(2)}) collective-permute-start(bf16[6,192,256]{2,1,0:T(8,128)(2,1)S(1)} %pad_maximum_fusion.2), channel_id=1, source_target_pairs={{0,1},{1,0},{2,3},{3,2},{4,5},{5,4},{6,7},{7,6},{8,9},{9,8},{10,11... | collective-permute-start | bytes 1769480 | tf_op jit(solution)/shard_map/att_seq/ppermute | solution.py:445
  58.1 25.7 %collective-permute-start.14 = (bf16[256,3072]{1,0:T(8,128)(2,1)S(1)}, bf16[256,3072]{1,0:T(8,128)(2,1)S(1)}, u32[]{:S(2)}, u32[]{:S(2)}) collective-permute-start(bf16[256,3072]{1,0:T(8,128)(2,1)S(1)} %collective-permute-done.3.refs_2_.refs_1_.refs_5_), channel_id=1, source_target_pairs={{0,2},{2,0},{4,6},{6,4},{8,10},{10,8},{12,14},{14,12},{16,18},{18,... | collective-permute-start | bytes 4718600 | tf_op jit(solution)/shard_map/gy_core/ppermute | solution.py:440
  58.1 25.7 %collective-permute-start.15 = (bf16[256,3072]{1,0:T(8,128)(2,1)S(1)}, bf16[256,3072]{1,0:T(8,128)(2,1)S(1)}, u32[]{:S(2)}, u32[]{:S(2)}) collective-permute-start(bf16[256,3072]{1,0:T(8,128)(2,1)S(1)} %collective-permute-done.4.refs_4_.refs_0_), channel_id=1, source_target_pairs={{0,2},{2,0},{4,6},{6,4},{8,10},{10,8},{12,14},{14,12},{16,18},{18,... | collective-permute-start | bytes 4718600 | tf_op jit(solution)/shard_map/gy_core/ppermute | solution.py:440
  79.6 4.2 %collective-permute-start.13 = (bf16[256,2048]{1,0:T(8,128)(2,1)S(1)}, bf16[256,2048]{1,0:T(8,128)(2,1)S(1)}, u32[]{:S(2)}, u32[]{:S(2)}) collective-permute-start(bf16[256,2048]{1,0:T(8,128)(2,1)S(1)} %collective-permute-done.12.refs_6_.refs_1_), channel_id=1, source_target_pairs={{0,2},{2,0},{4,6},{6,4},{8,10},{10,8},{12,14},{14,12},{16,18},{18,... | collective-permute-start | bytes 3145736 | tf_op jit(solution)/shard_map/gy_core/ppermute | solution.py:440
  87.8 16.2 %collective-permute-start.17 = (bf16[256,1024]{1,0:T(8,128)(2,1)S(1)}, bf16[256,1024]{1,0:T(8,128)(2,1)S(1)}, u32[]{:S(2)}, u32[]{:S(2)}) collective-permute-start(bf16[256,1024]{1,0:T(8,128)(2,1)S(1)} %slice.69), channel_id=1, source_target_pairs={{0,4},{2,6},{4,0},{6,2},{8,12},{10,14},{12,8},{14,10},{16,20},{18,... | collective-permute-start | bytes 1572872 | tf_op jit(solution)/shard_map/gy_plane_cross_b/ppermute | solution.py:440
  88.8 12.1 %collective-permute-start.18 = (bf16[192,1024]{1,0:T(8,128)(2,1)S(1)}, bf16[192,1024]{1,0:T(8,128)(2,1)S(1)}, u32[]{:S(2)}, u32[]{:S(2)}) collective-permute-start(bf16[192,1024]{1,0:T(8,128)(2,1)S(1)} %get-tuple-element.132), channel_id=1, source_target_pairs={{0,24},{2,26},{4,28},{6,30},{8,16},{10,18},{12,20},{14,22},{16,8},... | collective-permute-start | bytes 1179656 | tf_op jit(solution)/shard_map/grad_w_far/ppermute | solution.py:440
  93.8 10.2 %collective-permute-start.19 = (bf16[4,192,256]{2,1,0:T(8,128)(2,1)S(1)}, bf16[4,192,256]{2,1,0:T(8,128)(2,1)S(1)}, u32[]{:S(2)}, u32[]{:S(2)}) collective-permute-start(bf16[4,192,256]{2,1,0:T(8,128)(2,1)S(1)} %get-tuple-element.138), channel_id=1, source_target_pairs={{0,1},{1,0},{2,3},{3,2},{4,5},{5,4},{6,7},{7,6},{8,9},{9,8},{10,11... | collective-permute-start | bytes 1179656 | tf_op jit(solution)/shard_map/products_seq/ppermute | solution.py:445
  104.0 1.9 %collective-permute-start.21 = (bf16[256,1024]{1,0:T(8,128)(2,1)S(1)}, bf16[256,1024]{1,0:T(8,128)(2,1)S(1)}, u32[]{:S(2)}, u32[]{:S(2)}) collective-permute-start(bf16[256,1024]{1,0:T(8,128)(2,1)S(1)} %collective-permute-done.17.refs_5_.refs_6_), channel_id=1, source_target_pairs={{0,2},{2,0},{4,6},{6,4},{8,10},{10,8},{12,14},{14,12},{16,18},{18,... | collective-permute-start | bytes 1572872 | tf_op jit(solution)/shard_map/gy_core/ppermute | solution.py:440
  104.0 13.4 %collective-permute-start.20 = (bf16[192,1024]{1,0:T(8,128)(2,1)S(1)}, bf16[192,1024]{1,0:T(8,128)(2,1)S(1)}, u32[]{:S(2)}, u32[]{:S(2)}) collective-permute-start(bf16[192,1024]{1,0:T(8,128)(2,1)S(1)} %get-tuple-element.140), channel_id=1, source_target_pairs={{0,24},{2,26},{4,28},{6,30},{8,16},{10,18},{12,20},{14,22},{16,8},... | collective-permute-start | bytes 1179656 | tf_op jit(solution)/shard_map/grad_w_far/ppermute | solution.py:440
  109.3 1.8 %collective-permute-start.22 = (bf16[2,192,256]{2,1,0:T(8,128)(2,1)S(1)}, bf16[2,192,256]{2,1,0:T(8,128)(2,1)S(1)}, u32[]{:S(2)}, u32[]{:S(2)}) collective-permute-start(bf16[2,192,256]{2,1,0:T(8,128)(2,1)S(1)} %slice.81), channel_id=1, source_target_pairs={{0,2},{2,0},{4,6},{6,4},{8,10},{10,8},{12,14},{14,12},{16,18},{18,... | collective-permute-start | bytes 589832 | tf_op jit(solution)/shard_map/products_core/ppermute | solution.py:440
  109.5 11.4 %collective-permute-start.24 = (bf16[4,192,256]{2,1,0:T(8,128)(2,1)S(1)}, bf16[4,192,256]{2,1,0:T(8,128)(2,1)S(1)}, u32[]{:S(2)}, u32[]{:S(2)}) collective-permute-start(bf16[4,192,256]{2,1,0:T(8,128)(2,1)S(1)} %get-tuple-element.150), channel_id=1, source_target_pairs={{0,1},{1,0},{2,3},{3,2},{4,5},{5,4},{6,7},{7,6},{8,9},{9,8},{10,11... | collective-permute-start | bytes 1179656 | tf_op jit(solution)/shard_map/products_seq/ppermute | solution.py:445
  111.1 6.9 %collective-permute-start.23 = (bf16[2,192,256]{2,1,0:T(8,128)(2,1)S(1)}, bf16[2,192,256]{2,1,0:T(8,128)(2,1)S(1)}, u32[]{:S(2)}, u32[]{:S(2)}) collective-permute-start(bf16[2,192,256]{2,1,0:T(8,128)(2,1)S(1)} %pad_maximum_fusion.10), channel_id=1, source_target_pairs={{0,4},{2,6},{4,0},{6,2},{8,12},{10,14},{12,8},{14,10},{16,20},{18,... | collective-permute-start | bytes 589832 | tf_op jit(solution)/shard_map/products_group/ppermute | solution.py:440
  112.2 20.1 %copy-start.1 = (f32[2,12,256,128]{3,2,1,0:T(8,128)S(1)}, f32[2,12,256,128]{3,2,1,0:T(8,128)}, u32[]{:S(2)}) copy-start(f32[2,12,256,128]{3,2,1,0:T(8,128)} %get-tuple-element.95.hat_ref) | copy-start | bytes 9437188
  112.2 20.1 %copy-start.2 = (f32[2,12,256,128]{3,2,1,0:T(8,128)S(1)}, f32[2,12,256,128]{3,2,1,0:T(8,128)}, u32[]{:S(2)}) copy-start(f32[2,12,256,128]{3,2,1,0:T(8,128)} %get-tuple-element.96.inv_ref) | copy-start | bytes 9437188
  112.2 20.1 %copy-start.3 = (bf16[2,12,256,128]{3,2,1,0:T(8,128)(2,1)S(1)}, bf16[2,12,256,128]{3,2,1,0:T(8,128)(2,1)}, u32[]{:S(2)}) copy-start(bf16[2,12,256,128]{3,2,1,0:T(8,128)(2,1)} %get-tuple-element.97.low_ref) | copy-start | bytes 4718596
  120.9 11.5 %copy-start = (f32[12,256,256]{2,1,0:T(8,128)S(1)}, f32[12,256,256]{2,1,0:T(8,128)}, u32[]{:S(2)}) copy-start(f32[12,256,256]{2,1,0:T(8,128)} %get-tuple-element.94.p_ref) | copy-start | bytes 9437188
  121.0 11.4 %copy-start.4 = (bf16[12,256,128]{2,1,0:T(8,128)(2,1)S(1)}, bf16[12,256,128]{2,1,0:T(8,128)(2,1)}, u32[]{:S(2)}) copy-start(bf16[12,256,128]{2,1,0:T(8,128)(2,1)} %get-tuple-element.99.v_ref) | copy-start | bytes 2359300
  121.0 1.5 %collective-permute-start.25 = (bf16[2,192,256]{2,1,0:T(8,128)(2,1)S(1)}, bf16[2,192,256]{2,1,0:T(8,128)(2,1)S(1)}, u32[]{:S(2)}, u32[]{:S(2)}) collective-permute-start(bf16[2,192,256]{2,1,0:T(8,128)(2,1)S(1)} %slice.86), channel_id=1, source_target_pairs={{0,2},{2,0},{4,6},{6,4},{8,10},{10,8},{12,14},{14,12},{16,18},{18,... | collective-permute-start | bytes 589832 | tf_op jit(solution)/shard_map/products_core/ppermute | solution.py:440
  122.6 14.2 %collective-permute-start.27 = (bf16[2,192,256]{2,1,0:T(8,128)(2,1)S(1)}, bf16[2,192,256]{2,1,0:T(8,128)(2,1)S(1)}, u32[]{:S(2)}, u32[]{:S(2)}) collective-permute-start(bf16[2,192,256]{2,1,0:T(8,128)(2,1)S(1)} %pad_maximum_fusion.12), channel_id=1, source_target_pairs={{0,12},{2,14},{4,8},{6,10},{8,4},{10,6},{12,0},{14,2},{16,28},{18,... | collective-permute-start | bytes 589832 | tf_op jit(solution)/shard_map/products_group/ppermute | solution.py:440
  128.3 9.5 %collective-permute-start.26 = (bf16[2,192,256]{2,1,0:T(8,128)(2,1)S(1)}, bf16[2,192,256]{2,1,0:T(8,128)(2,1)S(1)}, u32[]{:S(2)}, u32[]{:S(2)}) collective-permute-start(bf16[2,192,256]{2,1,0:T(8,128)(2,1)S(1)} %pad_maximum_fusion.11), channel_id=1, source_target_pairs={{0,8},{2,10},{4,12},{6,14},{8,0},{10,2},{12,4},{14,6},{16,24},{18,... | collective-permute-start | bytes 589832 | tf_op jit(solution)/shard_map/products_group/ppermute | solution.py:440
  128.4 16.3 %collective-permute-start.28 = (bf16[192,512]{1,0:T(8,128)(2,1)S(1)}, bf16[192,512]{1,0:T(8,128)(2,1)S(1)}, u32[]{:S(2)}, u32[]{:S(2)}) collective-permute-start(bf16[192,512]{1,0:T(8,128)(2,1)S(1)} %get-tuple-element.180), channel_id=1, source_target_pairs={{0,24},{2,26},{4,28},{6,30},{8,16},{10,18},{12,20},{14,22},{16,8},... | collective-permute-start | bytes 589832 | tf_op jit(solution)/shard_map/grad_w_far/ppermute | solution.py:440
  130.6 17.5 %collective-permute-start.29 = (bf16[192,512]{1,0:T(8,128)(2,1)S(1)}, bf16[192,512]{1,0:T(8,128)(2,1)S(1)}, u32[]{:S(2)}, u32[]{:S(2)}) collective-permute-start(bf16[192,512]{1,0:T(8,128)(2,1)S(1)} %get-tuple-element.181), channel_id=1, source_target_pairs={{0,24},{2,26},{4,28},{6,30},{8,16},{10,18},{12,20},{14,22},{16,8},... | collective-permute-start | bytes 589832 | tf_op jit(solution)/shard_map/grad_w_far/ppermute | solution.py:440

commit v5 on v4

--- a/solution.py
+++ b/solution.py
@@ -524,7 +524,6 @@
     odd = move(summed1[2:], CORE, "products_core")
     next_plane = [jnp.stack([summed1[j], odd[j]]) for j in range(2)]
     next_plane = [move(next_plane[j], xor(4 + 2 * j), "products_group") for j in range(2)]
-    odd, sent = barrier((odd, sent))
     far += [move(part, FAR, "grad_w_far") for part in sent]
     grads = attention_backward(place, 0, 2, saved, jnp.stack(near), qg, kg)
     grads = attention_backward(place, 2, 2, saved, jnp.stack(next_plane), qg, kg, tuple(grads))

time: 151 us -> 148 us (0.980)
  starting transfers between devices: 40 us -> 38.1 us
    ppermute x24, starting transfers between devices: 31.7 us -> 29.8 us  [move(): return lax.ppermute(a, 'fsdp', perm)]
  transfers between devices with their start and end apart: 30 -> 30, of which waited for: 17 -> 16; matrix products, arithmetic and copies ran while one was open for 1% -> 1% of each run, Pallas kernels for 23% -> 21%
where the time goes in v5:
time: 148 us; the launch traced here: 147 us
  waiting for transfers between devices  64.1 us (43%)
  Pallas kernels  40 us (27%)
  starting transfers between devices  38.1 us (26%)
  local copies, waits for them, and re-layouts  2.51 us (2%)
  other arithmetic  1.61 us (1%)
    ppermute x24, waiting for transfers between devices, move(): return lax.ppermute(a, 'fsdp', perm)  32.2 us
    ppermute x6, waiting for transfers between devices, swap(): return lax.ppermute(a, 'seq', [(0, 1), (1, 0)])  31.9 us
    ppermute x24, starting transfers between devices, move(): return lax.ppermute(a, 'fsdp', perm)  29.8 us
    pallas_call x2, Pallas kernels, attention_backward(): pl.pallas_call(functools.partial(backward_kernel, per, dim, len(into)), g...  8.86 us
    pallas_call x1, Pallas kernels, attention_probabilities(): pl.pallas_call(functools.partial(probabilities_kernel, per, dim), grid_sp...  8.48 us
    ppermute x6, starting transfers between devices, swap(): return lax.ppermute(a, 'seq', [(0, 1), (1, 0)])  8.32 us
    pallas_call x2, Pallas kernels, gradient_products(): pl.pallas_call(functools.partial(products_kernel, n, [(first, wide, start...  6.47 us
    pallas_call x2, Pallas kernels, weight_terms(): pl.pallas_call(functools.partial(weight_kernel, n, half[1], parts), in_sp...  6.3 us
  transfers between devices with their start and end apart: 30, of which 16 were waited for; matrix products, arithmetic and copies ran while one was open for 1% of the time, Pallas kernels for 21%

profile of v5, /device:TPU:0, one launch (start us, length us, event | category | flops | bytes accessed | tf_op | source)
XLA Modules:
  0.0 147.4 jit_solution(18012054112466798482)
XLA Ops:
  0.6 0.0 copy-start.8
  0.6 1.2 dynamic-slice_bitcast_fusion
  1.9 0.9 pad_maximum_fusion
  2.9 3.0 %collective-permute-start.4 = (bf16[256,3072]{1,0:T(8,128)(2,1)}, bf16[256,3072]{1,0:T(8,128)(2,1)S(1)}, u32[]{:S(2)}, u32[]{:S(2)}) collective-permute-start(bf16[256,3072]{1,0:T(8,128)(2,1)} %refs_0_), channel_id=1, source_target_pairs={{0,8},{2,10},{4,12},{6,14},{8,0},{10,2},{12,4},{14,6},{16,24},{18,... | collective-permute-start | bytes 4718600 | tf_op jit(solution)/shard_map/gy_plane/ppermute | solution.py:440
  5.9 1.5 %collective-permute-start.3 = (bf16[256,3072]{1,0:T(8,128)(2,1)}, bf16[256,3072]{1,0:T(8,128)(2,1)S(1)}, u32[]{:S(2)}, u32[]{:S(2)}) collective-permute-start(bf16[256,3072]{1,0:T(8,128)(2,1)} %refs_0_), channel_id=1, source_target_pairs={{0,4},{2,6},{4,0},{6,2},{8,12},{10,14},{12,8},{14,10},{16,20},{18,... | collective-permute-start | bytes 4718600 | tf_op jit(solution)/shard_map/gy_cross/ppermute | solution.py:440
  7.4 1.5 %collective-permute-start = (bf16[2,128,1536]{2,1,0:T(8,128)(2,1)}, bf16[2,128,1536]{2,1,0:T(8,128)(2,1)}, u32[]{:S(2)}, u32[]{:S(2)}) collective-permute-start(bf16[2,128,1536]{2,1,0:T(8,128)(2,1)} %pad_maximum_fusion), channel_id=1, source_target_pairs={{0,1},{1,0},{2,3},{3,2},{4,5},{5,4},{6,7},{7,6},{8,9},{9,8},{10,11... | collective-permute-start | bytes 2359304 | tf_op jit(solution)/shard_map/qk_seq/ppermute | solution.py:445
  8.9 1.7 %collective-permute-start.5 = (bf16[192,3072]{1,0:T(8,128)(2,1)}, bf16[192,3072]{1,0:T(8,128)(2,1)}, u32[]{:S(2)}, u32[]{:S(2)}) collective-permute-start(bf16[192,3072]{1,0:T(8,128)(2,1)} %refs_1_.1), channel_id=1, source_target_pairs={{8,16},{10,18},{12,20},{14,22},{16,8},{18,10},{20,12},{22,14},{9,1... | collective-permute-start | bytes 3538952 | tf_op jit(solution)/shard_map/w_middle/ppermute | solution.py:440
  10.6 0.8 constant_dynamic-slice_fusion
  11.4 0.5 collective-permute-start.1
  11.9 0.1 copy.15.col_ref
  12.0 0.1 pad_add_fusion.place
  12.1 16.1 %collective-permute-done.came_ref = bf16[2,128,1536]{2,1,0:T(8,128)(2,1)} collective-permute-done((bf16[2,128,1536]{2,1,0:T(8,128)(2,1)}, bf16[2,128,1536]{2,1,0:T(8,128)(2,1)}, u32[]{:S(2)}, u32[]{:S(2)}) %collective-permute-start) | collective-permute-done | bytes 786464 | tf_op jit(solution)/shard_map/qk_seq/ppermute | solution.py:445
  28.2 8.5 %attention_probabilities.1 = (f32[12,256,256]{2,1,0:T(8,128)}, f32[2,12,256,128]{3,2,1,0:T(8,128)}, f32[2,12,256,128]{3,2,1,0:T(8,128)}, bf16[2,12,256,128]{3,2,1,0:T(8,128)(2,1)}, bf16[12,256,256]{2,1,0:T(8,128)(2,1)S(1)}) custom-call(s32[4]{0:T(128)S(1)} %pad_add_fusion.place, bf16[128,3072]{1,0:T(8,128)(2,1)} %q_ref.1, bf16[128,3072]{1,0:T(8,128)(2,1)} %k_ref.1, ...), custom_call_target="tpu_custom_call" | custom-call | flops 1000 | bytes 1000 | tf_op jit(solution)/shard_map/attention_probabilities/pallas_call | solution.py:219
  36.7 3.9 %attention_attended.1 = (bf16[4,192,256]{2,1,0:T(8,128)(2,1)S(1)}, bf16[4,192,256]{2,1,0:T(8,128)(2,1)S(1)}, bf16[12,256,128]{2,1,0:T(8,128)(2,1)}) custom-call(s32[4]{0:T(128)S(1)} %pad_add_fusion.place, bf16[12,256,256]{2,1,0:T(8,128)(2,1)S(1)} %get-tuple-element.96.p_low_ref, bf16[128,3072]{1,0:T(8,128)(2,1)} %v_ref.1, ...), custom_call_target="tpu_custom_call" | custom-call | flops 1000 | bytes 1000 | tf_op jit(solution)/shard_map/attention_attended/pallas_call | solution.py:242
  40.6 1.7 %collective-permute-done.2 = bf16[4,192,256]{2,1,0:T(8,128)(2,1)S(1)} collective-permute-done((bf16[4,192,256]{2,1,0:T(8,128)(2,1)S(1)}, bf16[4,192,256]{2,1,0:T(8,128)(2,1)S(1)}, u32[]{:S(2)}, u32[]{:S(2)}) %collective-permute-start.2) | collective-permute-done | bytes 393248 | tf_op jit(solution)/shard_map/att_core/ppermute | solution.py:440
  42.4 0.1 collective-permute-start.10
  42.6 1.0 collective-permute-start.6
  43.7 0.5 collective-permute-start.7
  44.2 1.6 %collective-permute-start.9 = (bf16[2,192,256]{2,1,0:T(8,128)(2,1)S(1)}, bf16[2,192,256]{2,1,0:T(8,128)(2,1)S(1)}, u32[]{:S(2)}, u32[]{:S(2)}) collective-permute-start(bf16[2,192,256]{2,1,0:T(8,128)(2,1)S(1)} %pad_maximum_fusion.5), channel_id=1, source_target_pairs={{0,1},{1,0},{2,3},{3,2},{4,5},{5,4},{6,7},{7,6},{8,9},{9,8},{10,11... | collective-permute-start | bytes 589832 | tf_op jit(solution)/shard_map/att_seq/ppermute | solution.py:445
  45.8 2.2 %collective-permute-start.8 = (bf16[2,192,256]{2,1,0:T(8,128)(2,1)S(1)}, bf16[2,192,256]{2,1,0:T(8,128)(2,1)S(1)}, u32[]{:S(2)}, u32[]{:S(2)}) collective-permute-start(bf16[2,192,256]{2,1,0:T(8,128)(2,1)S(1)} %pad_maximum_fusion.8), channel_id=1, source_target_pairs={{0,12},{2,14},{4,8},{6,10},{8,4},{10,6},{12,0},{14,2},{16,28},{18,... | collective-permute-start | bytes 589832 | tf_op jit(solution)/shard_map/att_group/ppermute | solution.py:440
  48.0 1.9 %collective-permute-done.6 = bf16[2,192,256]{2,1,0:T(8,128)(2,1)S(1)} collective-permute-done((bf16[2,192,256]{2,1,0:T(8,128)(2,1)S(1)}, bf16[2,192,256]{2,1,0:T(8,128)(2,1)S(1)}, u32[]{:S(2)}, u32[]{:S(2)}) %collective-permute-start.6) | collective-permute-done | bytes 196640 | tf_op jit(solution)/shard_map/att_group/ppermute | solution.py:440
  49.8 4.4 %collective-permute-start.16 = (bf16[192,3072]{1,0:T(8,128)(2,1)}, bf16[192,3072]{1,0:T(8,128)(2,1)S(1)}, u32[]{:S(2)}, u32[]{:S(2)}) collective-permute-start(bf16[192,3072]{1,0:T(8,128)(2,1)} %refs_1_.1), channel_id=1, source_target_pairs={{0,24},{2,26},{4,28},{6,30},{24,0},{26,2},{28,4},{30,6},{1,25},{3,... | collective-permute-start | bytes 3538952 | tf_op jit(solution)/shard_map/w_ends/ppermute | solution.py:440
  54.3 0.1 slice.68
  54.4 0.9 collective-permute-done.8
  55.3 1.1 collective-permute-start.12
  56.4 0.1 pad_maximum_fusion.2
  56.5 1.6 %collective-permute-start.11 = (bf16[6,192,256]{2,1,0:T(8,128)(2,1)S(1)}, bf16[6,192,256]{2,1,0:T(8,128)(2,1)S(1)}, u32[]{:S(2)}, u32[]{:S(2)}) collective-permute-start(bf16[6,192,256]{2,1,0:T(8,128)(2,1)S(1)} %pad_maximum_fusion.2), channel_id=1, source_target_pairs={{0,1},{1,0},{2,3},{3,2},{4,5},{5,4},{6,7},{7,6},{8,9},{9,8},{10,11... | collective-permute-start | bytes 1769480 | tf_op jit(solution)/shard_map/att_seq/ppermute | solution.py:445
  58.1 0.5 collective-permute-start.15
  58.6 2.5 %hold.1 = (bf16[256,3072]{1,0:T(8,128)(2,1)S(1)}, bf16[192,3072]{1,0:T(8,128)(2,1)S(1)}) custom-call(bf16[256,3072]{1,0:T(8,128)(2,1)} %refs_0_, bf16[192,3072]{1,0:T(8,128)(2,1)} %refs_1_.1), custom_call_target="tpu_custom_call" | custom-call | flops 1000 | bytes 1000 | tf_op jit(solution)/shard_map/hold/pallas_call | solution.py:300
  61.1 9.8 %collective-permute-done.11 = bf16[6,192,256]{2,1,0:T(8,128)(2,1)S(1)} collective-permute-done((bf16[6,192,256]{2,1,0:T(8,128)(2,1)S(1)}, bf16[6,192,256]{2,1,0:T(8,128)(2,1)S(1)}, u32[]{:S(2)}, u32[]{:S(2)}) %collective-permute-start.11) | collective-permute-done | bytes 589856 | tf_op jit(solution)/shard_map/att_seq/ppermute | solution.py:445
  70.9 0.1 pad_maximum_fusion.1.other_ref
  71.0 8.6 %collective-permute-done.12.refs_6_.refs_1_ = bf16[256,2048]{1,0:T(8,128)(2,1)S(1)} collective-permute-done((bf16[256,2048]{1,0:T(8,128)(2,1)S(1)}, bf16[256,2048]{1,0:T(8,128)(2,1)S(1)}, u32[]{:S(2)}, u32[]{:S(2)}) %collective-permute-start.12) | collective-permute-done | bytes 1048608 | tf_op jit(solution)/shard_map/gy_plane_cross_a/ppermute | solution.py:440
  79.6 2.6 %collective-permute-done.16.end_ref = bf16[192,3072]{1,0:T(8,128)(2,1)S(1)} collective-permute-done((bf16[192,3072]{1,0:T(8,128)(2,1)}, bf16[192,3072]{1,0:T(8,128)(2,1)S(1)}, u32[]{:S(2)}, u32[]{:S(2)}) %collective-permute-start.16) | collective-permute-done | bytes 1179680 | tf_op jit(solution)/shard_map/w_ends/ppermute | solution.py:440
  82.3 1.4 choose.1.far_ref
  83.8 4.0 %weight_terms.2 = (bf16[192,1024]{1,0:T(8,128)(2,1)S(1)}, bf16[192,1024]{1,0:T(8,128)(2,1)S(1)}, f32[192,2048]{1,0:T(8,128)S(1)}) custom-call(s32[4]{0:T(128)S(1)} %pad_add_fusion.place, bf16[8,192,256]{2,1,0:T(8,128)(2,1)S(1)} %constant_dynamic-update-slice_fusion.own_ref, bf16[8,192,256]{2,1,0:T(8,128)(2,1)S(1)} %pad_maximum_fusion.1.other_ref, ...), custom_call_target="tpu_custom_call" | custom-call | flops 1000 | bytes 1000 | tf_op jit(solution)/shard_map/weight_terms/pallas_call | solution.py:383
  87.8 1.0 collective-permute-start.17
  88.8 1.7 %collective-permute-start.18 = (bf16[192,1024]{1,0:T(8,128)(2,1)S(1)}, bf16[192,1024]{1,0:T(8,128)(2,1)S(1)}, u32[]{:S(2)}, u32[]{:S(2)}) collective-permute-start(bf16[192,1024]{1,0:T(8,128)(2,1)S(1)} %get-tuple-element.130), channel_id=1, source_target_pairs={{0,24},{2,26},{4,28},{6,30},{8,16},{10,18},{12,20},{14,22},{16,8},... | collective-permute-start | bytes 1179656 | tf_op jit(solution)/shard_map/grad_w_far/ppermute | solution.py:440
  90.5 3.2 %gradient_products.2 = (bf16[4,192,256]{2,1,0:T(8,128)(2,1)S(1)}, bf16[4,192,256]{2,1,0:T(8,128)(2,1)S(1)}) custom-call(s32[4]{0:T(128)S(1)} %pad_add_fusion.place, bf16[192,3072]{1,0:T(8,128)(2,1)S(1)} %get-tuple-element.132.w_ref, bf16[192,3072]{1,0:T(8,128)(2,1)S(1)} %choose.1.far_ref, bf16[256,3072]{1,0:T(8,128)(2,1)S(1)} %get-tuple-element.151.refs_0_.refs_4_, ...), custom_call_target="tpu_custom_call" | custom-call | flops 1000 | bytes 1000 | tf_op jit(solution)/shard_map/gradient_products/pallas_call | solution.py:351
  93.7 1.6 %collective-permute-start.19 = (bf16[4,192,256]{2,1,0:T(8,128)(2,1)S(1)}, bf16[4,192,256]{2,1,0:T(8,128)(2,1)S(1)}, u32[]{:S(2)}, u32[]{:S(2)}) collective-permute-start(bf16[4,192,256]{2,1,0:T(8,128)(2,1)S(1)} %get-tuple-element.136), channel_id=1, source_target_pairs={{0,1},{1,0},{2,3},{3,2},{4,5},{5,4},{6,7},{7,6},{8,9},{9,8},{10,11... | collective-permute-start | bytes 1179656 | tf_op jit(solution)/shard_map/products_seq/ppermute | solution.py:445
  95.3 5.5 %collective-permute-done.18.refs_2_ = bf16[192,1024]{1,0:T(8,128)(2,1)S(1)} collective-permute-done((bf16[192,1024]{1,0:T(8,128)(2,1)S(1)}, bf16[192,1024]{1,0:T(8,128)(2,1)S(1)}, u32[]{:S(2)}, u32[]{:S(2)}) %collective-permute-start.18) | collective-permute-done | bytes 393248 | tf_op jit(solution)/shard_map/grad_w_far/ppermute | solution.py:440
  100.8 3.2 %collective-permute-done.19 = bf16[4,192,256]{2,1,0:T(8,128)(2,1)S(1)} collective-permute-done((bf16[4,192,256]{2,1,0:T(8,128)(2,1)S(1)}, bf16[4,192,256]{2,1,0:T(8,128)(2,1)S(1)}, u32[]{:S(2)}, u32[]{:S(2)}) %collective-permute-start.19) | collective-permute-done | bytes 393248 | tf_op jit(solution)/shard_map/products_seq/ppermute | solution.py:445
  104.0 1.8 %collective-permute-start.20 = (bf16[192,1024]{1,0:T(8,128)(2,1)S(1)}, bf16[192,1024]{1,0:T(8,128)(2,1)S(1)}, u32[]{:S(2)}, u32[]{:S(2)}) collective-permute-start(bf16[192,1024]{1,0:T(8,128)(2,1)S(1)} %get-tuple-element.138), channel_id=1, source_target_pairs={{0,24},{2,26},{4,28},{6,30},{8,16},{10,18},{12,20},{14,22},{16,8},... | collective-permute-start | bytes 1179656 | tf_op jit(solution)/shard_map/grad_w_far/ppermute | solution.py:440
  105.8 0.1 collective-permute-done.21.refs_7_
  105.9 3.2 %gradient_products.3 = (bf16[4,192,256]{2,1,0:T(8,128)(2,1)S(1)}, bf16[4,192,256]{2,1,0:T(8,128)(2,1)S(1)}) custom-call(s32[4]{0:T(128)S(1)} %pad_add_fusion.place, bf16[192,3072]{1,0:T(8,128)(2,1)S(1)} %get-tuple-element.132.w_ref, bf16[192,3072]{1,0:T(8,128)(2,1)S(1)} %choose.1.far_ref, bf16[256,3072]{1,0:T(8,128)(2,1)S(1)} %collective-permute-done.4.refs_4_.refs_0_, ...), custom_call_target="tpu_custom_call" | custom-call | flops 1000 | bytes 1000 | tf_op jit(solution)/shard_map/gradient_products/pallas_call | solution.py:351
  109.1 0.1 add_convert_fusion.1
  109.3 0.2 collective-permute-start.22
  109.5 1.5 %collective-permute-start.24 = (bf16[4,192,256]{2,1,0:T(8,128)(2,1)S(1)}, bf16[4,192,256]{2,1,0:T(8,128)(2,1)S(1)}, u32[]{:S(2)}, u32[]{:S(2)}) collective-permute-start(bf16[4,192,256]{2,1,0:T(8,128)(2,1)S(1)} %get-tuple-element.148), channel_id=1, source_target_pairs={{0,1},{1,0},{2,3},{3,2},{4,5},{5,4},{6,7},{7,6},{8,9},{9,8},{10,11... | collective-permute-start | bytes 1179656 | tf_op jit(solution)/shard_map/products_seq/ppermute | solution.py:445
  111.1 1.1 collective-permute-start.23
  112.2 2.3 %weight_terms.3 = (bf16[192,512]{1,0:T(8,128)(2,1)S(1)}, bf16[192,512]{1,0:T(8,128)(2,1)S(1)}, f32[192,1024]{1,0:T(8,128)S(1)}) custom-call(s32[4]{0:T(128)S(1)} %pad_add_fusion.place, bf16[8,192,256]{2,1,0:T(8,128)(2,1)S(1)} %constant_dynamic-update-slice_fusion.own_ref, bf16[8,192,256]{2,1,0:T(8,128)(2,1)S(1)} %pad_maximum_fusion.1.other_ref, ...), custom_call_target="tpu_custom_call" | custom-call | flops 1000 | bytes 1000 | tf_op jit(solution)/shard_map/weight_terms/pallas_call | solution.py:383
  114.6 2.8 %collective-permute-done.20.refs_3_ = bf16[192,1024]{1,0:T(8,128)(2,1)S(1)} collective-permute-done((bf16[192,1024]{1,0:T(8,128)(2,1)S(1)}, bf16[192,1024]{1,0:T(8,128)(2,1)S(1)}, u32[]{:S(2)}, u32[]{:S(2)}) %collective-permute-start.20) | collective-permute-done | bytes 393248 | tf_op jit(solution)/shard_map/grad_w_far/ppermute | solution.py:440
  117.4 0.6 collective-permute-done.23
  118.0 2.8 %collective-permute-done.24 = bf16[4,192,256]{2,1,0:T(8,128)(2,1)S(1)} collective-permute-done((bf16[4,192,256]{2,1,0:T(8,128)(2,1)S(1)}, bf16[4,192,256]{2,1,0:T(8,128)(2,1)S(1)}, u32[]{:S(2)}, u32[]{:S(2)}) %collective-permute-start.24) | collective-permute-done | bytes 393248 | tf_op jit(solution)/shard_map/products_seq/ppermute | solution.py:445
  120.9 0.1 add_convert_fusion
  121.0 0.1 collective-permute-start.25
  121.1 2.0 %collective-permute-start.28 = (bf16[192,512]{1,0:T(8,128)(2,1)S(1)}, bf16[192,512]{1,0:T(8,128)(2,1)S(1)}, u32[]{:S(2)}, u32[]{:S(2)}) collective-permute-start(bf16[192,512]{1,0:T(8,128)(2,1)S(1)} %get-tuple-element.176), channel_id=1, source_target_pairs={{0,24},{2,26},{4,28},{6,30},{8,16},{10,18},{12,20},{14,22},{16,8},... | collective-permute-start | bytes 589832 | tf_op jit(solution)/shard_map/grad_w_far/ppermute | solution.py:440
  123.1 1.9 %collective-permute-start.29 = (bf16[192,512]{1,0:T(8,128)(2,1)S(1)}, bf16[192,512]{1,0:T(8,128)(2,1)S(1)}, u32[]{:S(2)}, u32[]{:S(2)}) collective-permute-start(bf16[192,512]{1,0:T(8,128)(2,1)S(1)} %get-tuple-element.177), channel_id=1, source_target_pairs={{0,24},{2,26},{4,28},{6,30},{8,16},{10,18},{12,20},{14,22},{16,8},... | collective-permute-start | bytes 589832 | tf_op jit(solution)/shard_map/grad_w_far/ppermute | solution.py:440
  125.1 3.9 %collective-permute-start.27 = (bf16[2,192,256]{2,1,0:T(8,128)(2,1)S(1)}, bf16[2,192,256]{2,1,0:T(8,128)(2,1)S(1)}, u32[]{:S(2)}, u32[]{:S(2)}) collective-permute-start(bf16[2,192,256]{2,1,0:T(8,128)(2,1)S(1)} %pad_maximum_fusion.12), channel_id=1, source_target_pairs={{0,12},{2,14},{4,8},{6,10},{8,4},{10,6},{12,0},{14,2},{16,28},{18,... | collective-permute-start | bytes 589832 | tf_op jit(solution)/shard_map/products_group/ppermute | solution.py:440
  129.0 0.1 collective-permute-start.26
  129.2 4.4 %attention_backward.2 = (bf16[12,256,128]{2,1,0:T(8,128)(2,1)}, bf16[12,256,128]{2,1,0:T(8,128)(2,1)}, bf16[12,256,128]{2,1,0:T(8,128)(2,1)}) custom-call(s32[4]{0:T(128)S(1)} %pad_add_fusion.place, f32[12,256,256]{2,1,0:T(8,128)S(1)} %copy-done, f32[2,12,256,128]{3,2,1,0:T(8,128)S(1)} %copy-done.1, f32[2,12,256,128]{3,2,1,0:T(8,128)S(1)} %copy-done.2, ...), custom_call_target="tpu_custom_call" | custom-call | flops 1000 | bytes 1000 | tf_op jit(solution)/shard_map/attention_backward/pallas_call | solution.py:268
  133.6 1.3 collective-permute-done.29.refs_5_
  134.9 2.0 %finish.1 = f32[192,3072]{1,0:T(8,128)} custom-call(f32[192,2048]{1,0:T(8,128)S(1)} %get-tuple-element.172.refs_0_, f32[192,1024]{1,0:T(8,128)S(1)} %get-tuple-element.173.refs_1_, bf16[192,1024]{1,0:T(8,128)(2,1)S(1)} %collective-permute-done.18.refs_2_, bf16[192,1024]{1,0:T(8,128)(2,1)S(1)} %collective-permute-done.20.refs_3_, ...), custom_call_target="tpu_custom_call" | custom-call | flops 1000 | bytes 1000 | tf_op jit(solution)/shard_map/finish/pallas_call | solution.py:416
  136.9 2.3 %collective-permute-done.27 = bf16[2,192,256]{2,1,0:T(8,128)(2,1)S(1)} collective-permute-done((bf16[2,192,256]{2,1,0:T(8,128)(2,1)S(1)}, bf16[2,192,256]{2,1,0:T(8,128)(2,1)S(1)}, u32[]{:S(2)}, u32[]{:S(2)}) %collective-permute-start.27) | collective-permute-done | bytes 196640 | tf_op jit(solution)/shard_map/products_group/ppermute | solution.py:440
  139.2 3.7 %collective-permute-done.26 = bf16[2,192,256]{2,1,0:T(8,128)(2,1)S(1)} collective-permute-done((bf16[2,192,256]{2,1,0:T(8,128)(2,1)S(1)}, bf16[2,192,256]{2,1,0:T(8,128)(2,1)S(1)}, u32[]{:S(2)}, u32[]{:S(2)}) %collective-permute-start.26) | collective-permute-done | bytes 196640 | tf_op jit(solution)/shard_map/products_group/ppermute | solution.py:440
  142.9 4.4 %attention_backward.3 = (bf16[12,256,128]{2,1,0:T(8,128)(2,1)}, bf16[12,256,128]{2,1,0:T(8,128)(2,1)}, bf16[12,256,128]{2,1,0:T(8,128)(2,1)}) custom-call(s32[4]{0:T(128)S(1)} %pad_add_fusion.place, f32[12,256,256]{2,1,0:T(8,128)S(1)} %copy-done, f32[2,12,256,128]{3,2,1,0:T(8,128)S(1)} %copy-done.1, ...), custom_call_target="tpu_custom_call", output_to_operand_aliasing={{0}: (9, {}), {1}: (10, {}), {2}: (11, {})} | custom-call | flops 1000 | bytes 1000 | tf_op jit(solution)/shard_map/attention_backward/pallas_call | solution.py:268
  (58 shorter events, 0.6 us)
Async XLA Ops:
  0.6 10.0 %copy-start.8 = (bf16[128,3072]{1,0:T(8,128)(2,1)S(1)}, bf16[128,3072]{1,0:T(8,128)(2,1)}, u32[]{:S(2)}) copy-start(bf16[128,3072]{1,0:T(8,128)(2,1)} %v_ref.1) | copy-start | bytes 2359300
  1.9 10.0 %copy-start.7 = (s32[1,256]{1,0:T(1,128)S(1)}, s32[1,256]{1,0:T(1,128)}, u32[]{:S(2)}) copy-start(s32[1,256]{1,0:T(1,128)} %row_ref.1) | copy-start | bytes 3076
  1.9 26.3 %copy-start.5 = (f32[128]{0:T(128)S(1)}, f32[128]{0:T(128)}, u32[]{:S(2)}) copy-start(f32[128]{0:T(128)} %param.12) | copy-start | bytes 1540
  1.9 26.3 %copy-start.6 = (f32[128]{0:T(128)S(1)}, f32[128]{0:T(128)}, u32[]{:S(2)}) copy-start(f32[128]{0:T(128)} %param.13) | copy-start | bytes 1540
  2.9 39.5 %collective-permute-start.4 = (bf16[256,3072]{1,0:T(8,128)(2,1)}, bf16[256,3072]{1,0:T(8,128)(2,1)S(1)}, u32[]{:S(2)}, u32[]{:S(2)}) collective-permute-start(bf16[256,3072]{1,0:T(8,128)(2,1)} %refs_0_), channel_id=1, source_target_pairs={{0,8},{2,10},{4,12},{6,14},{8,0},{10,2},{12,4},{14,6},{16,24},{18,... | collective-permute-start | bytes 4718600 | tf_op jit(solution)/shard_map/gy_plane/ppermute | solution.py:440
  5.9 36.5 %collective-permute-start.3 = (bf16[256,3072]{1,0:T(8,128)(2,1)}, bf16[256,3072]{1,0:T(8,128)(2,1)S(1)}, u32[]{:S(2)}, u32[]{:S(2)}) collective-permute-start(bf16[256,3072]{1,0:T(8,128)(2,1)} %refs_0_), channel_id=1, source_target_pairs={{0,4},{2,6},{4,0},{6,2},{8,12},{10,14},{12,8},{14,10},{16,20},{18,... | collective-permute-start | bytes 4718600 | tf_op jit(solution)/shard_map/gy_cross/ppermute | solution.py:440
  7.4 20.8 %collective-permute-start = (bf16[2,128,1536]{2,1,0:T(8,128)(2,1)}, bf16[2,128,1536]{2,1,0:T(8,128)(2,1)}, u32[]{:S(2)}, u32[]{:S(2)}) collective-permute-start(bf16[2,128,1536]{2,1,0:T(8,128)(2,1)} %pad_maximum_fusion), channel_id=1, source_target_pairs={{0,1},{1,0},{2,3},{3,2},{4,5},{5,4},{6,7},{7,6},{8,9},{9,8},{10,11... | collective-permute-start | bytes 2359304 | tf_op jit(solution)/shard_map/qk_seq/ppermute | solution.py:445
  8.9 31.7 %collective-permute-start.5 = (bf16[192,3072]{1,0:T(8,128)(2,1)}, bf16[192,3072]{1,0:T(8,128)(2,1)}, u32[]{:S(2)}, u32[]{:S(2)}) collective-permute-start(bf16[192,3072]{1,0:T(8,128)(2,1)} %refs_1_.1), channel_id=1, source_target_pairs={{8,16},{10,18},{12,20},{14,22},{16,8},{18,10},{20,12},{22,14},{9,1... | collective-permute-start | bytes 3538952 | tf_op jit(solution)/shard_map/w_middle/ppermute | solution.py:440
  11.4 25.3 %collective-permute-start.1 = (bf16[128,1536]{1,0:T(8,128)(2,1)}, bf16[128,1536]{1,0:T(8,128)(2,1)}, u32[]{:S(2)}, u32[]{:S(2)}) collective-permute-start(bf16[128,1536]{1,0:T(8,128)(2,1)} %constant_dynamic-slice_fusion), channel_id=1, source_target_pairs={{0,1},{1,0},{2,3},{3,2},{4,5},{5,4},{6,7},{7,6},{8,9},{9,8},{10,11... | collective-permute-start | bytes 1179656 | tf_op jit(solution)/shard_map/v_seq/ppermute | solution.py:445
  40.6 1.7 %collective-permute-start.2 = (bf16[4,192,256]{2,1,0:T(8,128)(2,1)S(1)}, bf16[4,192,256]{2,1,0:T(8,128)(2,1)S(1)}, u32[]{:S(2)}, u32[]{:S(2)}) collective-permute-start(bf16[4,192,256]{2,1,0:T(8,128)(2,1)S(1)} %get-tuple-element.99), channel_id=1, source_target_pairs={{0,2},{2,0},{4,6},{6,4},{8,10},{10,8},{12,14},{14,12},{16,18},{18,... | collective-permute-start | bytes 1179656 | tf_op jit(solution)/shard_map/att_core/ppermute | solution.py:440
  42.4 13.0 %collective-permute-start.10 = (bf16[256,3072]{1,0:T(8,128)(2,1)}, bf16[256,3072]{1,0:T(8,128)(2,1)S(1)}, u32[]{:S(2)}, u32[]{:S(2)}) collective-permute-start(bf16[256,3072]{1,0:T(8,128)(2,1)} %refs_0_), channel_id=1, source_target_pairs={{0,2},{2,0},{4,6},{6,4},{8,10},{10,8},{12,14},{14,12},{16,18},{18,... | collective-permute-start | bytes 4718600 | tf_op jit(solution)/shard_map/gy_core/ppermute | solution.py:440
  42.6 7.2 %collective-permute-start.6 = (bf16[2,192,256]{2,1,0:T(8,128)(2,1)S(1)}, bf16[2,192,256]{2,1,0:T(8,128)(2,1)S(1)}, u32[]{:S(2)}, u32[]{:S(2)}) collective-permute-start(bf16[2,192,256]{2,1,0:T(8,128)(2,1)S(1)} %pad_maximum_fusion.6), channel_id=1, source_target_pairs={{0,4},{2,6},{4,0},{6,2},{8,12},{10,14},{12,8},{14,10},{16,20},{18,... | collective-permute-start | bytes 589832 | tf_op jit(solution)/shard_map/att_group/ppermute | solution.py:440
  43.7 10.7 %collective-permute-start.7 = (bf16[2,192,256]{2,1,0:T(8,128)(2,1)S(1)}, bf16[2,192,256]{2,1,0:T(8,128)(2,1)S(1)}, u32[]{:S(2)}, u32[]{:S(2)}) collective-permute-start(bf16[2,192,256]{2,1,0:T(8,128)(2,1)S(1)} %pad_maximum_fusion.7), channel_id=1, source_target_pairs={{0,8},{2,10},{4,12},{6,14},{8,0},{10,2},{12,4},{14,6},{16,24},{18,... | collective-permute-start | bytes 589832 | tf_op jit(solution)/shard_map/att_group/ppermute | solution.py:440
  44.2 10.2 %collective-permute-start.9 = (bf16[2,192,256]{2,1,0:T(8,128)(2,1)S(1)}, bf16[2,192,256]{2,1,0:T(8,128)(2,1)S(1)}, u32[]{:S(2)}, u32[]{:S(2)}) collective-permute-start(bf16[2,192,256]{2,1,0:T(8,128)(2,1)S(1)} %pad_maximum_fusion.5), channel_id=1, source_target_pairs={{0,1},{1,0},{2,3},{3,2},{4,5},{5,4},{6,7},{7,6},{8,9},{9,8},{10,11... | collective-permute-start | bytes 589832 | tf_op jit(solution)/shard_map/att_seq/ppermute | solution.py:445
  45.8 9.5 %collective-permute-start.8 = (bf16[2,192,256]{2,1,0:T(8,128)(2,1)S(1)}, bf16[2,192,256]{2,1,0:T(8,128)(2,1)S(1)}, u32[]{:S(2)}, u32[]{:S(2)}) collective-permute-start(bf16[2,192,256]{2,1,0:T(8,128)(2,1)S(1)} %pad_maximum_fusion.8), channel_id=1, source_target_pairs={{0,12},{2,14},{4,8},{6,10},{8,4},{10,6},{12,0},{14,2},{16,28},{18,... | collective-permute-start | bytes 589832 | tf_op jit(solution)/shard_map/att_group/ppermute | solution.py:440
  49.8 32.4 %collective-permute-start.16 = (bf16[192,3072]{1,0:T(8,128)(2,1)}, bf16[192,3072]{1,0:T(8,128)(2,1)S(1)}, u32[]{:S(2)}, u32[]{:S(2)}) collective-permute-start(bf16[192,3072]{1,0:T(8,128)(2,1)} %refs_1_.1), channel_id=1, source_target_pairs={{0,24},{2,26},{4,28},{6,30},{24,0},{26,2},{28,4},{30,6},{1,25},{3,... | collective-permute-start | bytes 3538952 | tf_op jit(solution)/shard_map/w_ends/ppermute | solution.py:440
  55.3 24.3 %collective-permute-start.12 = (bf16[256,2048]{1,0:T(8,128)(2,1)S(1)}, bf16[256,2048]{1,0:T(8,128)(2,1)S(1)}, u32[]{:S(2)}, u32[]{:S(2)}) collective-permute-start(bf16[256,2048]{1,0:T(8,128)(2,1)S(1)} %slice.68), channel_id=1, source_target_pairs={{0,4},{2,6},{4,0},{6,2},{8,12},{10,14},{12,8},{14,10},{16,20},{18,... | collective-permute-start | bytes 3145736 | tf_op jit(solution)/shard_map/gy_plane_cross_a/ppermute | solution.py:440
  56.5 14.4 %collective-permute-start.11 = (bf16[6,192,256]{2,1,0:T(8,128)(2,1)S(1)}, bf16[6,192,256]{2,1,0:T(8,128)(2,1)S(1)}, u32[]{:S(2)}, u32[]{:S(2)}) collective-permute-start(bf16[6,192,256]{2,1,0:T(8,128)(2,1)S(1)} %pad_maximum_fusion.2), channel_id=1, source_target_pairs={{0,1},{1,0},{2,3},{3,2},{4,5},{5,4},{6,7},{7,6},{8,9},{9,8},{10,11... | collective-permute-start | bytes 1769480 | tf_op jit(solution)/shard_map/att_seq/ppermute | solution.py:445
  58.1 25.7 %collective-permute-start.14 = (bf16[256,3072]{1,0:T(8,128)(2,1)S(1)}, bf16[256,3072]{1,0:T(8,128)(2,1)S(1)}, u32[]{:S(2)}, u32[]{:S(2)}) collective-permute-start(bf16[256,3072]{1,0:T(8,128)(2,1)S(1)} %collective-permute-done.3.refs_2_.refs_1_.refs_5_), channel_id=1, source_target_pairs={{0,2},{2,0},{4,6},{6,4},{8,10},{10,8},{12,14},{14,12},{16,18},{18,... | collective-permute-start | bytes 4718600 | tf_op jit(solution)/shard_map/gy_core/ppermute | solution.py:440
  58.1 25.7 %collective-permute-start.15 = (bf16[256,3072]{1,0:T(8,128)(2,1)S(1)}, bf16[256,3072]{1,0:T(8,128)(2,1)S(1)}, u32[]{:S(2)}, u32[]{:S(2)}) collective-permute-start(bf16[256,3072]{1,0:T(8,128)(2,1)S(1)} %collective-permute-done.4.refs_4_.refs_0_), channel_id=1, source_target_pairs={{0,2},{2,0},{4,6},{6,4},{8,10},{10,8},{12,14},{14,12},{16,18},{18,... | collective-permute-start | bytes 4718600 | tf_op jit(solution)/shard_map/gy_core/ppermute | solution.py:440
  79.6 4.2 %collective-permute-start.13 = (bf16[256,2048]{1,0:T(8,128)(2,1)S(1)}, bf16[256,2048]{1,0:T(8,128)(2,1)S(1)}, u32[]{:S(2)}, u32[]{:S(2)}) collective-permute-start(bf16[256,2048]{1,0:T(8,128)(2,1)S(1)} %collective-permute-done.12.refs_6_.refs_1_), channel_id=1, source_target_pairs={{0,2},{2,0},{4,6},{6,4},{8,10},{10,8},{12,14},{14,12},{16,18},{18,... | collective-permute-start | bytes 3145736 | tf_op jit(solution)/shard_map/gy_core/ppermute | solution.py:440
  87.8 16.2 %collective-permute-start.17 = (bf16[256,1024]{1,0:T(8,128)(2,1)S(1)}, bf16[256,1024]{1,0:T(8,128)(2,1)S(1)}, u32[]{:S(2)}, u32[]{:S(2)}) collective-permute-start(bf16[256,1024]{1,0:T(8,128)(2,1)S(1)} %slice.69), channel_id=1, source_target_pairs={{0,4},{2,6},{4,0},{6,2},{8,12},{10,14},{12,8},{14,10},{16,20},{18,... | collective-permute-start | bytes 1572872 | tf_op jit(solution)/shard_map/gy_plane_cross_b/ppermute | solution.py:440
  88.8 12.1 %collective-permute-start.18 = (bf16[192,1024]{1,0:T(8,128)(2,1)S(1)}, bf16[192,1024]{1,0:T(8,128)(2,1)S(1)}, u32[]{:S(2)}, u32[]{:S(2)}) collective-permute-start(bf16[192,1024]{1,0:T(8,128)(2,1)S(1)} %get-tuple-element.130), channel_id=1, source_target_pairs={{0,24},{2,26},{4,28},{6,30},{8,16},{10,18},{12,20},{14,22},{16,8},... | collective-permute-start | bytes 1179656 | tf_op jit(solution)/shard_map/grad_w_far/ppermute | solution.py:440
  93.7 10.3 %collective-permute-start.19 = (bf16[4,192,256]{2,1,0:T(8,128)(2,1)S(1)}, bf16[4,192,256]{2,1,0:T(8,128)(2,1)S(1)}, u32[]{:S(2)}, u32[]{:S(2)}) collective-permute-start(bf16[4,192,256]{2,1,0:T(8,128)(2,1)S(1)} %get-tuple-element.136), channel_id=1, source_target_pairs={{0,1},{1,0},{2,3},{3,2},{4,5},{5,4},{6,7},{7,6},{8,9},{9,8},{10,11... | collective-permute-start | bytes 1179656 | tf_op jit(solution)/shard_map/products_seq/ppermute | solution.py:445
  104.0 1.9 %collective-permute-start.21 = (bf16[256,1024]{1,0:T(8,128)(2,1)S(1)}, bf16[256,1024]{1,0:T(8,128)(2,1)S(1)}, u32[]{:S(2)}, u32[]{:S(2)}) collective-permute-start(bf16[256,1024]{1,0:T(8,128)(2,1)S(1)} %collective-permute-done.17.refs_5_.refs_6_), channel_id=1, source_target_pairs={{0,2},{2,0},{4,6},{6,4},{8,10},{10,8},{12,14},{14,12},{16,18},{18,... | collective-permute-start | bytes 1572872 | tf_op jit(solution)/shard_map/gy_core/ppermute | solution.py:440
  104.0 13.4 %collective-permute-start.20 = (bf16[192,1024]{1,0:T(8,128)(2,1)S(1)}, bf16[192,1024]{1,0:T(8,128)(2,1)S(1)}, u32[]{:S(2)}, u32[]{:S(2)}) collective-permute-start(bf16[192,1024]{1,0:T(8,128)(2,1)S(1)} %get-tuple-element.138), channel_id=1, source_target_pairs={{0,24},{2,26},{4,28},{6,30},{8,16},{10,18},{12,20},{14,22},{16,8},... | collective-permute-start | bytes 1179656 | tf_op jit(solution)/shard_map/grad_w_far/ppermute | solution.py:440
  109.3 1.8 %collective-permute-start.22 = (bf16[2,192,256]{2,1,0:T(8,128)(2,1)S(1)}, bf16[2,192,256]{2,1,0:T(8,128)(2,1)S(1)}, u32[]{:S(2)}, u32[]{:S(2)}) collective-permute-start(bf16[2,192,256]{2,1,0:T(8,128)(2,1)S(1)} %slice.81), channel_id=1, source_target_pairs={{0,2},{2,0},{4,6},{6,4},{8,10},{10,8},{12,14},{14,12},{16,18},{18,... | collective-permute-start | bytes 589832 | tf_op jit(solution)/shard_map/products_core/ppermute | solution.py:440
  109.5 11.4 %collective-permute-start.24 = (bf16[4,192,256]{2,1,0:T(8,128)(2,1)S(1)}, bf16[4,192,256]{2,1,0:T(8,128)(2,1)S(1)}, u32[]{:S(2)}, u32[]{:S(2)}) collective-permute-start(bf16[4,192,256]{2,1,0:T(8,128)(2,1)S(1)} %get-tuple-element.148), channel_id=1, source_target_pairs={{0,1},{1,0},{2,3},{3,2},{4,5},{5,4},{6,7},{7,6},{8,9},{9,8},{10,11... | collective-permute-start | bytes 1179656 | tf_op jit(solution)/shard_map/products_seq/ppermute | solution.py:445
  111.1 6.9 %collective-permute-start.23 = (bf16[2,192,256]{2,1,0:T(8,128)(2,1)S(1)}, bf16[2,192,256]{2,1,0:T(8,128)(2,1)S(1)}, u32[]{:S(2)}, u32[]{:S(2)}) collective-permute-start(bf16[2,192,256]{2,1,0:T(8,128)(2,1)S(1)} %pad_maximum_fusion.10), channel_id=1, source_target_pairs={{0,4},{2,6},{4,0},{6,2},{8,12},{10,14},{12,8},{14,10},{16,20},{18,... | collective-permute-start | bytes 589832 | tf_op jit(solution)/shard_map/products_group/ppermute | solution.py:440
  112.2 16.9 %copy-start.1 = (f32[2,12,256,128]{3,2,1,0:T(8,128)S(1)}, f32[2,12,256,128]{3,2,1,0:T(8,128)}, u32[]{:S(2)}) copy-start(f32[2,12,256,128]{3,2,1,0:T(8,128)} %get-tuple-element.93.hat_ref) | copy-start | bytes 9437188
  112.2 16.9 %copy-start.2 = (f32[2,12,256,128]{3,2,1,0:T(8,128)S(1)}, f32[2,12,256,128]{3,2,1,0:T(8,128)}, u32[]{:S(2)}) copy-start(f32[2,12,256,128]{3,2,1,0:T(8,128)} %get-tuple-element.94.inv_ref) | copy-start | bytes 9437188
  112.2 16.9 %copy-start.3 = (bf16[2,12,256,128]{3,2,1,0:T(8,128)(2,1)S(1)}, bf16[2,12,256,128]{3,2,1,0:T(8,128)(2,1)}, u32[]{:S(2)}) copy-start(bf16[2,12,256,128]{3,2,1,0:T(8,128)(2,1)} %get-tuple-element.95.low_ref) | copy-start | bytes 4718596
  120.9 8.3 %copy-start = (f32[12,256,256]{2,1,0:T(8,128)S(1)}, f32[12,256,256]{2,1,0:T(8,128)}, u32[]{:S(2)}) copy-start(f32[12,256,256]{2,1,0:T(8,128)} %get-tuple-element.92.p_ref) | copy-start | bytes 9437188
  121.0 8.2 %copy-start.4 = (bf16[12,256,128]{2,1,0:T(8,128)(2,1)S(1)}, bf16[12,256,128]{2,1,0:T(8,128)(2,1)}, u32[]{:S(2)}) copy-start(bf16[12,256,128]{2,1,0:T(8,128)(2,1)} %get-tuple-element.97.v_ref) | copy-start | bytes 2359300
  121.0 4.0 %collective-permute-start.25 = (bf16[2,192,256]{2,1,0:T(8,128)(2,1)S(1)}, bf16[2,192,256]{2,1,0:T(8,128)(2,1)S(1)}, u32[]{:S(2)}, u32[]{:S(2)}) collective-permute-start(bf16[2,192,256]{2,1,0:T(8,128)(2,1)S(1)} %slice.86), channel_id=1, source_target_pairs={{0,2},{2,0},{4,6},{6,4},{8,10},{10,8},{12,14},{14,12},{16,18},{18,... | collective-permute-start | bytes 589832 | tf_op jit(solution)/shard_map/products_core/ppermute | solution.py:440
  121.1 12.5 %collective-permute-start.28 = (bf16[192,512]{1,0:T(8,128)(2,1)S(1)}, bf16[192,512]{1,0:T(8,128)(2,1)S(1)}, u32[]{:S(2)}, u32[]{:S(2)}) collective-permute-start(bf16[192,512]{1,0:T(8,128)(2,1)S(1)} %get-tuple-element.176), channel_id=1, source_target_pairs={{0,24},{2,26},{4,28},{6,30},{8,16},{10,18},{12,20},{14,22},{16,8},... | collective-permute-start | bytes 589832 | tf_op jit(solution)/shard_map/grad_w_far/ppermute | solution.py:440
  123.1 11.8 %collective-permute-start.29 = (bf16[192,512]{1,0:T(8,128)(2,1)S(1)}, bf16[192,512]{1,0:T(8,128)(2,1)S(1)}, u32[]{:S(2)}, u32[]{:S(2)}) collective-permute-start(bf16[192,512]{1,0:T(8,128)(2,1)S(1)} %get-tuple-element.177), channel_id=1, source_target_pairs={{0,24},{2,26},{4,28},{6,30},{8,16},{10,18},{12,20},{14,22},{16,8},... | collective-permute-start | bytes 589832 | tf_op jit(solution)/shard_map/grad_w_far/ppermute | solution.py:440
  125.1 14.1 %collective-permute-start.27 = (bf16[2,192,256]{2,1,0:T(8,128)(2,1)S(1)}, bf16[2,192,256]{2,1,0:T(8,128)(2,1)S(1)}, u32[]{:S(2)}, u32[]{:S(2)}) collective-permute-start(bf16[2,192,256]{2,1,0:T(8,128)(2,1)S(1)} %pad_maximum_fusion.12), channel_id=1, source_target_pairs={{0,12},{2,14},{4,8},{6,10},{8,4},{10,6},{12,0},{14,2},{16,28},{18,... | collective-permute-start | bytes 589832 | tf_op jit(solution)/shard_map/products_group/ppermute | solution.py:440
  129.0 13.9 %collective-permute-start.26 = (bf16[2,192,256]{2,1,0:T(8,128)(2,1)S(1)}, bf16[2,192,256]{2,1,0:T(8,128)(2,1)S(1)}, u32[]{:S(2)}, u32[]{:S(2)}) collective-permute-start(bf16[2,192,256]{2,1,0:T(8,128)(2,1)S(1)} %pad_maximum_fusion.11), channel_id=1, source_target_pairs={{0,8},{2,10},{4,12},{6,14},{8,0},{10,2},{12,4},{14,6},{16,24},{18,... | collective-permute-start | bytes 589832 | tf_op jit(solution)/shard_map/products_group/ppermute | solution.py:440

commit v6 on v5

--- a/solution.py
+++ b/solution.py
@@ -491,7 +491,7 @@
     other, g6a = barrier((other, g6a))
     g7a = move(g6a, CORE, "gy_core")
     blocks_a = [gy, g1, g2, g3, g4, g5, g6a, g7a]
-    *sent, kept_a = weight_terms(place, own, other, (blocks_a, (0,) * 8), (cut // 2, cut // 2), 1000)
+    *sent, kept_a = weight_terms(place, own, other, (blocks_a, (0,) * 8), (cut // 2,), 1000)
     own, other, g6a, g7a, g3, g5, g4b, w_far, sent, kept_a = barrier(
         (own, other, g6a, g7a, g3, g5, g4b, w_far, sent, kept_a)
     )
@@ -503,9 +503,11 @@
         place, *weights, [(near, (start,) * 4, start, depth) for start, depth in ((0, cut), (cut, width - cut))]
     )
     came0 = swap(send0, "products_seq")
-    g6b, far, sent, keep0, came0 = barrier((g6b, far, sent, keep0, came0))
+    own_c, keep0 = barrier((own, keep0))
+    *sent, kept_c = weight_terms(place, own_c, other, (blocks_a, (cut // 2,) * 8), (cut // 2,), 1000)
+    g6b, far, sent, kept_c, keep0, came0 = barrier((g6b, far, sent, kept_c, keep0, came0))
     g7b = move(g6b, CORE, "gy_core")
-    far.append(move(sent[1], FAR, "grad_w_far"))
+    far.append(move(sent[0], FAR, "grad_w_far"))
     keep1, send1 = gradient_products(
         place,
         *weights,
@@ -528,7 +530,7 @@
     grads = attention_backward(place, 0, 2, saved, jnp.stack(near), qg, kg)
     grads = attention_backward(place, 2, 2, saved, jnp.stack(next_plane), qg, kg, tuple(grads))
 
-    grad_w = finish((kept_a, kept_b), far, tokens ** (-0.5))
+    grad_w = finish((kept_a, kept_c, kept_b), far, tokens ** (-0.5))
     return (*(g.transpose(1, 0, 2) for g in grads), grad_w)
 
 

time: 148 us -> 146 us (0.986)
  waiting for transfers between devices: 64.1 us -> 61.6 us
    ppermute x24, waiting for transfers between devices: 32.2 us -> 29.7 us  [move(): return lax.ppermute(a, 'fsdp', perm)]
    pallas_call x2 -> x3, Pallas kernels: 6.3 us -> 7 us  [weight_terms(): pl.pallas_call(functools.partial(weight_kernel, n, half[1], parts), in_sp...]
  transfers between devices with their start and end apart: 30 -> 30, of which waited for: 16 -> 16; matrix products, arithmetic and copies ran while one was open for 1% -> 1% of each run, Pallas kernels for 21% -> 23%
where the time goes in v6:
time: 146 us
  waiting for transfers between devices  61.6 us (42%)
  Pallas kernels  40.7 us (28%)
  starting transfers between devices  38.3 us (26%)
  local copies, waits for them, and re-layouts  2.51 us (2%)
  other arithmetic  1.61 us (1%)
    ppermute x6, waiting for transfers between devices, swap(): return lax.ppermute(a, 'seq', [(0, 1), (1, 0)])  31.9 us
    ppermute x24, starting transfers between devices, move(): return lax.ppermute(a, 'fsdp', perm)  30 us
    ppermute x24, waiting for transfers between devices, move(): return lax.ppermute(a, 'fsdp', perm)  29.7 us
    pallas_call x2, Pallas kernels, attention_backward(): pl.pallas_call(functools.partial(backward_kernel, per, dim, len(into)), g...  8.87 us
    pallas_call x1, Pallas kernels, attention_probabilities(): pl.pallas_call(functools.partial(probabilities_kernel, per, dim), grid_sp...  8.48 us
    ppermute x6, starting transfers between devices, swap(): return lax.ppermute(a, 'seq', [(0, 1), (1, 0)])  8.3 us
    pallas_call x3, Pallas kernels, weight_terms(): pl.pallas_call(functools.partial(weight_kernel, n, half[1], parts), in_sp...  7 us
    pallas_call x2, Pallas kernels, gradient_products(): pl.pallas_call(functools.partial(products_kernel, n, [(first, wide, start...  6.47 us
  transfers between devices with their start and end apart: 30, of which 16 were waited for; matrix products, arithmetic and copies ran while one was open for 1% of the time, Pallas kernels for 23%

profile of v6, /device:TPU:0, one launch (start us, length us, event | category | flops | bytes accessed | tf_op | source)
XLA Modules:
  0.0 145.7 jit_solution(10908668383012771714)
XLA Ops:
  0.6 1.2 dynamic-slice_bitcast_fusion
  1.9 0.9 pad_maximum_fusion
  2.9 3.0 %collective-permute-start.4 = (bf16[256,3072]{1,0:T(8,128)(2,1)}, bf16[256,3072]{1,0:T(8,128)(2,1)S(1)}, u32[]{:S(2)}, u32[]{:S(2)}) collective-permute-start(bf16[256,3072]{1,0:T(8,128)(2,1)} %refs_0_), channel_id=1, source_target_pairs={{0,8},{2,10},{4,12},{6,14},{8,0},{10,2},{12,4},{14,6},{16,24},{18,... | collective-permute-start | bytes 4718600 | tf_op jit(solution)/shard_map/gy_plane/ppermute | solution.py:440
  5.9 1.5 %collective-permute-start.3 = (bf16[256,3072]{1,0:T(8,128)(2,1)}, bf16[256,3072]{1,0:T(8,128)(2,1)S(1)}, u32[]{:S(2)}, u32[]{:S(2)}) collective-permute-start(bf16[256,3072]{1,0:T(8,128)(2,1)} %refs_0_), channel_id=1, source_target_pairs={{0,4},{2,6},{4,0},{6,2},{8,12},{10,14},{12,8},{14,10},{16,20},{18,... | collective-permute-start | bytes 4718600 | tf_op jit(solution)/shard_map/gy_cross/ppermute | solution.py:440
  7.4 1.5 %collective-permute-start = (bf16[2,128,1536]{2,1,0:T(8,128)(2,1)}, bf16[2,128,1536]{2,1,0:T(8,128)(2,1)}, u32[]{:S(2)}, u32[]{:S(2)}) collective-permute-start(bf16[2,128,1536]{2,1,0:T(8,128)(2,1)} %pad_maximum_fusion), channel_id=1, source_target_pairs={{0,1},{1,0},{2,3},{3,2},{4,5},{5,4},{6,7},{7,6},{8,9},{9,8},{10,11... | collective-permute-start | bytes 2359304 | tf_op jit(solution)/shard_map/qk_seq/ppermute | solution.py:445
  8.9 1.7 %collective-permute-start.5 = (bf16[192,3072]{1,0:T(8,128)(2,1)}, bf16[192,3072]{1,0:T(8,128)(2,1)}, u32[]{:S(2)}, u32[]{:S(2)}) collective-permute-start(bf16[192,3072]{1,0:T(8,128)(2,1)} %refs_1_.1), channel_id=1, source_target_pairs={{8,16},{10,18},{12,20},{14,22},{16,8},{18,10},{20,12},{22,14},{9,1... | collective-permute-start | bytes 3538952 | tf_op jit(solution)/shard_map/w_middle/ppermute | solution.py:440
  10.6 0.8 constant_dynamic-slice_fusion
  11.4 0.5 collective-permute-start.1
  11.9 0.1 copy.15.col_ref
  12.0 0.1 pad_add_fusion.place
  12.1 16.1 %collective-permute-done.came_ref = bf16[2,128,1536]{2,1,0:T(8,128)(2,1)} collective-permute-done((bf16[2,128,1536]{2,1,0:T(8,128)(2,1)}, bf16[2,128,1536]{2,1,0:T(8,128)(2,1)}, u32[]{:S(2)}, u32[]{:S(2)}) %collective-permute-start) | collective-permute-done | bytes 786464 | tf_op jit(solution)/shard_map/qk_seq/ppermute | solution.py:445
  28.2 8.5 %attention_probabilities.1 = (f32[12,256,256]{2,1,0:T(8,128)}, f32[2,12,256,128]{3,2,1,0:T(8,128)}, f32[2,12,256,128]{3,2,1,0:T(8,128)}, bf16[2,12,256,128]{3,2,1,0:T(8,128)(2,1)}, bf16[12,256,256]{2,1,0:T(8,128)(2,1)S(1)}) custom-call(s32[4]{0:T(128)S(1)} %pad_add_fusion.place, bf16[128,3072]{1,0:T(8,128)(2,1)} %q_ref.1, bf16[128,3072]{1,0:T(8,128)(2,1)} %k_ref.1, ...), custom_call_target="tpu_custom_call" | custom-call | flops 1000 | bytes 1000 | tf_op jit(solution)/shard_map/attention_probabilities/pallas_call | solution.py:219
  36.7 3.9 %attention_attended.1 = (bf16[4,192,256]{2,1,0:T(8,128)(2,1)S(1)}, bf16[4,192,256]{2,1,0:T(8,128)(2,1)S(1)}, bf16[12,256,128]{2,1,0:T(8,128)(2,1)}) custom-call(s32[4]{0:T(128)S(1)} %pad_add_fusion.place, bf16[12,256,256]{2,1,0:T(8,128)(2,1)S(1)} %get-tuple-element.99.p_low_ref, bf16[128,3072]{1,0:T(8,128)(2,1)} %v_ref.1, ...), custom_call_target="tpu_custom_call" | custom-call | flops 1000 | bytes 1000 | tf_op jit(solution)/shard_map/attention_attended/pallas_call | solution.py:242
  40.6 1.7 %collective-permute-done.2 = bf16[4,192,256]{2,1,0:T(8,128)(2,1)S(1)} collective-permute-done((bf16[4,192,256]{2,1,0:T(8,128)(2,1)S(1)}, bf16[4,192,256]{2,1,0:T(8,128)(2,1)S(1)}, u32[]{:S(2)}, u32[]{:S(2)}) %collective-permute-start.2) | collective-permute-done | bytes 393248 | tf_op jit(solution)/shard_map/att_core/ppermute | solution.py:440
  42.4 0.1 collective-permute-start.10
  42.6 1.0 collective-permute-start.6
  43.7 0.5 collective-permute-start.7
  44.2 1.6 %collective-permute-start.9 = (bf16[2,192,256]{2,1,0:T(8,128)(2,1)S(1)}, bf16[2,192,256]{2,1,0:T(8,128)(2,1)S(1)}, u32[]{:S(2)}, u32[]{:S(2)}) collective-permute-start(bf16[2,192,256]{2,1,0:T(8,128)(2,1)S(1)} %pad_maximum_fusion.5), channel_id=1, source_target_pairs={{0,1},{1,0},{2,3},{3,2},{4,5},{5,4},{6,7},{7,6},{8,9},{9,8},{10,11... | collective-permute-start | bytes 589832 | tf_op jit(solution)/shard_map/att_seq/ppermute | solution.py:445
  45.8 2.2 %collective-permute-start.8 = (bf16[2,192,256]{2,1,0:T(8,128)(2,1)S(1)}, bf16[2,192,256]{2,1,0:T(8,128)(2,1)S(1)}, u32[]{:S(2)}, u32[]{:S(2)}) collective-permute-start(bf16[2,192,256]{2,1,0:T(8,128)(2,1)S(1)} %pad_maximum_fusion.8), channel_id=1, source_target_pairs={{0,12},{2,14},{4,8},{6,10},{8,4},{10,6},{12,0},{14,2},{16,28},{18,... | collective-permute-start | bytes 589832 | tf_op jit(solution)/shard_map/att_group/ppermute | solution.py:440
  48.0 1.9 %collective-permute-done.6 = bf16[2,192,256]{2,1,0:T(8,128)(2,1)S(1)} collective-permute-done((bf16[2,192,256]{2,1,0:T(8,128)(2,1)S(1)}, bf16[2,192,256]{2,1,0:T(8,128)(2,1)S(1)}, u32[]{:S(2)}, u32[]{:S(2)}) %collective-permute-start.6) | collective-permute-done | bytes 196640 | tf_op jit(solution)/shard_map/att_group/ppermute | solution.py:440
  49.8 4.6 %collective-permute-start.16 = (bf16[192,3072]{1,0:T(8,128)(2,1)}, bf16[192,3072]{1,0:T(8,128)(2,1)S(1)}, u32[]{:S(2)}, u32[]{:S(2)}) collective-permute-start(bf16[192,3072]{1,0:T(8,128)(2,1)} %refs_1_.1), channel_id=1, source_target_pairs={{0,24},{2,26},{4,28},{6,30},{24,0},{26,2},{28,4},{30,6},{1,25},{3,... | collective-permute-start | bytes 3538952 | tf_op jit(solution)/shard_map/w_ends/ppermute | solution.py:440
  54.4 0.1 slice.68
  54.6 0.8 collective-permute-done.8
  55.3 1.1 collective-permute-start.12
  56.4 0.1 pad_maximum_fusion.2
  56.5 1.6 %collective-permute-start.11 = (bf16[6,192,256]{2,1,0:T(8,128)(2,1)S(1)}, bf16[6,192,256]{2,1,0:T(8,128)(2,1)S(1)}, u32[]{:S(2)}, u32[]{:S(2)}) collective-permute-start(bf16[6,192,256]{2,1,0:T(8,128)(2,1)S(1)} %pad_maximum_fusion.2), channel_id=1, source_target_pairs={{0,1},{1,0},{2,3},{3,2},{4,5},{5,4},{6,7},{7,6},{8,9},{9,8},{10,11... | collective-permute-start | bytes 1769480 | tf_op jit(solution)/shard_map/att_seq/ppermute | solution.py:445
  58.1 0.5 collective-permute-start.15
  58.6 2.5 %hold.1 = (bf16[256,3072]{1,0:T(8,128)(2,1)S(1)}, bf16[192,3072]{1,0:T(8,128)(2,1)S(1)}) custom-call(bf16[256,3072]{1,0:T(8,128)(2,1)} %refs_0_, bf16[192,3072]{1,0:T(8,128)(2,1)} %refs_1_.1), custom_call_target="tpu_custom_call" | custom-call | flops 1000 | bytes 1000 | tf_op jit(solution)/shard_map/hold/pallas_call | solution.py:300
  61.1 9.8 %collective-permute-done.11 = bf16[6,192,256]{2,1,0:T(8,128)(2,1)S(1)} collective-permute-done((bf16[6,192,256]{2,1,0:T(8,128)(2,1)S(1)}, bf16[6,192,256]{2,1,0:T(8,128)(2,1)S(1)}, u32[]{:S(2)}, u32[]{:S(2)}) %collective-permute-start.11) | collective-permute-done | bytes 589856 | tf_op jit(solution)/shard_map/att_seq/ppermute | solution.py:445
  70.9 0.1 pad_maximum_fusion.1.other_ref
  71.0 8.6 %collective-permute-done.12.refs_6_.refs_1_ = bf16[256,2048]{1,0:T(8,128)(2,1)S(1)} collective-permute-done((bf16[256,2048]{1,0:T(8,128)(2,1)S(1)}, bf16[256,2048]{1,0:T(8,128)(2,1)S(1)}, u32[]{:S(2)}, u32[]{:S(2)}) %collective-permute-start.12) | collective-permute-done | bytes 1048608 | tf_op jit(solution)/shard_map/gy_plane_cross_a/ppermute | solution.py:440
  79.6 2.6 %collective-permute-done.16.end_ref = bf16[192,3072]{1,0:T(8,128)(2,1)S(1)} collective-permute-done((bf16[192,3072]{1,0:T(8,128)(2,1)}, bf16[192,3072]{1,0:T(8,128)(2,1)S(1)}, u32[]{:S(2)}, u32[]{:S(2)}) %collective-permute-start.16) | collective-permute-done | bytes 1179680 | tf_op jit(solution)/shard_map/w_ends/ppermute | solution.py:440
  82.3 1.4 choose.1.far_ref
  83.8 2.3 %weight_terms.3 = (bf16[192,1024]{1,0:T(8,128)(2,1)S(1)}, f32[192,1024]{1,0:T(8,128)S(1)}) custom-call(s32[4]{0:T(128)S(1)} %pad_add_fusion.place, bf16[8,192,256]{2,1,0:T(8,128)(2,1)S(1)} %constant_dynamic-update-slice_fusion.own_ref, bf16[8,192,256]{2,1,0:T(8,128)(2,1)S(1)} %pad_maximum_fusion.1.other_ref, ...), custom_call_target="tpu_custom_call" | custom-call | flops 1000 | bytes 1000 | tf_op jit(solution)/shard_map/weight_terms/pallas_call | solution.py:383
  86.1 1.0 collective-permute-start.17
  87.1 1.7 %collective-permute-start.18 = (bf16[192,1024]{1,0:T(8,128)(2,1)S(1)}, bf16[192,1024]{1,0:T(8,128)(2,1)S(1)}, u32[]{:S(2)}, u32[]{:S(2)}) collective-permute-start(bf16[192,1024]{1,0:T(8,128)(2,1)S(1)} %get-tuple-element.132), channel_id=1, source_target_pairs={{0,24},{2,26},{4,28},{6,30},{8,16},{10,18},{12,20},{14,22},{16,8},... | collective-permute-start | bytes 1179656 | tf_op jit(solution)/shard_map/grad_w_far/ppermute | solution.py:440
  88.9 3.2 %gradient_products.2 = (bf16[4,192,256]{2,1,0:T(8,128)(2,1)S(1)}, bf16[4,192,256]{2,1,0:T(8,128)(2,1)S(1)}) custom-call(s32[4]{0:T(128)S(1)} %pad_add_fusion.place, bf16[192,3072]{1,0:T(8,128)(2,1)S(1)} %get-tuple-element.134.w_ref, bf16[192,3072]{1,0:T(8,128)(2,1)S(1)} %choose.1.far_ref, bf16[256,3072]{1,0:T(8,128)(2,1)S(1)} %get-tuple-element.156.refs_0_.refs_4_, ...), custom_call_target="tpu_custom_call" | custom-call | flops 1000 | bytes 1000 | tf_op jit(solution)/shard_map/gradient_products/pallas_call | solution.py:351
  92.1 1.6 %collective-permute-start.19 = (bf16[4,192,256]{2,1,0:T(8,128)(2,1)S(1)}, bf16[4,192,256]{2,1,0:T(8,128)(2,1)S(1)}, u32[]{:S(2)}, u32[]{:S(2)}) collective-permute-start(bf16[4,192,256]{2,1,0:T(8,128)(2,1)S(1)} %get-tuple-element.143), channel_id=1, source_target_pairs={{0,1},{1,0},{2,3},{3,2},{4,5},{5,4},{6,7},{7,6},{8,9},{9,8},{10,11... | collective-permute-start | bytes 1179656 | tf_op jit(solution)/shard_map/products_seq/ppermute | solution.py:445
  93.7 2.3 %weight_terms.4 = (bf16[192,1024]{1,0:T(8,128)(2,1)S(1)}, f32[192,1024]{1,0:T(8,128)S(1)}) custom-call(s32[4]{0:T(128)S(1)} %pad_add_fusion.place, bf16[8,192,256]{2,1,0:T(8,128)(2,1)S(1)} %constant_dynamic-update-slice_fusion.own_ref, bf16[8,192,256]{2,1,0:T(8,128)(2,1)S(1)} %pad_maximum_fusion.1.other_ref, ...), custom_call_target="tpu_custom_call" | custom-call | flops 1000 | bytes 1000 | tf_op jit(solution)/shard_map/weight_terms/pallas_call | solution.py:383
  96.0 3.2 %collective-permute-done.18.refs_3_ = bf16[192,1024]{1,0:T(8,128)(2,1)S(1)} collective-permute-done((bf16[192,1024]{1,0:T(8,128)(2,1)S(1)}, bf16[192,1024]{1,0:T(8,128)(2,1)S(1)}, u32[]{:S(2)}, u32[]{:S(2)}) %collective-permute-start.18) | collective-permute-done | bytes 393248 | tf_op jit(solution)/shard_map/grad_w_far/ppermute | solution.py:440
  99.2 3.2 %collective-permute-done.19 = bf16[4,192,256]{2,1,0:T(8,128)(2,1)S(1)} collective-permute-done((bf16[4,192,256]{2,1,0:T(8,128)(2,1)S(1)}, bf16[4,192,256]{2,1,0:T(8,128)(2,1)S(1)}, u32[]{:S(2)}, u32[]{:S(2)}) %collective-permute-start.19) | collective-permute-done | bytes 393248 | tf_op jit(solution)/shard_map/products_seq/ppermute | solution.py:445
  102.4 1.8 %collective-permute-start.20 = (bf16[192,1024]{1,0:T(8,128)(2,1)S(1)}, bf16[192,1024]{1,0:T(8,128)(2,1)S(1)}, u32[]{:S(2)}, u32[]{:S(2)}) collective-permute-start(bf16[192,1024]{1,0:T(8,128)(2,1)S(1)} %get-tuple-element.145), channel_id=1, source_target_pairs={{0,24},{2,26},{4,28},{6,30},{8,16},{10,18},{12,20},{14,22},{16,8},... | collective-permute-start | bytes 1179656 | tf_op jit(solution)/shard_map/grad_w_far/ppermute | solution.py:440
  104.2 0.1 collective-permute-done.21.refs_7_
  104.3 3.2 %gradient_products.3 = (bf16[4,192,256]{2,1,0:T(8,128)(2,1)S(1)}, bf16[4,192,256]{2,1,0:T(8,128)(2,1)S(1)}) custom-call(s32[4]{0:T(128)S(1)} %pad_add_fusion.place, bf16[192,3072]{1,0:T(8,128)(2,1)S(1)} %get-tuple-element.134.w_ref, bf16[192,3072]{1,0:T(8,128)(2,1)S(1)} %choose.1.far_ref, bf16[256,3072]{1,0:T(8,128)(2,1)S(1)} %collective-permute-done.4.refs_4_.refs_0_, ...), custom_call_target="tpu_custom_call" | custom-call | flops 1000 | bytes 1000 | tf_op jit(solution)/shard_map/gradient_products/pallas_call | solution.py:351
  107.5 0.1 add_convert_fusion.1
  107.6 0.2 collective-permute-start.22
  107.8 1.5 %collective-permute-start.24 = (bf16[4,192,256]{2,1,0:T(8,128)(2,1)S(1)}, bf16[4,192,256]{2,1,0:T(8,128)(2,1)S(1)}, u32[]{:S(2)}, u32[]{:S(2)}) collective-permute-start(bf16[4,192,256]{2,1,0:T(8,128)(2,1)S(1)} %get-tuple-element.155), channel_id=1, source_target_pairs={{0,1},{1,0},{2,3},{3,2},{4,5},{5,4},{6,7},{7,6},{8,9},{9,8},{10,11... | collective-permute-start | bytes 1179656 | tf_op jit(solution)/shard_map/products_seq/ppermute | solution.py:445
  109.4 1.1 collective-permute-start.23
  110.6 2.3 %weight_terms.5 = (bf16[192,512]{1,0:T(8,128)(2,1)S(1)}, bf16[192,512]{1,0:T(8,128)(2,1)S(1)}, f32[192,1024]{1,0:T(8,128)S(1)}) custom-call(s32[4]{0:T(128)S(1)} %pad_add_fusion.place, bf16[8,192,256]{2,1,0:T(8,128)(2,1)S(1)} %constant_dynamic-update-slice_fusion.own_ref, bf16[8,192,256]{2,1,0:T(8,128)(2,1)S(1)} %pad_maximum_fusion.1.other_ref, ...), custom_call_target="tpu_custom_call" | custom-call | flops 1000 | bytes 1000 | tf_op jit(solution)/shard_map/weight_terms/pallas_call | solution.py:383
  112.9 2.8 %collective-permute-done.20.refs_4_ = bf16[192,1024]{1,0:T(8,128)(2,1)S(1)} collective-permute-done((bf16[192,1024]{1,0:T(8,128)(2,1)S(1)}, bf16[192,1024]{1,0:T(8,128)(2,1)S(1)}, u32[]{:S(2)}, u32[]{:S(2)}) %collective-permute-start.20) | collective-permute-done | bytes 393248 | tf_op jit(solution)/shard_map/grad_w_far/ppermute | solution.py:440
  115.8 0.6 collective-permute-done.23
  116.4 2.8 %collective-permute-done.24 = bf16[4,192,256]{2,1,0:T(8,128)(2,1)S(1)} collective-permute-done((bf16[4,192,256]{2,1,0:T(8,128)(2,1)S(1)}, bf16[4,192,256]{2,1,0:T(8,128)(2,1)S(1)}, u32[]{:S(2)}, u32[]{:S(2)}) %collective-permute-start.24) | collective-permute-done | bytes 393248 | tf_op jit(solution)/shard_map/products_seq/ppermute | solution.py:445
  119.2 0.1 add_convert_fusion
  119.4 0.1 collective-permute-start.25
  119.5 2.0 %collective-permute-start.28 = (bf16[192,512]{1,0:T(8,128)(2,1)S(1)}, bf16[192,512]{1,0:T(8,128)(2,1)S(1)}, u32[]{:S(2)}, u32[]{:S(2)}) collective-permute-start(bf16[192,512]{1,0:T(8,128)(2,1)S(1)} %get-tuple-element.182), channel_id=1, source_target_pairs={{0,24},{2,26},{4,28},{6,30},{8,16},{10,18},{12,20},{14,22},{16,8},... | collective-permute-start | bytes 589832 | tf_op jit(solution)/shard_map/grad_w_far/ppermute | solution.py:440
  121.4 1.9 %collective-permute-start.29 = (bf16[192,512]{1,0:T(8,128)(2,1)S(1)}, bf16[192,512]{1,0:T(8,128)(2,1)S(1)}, u32[]{:S(2)}, u32[]{:S(2)}) collective-permute-start(bf16[192,512]{1,0:T(8,128)(2,1)S(1)} %get-tuple-element.183), channel_id=1, source_target_pairs={{0,24},{2,26},{4,28},{6,30},{8,16},{10,18},{12,20},{14,22},{16,8},... | collective-permute-start | bytes 589832 | tf_op jit(solution)/shard_map/grad_w_far/ppermute | solution.py:440
  123.4 3.9 %collective-permute-start.27 = (bf16[2,192,256]{2,1,0:T(8,128)(2,1)S(1)}, bf16[2,192,256]{2,1,0:T(8,128)(2,1)S(1)}, u32[]{:S(2)}, u32[]{:S(2)}) collective-permute-start(bf16[2,192,256]{2,1,0:T(8,128)(2,1)S(1)} %pad_maximum_fusion.12), channel_id=1, source_target_pairs={{0,12},{2,14},{4,8},{6,10},{8,4},{10,6},{12,0},{14,2},{16,28},{18,... | collective-permute-start | bytes 589832 | tf_op jit(solution)/shard_map/products_group/ppermute | solution.py:440
  127.4 0.1 collective-permute-start.26
  127.5 4.4 %attention_backward.2 = (bf16[12,256,128]{2,1,0:T(8,128)(2,1)}, bf16[12,256,128]{2,1,0:T(8,128)(2,1)}, bf16[12,256,128]{2,1,0:T(8,128)(2,1)}) custom-call(s32[4]{0:T(128)S(1)} %pad_add_fusion.place, f32[12,256,256]{2,1,0:T(8,128)S(1)} %copy-done, f32[2,12,256,128]{3,2,1,0:T(8,128)S(1)} %copy-done.1, f32[2,12,256,128]{3,2,1,0:T(8,128)S(1)} %copy-done.2, ...), custom_call_target="tpu_custom_call" | custom-call | flops 1000 | bytes 1000 | tf_op jit(solution)/shard_map/attention_backward/pallas_call | solution.py:268
  132.0 1.3 collective-permute-done.29.refs_6_
  133.3 2.0 %finish.1 = f32[192,3072]{1,0:T(8,128)} custom-call(f32[192,1024]{1,0:T(8,128)S(1)} %get-tuple-element.177.refs_0_, f32[192,1024]{1,0:T(8,128)S(1)} %get-tuple-element.178.refs_1_, f32[192,1024]{1,0:T(8,128)S(1)} %get-tuple-element.179.refs_2_, bf16[192,1024]{1,0:T(8,128)(2,1)S(1)} %collective-permute-done.18.refs_3_, ...), custom_call_target="tpu_custom_call" | custom-call | flops 1000 | bytes 1000 | tf_op jit(solution)/shard_map/finish/pallas_call | solution.py:416
  135.3 2.3 %collective-permute-done.27 = bf16[2,192,256]{2,1,0:T(8,128)(2,1)S(1)} collective-permute-done((bf16[2,192,256]{2,1,0:T(8,128)(2,1)S(1)}, bf16[2,192,256]{2,1,0:T(8,128)(2,1)S(1)}, u32[]{:S(2)}, u32[]{:S(2)}) %collective-permute-start.27) | collective-permute-done | bytes 196640 | tf_op jit(solution)/shard_map/products_group/ppermute | solution.py:440
  137.5 3.7 %collective-permute-done.26 = bf16[2,192,256]{2,1,0:T(8,128)(2,1)S(1)} collective-permute-done((bf16[2,192,256]{2,1,0:T(8,128)(2,1)S(1)}, bf16[2,192,256]{2,1,0:T(8,128)(2,1)S(1)}, u32[]{:S(2)}, u32[]{:S(2)}) %collective-permute-start.26) | collective-permute-done | bytes 196640 | tf_op jit(solution)/shard_map/products_group/ppermute | solution.py:440
  141.3 4.4 %attention_backward.3 = (bf16[12,256,128]{2,1,0:T(8,128)(2,1)}, bf16[12,256,128]{2,1,0:T(8,128)(2,1)}, bf16[12,256,128]{2,1,0:T(8,128)(2,1)}) custom-call(s32[4]{0:T(128)S(1)} %pad_add_fusion.place, f32[12,256,256]{2,1,0:T(8,128)S(1)} %copy-done, f32[2,12,256,128]{3,2,1,0:T(8,128)S(1)} %copy-done.1, ...), custom_call_target="tpu_custom_call", output_to_operand_aliasing={{0}: (9, {}), {1}: (10, {}), {2}: (11, {})} | custom-call | flops 1000 | bytes 1000 | tf_op jit(solution)/shard_map/attention_backward/pallas_call | solution.py:268
  (59 shorter events, 0.6 us)
Async XLA Ops:
  0.6 10.0 %copy-start.8 = (bf16[128,3072]{1,0:T(8,128)(2,1)S(1)}, bf16[128,3072]{1,0:T(8,128)(2,1)}, u32[]{:S(2)}) copy-start(bf16[128,3072]{1,0:T(8,128)(2,1)} %v_ref.1) | copy-start | bytes 2359300
  1.9 10.0 %copy-start.7 = (s32[1,256]{1,0:T(1,128)S(1)}, s32[1,256]{1,0:T(1,128)}, u32[]{:S(2)}) copy-start(s32[1,256]{1,0:T(1,128)} %row_ref.1) | copy-start | bytes 3076
  1.9 26.3 %copy-start.5 = (f32[128]{0:T(128)S(1)}, f32[128]{0:T(128)}, u32[]{:S(2)}) copy-start(f32[128]{0:T(128)} %param.12) | copy-start | bytes 1540
  1.9 26.3 %copy-start.6 = (f32[128]{0:T(128)S(1)}, f32[128]{0:T(128)}, u32[]{:S(2)}) copy-start(f32[128]{0:T(128)} %param.13) | copy-start | bytes 1540
  2.9 39.5 %collective-permute-start.4 = (bf16[256,3072]{1,0:T(8,128)(2,1)}, bf16[256,3072]{1,0:T(8,128)(2,1)S(1)}, u32[]{:S(2)}, u32[]{:S(2)}) collective-permute-start(bf16[256,3072]{1,0:T(8,128)(2,1)} %refs_0_), channel_id=1, source_target_pairs={{0,8},{2,10},{4,12},{6,14},{8,0},{10,2},{12,4},{14,6},{16,24},{18,... | collective-permute-start | bytes 4718600 | tf_op jit(solution)/shard_map/gy_plane/ppermute | solution.py:440
  5.9 36.5 %collective-permute-start.3 = (bf16[256,3072]{1,0:T(8,128)(2,1)}, bf16[256,3072]{1,0:T(8,128)(2,1)S(1)}, u32[]{:S(2)}, u32[]{:S(2)}) collective-permute-start(bf16[256,3072]{1,0:T(8,128)(2,1)} %refs_0_), channel_id=1, source_target_pairs={{0,4},{2,6},{4,0},{6,2},{8,12},{10,14},{12,8},{14,10},{16,20},{18,... | collective-permute-start | bytes 4718600 | tf_op jit(solution)/shard_map/gy_cross/ppermute | solution.py:440
  7.4 20.8 %collective-permute-start = (bf16[2,128,1536]{2,1,0:T(8,128)(2,1)}, bf16[2,128,1536]{2,1,0:T(8,128)(2,1)}, u32[]{:S(2)}, u32[]{:S(2)}) collective-permute-start(bf16[2,128,1536]{2,1,0:T(8,128)(2,1)} %pad_maximum_fusion), channel_id=1, source_target_pairs={{0,1},{1,0},{2,3},{3,2},{4,5},{5,4},{6,7},{7,6},{8,9},{9,8},{10,11... | collective-permute-start | bytes 2359304 | tf_op jit(solution)/shard_map/qk_seq/ppermute | solution.py:445
  8.9 31.7 %collective-permute-start.5 = (bf16[192,3072]{1,0:T(8,128)(2,1)}, bf16[192,3072]{1,0:T(8,128)(2,1)}, u32[]{:S(2)}, u32[]{:S(2)}) collective-permute-start(bf16[192,3072]{1,0:T(8,128)(2,1)} %refs_1_.1), channel_id=1, source_target_pairs={{8,16},{10,18},{12,20},{14,22},{16,8},{18,10},{20,12},{22,14},{9,1... | collective-permute-start | bytes 3538952 | tf_op jit(solution)/shard_map/w_middle/ppermute | solution.py:440
  11.4 25.3 %collective-permute-start.1 = (bf16[128,1536]{1,0:T(8,128)(2,1)}, bf16[128,1536]{1,0:T(8,128)(2,1)}, u32[]{:S(2)}, u32[]{:S(2)}) collective-permute-start(bf16[128,1536]{1,0:T(8,128)(2,1)} %constant_dynamic-slice_fusion), channel_id=1, source_target_pairs={{0,1},{1,0},{2,3},{3,2},{4,5},{5,4},{6,7},{7,6},{8,9},{9,8},{10,11... | collective-permute-start | bytes 1179656 | tf_op jit(solution)/shard_map/v_seq/ppermute | solution.py:445
  40.6 1.7 %collective-permute-start.2 = (bf16[4,192,256]{2,1,0:T(8,128)(2,1)S(1)}, bf16[4,192,256]{2,1,0:T(8,128)(2,1)S(1)}, u32[]{:S(2)}, u32[]{:S(2)}) collective-permute-start(bf16[4,192,256]{2,1,0:T(8,128)(2,1)S(1)} %get-tuple-element.102), channel_id=1, source_target_pairs={{0,2},{2,0},{4,6},{6,4},{8,10},{10,8},{12,14},{14,12},{16,18},{18,... | collective-permute-start | bytes 1179656 | tf_op jit(solution)/shard_map/att_core/ppermute | solution.py:440
  42.4 13.0 %collective-permute-start.10 = (bf16[256,3072]{1,0:T(8,128)(2,1)}, bf16[256,3072]{1,0:T(8,128)(2,1)S(1)}, u32[]{:S(2)}, u32[]{:S(2)}) collective-permute-start(bf16[256,3072]{1,0:T(8,128)(2,1)} %refs_0_), channel_id=1, source_target_pairs={{0,2},{2,0},{4,6},{6,4},{8,10},{10,8},{12,14},{14,12},{16,18},{18,... | collective-permute-start | bytes 4718600 | tf_op jit(solution)/shard_map/gy_core/ppermute | solution.py:440
  42.6 7.2 %collective-permute-start.6 = (bf16[2,192,256]{2,1,0:T(8,128)(2,1)S(1)}, bf16[2,192,256]{2,1,0:T(8,128)(2,1)S(1)}, u32[]{:S(2)}, u32[]{:S(2)}) collective-permute-start(bf16[2,192,256]{2,1,0:T(8,128)(2,1)S(1)} %pad_maximum_fusion.6), channel_id=1, source_target_pairs={{0,4},{2,6},{4,0},{6,2},{8,12},{10,14},{12,8},{14,10},{16,20},{18,... | collective-permute-start | bytes 589832 | tf_op jit(solution)/shard_map/att_group/ppermute | solution.py:440
  43.7 10.9 %collective-permute-start.7 = (bf16[2,192,256]{2,1,0:T(8,128)(2,1)S(1)}, bf16[2,192,256]{2,1,0:T(8,128)(2,1)S(1)}, u32[]{:S(2)}, u32[]{:S(2)}) collective-permute-start(bf16[2,192,256]{2,1,0:T(8,128)(2,1)S(1)} %pad_maximum_fusion.7), channel_id=1, source_target_pairs={{0,8},{2,10},{4,12},{6,14},{8,0},{10,2},{12,4},{14,6},{16,24},{18,... | collective-permute-start | bytes 589832 | tf_op jit(solution)/shard_map/att_group/ppermute | solution.py:440
  44.2 10.4 %collective-permute-start.9 = (bf16[2,192,256]{2,1,0:T(8,128)(2,1)S(1)}, bf16[2,192,256]{2,1,0:T(8,128)(2,1)S(1)}, u32[]{:S(2)}, u32[]{:S(2)}) collective-permute-start(bf16[2,192,256]{2,1,0:T(8,128)(2,1)S(1)} %pad_maximum_fusion.5), channel_id=1, source_target_pairs={{0,1},{1,0},{2,3},{3,2},{4,5},{5,4},{6,7},{7,6},{8,9},{9,8},{10,11... | collective-permute-start | bytes 589832 | tf_op jit(solution)/shard_map/att_seq/ppermute | solution.py:445
  45.8 9.5 %collective-permute-start.8 = (bf16[2,192,256]{2,1,0:T(8,128)(2,1)S(1)}, bf16[2,192,256]{2,1,0:T(8,128)(2,1)S(1)}, u32[]{:S(2)}, u32[]{:S(2)}) collective-permute-start(bf16[2,192,256]{2,1,0:T(8,128)(2,1)S(1)} %pad_maximum_fusion.8), channel_id=1, source_target_pairs={{0,12},{2,14},{4,8},{6,10},{8,4},{10,6},{12,0},{14,2},{16,28},{18,... | collective-permute-start | bytes 589832 | tf_op jit(solution)/shard_map/att_group/ppermute | solution.py:440
  49.8 32.4 %collective-permute-start.16 = (bf16[192,3072]{1,0:T(8,128)(2,1)}, bf16[192,3072]{1,0:T(8,128)(2,1)S(1)}, u32[]{:S(2)}, u32[]{:S(2)}) collective-permute-start(bf16[192,3072]{1,0:T(8,128)(2,1)} %refs_1_.1), channel_id=1, source_target_pairs={{0,24},{2,26},{4,28},{6,30},{24,0},{26,2},{28,4},{30,6},{1,25},{3,... | collective-permute-start | bytes 3538952 | tf_op jit(solution)/shard_map/w_ends/ppermute | solution.py:440
  55.3 24.3 %collective-permute-start.12 = (bf16[256,2048]{1,0:T(8,128)(2,1)S(1)}, bf16[256,2048]{1,0:T(8,128)(2,1)S(1)}, u32[]{:S(2)}, u32[]{:S(2)}) collective-permute-start(bf16[256,2048]{1,0:T(8,128)(2,1)S(1)} %slice.68), channel_id=1, source_target_pairs={{0,4},{2,6},{4,0},{6,2},{8,12},{10,14},{12,8},{14,10},{16,20},{18,... | collective-permute-start | bytes 3145736 | tf_op jit(solution)/shard_map/gy_plane_cross_a/ppermute | solution.py:440
  56.5 14.4 %collective-permute-start.11 = (bf16[6,192,256]{2,1,0:T(8,128)(2,1)S(1)}, bf16[6,192,256]{2,1,0:T(8,128)(2,1)S(1)}, u32[]{:S(2)}, u32[]{:S(2)}) collective-permute-start(bf16[6,192,256]{2,1,0:T(8,128)(2,1)S(1)} %pad_maximum_fusion.2), channel_id=1, source_target_pairs={{0,1},{1,0},{2,3},{3,2},{4,5},{5,4},{6,7},{7,6},{8,9},{9,8},{10,11... | collective-permute-start | bytes 1769480 | tf_op jit(solution)/shard_map/att_seq/ppermute | solution.py:445
  58.1 25.7 %collective-permute-start.14 = (bf16[256,3072]{1,0:T(8,128)(2,1)S(1)}, bf16[256,3072]{1,0:T(8,128)(2,1)S(1)}, u32[]{:S(2)}, u32[]{:S(2)}) collective-permute-start(bf16[256,3072]{1,0:T(8,128)(2,1)S(1)} %collective-permute-done.3.refs_2_.refs_1_.refs_5_), channel_id=1, source_target_pairs={{0,2},{2,0},{4,6},{6,4},{8,10},{10,8},{12,14},{14,12},{16,18},{18,... | collective-permute-start | bytes 4718600 | tf_op jit(solution)/shard_map/gy_core/ppermute | solution.py:440
  58.1 25.7 %collective-permute-start.15 = (bf16[256,3072]{1,0:T(8,128)(2,1)S(1)}, bf16[256,3072]{1,0:T(8,128)(2,1)S(1)}, u32[]{:S(2)}, u32[]{:S(2)}) collective-permute-start(bf16[256,3072]{1,0:T(8,128)(2,1)S(1)} %collective-permute-done.4.refs_4_.refs_0_), channel_id=1, source_target_pairs={{0,2},{2,0},{4,6},{6,4},{8,10},{10,8},{12,14},{14,12},{16,18},{18,... | collective-permute-start | bytes 4718600 | tf_op jit(solution)/shard_map/gy_core/ppermute | solution.py:440
  79.6 4.2 %collective-permute-start.13 = (bf16[256,2048]{1,0:T(8,128)(2,1)S(1)}, bf16[256,2048]{1,0:T(8,128)(2,1)S(1)}, u32[]{:S(2)}, u32[]{:S(2)}) collective-permute-start(bf16[256,2048]{1,0:T(8,128)(2,1)S(1)} %collective-permute-done.12.refs_6_.refs_1_), channel_id=1, source_target_pairs={{0,2},{2,0},{4,6},{6,4},{8,10},{10,8},{12,14},{14,12},{16,18},{18,... | collective-permute-start | bytes 3145736 | tf_op jit(solution)/shard_map/gy_core/ppermute | solution.py:440
  86.1 16.2 %collective-permute-start.17 = (bf16[256,1024]{1,0:T(8,128)(2,1)S(1)}, bf16[256,1024]{1,0:T(8,128)(2,1)S(1)}, u32[]{:S(2)}, u32[]{:S(2)}) collective-permute-start(bf16[256,1024]{1,0:T(8,128)(2,1)S(1)} %slice.69), channel_id=1, source_target_pairs={{0,4},{2,6},{4,0},{6,2},{8,12},{10,14},{12,8},{14,10},{16,20},{18,... | collective-permute-start | bytes 1572872 | tf_op jit(solution)/shard_map/gy_plane_cross_b/ppermute | solution.py:440
  87.1 12.1 %collective-permute-start.18 = (bf16[192,1024]{1,0:T(8,128)(2,1)S(1)}, bf16[192,1024]{1,0:T(8,128)(2,1)S(1)}, u32[]{:S(2)}, u32[]{:S(2)}) collective-permute-start(bf16[192,1024]{1,0:T(8,128)(2,1)S(1)} %get-tuple-element.132), channel_id=1, source_target_pairs={{0,24},{2,26},{4,28},{6,30},{8,16},{10,18},{12,20},{14,22},{16,8},... | collective-permute-start | bytes 1179656 | tf_op jit(solution)/shard_map/grad_w_far/ppermute | solution.py:440
  92.1 10.3 %collective-permute-start.19 = (bf16[4,192,256]{2,1,0:T(8,128)(2,1)S(1)}, bf16[4,192,256]{2,1,0:T(8,128)(2,1)S(1)}, u32[]{:S(2)}, u32[]{:S(2)}) collective-permute-start(bf16[4,192,256]{2,1,0:T(8,128)(2,1)S(1)} %get-tuple-element.143), channel_id=1, source_target_pairs={{0,1},{1,0},{2,3},{3,2},{4,5},{5,4},{6,7},{7,6},{8,9},{9,8},{10,11... | collective-permute-start | bytes 1179656 | tf_op jit(solution)/shard_map/products_seq/ppermute | solution.py:445
  102.4 1.9 %collective-permute-start.21 = (bf16[256,1024]{1,0:T(8,128)(2,1)S(1)}, bf16[256,1024]{1,0:T(8,128)(2,1)S(1)}, u32[]{:S(2)}, u32[]{:S(2)}) collective-permute-start(bf16[256,1024]{1,0:T(8,128)(2,1)S(1)} %collective-permute-done.17.refs_5_.refs_6_), channel_id=1, source_target_pairs={{0,2},{2,0},{4,6},{6,4},{8,10},{10,8},{12,14},{14,12},{16,18},{18,... | collective-permute-start | bytes 1572872 | tf_op jit(solution)/shard_map/gy_core/ppermute | solution.py:440
  102.4 13.4 %collective-permute-start.20 = (bf16[192,1024]{1,0:T(8,128)(2,1)S(1)}, bf16[192,1024]{1,0:T(8,128)(2,1)S(1)}, u32[]{:S(2)}, u32[]{:S(2)}) collective-permute-start(bf16[192,1024]{1,0:T(8,128)(2,1)S(1)} %get-tuple-element.145), channel_id=1, source_target_pairs={{0,24},{2,26},{4,28},{6,30},{8,16},{10,18},{12,20},{14,22},{16,8},... | collective-permute-start | bytes 1179656 | tf_op jit(solution)/shard_map/grad_w_far/ppermute | solution.py:440
  107.6 1.8 %collective-permute-start.22 = (bf16[2,192,256]{2,1,0:T(8,128)(2,1)S(1)}, bf16[2,192,256]{2,1,0:T(8,128)(2,1)S(1)}, u32[]{:S(2)}, u32[]{:S(2)}) collective-permute-start(bf16[2,192,256]{2,1,0:T(8,128)(2,1)S(1)} %slice.81), channel_id=1, source_target_pairs={{0,2},{2,0},{4,6},{6,4},{8,10},{10,8},{12,14},{14,12},{16,18},{18,... | collective-permute-start | bytes 589832 | tf_op jit(solution)/shard_map/products_core/ppermute | solution.py:440
  107.8 11.4 %collective-permute-start.24 = (bf16[4,192,256]{2,1,0:T(8,128)(2,1)S(1)}, bf16[4,192,256]{2,1,0:T(8,128)(2,1)S(1)}, u32[]{:S(2)}, u32[]{:S(2)}) collective-permute-start(bf16[4,192,256]{2,1,0:T(8,128)(2,1)S(1)} %get-tuple-element.155), channel_id=1, source_target_pairs={{0,1},{1,0},{2,3},{3,2},{4,5},{5,4},{6,7},{7,6},{8,9},{9,8},{10,11... | collective-permute-start | bytes 1179656 | tf_op jit(solution)/shard_map/products_seq/ppermute | solution.py:445
  109.4 7.0 %collective-permute-start.23 = (bf16[2,192,256]{2,1,0:T(8,128)(2,1)S(1)}, bf16[2,192,256]{2,1,0:T(8,128)(2,1)S(1)}, u32[]{:S(2)}, u32[]{:S(2)}) collective-permute-start(bf16[2,192,256]{2,1,0:T(8,128)(2,1)S(1)} %pad_maximum_fusion.10), channel_id=1, source_target_pairs={{0,4},{2,6},{4,0},{6,2},{8,12},{10,14},{12,8},{14,10},{16,20},{18,... | collective-permute-start | bytes 589832 | tf_op jit(solution)/shard_map/products_group/ppermute | solution.py:440
  110.6 16.9 %copy-start.1 = (f32[2,12,256,128]{3,2,1,0:T(8,128)S(1)}, f32[2,12,256,128]{3,2,1,0:T(8,128)}, u32[]{:S(2)}) copy-start(f32[2,12,256,128]{3,2,1,0:T(8,128)} %get-tuple-element.96.hat_ref) | copy-start | bytes 9437188
  110.6 16.9 %copy-start.2 = (f32[2,12,256,128]{3,2,1,0:T(8,128)S(1)}, f32[2,12,256,128]{3,2,1,0:T(8,128)}, u32[]{:S(2)}) copy-start(f32[2,12,256,128]{3,2,1,0:T(8,128)} %get-tuple-element.97.inv_ref) | copy-start | bytes 9437188
  110.6 16.9 %copy-start.3 = (bf16[2,12,256,128]{3,2,1,0:T(8,128)(2,1)S(1)}, bf16[2,12,256,128]{3,2,1,0:T(8,128)(2,1)}, u32[]{:S(2)}) copy-start(bf16[2,12,256,128]{3,2,1,0:T(8,128)(2,1)} %get-tuple-element.98.low_ref) | copy-start | bytes 4718596
  119.2 8.3 %copy-start = (f32[12,256,256]{2,1,0:T(8,128)S(1)}, f32[12,256,256]{2,1,0:T(8,128)}, u32[]{:S(2)}) copy-start(f32[12,256,256]{2,1,0:T(8,128)} %get-tuple-element.95.p_ref) | copy-start | bytes 9437188
  119.3 8.2 %copy-start.4 = (bf16[12,256,128]{2,1,0:T(8,128)(2,1)S(1)}, bf16[12,256,128]{2,1,0:T(8,128)(2,1)}, u32[]{:S(2)}) copy-start(bf16[12,256,128]{2,1,0:T(8,128)(2,1)} %get-tuple-element.100.v_ref) | copy-start | bytes 2359300
  119.4 4.0 %collective-permute-start.25 = (bf16[2,192,256]{2,1,0:T(8,128)(2,1)S(1)}, bf16[2,192,256]{2,1,0:T(8,128)(2,1)S(1)}, u32[]{:S(2)}, u32[]{:S(2)}) collective-permute-start(bf16[2,192,256]{2,1,0:T(8,128)(2,1)S(1)} %slice.86), channel_id=1, source_target_pairs={{0,2},{2,0},{4,6},{6,4},{8,10},{10,8},{12,14},{14,12},{16,18},{18,... | collective-permute-start | bytes 589832 | tf_op jit(solution)/shard_map/products_core/ppermute | solution.py:440
  119.5 12.5 %collective-permute-start.28 = (bf16[192,512]{1,0:T(8,128)(2,1)S(1)}, bf16[192,512]{1,0:T(8,128)(2,1)S(1)}, u32[]{:S(2)}, u32[]{:S(2)}) collective-permute-start(bf16[192,512]{1,0:T(8,128)(2,1)S(1)} %get-tuple-element.182), channel_id=1, source_target_pairs={{0,24},{2,26},{4,28},{6,30},{8,16},{10,18},{12,20},{14,22},{16,8},... | collective-permute-start | bytes 589832 | tf_op jit(solution)/shard_map/grad_w_far/ppermute | solution.py:440
  121.4 11.8 %collective-permute-start.29 = (bf16[192,512]{1,0:T(8,128)(2,1)S(1)}, bf16[192,512]{1,0:T(8,128)(2,1)S(1)}, u32[]{:S(2)}, u32[]{:S(2)}) collective-permute-start(bf16[192,512]{1,0:T(8,128)(2,1)S(1)} %get-tuple-element.183), channel_id=1, source_target_pairs={{0,24},{2,26},{4,28},{6,30},{8,16},{10,18},{12,20},{14,22},{16,8},... | collective-permute-start | bytes 589832 | tf_op jit(solution)/shard_map/grad_w_far/ppermute | solution.py:440
  123.4 14.1 %collective-permute-start.27 = (bf16[2,192,256]{2,1,0:T(8,128)(2,1)S(1)}, bf16[2,192,256]{2,1,0:T(8,128)(2,1)S(1)}, u32[]{:S(2)}, u32[]{:S(2)}) collective-permute-start(bf16[2,192,256]{2,1,0:T(8,128)(2,1)S(1)} %pad_maximum_fusion.12), channel_id=1, source_target_pairs={{0,12},{2,14},{4,8},{6,10},{8,4},{10,6},{12,0},{14,2},{16,28},{18,... | collective-permute-start | bytes 589832 | tf_op jit(solution)/shard_map/products_group/ppermute | solution.py:440
  127.4 13.9 %collective-permute-start.26 = (bf16[2,192,256]{2,1,0:T(8,128)(2,1)S(1)}, bf16[2,192,256]{2,1,0:T(8,128)(2,1)S(1)}, u32[]{:S(2)}, u32[]{:S(2)}) collective-permute-start(bf16[2,192,256]{2,1,0:T(8,128)(2,1)S(1)} %pad_maximum_fusion.11), channel_id=1, source_target_pairs={{0,8},{2,10},{4,12},{6,14},{8,0},{10,2},{12,4},{14,6},{16,24},{18,... | collective-permute-start | bytes 589832 | tf_op jit(solution)/shard_map/products_group/ppermute | solution.py:440

commit v7 on v6

--- a/solution.py
+++ b/solution.py
@@ -393,36 +393,33 @@
     )(place, own, other, *half[0])
 
 
-def finish_kernel(n, scale, *refs):
-    kept_refs, far_refs, out_ref = refs[:n], refs[n:-1], refs[-1]
-    for group, cast in ((kept_refs, False), (far_refs, True)):
-        first = 0
-        for ref in group:
-            last = first + ref.shape[1]
-            if cast:
-                out_ref[:, first:last] = (out_ref[:, first:last] + ref[...].astype(F32)) * scale
-            else:
-                out_ref[:, first:last] = ref[...]
-            first = last
-
-
-def finish(kept, far, scale):
-    rows, depth = kept[0].shape[0], sum(a.shape[1] for a in kept)
-    tile = rows // 4
+def finish_kernel(scale, n_into, kept_ref, *refs):
+    far_refs, out_ref = refs[: len(refs) - 1 - n_into], refs[-1]
+    first = 0
+    for ref in far_refs:
+        cols = slice(first, first + ref.shape[1])
+        out_ref[:, cols] = (kept_ref[:, cols] + ref[...].astype(F32)) * scale
+        first = cols.stop
+
+
+def finish(kept, far, scale, first, depth, flops, into=()):
+    rows, wide = kept.shape
+    tile, place = rows // 4, first // wide
 
     def block(a):
         return pl.BlockSpec((tile, a.shape[1]), lambda i: (i, 0))
 
     return pl.pallas_call(
-        functools.partial(finish_kernel, len(kept), scale),
+        functools.partial(finish_kernel, scale, len(into)),
         grid=(rows // tile,),
-        in_specs=[block(a) for a in (*kept, *far)],
-        out_specs=pl.BlockSpec((tile, depth), lambda i: (i, 0)),
-        out_shape=jax.ShapeDtypeStruct((rows, depth), F32),
-        compiler_params=pltpu.CompilerParams(vmem_limit_bytes=16 << 20),
-        cost_estimate=pl.CostEstimate(flops=1000, bytes_accessed=1000, transcendentals=0),
+        in_specs=[block(a) for a in (kept, *far)] + [pl.BlockSpec(memory_space=pl.ANY)] * len(into),
+        out_specs=pl.BlockSpec((tile, wide), lambda i: (i, place)),
+        out_shape=pltpu.HBM((rows, depth), F32),
+        input_output_aliases={1 + len(far): 0} if into else {},
+        compiler_params=pltpu.CompilerParams(vmem_limit_bytes=16 << 20),
+        cost_estimate=pl.CostEstimate(flops=flops, bytes_accessed=1000, transcendentals=0),
         name="finish",
-    )(*kept, *far)
+    )(kept, *far, *into)
 
 
 def xor(k):
@@ -526,11 +523,15 @@
     odd = move(summed1[2:], CORE, "products_core")
     next_plane = [jnp.stack([summed1[j], odd[j]]) for j in range(2)]
     next_plane = [move(next_plane[j], xor(4 + 2 * j), "products_group") for j in range(2)]
-    far += [move(part, FAR, "grad_w_far") for part in sent]
+    last = [move(part, FAR, "grad_w_far") for part in sent]
+    scale = tokens ** (-0.5)
+    grad_w = finish(kept_a, far[:1], scale, 0, width, 1000)
+    grad_w = finish(kept_c, far[1:], scale, cut // 2, width, 1000, (grad_w,))
+    near, grad_w = barrier((near, grad_w))
     grads = attention_backward(place, 0, 2, saved, jnp.stack(near), qg, kg)
     grads = attention_backward(place, 2, 2, saved, jnp.stack(next_plane), qg, kg, tuple(grads))
 
-    grad_w = finish((kept_a, kept_c, kept_b), far, tokens ** (-0.5))
+    grad_w = finish(kept_b, last, scale, cut, width, 1000, (grad_w,))
     return (*(g.transpose(1, 0, 2) for g in grads), grad_w)
 
 

time: 146 us -> 146 us (level)
  waiting for transfers between devices: 61.6 us -> 57.2 us
  Pallas kernels: 40.7 us -> 43.2 us
  local copies, waits for them, and re-layouts: 2.51 us -> 4.26 us
    ppermute x24, waiting for transfers between devices: 29.7 us -> 25.4 us  [move(): return lax.ppermute(a, 'fsdp', perm)]
    pallas_call x1 -> x3, Pallas kernels: 1.99 us -> 4.45 us  [finish(): pl.pallas_call(functools.partial(finish_kernel, scale, len(into)), grid=(...]
    unnamed x21, local copies, waits for them, and re-layouts: 0.09 us -> 1.84 us
  transfers between devices with their start and end apart: 30 -> 30, of which waited for: 16 -> 14; matrix products, arithmetic and copies ran while one was open for 1% -> 1% of each run, Pallas kernels for 23% -> 25%
where the time goes in v7:
time: 146 us
  waiting for transfers between devices  57.2 us (39%)
  Pallas kernels  43.2 us (30%)
  starting transfers between devices  38.4 us (26%)
  local copies, waits for them, and re-layouts  4.26 us (3%)
  other arithmetic  1.61 us (1%)
    ppermute x6, waiting for transfers between devices, swap(): return lax.ppermute(a, 'seq', [(0, 1), (1, 0)])  31.8 us
    ppermute x24, starting transfers between devices, move(): return lax.ppermute(a, 'fsdp', perm)  30.1 us
    ppermute x24, waiting for transfers between devices, move(): return lax.ppermute(a, 'fsdp', perm)  25.4 us
    pallas_call x2, Pallas kernels, attention_backward(): pl.pallas_call(functools.partial(backward_kernel, per, dim, len(into)), g...  8.85 us
    pallas_call x1, Pallas kernels, attention_probabilities(): pl.pallas_call(functools.partial(probabilities_kernel, per, dim), grid_sp...  8.49 us
    ppermute x6, starting transfers between devices, swap(): return lax.ppermute(a, 'seq', [(0, 1), (1, 0)])  8.32 us
    pallas_call x3, Pallas kernels, weight_terms(): pl.pallas_call(functools.partial(weight_kernel, n, half[1], parts), in_sp...  7.01 us
    pallas_call x2, Pallas kernels, gradient_products(): pl.pallas_call(functools.partial(products_kernel, n, [(first, wide, start...  6.46 us
  transfers between devices with their start and end apart: 30, of which 14 were waited for; matrix products, arithmetic and copies ran while one was open for 1% of the time, Pallas kernels for 25%

profile of v7, /device:TPU:0, one launch (start us, length us, event | category | flops | bytes accessed | tf_op | source)
XLA Modules:
  0.0 145.7 jit_solution(8017327597943238613)
XLA Ops:
  0.6 1.2 dynamic-slice_bitcast_fusion
  1.9 0.9 pad_maximum_fusion
  2.9 3.0 %collective-permute-start.4 = (bf16[256,3072]{1,0:T(8,128)(2,1)}, bf16[256,3072]{1,0:T(8,128)(2,1)S(1)}, u32[]{:S(2)}, u32[]{:S(2)}) collective-permute-start(bf16[256,3072]{1,0:T(8,128)(2,1)} %refs_0_), channel_id=1, source_target_pairs={{0,8},{2,10},{4,12},{6,14},{8,0},{10,2},{12,4},{14,6},{16,24},{18,... | collective-permute-start | bytes 4718600 | tf_op jit(solution)/shard_map/gy_plane/ppermute | solution.py:437
  5.9 1.5 %collective-permute-start.3 = (bf16[256,3072]{1,0:T(8,128)(2,1)}, bf16[256,3072]{1,0:T(8,128)(2,1)S(1)}, u32[]{:S(2)}, u32[]{:S(2)}) collective-permute-start(bf16[256,3072]{1,0:T(8,128)(2,1)} %refs_0_), channel_id=1, source_target_pairs={{0,4},{2,6},{4,0},{6,2},{8,12},{10,14},{12,8},{14,10},{16,20},{18,... | collective-permute-start | bytes 4718600 | tf_op jit(solution)/shard_map/gy_cross/ppermute | solution.py:437
  7.4 1.5 %collective-permute-start = (bf16[2,128,1536]{2,1,0:T(8,128)(2,1)}, bf16[2,128,1536]{2,1,0:T(8,128)(2,1)}, u32[]{:S(2)}, u32[]{:S(2)}) collective-permute-start(bf16[2,128,1536]{2,1,0:T(8,128)(2,1)} %pad_maximum_fusion), channel_id=1, source_target_pairs={{0,1},{1,0},{2,3},{3,2},{4,5},{5,4},{6,7},{7,6},{8,9},{9,8},{10,11... | collective-permute-start | bytes 2359304 | tf_op jit(solution)/shard_map/qk_seq/ppermute | solution.py:442
  8.9 1.7 %collective-permute-start.5 = (bf16[192,3072]{1,0:T(8,128)(2,1)}, bf16[192,3072]{1,0:T(8,128)(2,1)}, u32[]{:S(2)}, u32[]{:S(2)}) collective-permute-start(bf16[192,3072]{1,0:T(8,128)(2,1)} %refs_1_.1), channel_id=1, source_target_pairs={{8,16},{10,18},{12,20},{14,22},{16,8},{18,10},{20,12},{22,14},{9,1... | collective-permute-start | bytes 3538952 | tf_op jit(solution)/shard_map/w_middle/ppermute | solution.py:437
  10.6 0.8 constant_dynamic-slice_fusion
  11.4 0.5 collective-permute-start.1
  11.9 0.1 copy.17.col_ref
  12.0 0.1 pad_add_fusion.place
  12.1 16.1 %collective-permute-done.came_ref = bf16[2,128,1536]{2,1,0:T(8,128)(2,1)} collective-permute-done((bf16[2,128,1536]{2,1,0:T(8,128)(2,1)}, bf16[2,128,1536]{2,1,0:T(8,128)(2,1)}, u32[]{:S(2)}, u32[]{:S(2)}) %collective-permute-start) | collective-permute-done | bytes 786464 | tf_op jit(solution)/shard_map/qk_seq/ppermute | solution.py:442
  28.2 8.5 %attention_probabilities.1 = (f32[12,256,256]{2,1,0:T(8,128)}, f32[2,12,256,128]{3,2,1,0:T(8,128)}, f32[2,12,256,128]{3,2,1,0:T(8,128)}, bf16[2,12,256,128]{3,2,1,0:T(8,128)(2,1)}, bf16[12,256,256]{2,1,0:T(8,128)(2,1)S(1)}) custom-call(s32[4]{0:T(128)S(1)} %pad_add_fusion.place, bf16[128,3072]{1,0:T(8,128)(2,1)} %q_ref.1, bf16[128,3072]{1,0:T(8,128)(2,1)} %k_ref.1, ...), custom_call_target="tpu_custom_call" | custom-call | flops 1000 | bytes 1000 | tf_op jit(solution)/shard_map/attention_probabilities/pallas_call | solution.py:219
  36.7 3.9 %attention_attended.1 = (bf16[4,192,256]{2,1,0:T(8,128)(2,1)S(1)}, bf16[4,192,256]{2,1,0:T(8,128)(2,1)S(1)}, bf16[12,256,128]{2,1,0:T(8,128)(2,1)}) custom-call(s32[4]{0:T(128)S(1)} %pad_add_fusion.place, bf16[12,256,256]{2,1,0:T(8,128)(2,1)S(1)} %get-tuple-element.102.p_low_ref, bf16[128,3072]{1,0:T(8,128)(2,1)} %v_ref.1, ...), custom_call_target="tpu_custom_call" | custom-call | flops 1000 | bytes 1000 | tf_op jit(solution)/shard_map/attention_attended/pallas_call | solution.py:242
  40.6 1.7 %collective-permute-done.2 = bf16[4,192,256]{2,1,0:T(8,128)(2,1)S(1)} collective-permute-done((bf16[4,192,256]{2,1,0:T(8,128)(2,1)S(1)}, bf16[4,192,256]{2,1,0:T(8,128)(2,1)S(1)}, u32[]{:S(2)}, u32[]{:S(2)}) %collective-permute-start.2) | collective-permute-done | bytes 393248 | tf_op jit(solution)/shard_map/att_core/ppermute | solution.py:437
  42.4 0.1 collective-permute-start.10
  42.6 1.0 collective-permute-start.6
  43.7 0.5 collective-permute-start.7
  44.2 1.6 %collective-permute-start.9 = (bf16[2,192,256]{2,1,0:T(8,128)(2,1)S(1)}, bf16[2,192,256]{2,1,0:T(8,128)(2,1)S(1)}, u32[]{:S(2)}, u32[]{:S(2)}) collective-permute-start(bf16[2,192,256]{2,1,0:T(8,128)(2,1)S(1)} %pad_maximum_fusion.5), channel_id=1, source_target_pairs={{0,1},{1,0},{2,3},{3,2},{4,5},{5,4},{6,7},{7,6},{8,9},{9,8},{10,11... | collective-permute-start | bytes 589832 | tf_op jit(solution)/shard_map/att_seq/ppermute | solution.py:442
  45.8 2.2 %collective-permute-start.8 = (bf16[2,192,256]{2,1,0:T(8,128)(2,1)S(1)}, bf16[2,192,256]{2,1,0:T(8,128)(2,1)S(1)}, u32[]{:S(2)}, u32[]{:S(2)}) collective-permute-start(bf16[2,192,256]{2,1,0:T(8,128)(2,1)S(1)} %pad_maximum_fusion.8), channel_id=1, source_target_pairs={{0,12},{2,14},{4,8},{6,10},{8,4},{10,6},{12,0},{14,2},{16,28},{18,... | collective-permute-start | bytes 589832 | tf_op jit(solution)/shard_map/att_group/ppermute | solution.py:437
  48.0 1.9 %collective-permute-done.6 = bf16[2,192,256]{2,1,0:T(8,128)(2,1)S(1)} collective-permute-done((bf16[2,192,256]{2,1,0:T(8,128)(2,1)S(1)}, bf16[2,192,256]{2,1,0:T(8,128)(2,1)S(1)}, u32[]{:S(2)}, u32[]{:S(2)}) %collective-permute-start.6) | collective-permute-done | bytes 196640 | tf_op jit(solution)/shard_map/att_group/ppermute | solution.py:437
  49.9 4.6 %collective-permute-start.16 = (bf16[192,3072]{1,0:T(8,128)(2,1)}, bf16[192,3072]{1,0:T(8,128)(2,1)S(1)}, u32[]{:S(2)}, u32[]{:S(2)}) collective-permute-start(bf16[192,3072]{1,0:T(8,128)(2,1)} %refs_1_.1), channel_id=1, source_target_pairs={{0,24},{2,26},{4,28},{6,30},{24,0},{26,2},{28,4},{30,6},{1,25},{3,... | collective-permute-start | bytes 3538952 | tf_op jit(solution)/shard_map/w_ends/ppermute | solution.py:437
  54.5 0.1 slice.68
  54.6 0.8 collective-permute-done.8
  55.3 1.1 collective-permute-start.12
  56.5 1.6 %collective-permute-start.11 = (bf16[6,192,256]{2,1,0:T(8,128)(2,1)S(1)}, bf16[6,192,256]{2,1,0:T(8,128)(2,1)S(1)}, u32[]{:S(2)}, u32[]{:S(2)}) collective-permute-start(bf16[6,192,256]{2,1,0:T(8,128)(2,1)S(1)} %pad_maximum_fusion.2), channel_id=1, source_target_pairs={{0,1},{1,0},{2,3},{3,2},{4,5},{5,4},{6,7},{7,6},{8,9},{9,8},{10,11... | collective-permute-start | bytes 1769480 | tf_op jit(solution)/shard_map/att_seq/ppermute | solution.py:442
  58.1 0.5 collective-permute-start.15
  58.6 2.5 %hold.1 = (bf16[256,3072]{1,0:T(8,128)(2,1)S(1)}, bf16[192,3072]{1,0:T(8,128)(2,1)S(1)}) custom-call(bf16[256,3072]{1,0:T(8,128)(2,1)} %refs_0_, bf16[192,3072]{1,0:T(8,128)(2,1)} %refs_1_.1), custom_call_target="tpu_custom_call" | custom-call | flops 1000 | bytes 1000 | tf_op jit(solution)/shard_map/hold/pallas_call | solution.py:300
  61.1 9.8 %collective-permute-done.11 = bf16[6,192,256]{2,1,0:T(8,128)(2,1)S(1)} collective-permute-done((bf16[6,192,256]{2,1,0:T(8,128)(2,1)S(1)}, bf16[6,192,256]{2,1,0:T(8,128)(2,1)S(1)}, u32[]{:S(2)}, u32[]{:S(2)}) %collective-permute-start.11) | collective-permute-done | bytes 589856 | tf_op jit(solution)/shard_map/att_seq/ppermute | solution.py:442
  71.0 8.6 %collective-permute-done.12.refs_6_.refs_1_ = bf16[256,2048]{1,0:T(8,128)(2,1)S(1)} collective-permute-done((bf16[256,2048]{1,0:T(8,128)(2,1)S(1)}, bf16[256,2048]{1,0:T(8,128)(2,1)S(1)}, u32[]{:S(2)}, u32[]{:S(2)}) %collective-permute-start.12) | collective-permute-done | bytes 1048608 | tf_op jit(solution)/shard_map/gy_plane_cross_a/ppermute | solution.py:437
  79.6 2.6 %collective-permute-done.16.end_ref = bf16[192,3072]{1,0:T(8,128)(2,1)S(1)} collective-permute-done((bf16[192,3072]{1,0:T(8,128)(2,1)}, bf16[192,3072]{1,0:T(8,128)(2,1)S(1)}, u32[]{:S(2)}, u32[]{:S(2)}) %collective-permute-start.16) | collective-permute-done | bytes 1179680 | tf_op jit(solution)/shard_map/w_ends/ppermute | solution.py:437
  82.3 1.4 choose.1.far_ref
  83.8 2.3 %weight_terms.3 = (bf16[192,1024]{1,0:T(8,128)(2,1)S(1)}, f32[192,1024]{1,0:T(8,128)S(1)}) custom-call(s32[4]{0:T(128)S(1)} %pad_add_fusion.place, bf16[8,192,256]{2,1,0:T(8,128)(2,1)S(1)} %constant_dynamic-update-slice_fusion.own_ref, bf16[8,192,256]{2,1,0:T(8,128)(2,1)S(1)} %pad_maximum_fusion.1.other_ref, ...), custom_call_target="tpu_custom_call" | custom-call | flops 1000 | bytes 1000 | tf_op jit(solution)/shard_map/weight_terms/pallas_call | solution.py:383
  86.2 1.0 collective-permute-start.17
  87.2 1.7 %collective-permute-start.18 = (bf16[192,1024]{1,0:T(8,128)(2,1)S(1)}, bf16[192,1024]{1,0:T(8,128)(2,1)S(1)}, u32[]{:S(2)}, u32[]{:S(2)}) collective-permute-start(bf16[192,1024]{1,0:T(8,128)(2,1)S(1)} %get-tuple-element.135), channel_id=1, source_target_pairs={{0,24},{2,26},{4,28},{6,30},{8,16},{10,18},{12,20},{14,22},{16,8},... | collective-permute-start | bytes 1179656 | tf_op jit(solution)/shard_map/grad_w_far/ppermute | solution.py:437
  88.9 3.2 %gradient_products.2 = (bf16[4,192,256]{2,1,0:T(8,128)(2,1)S(1)}, bf16[4,192,256]{2,1,0:T(8,128)(2,1)S(1)}) custom-call(s32[4]{0:T(128)S(1)} %pad_add_fusion.place, bf16[192,3072]{1,0:T(8,128)(2,1)S(1)} %get-tuple-element.137.w_ref, bf16[192,3072]{1,0:T(8,128)(2,1)S(1)} %choose.1.far_ref, bf16[256,3072]{1,0:T(8,128)(2,1)S(1)} %get-tuple-element.159.refs_0_.refs_4_, ...), custom_call_target="tpu_custom_call" | custom-call | flops 1000 | bytes 1000 | tf_op jit(solution)/shard_map/gradient_products/pallas_call | solution.py:351
  92.1 1.6 %collective-permute-start.19 = (bf16[4,192,256]{2,1,0:T(8,128)(2,1)S(1)}, bf16[4,192,256]{2,1,0:T(8,128)(2,1)S(1)}, u32[]{:S(2)}, u32[]{:S(2)}) collective-permute-start(bf16[4,192,256]{2,1,0:T(8,128)(2,1)S(1)} %get-tuple-element.146), channel_id=1, source_target_pairs={{0,1},{1,0},{2,3},{3,2},{4,5},{5,4},{6,7},{7,6},{8,9},{9,8},{10,11... | collective-permute-start | bytes 1179656 | tf_op jit(solution)/shard_map/products_seq/ppermute | solution.py:442
  93.7 2.3 %weight_terms.4 = (bf16[192,1024]{1,0:T(8,128)(2,1)S(1)}, f32[192,1024]{1,0:T(8,128)S(1)}) custom-call(s32[4]{0:T(128)S(1)} %pad_add_fusion.place, bf16[8,192,256]{2,1,0:T(8,128)(2,1)S(1)} %constant_dynamic-update-slice_fusion.own_ref, bf16[8,192,256]{2,1,0:T(8,128)(2,1)S(1)} %pad_maximum_fusion.1.other_ref, ...), custom_call_target="tpu_custom_call" | custom-call | flops 1000 | bytes 1000 | tf_op jit(solution)/shard_map/weight_terms/pallas_call | solution.py:383
  96.1 3.2 %collective-permute-done.18.refs_0_ = bf16[192,1024]{1,0:T(8,128)(2,1)S(1)} collective-permute-done((bf16[192,1024]{1,0:T(8,128)(2,1)S(1)}, bf16[192,1024]{1,0:T(8,128)(2,1)S(1)}, u32[]{:S(2)}, u32[]{:S(2)}) %collective-permute-start.18) | collective-permute-done | bytes 393248 | tf_op jit(solution)/shard_map/grad_w_far/ppermute | solution.py:437
  99.2 3.1 %collective-permute-done.19 = bf16[4,192,256]{2,1,0:T(8,128)(2,1)S(1)} collective-permute-done((bf16[4,192,256]{2,1,0:T(8,128)(2,1)S(1)}, bf16[4,192,256]{2,1,0:T(8,128)(2,1)S(1)}, u32[]{:S(2)}, u32[]{:S(2)}) %collective-permute-start.19) | collective-permute-done | bytes 393248 | tf_op jit(solution)/shard_map/products_seq/ppermute | solution.py:442
  102.4 1.8 %collective-permute-start.20 = (bf16[192,1024]{1,0:T(8,128)(2,1)S(1)}, bf16[192,1024]{1,0:T(8,128)(2,1)S(1)}, u32[]{:S(2)}, u32[]{:S(2)}) collective-permute-start(bf16[192,1024]{1,0:T(8,128)(2,1)S(1)} %get-tuple-element.148), channel_id=1, source_target_pairs={{0,24},{2,26},{4,28},{6,30},{8,16},{10,18},{12,20},{14,22},{16,8},... | collective-permute-start | bytes 1179656 | tf_op jit(solution)/shard_map/grad_w_far/ppermute | solution.py:437
  104.2 0.1 collective-permute-done.21.refs_7_
  104.3 3.2 %gradient_products.3 = (bf16[4,192,256]{2,1,0:T(8,128)(2,1)S(1)}, bf16[4,192,256]{2,1,0:T(8,128)(2,1)S(1)}) custom-call(s32[4]{0:T(128)S(1)} %pad_add_fusion.place, bf16[192,3072]{1,0:T(8,128)(2,1)S(1)} %get-tuple-element.137.w_ref, bf16[192,3072]{1,0:T(8,128)(2,1)S(1)} %choose.1.far_ref, bf16[256,3072]{1,0:T(8,128)(2,1)S(1)} %collective-permute-done.4.refs_4_.refs_0_, ...), custom_call_target="tpu_custom_call" | custom-call | flops 1000 | bytes 1000 | tf_op jit(solution)/shard_map/gradient_products/pallas_call | solution.py:351
  107.5 0.1 add_convert_fusion.1
  107.6 0.2 collective-permute-start.22
  107.8 1.5 %collective-permute-start.24 = (bf16[4,192,256]{2,1,0:T(8,128)(2,1)S(1)}, bf16[4,192,256]{2,1,0:T(8,128)(2,1)S(1)}, u32[]{:S(2)}, u32[]{:S(2)}) collective-permute-start(bf16[4,192,256]{2,1,0:T(8,128)(2,1)S(1)} %get-tuple-element.158), channel_id=1, source_target_pairs={{0,1},{1,0},{2,3},{3,2},{4,5},{5,4},{6,7},{7,6},{8,9},{9,8},{10,11... | collective-permute-start | bytes 1179656 | tf_op jit(solution)/shard_map/products_seq/ppermute | solution.py:442
  109.5 1.2 collective-permute-start.23
  110.6 2.3 %weight_terms.5 = (bf16[192,512]{1,0:T(8,128)(2,1)S(1)}, bf16[192,512]{1,0:T(8,128)(2,1)S(1)}, f32[192,1024]{1,0:T(8,128)S(1)}) custom-call(s32[4]{0:T(128)S(1)} %pad_add_fusion.place, bf16[8,192,256]{2,1,0:T(8,128)(2,1)S(1)} %constant_dynamic-update-slice_fusion.own_ref, bf16[8,192,256]{2,1,0:T(8,128)(2,1)S(1)} %pad_maximum_fusion.1.other_ref, ...), custom_call_target="tpu_custom_call" | custom-call | flops 1000 | bytes 1000 | tf_op jit(solution)/shard_map/weight_terms/pallas_call | solution.py:383
  113.0 2.8 %collective-permute-done.20.refs_0_ = bf16[192,1024]{1,0:T(8,128)(2,1)S(1)} collective-permute-done((bf16[192,1024]{1,0:T(8,128)(2,1)S(1)}, bf16[192,1024]{1,0:T(8,128)(2,1)S(1)}, u32[]{:S(2)}, u32[]{:S(2)}) %collective-permute-start.20) | collective-permute-done | bytes 393248 | tf_op jit(solution)/shard_map/grad_w_far/ppermute | solution.py:437
  115.8 0.6 collective-permute-done.23
  116.4 2.8 %collective-permute-done.24 = bf16[4,192,256]{2,1,0:T(8,128)(2,1)S(1)} collective-permute-done((bf16[4,192,256]{2,1,0:T(8,128)(2,1)S(1)}, bf16[4,192,256]{2,1,0:T(8,128)(2,1)S(1)}, u32[]{:S(2)}, u32[]{:S(2)}) %collective-permute-start.24) | collective-permute-done | bytes 393248 | tf_op jit(solution)/shard_map/products_seq/ppermute | solution.py:442
  119.2 0.1 add_convert_fusion
  119.4 0.1 collective-permute-start.25
  119.4 2.0 %collective-permute-start.28 = (bf16[192,512]{1,0:T(8,128)(2,1)S(1)}, bf16[192,512]{1,0:T(8,128)(2,1)S(1)}, u32[]{:S(2)}, u32[]{:S(2)}) collective-permute-start(bf16[192,512]{1,0:T(8,128)(2,1)S(1)} %get-tuple-element.187), channel_id=1, source_target_pairs={{0,24},{2,26},{4,28},{6,30},{8,16},{10,18},{12,20},{14,22},{16,8},... | collective-permute-start | bytes 589832 | tf_op jit(solution)/shard_map/grad_w_far/ppermute | solution.py:437
  121.4 1.9 %collective-permute-start.29 = (bf16[192,512]{1,0:T(8,128)(2,1)S(1)}, bf16[192,512]{1,0:T(8,128)(2,1)S(1)}, u32[]{:S(2)}, u32[]{:S(2)}) collective-permute-start(bf16[192,512]{1,0:T(8,128)(2,1)S(1)} %get-tuple-element.188), channel_id=1, source_target_pairs={{0,24},{2,26},{4,28},{6,30},{8,16},{10,18},{12,20},{14,22},{16,8},... | collective-permute-start | bytes 589832 | tf_op jit(solution)/shard_map/grad_w_far/ppermute | solution.py:437
  123.4 3.9 %collective-permute-start.27 = (bf16[2,192,256]{2,1,0:T(8,128)(2,1)S(1)}, bf16[2,192,256]{2,1,0:T(8,128)(2,1)S(1)}, u32[]{:S(2)}, u32[]{:S(2)}) collective-permute-start(bf16[2,192,256]{2,1,0:T(8,128)(2,1)S(1)} %pad_maximum_fusion.12), channel_id=1, source_target_pairs={{0,12},{2,14},{4,8},{6,10},{8,4},{10,6},{12,0},{14,2},{16,28},{18,... | collective-permute-start | bytes 589832 | tf_op jit(solution)/shard_map/products_group/ppermute | solution.py:437
  127.4 0.1 collective-permute-start.26
  127.5 1.5 %finish.3.refs_1_ = f32[192,3072]{1,0:T(8,128)} custom-call(f32[192,1024]{1,0:T(8,128)S(1)} %get-tuple-element.176.kept_ref, bf16[192,1024]{1,0:T(8,128)(2,1)S(1)} %collective-permute-done.18.refs_0_), custom_call_target="tpu_custom_call" | custom-call | flops 1000 | bytes 1000 | tf_op jit(solution)/shard_map/finish/pallas_call | solution.py:412
  129.0 1.5 %finish.4.refs_2_ = f32[192,3072]{1,0:T(8,128)} custom-call(f32[192,1024]{1,0:T(8,128)S(1)} %get-tuple-element.174.kept_ref, bf16[192,1024]{1,0:T(8,128)(2,1)S(1)} %collective-permute-done.20.refs_0_, f32[192,3072]{1,0:T(8,128)} %finish.3.refs_1_), custom_call_target="tpu_custom_call", output_to_operand_aliasing={{}: (2, {})} | custom-call | flops 1000 | bytes 1000 | tf_op jit(solution)/shard_map/finish/pallas_call | solution.py:412
  130.5 0.9 copy-done
  131.3 0.9 copy-done.1
  132.2 4.4 %attention_backward.2 = (bf16[12,256,128]{2,1,0:T(8,128)(2,1)}, bf16[12,256,128]{2,1,0:T(8,128)(2,1)}, bf16[12,256,128]{2,1,0:T(8,128)(2,1)}) custom-call(s32[4]{0:T(128)S(1)} %pad_add_fusion.place, f32[12,256,256]{2,1,0:T(8,128)S(1)} %copy-done, f32[2,12,256,128]{3,2,1,0:T(8,128)S(1)} %copy-done.1, f32[2,12,256,128]{3,2,1,0:T(8,128)S(1)} %copy-done.2, ...), custom_call_target="tpu_custom_call" | custom-call | flops 1000 | bytes 1000 | tf_op jit(solution)/shard_map/attention_backward/pallas_call | solution.py:268
  136.7 1.5 %finish.5 = f32[192,3072]{1,0:T(8,128)} custom-call(f32[192,1024]{1,0:T(8,128)S(1)} %get-tuple-element.186.kept_ref, bf16[192,512]{1,0:T(8,128)(2,1)S(1)} %collective-permute-done.28.refs_0_, bf16[192,512]{1,0:T(8,128)(2,1)S(1)} %collective-permute-done.29.refs_1_, f32[192,3072]{1,0:T(8,128)} %finish.4.refs_2_), custom_call_target="tpu_custom_call", output_to_operand_aliasing={{}: (3, {})} | custom-call | flops 1000 | bytes 1000 | tf_op jit(solution)/shard_map/finish/pallas_call | solution.py:412
  138.2 3.1 %collective-permute-done.26 = bf16[2,192,256]{2,1,0:T(8,128)(2,1)S(1)} collective-permute-done((bf16[2,192,256]{2,1,0:T(8,128)(2,1)S(1)}, bf16[2,192,256]{2,1,0:T(8,128)(2,1)S(1)}, u32[]{:S(2)}, u32[]{:S(2)}) %collective-permute-start.26) | collective-permute-done | bytes 196640 | tf_op jit(solution)/shard_map/products_group/ppermute | solution.py:437
  141.3 4.4 %attention_backward.3 = (bf16[12,256,128]{2,1,0:T(8,128)(2,1)}, bf16[12,256,128]{2,1,0:T(8,128)(2,1)}, bf16[12,256,128]{2,1,0:T(8,128)(2,1)}) custom-call(s32[4]{0:T(128)S(1)} %pad_add_fusion.place, f32[12,256,256]{2,1,0:T(8,128)S(1)} %copy-done, f32[2,12,256,128]{3,2,1,0:T(8,128)S(1)} %copy-done.1, ...), custom_call_target="tpu_custom_call", output_to_operand_aliasing={{0}: (9, {}), {1}: (10, {}), {2}: (11, {})} | custom-call | flops 1000 | bytes 1000 | tf_op jit(solution)/shard_map/attention_backward/pallas_call | solution.py:268
  (61 shorter events, 0.7 us)
Async XLA Ops:
  0.6 10.0 %copy-start.8 = (bf16[128,3072]{1,0:T(8,128)(2,1)S(1)}, bf16[128,3072]{1,0:T(8,128)(2,1)}, u32[]{:S(2)}) copy-start(bf16[128,3072]{1,0:T(8,128)(2,1)} %v_ref.1) | copy-start | bytes 2359300
  1.9 10.0 %copy-start.7 = (s32[1,256]{1,0:T(1,128)S(1)}, s32[1,256]{1,0:T(1,128)}, u32[]{:S(2)}) copy-start(s32[1,256]{1,0:T(1,128)} %row_ref.1) | copy-start | bytes 3076
  1.9 26.3 %copy-start.5 = (f32[128]{0:T(128)S(1)}, f32[128]{0:T(128)}, u32[]{:S(2)}) copy-start(f32[128]{0:T(128)} %param.12) | copy-start | bytes 1540
  1.9 26.3 %copy-start.6 = (f32[128]{0:T(128)S(1)}, f32[128]{0:T(128)}, u32[]{:S(2)}) copy-start(f32[128]{0:T(128)} %param.13) | copy-start | bytes 1540
  2.9 39.5 %collective-permute-start.4 = (bf16[256,3072]{1,0:T(8,128)(2,1)}, bf16[256,3072]{1,0:T(8,128)(2,1)S(1)}, u32[]{:S(2)}, u32[]{:S(2)}) collective-permute-start(bf16[256,3072]{1,0:T(8,128)(2,1)} %refs_0_), channel_id=1, source_target_pairs={{0,8},{2,10},{4,12},{6,14},{8,0},{10,2},{12,4},{14,6},{16,24},{18,... | collective-permute-start | bytes 4718600 | tf_op jit(solution)/shard_map/gy_plane/ppermute | solution.py:437
  5.9 36.5 %collective-permute-start.3 = (bf16[256,3072]{1,0:T(8,128)(2,1)}, bf16[256,3072]{1,0:T(8,128)(2,1)S(1)}, u32[]{:S(2)}, u32[]{:S(2)}) collective-permute-start(bf16[256,3072]{1,0:T(8,128)(2,1)} %refs_0_), channel_id=1, source_target_pairs={{0,4},{2,6},{4,0},{6,2},{8,12},{10,14},{12,8},{14,10},{16,20},{18,... | collective-permute-start | bytes 4718600 | tf_op jit(solution)/shard_map/gy_cross/ppermute | solution.py:437
  7.4 20.8 %collective-permute-start = (bf16[2,128,1536]{2,1,0:T(8,128)(2,1)}, bf16[2,128,1536]{2,1,0:T(8,128)(2,1)}, u32[]{:S(2)}, u32[]{:S(2)}) collective-permute-start(bf16[2,128,1536]{2,1,0:T(8,128)(2,1)} %pad_maximum_fusion), channel_id=1, source_target_pairs={{0,1},{1,0},{2,3},{3,2},{4,5},{5,4},{6,7},{7,6},{8,9},{9,8},{10,11... | collective-permute-start | bytes 2359304 | tf_op jit(solution)/shard_map/qk_seq/ppermute | solution.py:442
  8.9 31.7 %collective-permute-start.5 = (bf16[192,3072]{1,0:T(8,128)(2,1)}, bf16[192,3072]{1,0:T(8,128)(2,1)}, u32[]{:S(2)}, u32[]{:S(2)}) collective-permute-start(bf16[192,3072]{1,0:T(8,128)(2,1)} %refs_1_.1), channel_id=1, source_target_pairs={{8,16},{10,18},{12,20},{14,22},{16,8},{18,10},{20,12},{22,14},{9,1... | collective-permute-start | bytes 3538952 | tf_op jit(solution)/shard_map/w_middle/ppermute | solution.py:437
  11.4 25.3 %collective-permute-start.1 = (bf16[128,1536]{1,0:T(8,128)(2,1)}, bf16[128,1536]{1,0:T(8,128)(2,1)}, u32[]{:S(2)}, u32[]{:S(2)}) collective-permute-start(bf16[128,1536]{1,0:T(8,128)(2,1)} %constant_dynamic-slice_fusion), channel_id=1, source_target_pairs={{0,1},{1,0},{2,3},{3,2},{4,5},{5,4},{6,7},{7,6},{8,9},{9,8},{10,11... | collective-permute-start | bytes 1179656 | tf_op jit(solution)/shard_map/v_seq/ppermute | solution.py:442
  40.6 1.7 %collective-permute-start.2 = (bf16[4,192,256]{2,1,0:T(8,128)(2,1)S(1)}, bf16[4,192,256]{2,1,0:T(8,128)(2,1)S(1)}, u32[]{:S(2)}, u32[]{:S(2)}) collective-permute-start(bf16[4,192,256]{2,1,0:T(8,128)(2,1)S(1)} %get-tuple-element.105), channel_id=1, source_target_pairs={{0,2},{2,0},{4,6},{6,4},{8,10},{10,8},{12,14},{14,12},{16,18},{18,... | collective-permute-start | bytes 1179656 | tf_op jit(solution)/shard_map/att_core/ppermute | solution.py:437
  42.4 13.0 %collective-permute-start.10 = (bf16[256,3072]{1,0:T(8,128)(2,1)}, bf16[256,3072]{1,0:T(8,128)(2,1)S(1)}, u32[]{:S(2)}, u32[]{:S(2)}) collective-permute-start(bf16[256,3072]{1,0:T(8,128)(2,1)} %refs_0_), channel_id=1, source_target_pairs={{0,2},{2,0},{4,6},{6,4},{8,10},{10,8},{12,14},{14,12},{16,18},{18,... | collective-permute-start | bytes 4718600 | tf_op jit(solution)/shard_map/gy_core/ppermute | solution.py:437
  42.6 7.2 %collective-permute-start.6 = (bf16[2,192,256]{2,1,0:T(8,128)(2,1)S(1)}, bf16[2,192,256]{2,1,0:T(8,128)(2,1)S(1)}, u32[]{:S(2)}, u32[]{:S(2)}) collective-permute-start(bf16[2,192,256]{2,1,0:T(8,128)(2,1)S(1)} %pad_maximum_fusion.6), channel_id=1, source_target_pairs={{0,4},{2,6},{4,0},{6,2},{8,12},{10,14},{12,8},{14,10},{16,20},{18,... | collective-permute-start | bytes 589832 | tf_op jit(solution)/shard_map/att_group/ppermute | solution.py:437
  43.7 10.9 %collective-permute-start.7 = (bf16[2,192,256]{2,1,0:T(8,128)(2,1)S(1)}, bf16[2,192,256]{2,1,0:T(8,128)(2,1)S(1)}, u32[]{:S(2)}, u32[]{:S(2)}) collective-permute-start(bf16[2,192,256]{2,1,0:T(8,128)(2,1)S(1)} %pad_maximum_fusion.7), channel_id=1, source_target_pairs={{0,8},{2,10},{4,12},{6,14},{8,0},{10,2},{12,4},{14,6},{16,24},{18,... | collective-permute-start | bytes 589832 | tf_op jit(solution)/shard_map/att_group/ppermute | solution.py:437
  44.2 10.4 %collective-permute-start.9 = (bf16[2,192,256]{2,1,0:T(8,128)(2,1)S(1)}, bf16[2,192,256]{2,1,0:T(8,128)(2,1)S(1)}, u32[]{:S(2)}, u32[]{:S(2)}) collective-permute-start(bf16[2,192,256]{2,1,0:T(8,128)(2,1)S(1)} %pad_maximum_fusion.5), channel_id=1, source_target_pairs={{0,1},{1,0},{2,3},{3,2},{4,5},{5,4},{6,7},{7,6},{8,9},{9,8},{10,11... | collective-permute-start | bytes 589832 | tf_op jit(solution)/shard_map/att_seq/ppermute | solution.py:442
  45.8 9.5 %collective-permute-start.8 = (bf16[2,192,256]{2,1,0:T(8,128)(2,1)S(1)}, bf16[2,192,256]{2,1,0:T(8,128)(2,1)S(1)}, u32[]{:S(2)}, u32[]{:S(2)}) collective-permute-start(bf16[2,192,256]{2,1,0:T(8,128)(2,1)S(1)} %pad_maximum_fusion.8), channel_id=1, source_target_pairs={{0,12},{2,14},{4,8},{6,10},{8,4},{10,6},{12,0},{14,2},{16,28},{18,... | collective-permute-start | bytes 589832 | tf_op jit(solution)/shard_map/att_group/ppermute | solution.py:437
  49.9 32.4 %collective-permute-start.16 = (bf16[192,3072]{1,0:T(8,128)(2,1)}, bf16[192,3072]{1,0:T(8,128)(2,1)S(1)}, u32[]{:S(2)}, u32[]{:S(2)}) collective-permute-start(bf16[192,3072]{1,0:T(8,128)(2,1)} %refs_1_.1), channel_id=1, source_target_pairs={{0,24},{2,26},{4,28},{6,30},{24,0},{26,2},{28,4},{30,6},{1,25},{3,... | collective-permute-start | bytes 3538952 | tf_op jit(solution)/shard_map/w_ends/ppermute | solution.py:437
  55.3 24.3 %collective-permute-start.12 = (bf16[256,2048]{1,0:T(8,128)(2,1)S(1)}, bf16[256,2048]{1,0:T(8,128)(2,1)S(1)}, u32[]{:S(2)}, u32[]{:S(2)}) collective-permute-start(bf16[256,2048]{1,0:T(8,128)(2,1)S(1)} %slice.68), channel_id=1, source_target_pairs={{0,4},{2,6},{4,0},{6,2},{8,12},{10,14},{12,8},{14,10},{16,20},{18,... | collective-permute-start | bytes 3145736 | tf_op jit(solution)/shard_map/gy_plane_cross_a/ppermute | solution.py:437
  56.5 14.4 %collective-permute-start.11 = (bf16[6,192,256]{2,1,0:T(8,128)(2,1)S(1)}, bf16[6,192,256]{2,1,0:T(8,128)(2,1)S(1)}, u32[]{:S(2)}, u32[]{:S(2)}) collective-permute-start(bf16[6,192,256]{2,1,0:T(8,128)(2,1)S(1)} %pad_maximum_fusion.2), channel_id=1, source_target_pairs={{0,1},{1,0},{2,3},{3,2},{4,5},{5,4},{6,7},{7,6},{8,9},{9,8},{10,11... | collective-permute-start | bytes 1769480 | tf_op jit(solution)/shard_map/att_seq/ppermute | solution.py:442
  58.1 25.7 %collective-permute-start.14 = (bf16[256,3072]{1,0:T(8,128)(2,1)S(1)}, bf16[256,3072]{1,0:T(8,128)(2,1)S(1)}, u32[]{:S(2)}, u32[]{:S(2)}) collective-permute-start(bf16[256,3072]{1,0:T(8,128)(2,1)S(1)} %collective-permute-done.3.refs_2_.refs_1_.refs_5_), channel_id=1, source_target_pairs={{0,2},{2,0},{4,6},{6,4},{8,10},{10,8},{12,14},{14,12},{16,18},{18,... | collective-permute-start | bytes 4718600 | tf_op jit(solution)/shard_map/gy_core/ppermute | solution.py:437
  58.1 25.7 %collective-permute-start.15 = (bf16[256,3072]{1,0:T(8,128)(2,1)S(1)}, bf16[256,3072]{1,0:T(8,128)(2,1)S(1)}, u32[]{:S(2)}, u32[]{:S(2)}) collective-permute-start(bf16[256,3072]{1,0:T(8,128)(2,1)S(1)} %collective-permute-done.4.refs_4_.refs_0_), channel_id=1, source_target_pairs={{0,2},{2,0},{4,6},{6,4},{8,10},{10,8},{12,14},{14,12},{16,18},{18,... | collective-permute-start | bytes 4718600 | tf_op jit(solution)/shard_map/gy_core/ppermute | solution.py:437
  79.6 4.2 %collective-permute-start.13 = (bf16[256,2048]{1,0:T(8,128)(2,1)S(1)}, bf16[256,2048]{1,0:T(8,128)(2,1)S(1)}, u32[]{:S(2)}, u32[]{:S(2)}) collective-permute-start(bf16[256,2048]{1,0:T(8,128)(2,1)S(1)} %collective-permute-done.12.refs_6_.refs_1_), channel_id=1, source_target_pairs={{0,2},{2,0},{4,6},{6,4},{8,10},{10,8},{12,14},{14,12},{16,18},{18,... | collective-permute-start | bytes 3145736 | tf_op jit(solution)/shard_map/gy_core/ppermute | solution.py:437
  86.2 16.2 %collective-permute-start.17 = (bf16[256,1024]{1,0:T(8,128)(2,1)S(1)}, bf16[256,1024]{1,0:T(8,128)(2,1)S(1)}, u32[]{:S(2)}, u32[]{:S(2)}) collective-permute-start(bf16[256,1024]{1,0:T(8,128)(2,1)S(1)} %slice.69), channel_id=1, source_target_pairs={{0,4},{2,6},{4,0},{6,2},{8,12},{10,14},{12,8},{14,10},{16,20},{18,... | collective-permute-start | bytes 1572872 | tf_op jit(solution)/shard_map/gy_plane_cross_b/ppermute | solution.py:437
  87.2 12.1 %collective-permute-start.18 = (bf16[192,1024]{1,0:T(8,128)(2,1)S(1)}, bf16[192,1024]{1,0:T(8,128)(2,1)S(1)}, u32[]{:S(2)}, u32[]{:S(2)}) collective-permute-start(bf16[192,1024]{1,0:T(8,128)(2,1)S(1)} %get-tuple-element.135), channel_id=1, source_target_pairs={{0,24},{2,26},{4,28},{6,30},{8,16},{10,18},{12,20},{14,22},{16,8},... | collective-permute-start | bytes 1179656 | tf_op jit(solution)/shard_map/grad_w_far/ppermute | solution.py:437
  92.1 10.2 %collective-permute-start.19 = (bf16[4,192,256]{2,1,0:T(8,128)(2,1)S(1)}, bf16[4,192,256]{2,1,0:T(8,128)(2,1)S(1)}, u32[]{:S(2)}, u32[]{:S(2)}) collective-permute-start(bf16[4,192,256]{2,1,0:T(8,128)(2,1)S(1)} %get-tuple-element.146), channel_id=1, source_target_pairs={{0,1},{1,0},{2,3},{3,2},{4,5},{5,4},{6,7},{7,6},{8,9},{9,8},{10,11... | collective-permute-start | bytes 1179656 | tf_op jit(solution)/shard_map/products_seq/ppermute | solution.py:442
  102.4 1.9 %collective-permute-start.21 = (bf16[256,1024]{1,0:T(8,128)(2,1)S(1)}, bf16[256,1024]{1,0:T(8,128)(2,1)S(1)}, u32[]{:S(2)}, u32[]{:S(2)}) collective-permute-start(bf16[256,1024]{1,0:T(8,128)(2,1)S(1)} %collective-permute-done.17.refs_5_.refs_6_), channel_id=1, source_target_pairs={{0,2},{2,0},{4,6},{6,4},{8,10},{10,8},{12,14},{14,12},{16,18},{18,... | collective-permute-start | bytes 1572872 | tf_op jit(solution)/shard_map/gy_core/ppermute | solution.py:437
  102.4 13.4 %collective-permute-start.20 = (bf16[192,1024]{1,0:T(8,128)(2,1)S(1)}, bf16[192,1024]{1,0:T(8,128)(2,1)S(1)}, u32[]{:S(2)}, u32[]{:S(2)}) collective-permute-start(bf16[192,1024]{1,0:T(8,128)(2,1)S(1)} %get-tuple-element.148), channel_id=1, source_target_pairs={{0,24},{2,26},{4,28},{6,30},{8,16},{10,18},{12,20},{14,22},{16,8},... | collective-permute-start | bytes 1179656 | tf_op jit(solution)/shard_map/grad_w_far/ppermute | solution.py:437
  107.6 1.8 %collective-permute-start.22 = (bf16[2,192,256]{2,1,0:T(8,128)(2,1)S(1)}, bf16[2,192,256]{2,1,0:T(8,128)(2,1)S(1)}, u32[]{:S(2)}, u32[]{:S(2)}) collective-permute-start(bf16[2,192,256]{2,1,0:T(8,128)(2,1)S(1)} %slice.81), channel_id=1, source_target_pairs={{0,2},{2,0},{4,6},{6,4},{8,10},{10,8},{12,14},{14,12},{16,18},{18,... | collective-permute-start | bytes 589832 | tf_op jit(solution)/shard_map/products_core/ppermute | solution.py:437
  107.8 11.4 %collective-permute-start.24 = (bf16[4,192,256]{2,1,0:T(8,128)(2,1)S(1)}, bf16[4,192,256]{2,1,0:T(8,128)(2,1)S(1)}, u32[]{:S(2)}, u32[]{:S(2)}) collective-permute-start(bf16[4,192,256]{2,1,0:T(8,128)(2,1)S(1)} %get-tuple-element.158), channel_id=1, source_target_pairs={{0,1},{1,0},{2,3},{3,2},{4,5},{5,4},{6,7},{7,6},{8,9},{9,8},{10,11... | collective-permute-start | bytes 1179656 | tf_op jit(solution)/shard_map/products_seq/ppermute | solution.py:442
  109.5 6.9 %collective-permute-start.23 = (bf16[2,192,256]{2,1,0:T(8,128)(2,1)S(1)}, bf16[2,192,256]{2,1,0:T(8,128)(2,1)S(1)}, u32[]{:S(2)}, u32[]{:S(2)}) collective-permute-start(bf16[2,192,256]{2,1,0:T(8,128)(2,1)S(1)} %pad_maximum_fusion.10), channel_id=1, source_target_pairs={{0,4},{2,6},{4,0},{6,2},{8,12},{10,14},{12,8},{14,10},{16,20},{18,... | collective-permute-start | bytes 589832 | tf_op jit(solution)/shard_map/products_group/ppermute | solution.py:437
  119.4 4.0 %collective-permute-start.25 = (bf16[2,192,256]{2,1,0:T(8,128)(2,1)S(1)}, bf16[2,192,256]{2,1,0:T(8,128)(2,1)S(1)}, u32[]{:S(2)}, u32[]{:S(2)}) collective-permute-start(bf16[2,192,256]{2,1,0:T(8,128)(2,1)S(1)} %slice.86), channel_id=1, source_target_pairs={{0,2},{2,0},{4,6},{6,4},{8,10},{10,8},{12,14},{14,12},{16,18},{18,... | collective-permute-start | bytes 589832 | tf_op jit(solution)/shard_map/products_core/ppermute | solution.py:437
  119.4 17.2 %collective-permute-start.28 = (bf16[192,512]{1,0:T(8,128)(2,1)S(1)}, bf16[192,512]{1,0:T(8,128)(2,1)S(1)}, u32[]{:S(2)}, u32[]{:S(2)}) collective-permute-start(bf16[192,512]{1,0:T(8,128)(2,1)S(1)} %get-tuple-element.187), channel_id=1, source_target_pairs={{0,24},{2,26},{4,28},{6,30},{8,16},{10,18},{12,20},{14,22},{16,8},... | collective-permute-start | bytes 589832 | tf_op jit(solution)/shard_map/grad_w_far/ppermute | solution.py:437
  121.4 15.2 %collective-permute-start.29 = (bf16[192,512]{1,0:T(8,128)(2,1)S(1)}, bf16[192,512]{1,0:T(8,128)(2,1)S(1)}, u32[]{:S(2)}, u32[]{:S(2)}) collective-permute-start(bf16[192,512]{1,0:T(8,128)(2,1)S(1)} %get-tuple-element.188), channel_id=1, source_target_pairs={{0,24},{2,26},{4,28},{6,30},{8,16},{10,18},{12,20},{14,22},{16,8},... | collective-permute-start | bytes 589832 | tf_op jit(solution)/shard_map/grad_w_far/ppermute | solution.py:437
  123.3 7.1 %copy-start.3 = (bf16[2,12,256,128]{3,2,1,0:T(8,128)(2,1)S(1)}, bf16[2,12,256,128]{3,2,1,0:T(8,128)(2,1)}, u32[]{:S(2)}) copy-start(bf16[2,12,256,128]{3,2,1,0:T(8,128)(2,1)} %get-tuple-element.101.low_ref) | copy-start | bytes 4718596
  123.4 14.8 %collective-permute-start.27 = (bf16[2,192,256]{2,1,0:T(8,128)(2,1)S(1)}, bf16[2,192,256]{2,1,0:T(8,128)(2,1)S(1)}, u32[]{:S(2)}, u32[]{:S(2)}) collective-permute-start(bf16[2,192,256]{2,1,0:T(8,128)(2,1)S(1)} %pad_maximum_fusion.12), channel_id=1, source_target_pairs={{0,12},{2,14},{4,8},{6,10},{8,4},{10,6},{12,0},{14,2},{16,28},{18,... | collective-permute-start | bytes 589832 | tf_op jit(solution)/shard_map/products_group/ppermute | solution.py:437
  127.4 13.9 %collective-permute-start.26 = (bf16[2,192,256]{2,1,0:T(8,128)(2,1)S(1)}, bf16[2,192,256]{2,1,0:T(8,128)(2,1)S(1)}, u32[]{:S(2)}, u32[]{:S(2)}) collective-permute-start(bf16[2,192,256]{2,1,0:T(8,128)(2,1)S(1)} %pad_maximum_fusion.11), channel_id=1, source_target_pairs={{0,8},{2,10},{4,12},{6,14},{8,0},{10,2},{12,4},{14,6},{16,24},{18,... | collective-permute-start | bytes 589832 | tf_op jit(solution)/shard_map/products_group/ppermute | solution.py:437
  127.4 3.0 %copy-start.2 = (f32[2,12,256,128]{3,2,1,0:T(8,128)S(1)}, f32[2,12,256,128]{3,2,1,0:T(8,128)}, u32[]{:S(2)}) copy-start(f32[2,12,256,128]{3,2,1,0:T(8,128)} %get-tuple-element.100.inv_ref) | copy-start | bytes 9437188
  127.5 3.0 %copy-start.4 = (bf16[12,256,128]{2,1,0:T(8,128)(2,1)S(1)}, bf16[12,256,128]{2,1,0:T(8,128)(2,1)}, u32[]{:S(2)}) copy-start(bf16[12,256,128]{2,1,0:T(8,128)(2,1)} %get-tuple-element.103.v_ref) | copy-start | bytes 2359300
  129.0 2.4 %copy-start = (f32[12,256,256]{2,1,0:T(8,128)S(1)}, f32[12,256,256]{2,1,0:T(8,128)}, u32[]{:S(2)}) copy-start(f32[12,256,256]{2,1,0:T(8,128)} %get-tuple-element.98.p_ref) | copy-start | bytes 9437188
  129.0 3.3 %copy-start.1 = (f32[2,12,256,128]{3,2,1,0:T(8,128)S(1)}, f32[2,12,256,128]{3,2,1,0:T(8,128)}, u32[]{:S(2)}) copy-start(f32[2,12,256,128]{3,2,1,0:T(8,128)} %get-tuple-element.99.hat_ref) | copy-start | bytes 9437188

commit v8 on v7

--- a/solution.py
+++ b/solution.py
@@ -404,7 +404,7 @@
 
 def finish(kept, far, scale, first, depth, flops, into=()):
     rows, wide = kept.shape
-    tile, place = rows // 4, first // wide
+    tile, place = rows // 2, first // wide
 
     def block(a):
         return pl.BlockSpec((tile, a.shape[1]), lambda i: (i, 0))

time: 146 us -> 146 us (level)
  Pallas kernels: 43.2 us -> 41.5 us
    pallas_call x3, Pallas kernels: 4.45 us -> 2.82 us  [finish(): pl.pallas_call(functools.partial(finish_kernel, scale, len(into)), grid=(...]
  transfers between devices with their start and end apart: 30 -> 30, of which waited for: 14 -> 14; matrix products, arithmetic and copies ran while one was open for 1% -> 1% of each run, Pallas kernels for 25% -> 24%
where the time goes in v8:
time: 146 us
  waiting for transfers between devices  57.9 us (40%)
  Pallas kernels  41.5 us (28%)
  starting transfers between devices  38.4 us (26%)
  local copies, waits for them, and re-layouts  5.28 us (4%)
  other arithmetic  1.61 us (1%)
    ppermute x6, waiting for transfers between devices, swap(): return lax.ppermute(a, 'seq', [(0, 1), (1, 0)])  31.8 us
    ppermute x24, starting transfers between devices, move(): return lax.ppermute(a, 'fsdp', perm)  30.1 us
    ppermute x24, waiting for transfers between devices, move(): return lax.ppermute(a, 'fsdp', perm)  26 us
    pallas_call x2, Pallas kernels, attention_backward(): pl.pallas_call(functools.partial(backward_kernel, per, dim, len(into)), g...  8.85 us
    pallas_call x1, Pallas kernels, attention_probabilities(): pl.pallas_call(functools.partial(probabilities_kernel, per, dim), grid_sp...  8.49 us
    ppermute x6, starting transfers between devices, swap(): return lax.ppermute(a, 'seq', [(0, 1), (1, 0)])  8.32 us
    pallas_call x3, Pallas kernels, weight_terms(): pl.pallas_call(functools.partial(weight_kernel, n, half[1], parts), in_sp...  7.01 us
    pallas_call x2, Pallas kernels, gradient_products(): pl.pallas_call(functools.partial(products_kernel, n, [(first, wide, start...  6.46 us
  transfers between devices with their start and end apart: 30, of which 14 were waited for; matrix products, arithmetic and copies ran while one was open for 1% of the time, Pallas kernels for 24%

profile of v8, /device:TPU:0, one launch (start us, length us, event | category | flops | bytes accessed | tf_op | source)
XLA Modules:
  0.0 145.7 jit_solution(14445153137219000221)
XLA Ops:
  0.6 1.2 dynamic-slice_bitcast_fusion
  1.9 0.9 pad_maximum_fusion
  2.9 3.0 %collective-permute-start.4 = (bf16[256,3072]{1,0:T(8,128)(2,1)}, bf16[256,3072]{1,0:T(8,128)(2,1)S(1)}, u32[]{:S(2)}, u32[]{:S(2)}) collective-permute-start(bf16[256,3072]{1,0:T(8,128)(2,1)} %refs_0_), channel_id=1, source_target_pairs={{0,8},{2,10},{4,12},{6,14},{8,0},{10,2},{12,4},{14,6},{16,24},{18,... | collective-permute-start | bytes 4718600 | tf_op jit(solution)/shard_map/gy_plane/ppermute | solution.py:437
  5.9 1.5 %collective-permute-start.3 = (bf16[256,3072]{1,0:T(8,128)(2,1)}, bf16[256,3072]{1,0:T(8,128)(2,1)S(1)}, u32[]{:S(2)}, u32[]{:S(2)}) collective-permute-start(bf16[256,3072]{1,0:T(8,128)(2,1)} %refs_0_), channel_id=1, source_target_pairs={{0,4},{2,6},{4,0},{6,2},{8,12},{10,14},{12,8},{14,10},{16,20},{18,... | collective-permute-start | bytes 4718600 | tf_op jit(solution)/shard_map/gy_cross/ppermute | solution.py:437
  7.4 1.5 %collective-permute-start = (bf16[2,128,1536]{2,1,0:T(8,128)(2,1)}, bf16[2,128,1536]{2,1,0:T(8,128)(2,1)}, u32[]{:S(2)}, u32[]{:S(2)}) collective-permute-start(bf16[2,128,1536]{2,1,0:T(8,128)(2,1)} %pad_maximum_fusion), channel_id=1, source_target_pairs={{0,1},{1,0},{2,3},{3,2},{4,5},{5,4},{6,7},{7,6},{8,9},{9,8},{10,11... | collective-permute-start | bytes 2359304 | tf_op jit(solution)/shard_map/qk_seq/ppermute | solution.py:442
  8.9 1.7 %collective-permute-start.5 = (bf16[192,3072]{1,0:T(8,128)(2,1)}, bf16[192,3072]{1,0:T(8,128)(2,1)}, u32[]{:S(2)}, u32[]{:S(2)}) collective-permute-start(bf16[192,3072]{1,0:T(8,128)(2,1)} %refs_1_.1), channel_id=1, source_target_pairs={{8,16},{10,18},{12,20},{14,22},{16,8},{18,10},{20,12},{22,14},{9,1... | collective-permute-start | bytes 3538952 | tf_op jit(solution)/shard_map/w_middle/ppermute | solution.py:437
  10.6 0.8 constant_dynamic-slice_fusion
  11.4 0.5 collective-permute-start.1
  11.9 0.1 copy.17.col_ref
  12.0 0.1 pad_add_fusion.place
  12.1 16.1 %collective-permute-done.came_ref = bf16[2,128,1536]{2,1,0:T(8,128)(2,1)} collective-permute-done((bf16[2,128,1536]{2,1,0:T(8,128)(2,1)}, bf16[2,128,1536]{2,1,0:T(8,128)(2,1)}, u32[]{:S(2)}, u32[]{:S(2)}) %collective-permute-start) | collective-permute-done | bytes 786464 | tf_op jit(solution)/shard_map/qk_seq/ppermute | solution.py:442
  28.2 8.5 %attention_probabilities.1 = (f32[12,256,256]{2,1,0:T(8,128)}, f32[2,12,256,128]{3,2,1,0:T(8,128)}, f32[2,12,256,128]{3,2,1,0:T(8,128)}, bf16[2,12,256,128]{3,2,1,0:T(8,128)(2,1)}, bf16[12,256,256]{2,1,0:T(8,128)(2,1)S(1)}) custom-call(s32[4]{0:T(128)S(1)} %pad_add_fusion.place, bf16[128,3072]{1,0:T(8,128)(2,1)} %q_ref.1, bf16[128,3072]{1,0:T(8,128)(2,1)} %k_ref.1, ...), custom_call_target="tpu_custom_call" | custom-call | flops 1000 | bytes 1000 | tf_op jit(solution)/shard_map/attention_probabilities/pallas_call | solution.py:219
  36.7 3.9 %attention_attended.1 = (bf16[4,192,256]{2,1,0:T(8,128)(2,1)S(1)}, bf16[4,192,256]{2,1,0:T(8,128)(2,1)S(1)}, bf16[12,256,128]{2,1,0:T(8,128)(2,1)}) custom-call(s32[4]{0:T(128)S(1)} %pad_add_fusion.place, bf16[12,256,256]{2,1,0:T(8,128)(2,1)S(1)} %get-tuple-element.102.p_low_ref, bf16[128,3072]{1,0:T(8,128)(2,1)} %v_ref.1, ...), custom_call_target="tpu_custom_call" | custom-call | flops 1000 | bytes 1000 | tf_op jit(solution)/shard_map/attention_attended/pallas_call | solution.py:242
  40.6 1.7 %collective-permute-done.2 = bf16[4,192,256]{2,1,0:T(8,128)(2,1)S(1)} collective-permute-done((bf16[4,192,256]{2,1,0:T(8,128)(2,1)S(1)}, bf16[4,192,256]{2,1,0:T(8,128)(2,1)S(1)}, u32[]{:S(2)}, u32[]{:S(2)}) %collective-permute-start.2) | collective-permute-done | bytes 393248 | tf_op jit(solution)/shard_map/att_core/ppermute | solution.py:437
  42.4 0.1 collective-permute-start.10
  42.6 1.0 collective-permute-start.6
  43.7 0.5 collective-permute-start.7
  44.2 1.6 %collective-permute-start.9 = (bf16[2,192,256]{2,1,0:T(8,128)(2,1)S(1)}, bf16[2,192,256]{2,1,0:T(8,128)(2,1)S(1)}, u32[]{:S(2)}, u32[]{:S(2)}) collective-permute-start(bf16[2,192,256]{2,1,0:T(8,128)(2,1)S(1)} %pad_maximum_fusion.5), channel_id=1, source_target_pairs={{0,1},{1,0},{2,3},{3,2},{4,5},{5,4},{6,7},{7,6},{8,9},{9,8},{10,11... | collective-permute-start | bytes 589832 | tf_op jit(solution)/shard_map/att_seq/ppermute | solution.py:442
  45.8 2.2 %collective-permute-start.8 = (bf16[2,192,256]{2,1,0:T(8,128)(2,1)S(1)}, bf16[2,192,256]{2,1,0:T(8,128)(2,1)S(1)}, u32[]{:S(2)}, u32[]{:S(2)}) collective-permute-start(bf16[2,192,256]{2,1,0:T(8,128)(2,1)S(1)} %pad_maximum_fusion.8), channel_id=1, source_target_pairs={{0,12},{2,14},{4,8},{6,10},{8,4},{10,6},{12,0},{14,2},{16,28},{18,... | collective-permute-start | bytes 589832 | tf_op jit(solution)/shard_map/att_group/ppermute | solution.py:437
  48.0 1.9 %collective-permute-done.6 = bf16[2,192,256]{2,1,0:T(8,128)(2,1)S(1)} collective-permute-done((bf16[2,192,256]{2,1,0:T(8,128)(2,1)S(1)}, bf16[2,192,256]{2,1,0:T(8,128)(2,1)S(1)}, u32[]{:S(2)}, u32[]{:S(2)}) %collective-permute-start.6) | collective-permute-done | bytes 196640 | tf_op jit(solution)/shard_map/att_group/ppermute | solution.py:437
  49.9 4.6 %collective-permute-start.16 = (bf16[192,3072]{1,0:T(8,128)(2,1)}, bf16[192,3072]{1,0:T(8,128)(2,1)S(1)}, u32[]{:S(2)}, u32[]{:S(2)}) collective-permute-start(bf16[192,3072]{1,0:T(8,128)(2,1)} %refs_1_.1), channel_id=1, source_target_pairs={{0,24},{2,26},{4,28},{6,30},{24,0},{26,2},{28,4},{30,6},{1,25},{3,... | collective-permute-start | bytes 3538952 | tf_op jit(solution)/shard_map/w_ends/ppermute | solution.py:437
  54.5 0.1 slice.68
  54.6 0.8 collective-permute-done.8
  55.3 1.1 collective-permute-start.12
  56.5 1.6 %collective-permute-start.11 = (bf16[6,192,256]{2,1,0:T(8,128)(2,1)S(1)}, bf16[6,192,256]{2,1,0:T(8,128)(2,1)S(1)}, u32[]{:S(2)}, u32[]{:S(2)}) collective-permute-start(bf16[6,192,256]{2,1,0:T(8,128)(2,1)S(1)} %pad_maximum_fusion.2), channel_id=1, source_target_pairs={{0,1},{1,0},{2,3},{3,2},{4,5},{5,4},{6,7},{7,6},{8,9},{9,8},{10,11... | collective-permute-start | bytes 1769480 | tf_op jit(solution)/shard_map/att_seq/ppermute | solution.py:442
  58.1 0.5 collective-permute-start.15
  58.6 2.5 %hold.1 = (bf16[256,3072]{1,0:T(8,128)(2,1)S(1)}, bf16[192,3072]{1,0:T(8,128)(2,1)S(1)}) custom-call(bf16[256,3072]{1,0:T(8,128)(2,1)} %refs_0_, bf16[192,3072]{1,0:T(8,128)(2,1)} %refs_1_.1), custom_call_target="tpu_custom_call" | custom-call | flops 1000 | bytes 1000 | tf_op jit(solution)/shard_map/hold/pallas_call | solution.py:300
  61.1 9.8 %collective-permute-done.11 = bf16[6,192,256]{2,1,0:T(8,128)(2,1)S(1)} collective-permute-done((bf16[6,192,256]{2,1,0:T(8,128)(2,1)S(1)}, bf16[6,192,256]{2,1,0:T(8,128)(2,1)S(1)}, u32[]{:S(2)}, u32[]{:S(2)}) %collective-permute-start.11) | collective-permute-done | bytes 589856 | tf_op jit(solution)/shard_map/att_seq/ppermute | solution.py:442
  71.0 8.6 %collective-permute-done.12.refs_6_.refs_1_ = bf16[256,2048]{1,0:T(8,128)(2,1)S(1)} collective-permute-done((bf16[256,2048]{1,0:T(8,128)(2,1)S(1)}, bf16[256,2048]{1,0:T(8,128)(2,1)S(1)}, u32[]{:S(2)}, u32[]{:S(2)}) %collective-permute-start.12) | collective-permute-done | bytes 1048608 | tf_op jit(solution)/shard_map/gy_plane_cross_a/ppermute | solution.py:437
  79.6 2.6 %collective-permute-done.16.end_ref = bf16[192,3072]{1,0:T(8,128)(2,1)S(1)} collective-permute-done((bf16[192,3072]{1,0:T(8,128)(2,1)}, bf16[192,3072]{1,0:T(8,128)(2,1)S(1)}, u32[]{:S(2)}, u32[]{:S(2)}) %collective-permute-start.16) | collective-permute-done | bytes 1179680 | tf_op jit(solution)/shard_map/w_ends/ppermute | solution.py:437
  82.3 1.4 choose.1.far_ref
  83.8 2.3 %weight_terms.3 = (bf16[192,1024]{1,0:T(8,128)(2,1)S(1)}, f32[192,1024]{1,0:T(8,128)S(1)}) custom-call(s32[4]{0:T(128)S(1)} %pad_add_fusion.place, bf16[8,192,256]{2,1,0:T(8,128)(2,1)S(1)} %constant_dynamic-update-slice_fusion.own_ref, bf16[8,192,256]{2,1,0:T(8,128)(2,1)S(1)} %pad_maximum_fusion.1.other_ref, ...), custom_call_target="tpu_custom_call" | custom-call | flops 1000 | bytes 1000 | tf_op jit(solution)/shard_map/weight_terms/pallas_call | solution.py:383
  86.2 1.0 collective-permute-start.17
  87.2 1.7 %collective-permute-start.18 = (bf16[192,1024]{1,0:T(8,128)(2,1)S(1)}, bf16[192,1024]{1,0:T(8,128)(2,1)S(1)}, u32[]{:S(2)}, u32[]{:S(2)}) collective-permute-start(bf16[192,1024]{1,0:T(8,128)(2,1)S(1)} %get-tuple-element.135), channel_id=1, source_target_pairs={{0,24},{2,26},{4,28},{6,30},{8,16},{10,18},{12,20},{14,22},{16,8},... | collective-permute-start | bytes 1179656 | tf_op jit(solution)/shard_map/grad_w_far/ppermute | solution.py:437
  88.9 3.2 %gradient_products.2 = (bf16[4,192,256]{2,1,0:T(8,128)(2,1)S(1)}, bf16[4,192,256]{2,1,0:T(8,128)(2,1)S(1)}) custom-call(s32[4]{0:T(128)S(1)} %pad_add_fusion.place, bf16[192,3072]{1,0:T(8,128)(2,1)S(1)} %get-tuple-element.137.w_ref, bf16[192,3072]{1,0:T(8,128)(2,1)S(1)} %choose.1.far_ref, bf16[256,3072]{1,0:T(8,128)(2,1)S(1)} %get-tuple-element.159.refs_0_.refs_4_, ...), custom_call_target="tpu_custom_call" | custom-call | flops 1000 | bytes 1000 | tf_op jit(solution)/shard_map/gradient_products/pallas_call | solution.py:351
  92.1 1.6 %collective-permute-start.19 = (bf16[4,192,256]{2,1,0:T(8,128)(2,1)S(1)}, bf16[4,192,256]{2,1,0:T(8,128)(2,1)S(1)}, u32[]{:S(2)}, u32[]{:S(2)}) collective-permute-start(bf16[4,192,256]{2,1,0:T(8,128)(2,1)S(1)} %get-tuple-element.146), channel_id=1, source_target_pairs={{0,1},{1,0},{2,3},{3,2},{4,5},{5,4},{6,7},{7,6},{8,9},{9,8},{10,11... | collective-permute-start | bytes 1179656 | tf_op jit(solution)/shard_map/products_seq/ppermute | solution.py:442
  93.7 2.3 %weight_terms.4 = (bf16[192,1024]{1,0:T(8,128)(2,1)S(1)}, f32[192,1024]{1,0:T(8,128)S(1)}) custom-call(s32[4]{0:T(128)S(1)} %pad_add_fusion.place, bf16[8,192,256]{2,1,0:T(8,128)(2,1)S(1)} %constant_dynamic-update-slice_fusion.own_ref, bf16[8,192,256]{2,1,0:T(8,128)(2,1)S(1)} %pad_maximum_fusion.1.other_ref, ...), custom_call_target="tpu_custom_call" | custom-call | flops 1000 | bytes 1000 | tf_op jit(solution)/shard_map/weight_terms/pallas_call | solution.py:383
  96.1 3.2 %collective-permute-done.18.refs_0_ = bf16[192,1024]{1,0:T(8,128)(2,1)S(1)} collective-permute-done((bf16[192,1024]{1,0:T(8,128)(2,1)S(1)}, bf16[192,1024]{1,0:T(8,128)(2,1)S(1)}, u32[]{:S(2)}, u32[]{:S(2)}) %collective-permute-start.18) | collective-permute-done | bytes 393248 | tf_op jit(solution)/shard_map/grad_w_far/ppermute | solution.py:437
  99.2 3.1 %collective-permute-done.19 = bf16[4,192,256]{2,1,0:T(8,128)(2,1)S(1)} collective-permute-done((bf16[4,192,256]{2,1,0:T(8,128)(2,1)S(1)}, bf16[4,192,256]{2,1,0:T(8,128)(2,1)S(1)}, u32[]{:S(2)}, u32[]{:S(2)}) %collective-permute-start.19) | collective-permute-done | bytes 393248 | tf_op jit(solution)/shard_map/products_seq/ppermute | solution.py:442
  102.4 1.8 %collective-permute-start.20 = (bf16[192,1024]{1,0:T(8,128)(2,1)S(1)}, bf16[192,1024]{1,0:T(8,128)(2,1)S(1)}, u32[]{:S(2)}, u32[]{:S(2)}) collective-permute-start(bf16[192,1024]{1,0:T(8,128)(2,1)S(1)} %get-tuple-element.148), channel_id=1, source_target_pairs={{0,24},{2,26},{4,28},{6,30},{8,16},{10,18},{12,20},{14,22},{16,8},... | collective-permute-start | bytes 1179656 | tf_op jit(solution)/shard_map/grad_w_far/ppermute | solution.py:437
  104.2 0.1 collective-permute-done.21.refs_7_
  104.3 3.2 %gradient_products.3 = (bf16[4,192,256]{2,1,0:T(8,128)(2,1)S(1)}, bf16[4,192,256]{2,1,0:T(8,128)(2,1)S(1)}) custom-call(s32[4]{0:T(128)S(1)} %pad_add_fusion.place, bf16[192,3072]{1,0:T(8,128)(2,1)S(1)} %get-tuple-element.137.w_ref, bf16[192,3072]{1,0:T(8,128)(2,1)S(1)} %choose.1.far_ref, bf16[256,3072]{1,0:T(8,128)(2,1)S(1)} %collective-permute-done.4.refs_4_.refs_0_, ...), custom_call_target="tpu_custom_call" | custom-call | flops 1000 | bytes 1000 | tf_op jit(solution)/shard_map/gradient_products/pallas_call | solution.py:351
  107.5 0.1 add_convert_fusion.1
  107.6 0.2 collective-permute-start.22
  107.8 1.5 %collective-permute-start.24 = (bf16[4,192,256]{2,1,0:T(8,128)(2,1)S(1)}, bf16[4,192,256]{2,1,0:T(8,128)(2,1)S(1)}, u32[]{:S(2)}, u32[]{:S(2)}) collective-permute-start(bf16[4,192,256]{2,1,0:T(8,128)(2,1)S(1)} %get-tuple-element.158), channel_id=1, source_target_pairs={{0,1},{1,0},{2,3},{3,2},{4,5},{5,4},{6,7},{7,6},{8,9},{9,8},{10,11... | collective-permute-start | bytes 1179656 | tf_op jit(solution)/shard_map/products_seq/ppermute | solution.py:442
  109.5 1.2 collective-permute-start.23
  110.6 2.3 %weight_terms.5 = (bf16[192,512]{1,0:T(8,128)(2,1)S(1)}, bf16[192,512]{1,0:T(8,128)(2,1)S(1)}, f32[192,1024]{1,0:T(8,128)S(1)}) custom-call(s32[4]{0:T(128)S(1)} %pad_add_fusion.place, bf16[8,192,256]{2,1,0:T(8,128)(2,1)S(1)} %constant_dynamic-update-slice_fusion.own_ref, bf16[8,192,256]{2,1,0:T(8,128)(2,1)S(1)} %pad_maximum_fusion.1.other_ref, ...), custom_call_target="tpu_custom_call" | custom-call | flops 1000 | bytes 1000 | tf_op jit(solution)/shard_map/weight_terms/pallas_call | solution.py:383
  113.0 2.8 %collective-permute-done.20.refs_0_ = bf16[192,1024]{1,0:T(8,128)(2,1)S(1)} collective-permute-done((bf16[192,1024]{1,0:T(8,128)(2,1)S(1)}, bf16[192,1024]{1,0:T(8,128)(2,1)S(1)}, u32[]{:S(2)}, u32[]{:S(2)}) %collective-permute-start.20) | collective-permute-done | bytes 393248 | tf_op jit(solution)/shard_map/grad_w_far/ppermute | solution.py:437
  115.8 0.6 collective-permute-done.23
  116.4 2.8 %collective-permute-done.24 = bf16[4,192,256]{2,1,0:T(8,128)(2,1)S(1)} collective-permute-done((bf16[4,192,256]{2,1,0:T(8,128)(2,1)S(1)}, bf16[4,192,256]{2,1,0:T(8,128)(2,1)S(1)}, u32[]{:S(2)}, u32[]{:S(2)}) %collective-permute-start.24) | collective-permute-done | bytes 393248 | tf_op jit(solution)/shard_map/products_seq/ppermute | solution.py:442
  119.2 0.1 add_convert_fusion
  119.4 2.0 %collective-permute-start.28 = (bf16[192,512]{1,0:T(8,128)(2,1)S(1)}, bf16[192,512]{1,0:T(8,128)(2,1)S(1)}, u32[]{:S(2)}, u32[]{:S(2)}) collective-permute-start(bf16[192,512]{1,0:T(8,128)(2,1)S(1)} %get-tuple-element.187), channel_id=1, source_target_pairs={{0,24},{2,26},{4,28},{6,30},{8,16},{10,18},{12,20},{14,22},{16,8},... | collective-permute-start | bytes 589832 | tf_op jit(solution)/shard_map/grad_w_far/ppermute | solution.py:437
  121.4 1.9 %collective-permute-start.29 = (bf16[192,512]{1,0:T(8,128)(2,1)S(1)}, bf16[192,512]{1,0:T(8,128)(2,1)S(1)}, u32[]{:S(2)}, u32[]{:S(2)}) collective-permute-start(bf16[192,512]{1,0:T(8,128)(2,1)S(1)} %get-tuple-element.188), channel_id=1, source_target_pairs={{0,24},{2,26},{4,28},{6,30},{8,16},{10,18},{12,20},{14,22},{16,8},... | collective-permute-start | bytes 589832 | tf_op jit(solution)/shard_map/grad_w_far/ppermute | solution.py:437
  123.4 3.9 %collective-permute-start.27 = (bf16[2,192,256]{2,1,0:T(8,128)(2,1)S(1)}, bf16[2,192,256]{2,1,0:T(8,128)(2,1)S(1)}, u32[]{:S(2)}, u32[]{:S(2)}) collective-permute-start(bf16[2,192,256]{2,1,0:T(8,128)(2,1)S(1)} %pad_maximum_fusion.12), channel_id=1, source_target_pairs={{0,12},{2,14},{4,8},{6,10},{8,4},{10,6},{12,0},{14,2},{16,28},{18,... | collective-permute-start | bytes 589832 | tf_op jit(solution)/shard_map/products_group/ppermute | solution.py:437
  127.5 0.9 finish.3.refs_1_
  128.4 0.9 finish.4.refs_2_
  129.4 0.5 copy-done.2
  129.9 0.2 copy-done.4
  130.1 1.2 copy-done
  131.3 0.9 copy-done.1
  132.2 4.4 %attention_backward.2 = (bf16[12,256,128]{2,1,0:T(8,128)(2,1)}, bf16[12,256,128]{2,1,0:T(8,128)(2,1)}, bf16[12,256,128]{2,1,0:T(8,128)(2,1)}) custom-call(s32[4]{0:T(128)S(1)} %pad_add_fusion.place, f32[12,256,256]{2,1,0:T(8,128)S(1)} %copy-done, f32[2,12,256,128]{3,2,1,0:T(8,128)S(1)} %copy-done.1, f32[2,12,256,128]{3,2,1,0:T(8,128)S(1)} %copy-done.2, ...), custom_call_target="tpu_custom_call" | custom-call | flops 1000 | bytes 1000 | tf_op jit(solution)/shard_map/attention_backward/pallas_call | solution.py:268
  136.6 1.0 finish.5
  137.6 3.7 %collective-permute-done.26 = bf16[2,192,256]{2,1,0:T(8,128)(2,1)S(1)} collective-permute-done((bf16[2,192,256]{2,1,0:T(8,128)(2,1)S(1)}, bf16[2,192,256]{2,1,0:T(8,128)(2,1)S(1)}, u32[]{:S(2)}, u32[]{:S(2)}) %collective-permute-start.26) | collective-permute-done | bytes 196640 | tf_op jit(solution)/shard_map/products_group/ppermute | solution.py:437
  141.3 4.4 %attention_backward.3 = (bf16[12,256,128]{2,1,0:T(8,128)(2,1)}, bf16[12,256,128]{2,1,0:T(8,128)(2,1)}, bf16[12,256,128]{2,1,0:T(8,128)(2,1)}) custom-call(s32[4]{0:T(128)S(1)} %pad_add_fusion.place, f32[12,256,256]{2,1,0:T(8,128)S(1)} %copy-done, f32[2,12,256,128]{3,2,1,0:T(8,128)S(1)} %copy-done.1, ...), custom_call_target="tpu_custom_call", output_to_operand_aliasing={{0}: (9, {}), {1}: (10, {}), {2}: (11, {})} | custom-call | flops 1000 | bytes 1000 | tf_op jit(solution)/shard_map/attention_backward/pallas_call | solution.py:268
  (61 shorter events, 0.9 us)
Async XLA Ops:
  0.6 10.0 %copy-start.8 = (bf16[128,3072]{1,0:T(8,128)(2,1)S(1)}, bf16[128,3072]{1,0:T(8,128)(2,1)}, u32[]{:S(2)}) copy-start(bf16[128,3072]{1,0:T(8,128)(2,1)} %v_ref.1) | copy-start | bytes 2359300
  1.9 10.0 %copy-start.7 = (s32[1,256]{1,0:T(1,128)S(1)}, s32[1,256]{1,0:T(1,128)}, u32[]{:S(2)}) copy-start(s32[1,256]{1,0:T(1,128)} %row_ref.1) | copy-start | bytes 3076
  1.9 26.3 %copy-start.5 = (f32[128]{0:T(128)S(1)}, f32[128]{0:T(128)}, u32[]{:S(2)}) copy-start(f32[128]{0:T(128)} %param.12) | copy-start | bytes 1540
  1.9 26.3 %copy-start.6 = (f32[128]{0:T(128)S(1)}, f32[128]{0:T(128)}, u32[]{:S(2)}) copy-start(f32[128]{0:T(128)} %param.13) | copy-start | bytes 1540
  2.9 39.5 %collective-permute-start.4 = (bf16[256,3072]{1,0:T(8,128)(2,1)}, bf16[256,3072]{1,0:T(8,128)(2,1)S(1)}, u32[]{:S(2)}, u32[]{:S(2)}) collective-permute-start(bf16[256,3072]{1,0:T(8,128)(2,1)} %refs_0_), channel_id=1, source_target_pairs={{0,8},{2,10},{4,12},{6,14},{8,0},{10,2},{12,4},{14,6},{16,24},{18,... | collective-permute-start | bytes 4718600 | tf_op jit(solution)/shard_map/gy_plane/ppermute | solution.py:437
  5.9 36.5 %collective-permute-start.3 = (bf16[256,3072]{1,0:T(8,128)(2,1)}, bf16[256,3072]{1,0:T(8,128)(2,1)S(1)}, u32[]{:S(2)}, u32[]{:S(2)}) collective-permute-start(bf16[256,3072]{1,0:T(8,128)(2,1)} %refs_0_), channel_id=1, source_target_pairs={{0,4},{2,6},{4,0},{6,2},{8,12},{10,14},{12,8},{14,10},{16,20},{18,... | collective-permute-start | bytes 4718600 | tf_op jit(solution)/shard_map/gy_cross/ppermute | solution.py:437
  7.4 20.8 %collective-permute-start = (bf16[2,128,1536]{2,1,0:T(8,128)(2,1)}, bf16[2,128,1536]{2,1,0:T(8,128)(2,1)}, u32[]{:S(2)}, u32[]{:S(2)}) collective-permute-start(bf16[2,128,1536]{2,1,0:T(8,128)(2,1)} %pad_maximum_fusion), channel_id=1, source_target_pairs={{0,1},{1,0},{2,3},{3,2},{4,5},{5,4},{6,7},{7,6},{8,9},{9,8},{10,11... | collective-permute-start | bytes 2359304 | tf_op jit(solution)/shard_map/qk_seq/ppermute | solution.py:442
  8.9 31.7 %collective-permute-start.5 = (bf16[192,3072]{1,0:T(8,128)(2,1)}, bf16[192,3072]{1,0:T(8,128)(2,1)}, u32[]{:S(2)}, u32[]{:S(2)}) collective-permute-start(bf16[192,3072]{1,0:T(8,128)(2,1)} %refs_1_.1), channel_id=1, source_target_pairs={{8,16},{10,18},{12,20},{14,22},{16,8},{18,10},{20,12},{22,14},{9,1... | collective-permute-start | bytes 3538952 | tf_op jit(solution)/shard_map/w_middle/ppermute | solution.py:437
  11.4 25.3 %collective-permute-start.1 = (bf16[128,1536]{1,0:T(8,128)(2,1)}, bf16[128,1536]{1,0:T(8,128)(2,1)}, u32[]{:S(2)}, u32[]{:S(2)}) collective-permute-start(bf16[128,1536]{1,0:T(8,128)(2,1)} %constant_dynamic-slice_fusion), channel_id=1, source_target_pairs={{0,1},{1,0},{2,3},{3,2},{4,5},{5,4},{6,7},{7,6},{8,9},{9,8},{10,11... | collective-permute-start | bytes 1179656 | tf_op jit(solution)/shard_map/v_seq/ppermute | solution.py:442
  40.6 1.7 %collective-permute-start.2 = (bf16[4,192,256]{2,1,0:T(8,128)(2,1)S(1)}, bf16[4,192,256]{2,1,0:T(8,128)(2,1)S(1)}, u32[]{:S(2)}, u32[]{:S(2)}) collective-permute-start(bf16[4,192,256]{2,1,0:T(8,128)(2,1)S(1)} %get-tuple-element.105), channel_id=1, source_target_pairs={{0,2},{2,0},{4,6},{6,4},{8,10},{10,8},{12,14},{14,12},{16,18},{18,... | collective-permute-start | bytes 1179656 | tf_op jit(solution)/shard_map/att_core/ppermute | solution.py:437
  42.4 13.0 %collective-permute-start.10 = (bf16[256,3072]{1,0:T(8,128)(2,1)}, bf16[256,3072]{1,0:T(8,128)(2,1)S(1)}, u32[]{:S(2)}, u32[]{:S(2)}) collective-permute-start(bf16[256,3072]{1,0:T(8,128)(2,1)} %refs_0_), channel_id=1, source_target_pairs={{0,2},{2,0},{4,6},{6,4},{8,10},{10,8},{12,14},{14,12},{16,18},{18,... | collective-permute-start | bytes 4718600 | tf_op jit(solution)/shard_map/gy_core/ppermute | solution.py:437
  42.6 7.2 %collective-permute-start.6 = (bf16[2,192,256]{2,1,0:T(8,128)(2,1)S(1)}, bf16[2,192,256]{2,1,0:T(8,128)(2,1)S(1)}, u32[]{:S(2)}, u32[]{:S(2)}) collective-permute-start(bf16[2,192,256]{2,1,0:T(8,128)(2,1)S(1)} %pad_maximum_fusion.6), channel_id=1, source_target_pairs={{0,4},{2,6},{4,0},{6,2},{8,12},{10,14},{12,8},{14,10},{16,20},{18,... | collective-permute-start | bytes 589832 | tf_op jit(solution)/shard_map/att_group/ppermute | solution.py:437
  43.7 10.9 %collective-permute-start.7 = (bf16[2,192,256]{2,1,0:T(8,128)(2,1)S(1)}, bf16[2,192,256]{2,1,0:T(8,128)(2,1)S(1)}, u32[]{:S(2)}, u32[]{:S(2)}) collective-permute-start(bf16[2,192,256]{2,1,0:T(8,128)(2,1)S(1)} %pad_maximum_fusion.7), channel_id=1, source_target_pairs={{0,8},{2,10},{4,12},{6,14},{8,0},{10,2},{12,4},{14,6},{16,24},{18,... | collective-permute-start | bytes 589832 | tf_op jit(solution)/shard_map/att_group/ppermute | solution.py:437
  44.2 10.4 %collective-permute-start.9 = (bf16[2,192,256]{2,1,0:T(8,128)(2,1)S(1)}, bf16[2,192,256]{2,1,0:T(8,128)(2,1)S(1)}, u32[]{:S(2)}, u32[]{:S(2)}) collective-permute-start(bf16[2,192,256]{2,1,0:T(8,128)(2,1)S(1)} %pad_maximum_fusion.5), channel_id=1, source_target_pairs={{0,1},{1,0},{2,3},{3,2},{4,5},{5,4},{6,7},{7,6},{8,9},{9,8},{10,11... | collective-permute-start | bytes 589832 | tf_op jit(solution)/shard_map/att_seq/ppermute | solution.py:442
  45.8 9.5 %collective-permute-start.8 = (bf16[2,192,256]{2,1,0:T(8,128)(2,1)S(1)}, bf16[2,192,256]{2,1,0:T(8,128)(2,1)S(1)}, u32[]{:S(2)}, u32[]{:S(2)}) collective-permute-start(bf16[2,192,256]{2,1,0:T(8,128)(2,1)S(1)} %pad_maximum_fusion.8), channel_id=1, source_target_pairs={{0,12},{2,14},{4,8},{6,10},{8,4},{10,6},{12,0},{14,2},{16,28},{18,... | collective-permute-start | bytes 589832 | tf_op jit(solution)/shard_map/att_group/ppermute | solution.py:437
  49.9 32.4 %collective-permute-start.16 = (bf16[192,3072]{1,0:T(8,128)(2,1)}, bf16[192,3072]{1,0:T(8,128)(2,1)S(1)}, u32[]{:S(2)}, u32[]{:S(2)}) collective-permute-start(bf16[192,3072]{1,0:T(8,128)(2,1)} %refs_1_.1), channel_id=1, source_target_pairs={{0,24},{2,26},{4,28},{6,30},{24,0},{26,2},{28,4},{30,6},{1,25},{3,... | collective-permute-start | bytes 3538952 | tf_op jit(solution)/shard_map/w_ends/ppermute | solution.py:437
  55.3 24.3 %collective-permute-start.12 = (bf16[256,2048]{1,0:T(8,128)(2,1)S(1)}, bf16[256,2048]{1,0:T(8,128)(2,1)S(1)}, u32[]{:S(2)}, u32[]{:S(2)}) collective-permute-start(bf16[256,2048]{1,0:T(8,128)(2,1)S(1)} %slice.68), channel_id=1, source_target_pairs={{0,4},{2,6},{4,0},{6,2},{8,12},{10,14},{12,8},{14,10},{16,20},{18,... | collective-permute-start | bytes 3145736 | tf_op jit(solution)/shard_map/gy_plane_cross_a/ppermute | solution.py:437
  56.5 14.4 %collective-permute-start.11 = (bf16[6,192,256]{2,1,0:T(8,128)(2,1)S(1)}, bf16[6,192,256]{2,1,0:T(8,128)(2,1)S(1)}, u32[]{:S(2)}, u32[]{:S(2)}) collective-permute-start(bf16[6,192,256]{2,1,0:T(8,128)(2,1)S(1)} %pad_maximum_fusion.2), channel_id=1, source_target_pairs={{0,1},{1,0},{2,3},{3,2},{4,5},{5,4},{6,7},{7,6},{8,9},{9,8},{10,11... | collective-permute-start | bytes 1769480 | tf_op jit(solution)/shard_map/att_seq/ppermute | solution.py:442
  58.1 25.7 %collective-permute-start.14 = (bf16[256,3072]{1,0:T(8,128)(2,1)S(1)}, bf16[256,3072]{1,0:T(8,128)(2,1)S(1)}, u32[]{:S(2)}, u32[]{:S(2)}) collective-permute-start(bf16[256,3072]{1,0:T(8,128)(2,1)S(1)} %collective-permute-done.3.refs_2_.refs_1_.refs_5_), channel_id=1, source_target_pairs={{0,2},{2,0},{4,6},{6,4},{8,10},{10,8},{12,14},{14,12},{16,18},{18,... | collective-permute-start | bytes 4718600 | tf_op jit(solution)/shard_map/gy_core/ppermute | solution.py:437
  58.1 25.7 %collective-permute-start.15 = (bf16[256,3072]{1,0:T(8,128)(2,1)S(1)}, bf16[256,3072]{1,0:T(8,128)(2,1)S(1)}, u32[]{:S(2)}, u32[]{:S(2)}) collective-permute-start(bf16[256,3072]{1,0:T(8,128)(2,1)S(1)} %collective-permute-done.4.refs_4_.refs_0_), channel_id=1, source_target_pairs={{0,2},{2,0},{4,6},{6,4},{8,10},{10,8},{12,14},{14,12},{16,18},{18,... | collective-permute-start | bytes 4718600 | tf_op jit(solution)/shard_map/gy_core/ppermute | solution.py:437
  79.6 4.2 %collective-permute-start.13 = (bf16[256,2048]{1,0:T(8,128)(2,1)S(1)}, bf16[256,2048]{1,0:T(8,128)(2,1)S(1)}, u32[]{:S(2)}, u32[]{:S(2)}) collective-permute-start(bf16[256,2048]{1,0:T(8,128)(2,1)S(1)} %collective-permute-done.12.refs_6_.refs_1_), channel_id=1, source_target_pairs={{0,2},{2,0},{4,6},{6,4},{8,10},{10,8},{12,14},{14,12},{16,18},{18,... | collective-permute-start | bytes 3145736 | tf_op jit(solution)/shard_map/gy_core/ppermute | solution.py:437
  86.2 16.2 %collective-permute-start.17 = (bf16[256,1024]{1,0:T(8,128)(2,1)S(1)}, bf16[256,1024]{1,0:T(8,128)(2,1)S(1)}, u32[]{:S(2)}, u32[]{:S(2)}) collective-permute-start(bf16[256,1024]{1,0:T(8,128)(2,1)S(1)} %slice.69), channel_id=1, source_target_pairs={{0,4},{2,6},{4,0},{6,2},{8,12},{10,14},{12,8},{14,10},{16,20},{18,... | collective-permute-start | bytes 1572872 | tf_op jit(solution)/shard_map/gy_plane_cross_b/ppermute | solution.py:437
  87.2 12.1 %collective-permute-start.18 = (bf16[192,1024]{1,0:T(8,128)(2,1)S(1)}, bf16[192,1024]{1,0:T(8,128)(2,1)S(1)}, u32[]{:S(2)}, u32[]{:S(2)}) collective-permute-start(bf16[192,1024]{1,0:T(8,128)(2,1)S(1)} %get-tuple-element.135), channel_id=1, source_target_pairs={{0,24},{2,26},{4,28},{6,30},{8,16},{10,18},{12,20},{14,22},{16,8},... | collective-permute-start | bytes 1179656 | tf_op jit(solution)/shard_map/grad_w_far/ppermute | solution.py:437
  92.1 10.2 %collective-permute-start.19 = (bf16[4,192,256]{2,1,0:T(8,128)(2,1)S(1)}, bf16[4,192,256]{2,1,0:T(8,128)(2,1)S(1)}, u32[]{:S(2)}, u32[]{:S(2)}) collective-permute-start(bf16[4,192,256]{2,1,0:T(8,128)(2,1)S(1)} %get-tuple-element.146), channel_id=1, source_target_pairs={{0,1},{1,0},{2,3},{3,2},{4,5},{5,4},{6,7},{7,6},{8,9},{9,8},{10,11... | collective-permute-start | bytes 1179656 | tf_op jit(solution)/shard_map/products_seq/ppermute | solution.py:442
  102.4 1.9 %collective-permute-start.21 = (bf16[256,1024]{1,0:T(8,128)(2,1)S(1)}, bf16[256,1024]{1,0:T(8,128)(2,1)S(1)}, u32[]{:S(2)}, u32[]{:S(2)}) collective-permute-start(bf16[256,1024]{1,0:T(8,128)(2,1)S(1)} %collective-permute-done.17.refs_5_.refs_6_), channel_id=1, source_target_pairs={{0,2},{2,0},{4,6},{6,4},{8,10},{10,8},{12,14},{14,12},{16,18},{18,... | collective-permute-start | bytes 1572872 | tf_op jit(solution)/shard_map/gy_core/ppermute | solution.py:437
  102.4 13.4 %collective-permute-start.20 = (bf16[192,1024]{1,0:T(8,128)(2,1)S(1)}, bf16[192,1024]{1,0:T(8,128)(2,1)S(1)}, u32[]{:S(2)}, u32[]{:S(2)}) collective-permute-start(bf16[192,1024]{1,0:T(8,128)(2,1)S(1)} %get-tuple-element.148), channel_id=1, source_target_pairs={{0,24},{2,26},{4,28},{6,30},{8,16},{10,18},{12,20},{14,22},{16,8},... | collective-permute-start | bytes 1179656 | tf_op jit(solution)/shard_map/grad_w_far/ppermute | solution.py:437
  107.6 1.8 %collective-permute-start.22 = (bf16[2,192,256]{2,1,0:T(8,128)(2,1)S(1)}, bf16[2,192,256]{2,1,0:T(8,128)(2,1)S(1)}, u32[]{:S(2)}, u32[]{:S(2)}) collective-permute-start(bf16[2,192,256]{2,1,0:T(8,128)(2,1)S(1)} %slice.81), channel_id=1, source_target_pairs={{0,2},{2,0},{4,6},{6,4},{8,10},{10,8},{12,14},{14,12},{16,18},{18,... | collective-permute-start | bytes 589832 | tf_op jit(solution)/shard_map/products_core/ppermute | solution.py:437
  107.8 11.4 %collective-permute-start.24 = (bf16[4,192,256]{2,1,0:T(8,128)(2,1)S(1)}, bf16[4,192,256]{2,1,0:T(8,128)(2,1)S(1)}, u32[]{:S(2)}, u32[]{:S(2)}) collective-permute-start(bf16[4,192,256]{2,1,0:T(8,128)(2,1)S(1)} %get-tuple-element.158), channel_id=1, source_target_pairs={{0,1},{1,0},{2,3},{3,2},{4,5},{5,4},{6,7},{7,6},{8,9},{9,8},{10,11... | collective-permute-start | bytes 1179656 | tf_op jit(solution)/shard_map/products_seq/ppermute | solution.py:442
  109.5 6.9 %collective-permute-start.23 = (bf16[2,192,256]{2,1,0:T(8,128)(2,1)S(1)}, bf16[2,192,256]{2,1,0:T(8,128)(2,1)S(1)}, u32[]{:S(2)}, u32[]{:S(2)}) collective-permute-start(bf16[2,192,256]{2,1,0:T(8,128)(2,1)S(1)} %pad_maximum_fusion.10), channel_id=1, source_target_pairs={{0,4},{2,6},{4,0},{6,2},{8,12},{10,14},{12,8},{14,10},{16,20},{18,... | collective-permute-start | bytes 589832 | tf_op jit(solution)/shard_map/products_group/ppermute | solution.py:437
  119.4 4.0 %collective-permute-start.25 = (bf16[2,192,256]{2,1,0:T(8,128)(2,1)S(1)}, bf16[2,192,256]{2,1,0:T(8,128)(2,1)S(1)}, u32[]{:S(2)}, u32[]{:S(2)}) collective-permute-start(bf16[2,192,256]{2,1,0:T(8,128)(2,1)S(1)} %slice.86), channel_id=1, source_target_pairs={{0,2},{2,0},{4,6},{6,4},{8,10},{10,8},{12,14},{14,12},{16,18},{18,... | collective-permute-start | bytes 589832 | tf_op jit(solution)/shard_map/products_core/ppermute | solution.py:437
  119.4 17.1 %collective-permute-start.28 = (bf16[192,512]{1,0:T(8,128)(2,1)S(1)}, bf16[192,512]{1,0:T(8,128)(2,1)S(1)}, u32[]{:S(2)}, u32[]{:S(2)}) collective-permute-start(bf16[192,512]{1,0:T(8,128)(2,1)S(1)} %get-tuple-element.187), channel_id=1, source_target_pairs={{0,24},{2,26},{4,28},{6,30},{8,16},{10,18},{12,20},{14,22},{16,8},... | collective-permute-start | bytes 589832 | tf_op jit(solution)/shard_map/grad_w_far/ppermute | solution.py:437
  121.4 15.2 %collective-permute-start.29 = (bf16[192,512]{1,0:T(8,128)(2,1)S(1)}, bf16[192,512]{1,0:T(8,128)(2,1)S(1)}, u32[]{:S(2)}, u32[]{:S(2)}) collective-permute-start(bf16[192,512]{1,0:T(8,128)(2,1)S(1)} %get-tuple-element.188), channel_id=1, source_target_pairs={{0,24},{2,26},{4,28},{6,30},{8,16},{10,18},{12,20},{14,22},{16,8},... | collective-permute-start | bytes 589832 | tf_op jit(solution)/shard_map/grad_w_far/ppermute | solution.py:437
  123.3 6.0 %copy-start.3 = (bf16[2,12,256,128]{3,2,1,0:T(8,128)(2,1)S(1)}, bf16[2,12,256,128]{3,2,1,0:T(8,128)(2,1)}, u32[]{:S(2)}) copy-start(bf16[2,12,256,128]{3,2,1,0:T(8,128)(2,1)} %get-tuple-element.101.low_ref) | copy-start | bytes 4718596
  123.4 14.2 %collective-permute-start.27 = (bf16[2,192,256]{2,1,0:T(8,128)(2,1)S(1)}, bf16[2,192,256]{2,1,0:T(8,128)(2,1)S(1)}, u32[]{:S(2)}, u32[]{:S(2)}) collective-permute-start(bf16[2,192,256]{2,1,0:T(8,128)(2,1)S(1)} %pad_maximum_fusion.12), channel_id=1, source_target_pairs={{0,12},{2,14},{4,8},{6,10},{8,4},{10,6},{12,0},{14,2},{16,28},{18,... | collective-permute-start | bytes 589832 | tf_op jit(solution)/shard_map/products_group/ppermute | solution.py:437
  127.4 13.9 %collective-permute-start.26 = (bf16[2,192,256]{2,1,0:T(8,128)(2,1)S(1)}, bf16[2,192,256]{2,1,0:T(8,128)(2,1)S(1)}, u32[]{:S(2)}, u32[]{:S(2)}) collective-permute-start(bf16[2,192,256]{2,1,0:T(8,128)(2,1)S(1)} %pad_maximum_fusion.11), channel_id=1, source_target_pairs={{0,8},{2,10},{4,12},{6,14},{8,0},{10,2},{12,4},{14,6},{16,24},{18,... | collective-permute-start | bytes 589832 | tf_op jit(solution)/shard_map/products_group/ppermute | solution.py:437
  127.4 2.5 %copy-start.2 = (f32[2,12,256,128]{3,2,1,0:T(8,128)S(1)}, f32[2,12,256,128]{3,2,1,0:T(8,128)}, u32[]{:S(2)}) copy-start(f32[2,12,256,128]{3,2,1,0:T(8,128)} %get-tuple-element.100.inv_ref) | copy-start | bytes 9437188
  127.5 2.6 %copy-start.4 = (bf16[12,256,128]{2,1,0:T(8,128)(2,1)S(1)}, bf16[12,256,128]{2,1,0:T(8,128)(2,1)}, u32[]{:S(2)}) copy-start(bf16[12,256,128]{2,1,0:T(8,128)(2,1)} %get-tuple-element.103.v_ref) | copy-start | bytes 2359300
  128.4 2.9 %copy-start = (f32[12,256,256]{2,1,0:T(8,128)S(1)}, f32[12,256,256]{2,1,0:T(8,128)}, u32[]{:S(2)}) copy-start(f32[12,256,256]{2,1,0:T(8,128)} %get-tuple-element.98.p_ref) | copy-start | bytes 9437188
  128.4 3.7 %copy-start.1 = (f32[2,12,256,128]{3,2,1,0:T(8,128)S(1)}, f32[2,12,256,128]{3,2,1,0:T(8,128)}, u32[]{:S(2)}) copy-start(f32[2,12,256,128]{3,2,1,0:T(8,128)} %get-tuple-element.99.hat_ref) | copy-start | bytes 9437188
